TPU v7x, 32 devices: a whole 2x2x4 slice. The times are simulated.
32 devices in a mesh: tok: 4 (over y, x), col: 8 (over z, core).
Axes of the slice: x: 2, y: 2, z: 4, core: 2. Of those that a mesh axis runs over, the one named last changes fastest.
Arguments:
- tokens: bfloat16 [512, 8192], P('tok', 'col'), may hold values from -36 to 36, as said below
- norm_gain: float32 [8192], replicated, may hold values from 0.1 to 1.9
- gate_block_entries: bfloat16 [4, 1728, 128, 128], P('tok', 'col'), may hold values from -0.09375 to 0.09375
- gate_block_places: int32 [4, 1728], P('tok', 'col'), may hold values from -1 to 383, as said below
- up_block_entries: bfloat16 [4, 1728, 128, 128], P('tok', 'col'), may hold values from -0.09375 to 0.09375
- up_block_places: int32 [4, 1728], P('tok', 'col'), may hold values from -1 to 383, as said below
- down_values: bfloat16 [8, 864, 128, 128], P(None, 'col'), may hold values from -0.0546875 to 0.0546875
- down_slots: int32 [8, 864], P(None, 'col'), may hold values from -1 to 191, as said below
Outputs:
- mixed: bfloat16 [512, 8192], P('tok', 'col')
Inputs may be any that keep to these rules, and one draw needn't show every extreme that they name: `tokens`: entries are bounded by construction. `gate_block_places`: A panel is one index of the first dimension and 216 consecutive entries of the second. Its entries that are not -1 are distinct block positions, -1 marks an unused entry; a panel lists at most 216 blocks, and some panel lists exactly 216 in every draw. `up_block_places`: as for gate_block_places, with its own draw. `down_slots`: A panel is one index of the first dimension and 108 consecutive entries of the second. Its entries that are not -1 are distinct block positions, -1 marks an unused entry; a panel lists at most 108 blocks, and some panel lists exactly 108 in every draw.
All inputs are finite; a program needn't handle non-finite values.
Results may differ from a plain program's by a relative error of at most 0.0065.
Values may be sent and summed in bfloat16 or wider, within the bound.
No kernel may reach another device: no remote copies, remote signals or barrier semaphores. Data moves between devices by JAX's collectives and lax.ppermute only.
A program may use at most 320 MiB of HBM per device.

v0:
```python
import jax
import jax.numpy as jnp
from jax import lax
from jax.sharding import PartitionSpec as P

MODEL_WIDTH = 8192
HIDDEN_UNITS = 24576


EPSILON = 1e-05


def dense_panel(values, slot_ids, rows_per, cols_per):
    panel_count, capacity = slot_ids.shape
    block_edge = values.shape[-1]
    listed = slot_ids >= 0
    clipped = jnp.where(listed, slot_ids, 0)
    panels = jnp.arange(panel_count, dtype=jnp.int32)[:, None]
    block_rows = jnp.where(
        listed, panels * rows_per + clipped // cols_per, panel_count * rows_per
    ).reshape(-1)
    block_cols = (clipped % cols_per).reshape(-1)
    blocks = jnp.zeros((panel_count * rows_per, cols_per, block_edge, block_edge), values.dtype)
    blocks = blocks.at[block_rows, block_cols].set(
        values.reshape(panel_count * capacity, block_edge, block_edge), mode="drop"
    )
    return blocks.transpose(0, 2, 1, 3).reshape(
        panel_count * rows_per * block_edge, cols_per * block_edge
    )


def shards(
    tokens,
    norm_gain,
    gate_block_entries,
    gate_block_places,
    up_block_entries,
    up_block_places,
    down_values,
    down_slots,
):
    block_edge = gate_block_entries.shape[-1]
    tok_size = lax.axis_size("tok")
    col_size = lax.axis_size("col")
    rows_per = MODEL_WIDTH // block_edge // tok_size
    cols_per = HIDDEN_UNITS // block_edge // col_size
    ff_blocks = HIDDEN_UNITS // block_edge // col_size
    width_blocks = MODEL_WIDTH // block_edge // col_size
    gathered = lax.all_gather(tokens, "col", axis=1, tiled=True)
    widened = gathered.astype(jnp.float32)
    mean_square = jnp.mean(widened * widened, axis=1, keepdims=True)
    normed = (widened * lax.rsqrt(mean_square + EPSILON) * norm_gain).astype(jnp.bfloat16)
    gate_part = lax.all_gather(gate_block_entries, "tok", axis=0, tiled=True)
    gate_ids = lax.all_gather(gate_block_places, "tok", axis=0, tiled=True)
    up_part = lax.all_gather(up_block_entries, "tok", axis=0, tiled=True)
    up_ids = lax.all_gather(up_block_places, "tok", axis=0, tiled=True)
    gate_dense = dense_panel(gate_part, gate_ids, rows_per, cols_per)
    up_dense = dense_panel(up_part, up_ids, rows_per, cols_per)
    gate_sum = jnp.dot(normed, gate_dense, preferred_element_type=jnp.float32)
    up_sum = jnp.dot(normed, up_dense, preferred_element_type=jnp.float32)
    hidden = (jax.nn.silu(gate_sum) * up_sum).astype(jnp.bfloat16)
    down_dense = dense_panel(down_values, down_slots, ff_blocks, width_blocks)
    summed = jnp.dot(
        lax.all_gather(hidden, "col", axis=1, tiled=True),
        down_dense,
        preferred_element_type=jnp.float32,
    )
    mixed = summed.astype(jnp.bfloat16)
    return mixed


def solution(mesh):
    return jax.shard_map(
        shards,
        mesh=mesh,
        in_specs=(
            P("tok", "col"),
            P(),
            P("tok", "col", None, None),
            P("tok", "col"),
            P("tok", "col", None, None),
            P("tok", "col"),
            P(None, "col", None, None),
            P(None, "col"),
        ),
        out_specs=P("tok", "col"),
        check_vma=False,
    )
```

profile of v0, /device:TPU:0, one launch (start us, length us, event | category | flops | bytes accessed | tf_op | source)
XLA Modules:
  0.0 1035.6 jit_solution(14295101396365847604)
XLA Ops:
  6.5 0.7 all-gather.7.cloned.1.call-update
  7.3 0.0 all-gather.9.cloned.1.call-start
  7.3 0.7 all-gather.9.cloned.1.call-update
  8.0 0.0 all-gather.11.cloned.1.call-start
  8.1 0.7 all-gather.11.cloned.1.call-update
  8.7 0.0 all-gather.13.cloned.1.call-start
  8.8 9.6 all-gather
  18.4 7.9 all-gather.1
  26.3 0.1 compare_select_fusion.10
  26.4 0.1 reshape.223
  26.5 0.1 reshape.224
  26.6 0.1 reshape.227
  26.7 0.1 reshape.228
  26.8 14.0 %all-gather.7.cloned.1.call-done = bf16[128,8192]{1,0:T(8,128)(2,1)} async-done(((bf16[128,1024]{1,0:T(8,128)(2,1)}), bf16[128,8192]{1,0:T(8,128)(2,1)}) %all-gather.7.cloned.1.call-update) | async-done | bytes 2097168 | tf_op jit(solution)/shard_map/all_gather | solution.py:49
  40.8 2.1 fusion.9
  42.9 252.9 %all-gather.9.cloned.1.call-done = bf16[4,216,128,128]{3,2,1,0:T(8,128)(2,1)} async-done(((bf16[1,216,128,128]{3,2,1,0:T(8,128)(2,1)}), bf16[4,216,128,128]{3,2,1,0:T(8,128)(2,1)}) %all-gather.9.cloned.1.call-update) | async-done | bytes 28311568 | tf_op jit(solution)/shard_map/all_gather | solution.py:53
  295.8 22.9 %broadcast.143.clone.1 = bf16[64,24,128,128]{3,2,1,0:T(8,128)(2,1)} broadcast(bf16[]{:T(256)} %constant.67.clone.1), dimensions={} | broadcast | bytes 50331648 | tf_op jit(solution)/shard_map/broadcast.17
  318.7 136.4 %scatter_fusion = bf16[64,24,128,128]{3,2,1,0:T(8,128)(2,1)} fusion(bf16[64,24,128,128]{3,2,1,0:T(8,128)(2,1)} %broadcast.143.clone.1, s32[864]{0:T(1024)S(1)} %fusion.32, bf16[864,128,128]{2,1,0:T(8,128)(2,1)} %bitcast.68), kind=kCustom, calls=%fused_computation | custom fusion | bytes 84941568 | tf_op jit(solution)/shard_map/scatter | solution.py:24
  455.0 53.4 %copy.15 = bf16[64,128,24,128]{3,2,1,0:T(8,128)(2,1)} copy(bf16[64,128,24,128]{3,1,2,0:T(8,128)(2,1)} %bitcast.60) | data formatting | bytes 100663296 | tf_op jit(solution)/shard_map/transpose | solution.py:27
  508.4 42.9 %all-gather.11.cloned.1.call-done = bf16[4,216,128,128]{3,2,1,0:T(8,128)(2,1)} async-done(((bf16[1,216,128,128]{3,2,1,0:T(8,128)(2,1)}), bf16[4,216,128,128]{3,2,1,0:T(8,128)(2,1)}) %all-gather.11.cloned.1.call-update) | async-done | bytes 28311568 | tf_op jit(solution)/shard_map/all_gather | solution.py:55
  551.3 16.3 %broadcast.143.clone = bf16[64,24,128,128]{3,2,1,0:T(8,128)(2,1)} broadcast(bf16[]{:T(256)} %constant.67.clone.1), dimensions={} | broadcast | bytes 50331648 | tf_op jit(solution)/shard_map/broadcast.17
  567.6 134.3 %scatter_fusion.1 = bf16[64,24,128,128]{3,2,1,0:T(8,128)(2,1)} fusion(bf16[64,24,128,128]{3,2,1,0:T(8,128)(2,1)} %broadcast.143.clone, s32[864]{0:T(1024)S(1)} %fusion.33, bf16[864,128,128]{2,1,0:T(8,128)(2,1)} %bitcast.67), kind=kCustom, calls=%fused_computation.1 | custom fusion | bytes 84941568 | tf_op jit(solution)/shard_map/scatter | solution.py:24
  701.9 53.5 %copy.16 = bf16[64,128,24,128]{3,2,1,0:T(8,128)(2,1)} copy(bf16[64,128,24,128]{3,1,2,0:T(8,128)(2,1)} %bitcast.61) | data formatting | bytes 100663296 | tf_op jit(solution)/shard_map/transpose | solution.py:27
  755.4 23.3 %fusion.6 = f32[128,3072]{1,0:T(8,128)} fusion(bf16[1024,8,24,128]{3,2,1,0:T(8,128)(2,1)} %bitcast.63, bf16[128,8192]{1,0:T(8,128)(2,1)S(1)} %copy-done, f32[8192]{0:T(1024)S(1)} %copy-done.2, f32[128]{0:T(128)S(1)} %add_rsqrt_fusion), kind=kOutput, calls=%fused_computation.9 | convolution fusion | flops 6446645248 | bytes 54034944 | tf_op jit(solution)/shard_map/dot_general | solution.py:59
  778.7 23.9 %fusion.15 = bf16[128,3072]{1,0:T(8,128)(2,1)} fusion(bf16[1024,8,24,128]{3,2,1,0:T(8,128)(2,1)} %bitcast.65, f32[128,3072]{1,0:T(8,128)} %fusion.6, bf16[128,8192]{1,0:T(8,128)(2,1)S(1)} %copy-done, f32[8192]{0:T(1024)S(1)} %copy-done.2, f32[128]{0:T(128)S(1)} %add_rsqrt_fusion), kind=kOutput, calls=%fused_computation.18 | convolution fusion | flops 6449004544 | bytes 54821376 | tf_op jit(solution)/shard_map/dot_general | solution.py:60
  802.6 0.1 compare_select_fusion.6
  802.7 0.1 reshape.231
  802.8 0.1 reshape.232
  802.9 16.9 %broadcast_in_dim.15 = bf16[192,8,128,128]{3,2,1,0:T(8,128)(2,1)} broadcast(bf16[]{:T(256)} %constant.67.clone.1), dimensions={} | broadcast | bytes 50331648 | tf_op jit(solution)/shard_map/broadcast_in_dim | solution.py:23
  819.8 134.7 %scatter_fusion.2 = bf16[192,8,128,128]{3,2,1,0:T(8,128)(2,1)} fusion(bf16[192,8,128,128]{3,2,1,0:T(8,128)(2,1)} %broadcast_in_dim.15, s32[864]{0:T(1024)S(1)} %fusion.34, bf16[864,128,128]{2,1,0:T(8,128)(2,1)} %bitcast.66), kind=kCustom, calls=%fused_computation.2 | custom fusion | bytes 84941568 | tf_op jit(solution)/shard_map/scatter | solution.py:24
  954.5 49.7 %copy.17 = bf16[192,128,8,128]{3,2,1,0:T(8,128)(2,1)} copy(bf16[192,128,8,128]{3,1,2,0:T(8,128)(2,1)} %bitcast.62) | data formatting | bytes 100663296 | tf_op jit(solution)/shard_map/transpose | solution.py:27
  1004.2 24.9 %fusion.18 = bf16[128,1024]{1,0:T(8,128)(2,1)} fusion(bf16[128,24576]{1,0:T(8,128)(2,1)} %all-gather.13.cloned.1.call-done, bf16[3072,8,8,128]{3,2,1,0:T(8,128)(2,1)} %bitcast.64), kind=kOutput, calls=%fused_computation.19 | convolution fusion | flops 6442582016 | bytes 56885248 | tf_op jit(solution)/shard_map/dot_general | solution.py:63
  (15 shorter events, 0.1 us)
Async XLA Ops:
  6.5 34.3 %all-gather.7.cloned.1.call-start = ((), (), s32[]{:S(2)}) async-start(), calls=%async_computation | async-start | bytes 2359296 | tf_op jit(solution)/shard_map/all_gather | solution.py:49
  7.3 288.5 %all-gather.9.cloned.1.call-start = ((), (), s32[]{:S(2)}) async-start(), calls=%async_computation.1 | async-start | bytes 35389440 | tf_op jit(solution)/shard_map/all_gather | solution.py:53
  8.0 543.3 %all-gather.11.cloned.1.call-start = ((), (), s32[]{:S(2)}) async-start(), calls=%async_computation.2 | async-start | bytes 35389440 | tf_op jit(solution)/shard_map/all_gather | solution.py:55
  8.7 995.4 %all-gather.13.cloned.1.call-start = ((), (), s32[]{:S(2)}) async-start(), calls=%async_computation.3 | async-start | bytes 7077888 | tf_op jit(solution)/shard_map/all_gather | solution.py:64
  701.9 53.5 %copy-start = (bf16[128,8192]{1,0:T(8,128)(2,1)S(1)}, bf16[128,8192]{1,0:T(8,128)(2,1)}, u32[]{:S(2)}) copy-start(bf16[128,8192]{1,0:T(8,128)(2,1)} %all-gather.7.cloned.1.call-done) | copy-start | bytes 6291460
  701.9 53.5 %copy-start.2 = (f32[8192]{0:T(1024)S(1)}, f32[8192]{0:T(1024)}, u32[]{:S(2)}) copy-start(f32[8192]{0:T(1024)} %param.9) | copy-start | bytes 98308
  778.7 23.9 %copy-start.1 = (s32[8,108]{1,0:T(8,128)S(1)}, s32[8,108]{1,0:T(8,128)}, u32[]{:S(2)}) copy-start(s32[8,108]{1,0:T(8,128)} %param.15) | copy-start | bytes 10372
Sparse Core Ops, SparseCore 0:
  9.0 31.7 all-gather.6
  42.7 253.0 all-gather.8
  297.7 253.5 all-gather.10
  802.7 64.8 all-gather.12
where the time goes:
time: 1040 us
  local copies, waits for them, and re-layouts  618 us (59%)
  waiting for transfers between devices  312 us (30%)
  matrix products  72 us (7%)
  blocking collectives  17.5 us (2%)
  between operations  13.2 us (1%)
    scatter x3, local copies, waits for them, and re-layouts, dense_panel(): blocks.at[block_rows, block_cols]  405 us
    all_gather x1, waiting for transfers between devices, shards(): gate_part = lax.all_gather(gate_block_entries, 'tok', axis=0, tiled=True)  253 us
    transpose x3, local copies, waits for them, and re-layouts, dense_panel(): blocks.transpose(0, 2, 1, 3)  156 us
    all_gather x1, waiting for transfers between devices, shards(): up_part = lax.all_gather(up_block_entries, 'tok', axis=0, tiled=True)  42.9 us
    another operation x2, local copies, waits for them, and re-layouts  39.2 us
    dot_general x1, matrix products, shards(): jnp.dot(lax.all_gather(hidden, 'col', axis=1, tiled=True), down_dense, pr...  24.9 us
    dot_general x1, matrix products, shards(): up_sum = jnp.dot(normed, up_dense, preferred_element_type=jnp.float32)  23.9 us
    dot_general x1, matrix products, shards(): gate_sum = jnp.dot(normed, gate_dense, preferred_element_type=jnp.float32)  23.3 us
  transfers between devices with their start and end apart: 4, of which 3 were waited for; matrix products, arithmetic and copies ran while one was open for 40% of the time, Pallas kernels for 0%

commit v1 on v0

v1 whole, which is shorter than its diff:
```python
import functools

import jax
import jax.numpy as jnp
from jax import lax
from jax.experimental import pallas as pl
from jax.experimental.pallas import tpu as pltpu
from jax.sharding import PartitionSpec as P

MODEL_WIDTH = 8192
HIDDEN_UNITS = 24576

EPSILON = 1e-05
MIB = 1 << 20


def lookup(places, slots):
    hit = places[..., None, :] == slots[:, None]
    entry = jnp.arange(places.shape[-1], dtype=jnp.int32)
    return jnp.max(jnp.where(hit, entry, -1), axis=-1)


def put(out_ref, row, col, source_ref, entry):
    edge = source_ref.shape[-1]
    block = source_ref[0, jnp.maximum(entry, 0)]
    block = jnp.where(entry >= 0, block, jnp.zeros_like(block))
    out_ref[0, pl.ds(pl.multiple_of(row * edge, edge), edge), col * edge:(col + 1) * edge] = block


def spread_gate_up_kernel(gate_at, up_at, gate_ref, up_ref, out_ref, *, rows, cols):
    chunk = pl.program_id(0)

    @pl.loop(0, rows)
    def _(row):
        for col in range(cols):
            at = (chunk * rows + row) * cols + col
            put(out_ref, row, col, gate_ref, gate_at[at])
            put(out_ref, row, cols + col, up_ref, up_at[at])


def spread_gate_up(gate_at, up_at, gate, up, chunks, rows, cols):
    edge = gate.shape[-1]
    whole = pl.BlockSpec(gate.shape, lambda k, *_: (0, 0, 0, 0), pipeline_mode=pl.Buffered(1))
    out = jax.ShapeDtypeStruct((chunks, rows * edge, 2 * cols * edge), gate.dtype)
    return pl.pallas_call(
        functools.partial(spread_gate_up_kernel, rows=rows, cols=cols),
        out_shape=out,
        grid_spec=pltpu.PrefetchScalarGridSpec(
            num_scalar_prefetch=2,
            grid=(chunks,),
            in_specs=[whole, whole],
            out_specs=pl.BlockSpec((1,) + out.shape[1:], lambda k, *_: (k, 0, 0)),
        ),
        compiler_params=pltpu.CompilerParams(vmem_limit_bytes=48 * MIB),
        cost_estimate=pl.CostEstimate(
            flops=0, bytes_accessed=2 * (2 * gate.size + out.size), transcendentals=0
        ),
        name="spread_gate_up",
    )(gate_at, up_at, gate, up)


def spread_down_kernel(at_ref, values_ref, out_ref, *, rows, cols):
    panel, chunk = pl.program_id(0), pl.program_id(1)
    base = (panel * pl.num_programs(1) + chunk) * rows * cols

    @pl.loop(0, rows)
    def _(row):
        for col in range(cols):
            put(out_ref.at[0], row, col, values_ref, at_ref[base + row * cols + col])


def spread_down(at, values, chunks, rows, cols):
    panels, _, edge, _ = values.shape
    out = jax.ShapeDtypeStruct((chunks, panels, rows * edge, cols * edge), values.dtype)
    return pl.pallas_call(
        functools.partial(spread_down_kernel, rows=rows, cols=cols),
        out_shape=out,
        grid_spec=pltpu.PrefetchScalarGridSpec(
            num_scalar_prefetch=1,
            grid=(panels, chunks),
            in_specs=[pl.BlockSpec((1,) + values.shape[1:], lambda g, k, *_: (g, 0, 0, 0))],
            out_specs=pl.BlockSpec((1, 1) + out.shape[2:], lambda g, k, *_: (k, g, 0, 0)),
        ),
        compiler_params=pltpu.CompilerParams(vmem_limit_bytes=48 * MIB),
        cost_estimate=pl.CostEstimate(
            flops=0, bytes_accessed=2 * (values.size + out.size), transcendentals=0
        ),
        name="spread_down",
    )(at, values)


def gate_up_kernel(*refs, parts):
    own, other = refs[:parts], refs[parts:2 * parts]
    weight = refs[2 * parts]
    outs, held = refs[2 * parts + 1:3 * parts + 1], refs[-1]
    count, half = own[0].shape

    @pl.when(pl.program_id(0) == 0)
    def _():
        for part in range(parts):
            rows = slice(part * count, (part + 1) * count)
            held[rows, :half] = own[part][...]
            held[rows, half:] = other[part][...]

    product = jnp.dot(held[...], weight[0], preferred_element_type=jnp.float32)
    for part in range(parts):
        outs[part][...] = product[part * count:(part + 1) * count].astype(outs[part].dtype)


def gate_up(own, other, dense, chunk):
    parts = len(own)
    count, half = own[0].shape
    _, depth, width = dense.shape
    tile = 256
    out = jax.ShapeDtypeStruct((count, width), own[0].dtype)
    return pl.pallas_call(
        functools.partial(gate_up_kernel, parts=parts),
        out_shape=[out] * parts,
        grid=(width // tile,),
        in_specs=[pl.BlockSpec((count, half), lambda n: (0, 0))] * (2 * parts)
        + [pl.BlockSpec((1, depth, tile), lambda n: (chunk, 0, n))],
        out_specs=[pl.BlockSpec((count, tile), lambda n: (0, n))] * parts,
        scratch_shapes=[pltpu.VMEM((parts * count, 2 * half), own[0].dtype)],
        compiler_params=pltpu.CompilerParams(vmem_limit_bytes=32 * MIB),
        cost_estimate=pl.CostEstimate(
            flops=2 * parts * count * depth * width,
            bytes_accessed=2 * (depth * width + parts * count * (depth + width)),
            transcendentals=0,
        ),
        name=f"gate_up_{chunk}",
    )(*own, *other, dense)


def down_kernel(hidden_ref, weight_ref, before_ref, out_ref, total):
    panel = pl.program_id(0)

    @pl.when(panel == 0)
    def _():
        total[...] = before_ref[...]

    total[...] += jnp.dot(hidden_ref[0], weight_ref[0, 0], preferred_element_type=jnp.float32)

    @pl.when(panel == pl.num_programs(0) - 1)
    def _():
        out_ref[...] = total[...].astype(out_ref.dtype)


def down(hidden, dense, before, chunk, dtype):
    panels, count, depth = hidden.shape
    width = dense.shape[-1]
    return pl.pallas_call(
        down_kernel,
        out_shape=jax.ShapeDtypeStruct((count, width), dtype),
        grid=(panels,),
        in_specs=[
            pl.BlockSpec((1, count, depth), lambda g: (g, 0, 0)),
            pl.BlockSpec((1, 1, depth, width), lambda g: (chunk, g, 0, 0)),
            pl.BlockSpec((count, width), lambda g: (0, 0)),
        ],
        out_specs=pl.BlockSpec((count, width), lambda g: (0, 0)),
        scratch_shapes=[pltpu.VMEM((count, width), jnp.float32)],
        compiler_params=pltpu.CompilerParams(vmem_limit_bytes=32 * MIB),
        cost_estimate=pl.CostEstimate(
            flops=2 * panels * count * depth * width,
            bytes_accessed=2 * panels * depth * (width + count) + 6 * count * width,
            transcendentals=0,
        ),
        name=f"down_{chunk}",
    )(hidden, dense, before)


def shards(
    tokens,
    norm_gain,
    gate_block_entries,
    gate_block_places,
    up_block_entries,
    up_block_places,
    down_values,
    down_slots,
):
    edge = gate_block_entries.shape[-1]
    tok_size = lax.axis_size("tok")
    col_size = lax.axis_size("col")
    rows_per = MODEL_WIDTH // edge // tok_size
    cols_per = HIDDEN_UNITS // edge // col_size
    width_blocks = MODEL_WIDTH // edge // col_size
    chunks = 4 if cols_per % 4 == 0 else 1
    chunk_cols = cols_per // chunks
    count, features = tokens.shape
    half = MODEL_WIDTH // tok_size // 2
    tok, col = lax.axis_index("tok"), lax.axis_index("col")
    side = col % 2

    def swap_tok(array, step):
        return lax.ppermute(array, "tok", [(i, i ^ step) for i in range(tok_size)])

    def swap_core(array):
        return lax.ppermute(array, "col", [(i, i ^ 1) for i in range(col_size)])

    k, r, q = jnp.meshgrid(
        jnp.arange(chunks), jnp.arange(rows_per), jnp.arange(chunk_cols), indexing="ij"
    )
    row = (r + side * (rows_per // 2)) % rows_per
    slots = (row * cols_per + k * chunk_cols + q).reshape(-1).astype(jnp.int32)
    gate_at = lookup(gate_block_places[0], slots)
    up_at = lookup(up_block_places[0], slots)
    down_at = lookup(down_slots, jnp.arange(cols_per * width_blocks, dtype=jnp.int32)).reshape(-1)

    gathered = lax.all_gather(tokens, "col")
    dense = spread_gate_up(
        gate_at, up_at, gate_block_entries, up_block_entries, chunks, rows_per, chunk_cols
    )
    down_dense = spread_down(down_at, down_values, chunks, chunk_cols, width_blocks)

    widened = gathered.astype(jnp.float32)
    mean_square = jnp.mean(widened * widened, axis=(0, 2))[:, None]
    scale = lax.rsqrt(mean_square + EPSILON)
    subs = half // features

    def normed(panel):
        at = panel * 2 + side
        piece = lax.dynamic_slice_in_dim(gathered, at * subs, subs, 0)
        piece = piece.transpose(1, 0, 2).reshape(count, half).astype(jnp.float32)
        gain = lax.dynamic_slice_in_dim(norm_gain, at * half, half, 0)
        return (piece * scale * gain).astype(jnp.bfloat16)

    own = [normed(tok ^ part) for part in range(tok_size)]
    own = [own[0]] + [swap_tok(own[part], part) for part in range(1, tok_size)]
    other = [swap_core(part) for part in own]

    hiddens = []
    for chunk in range(chunks):
        sums = gate_up(own, other, dense, chunk)
        terms = [sums[0]] + [swap_tok(sums[part], part) for part in range(1, tok_size)]
        total = functools.reduce(jnp.add, [term.astype(jnp.float32) for term in terms])
        gate_sum, up_sum = jnp.split(total, 2, axis=1)
        hiddens.append((jax.nn.silu(gate_sum) * up_sum).astype(jnp.bfloat16))

    mixed = jnp.zeros((count, width_blocks * edge), jnp.float32)
    for chunk in range(chunks):
        hidden = lax.all_gather(hiddens[chunk], "col")
        last = chunk == chunks - 1
        mixed = down(hidden, down_dense, mixed, chunk, jnp.bfloat16 if last else jnp.float32)
    return mixed


def solution(mesh):
    return jax.shard_map(
        shards,
        mesh=mesh,
        in_specs=(
            P("tok", "col"),
            P(),
            P("tok", "col", None, None),
            P("tok", "col"),
            P("tok", "col", None, None),
            P("tok", "col"),
            P(None, "col", None, None),
            P(None, "col"),
        ),
        out_specs=P("tok", "col"),
        check_vma=False,
    )
```

time: 1040 us -> 275 us (0.26)
  local copies, waits for them, and re-layouts: 618 us -> 7.04 us
  waiting for transfers between devices: 312 us -> 105 us
  Pallas kernels: 0 us -> 121 us
  matrix products: 72 us -> 0 us
  starting transfers between devices: 0.12 us -> 18.5 us
  blocking collectives: 17.5 us -> 0 us
    scatter x3 -> x0, local copies, waits for them, and re-layouts: 405 us -> none  [dense_panel(): blocks.at[block_rows, block_cols]]
    all_gather x4 -> x5, waiting for transfers between devices: 310 us -> 32.7 us  [the longest x1 32.7 us: shards(): gathered = lax.all_gather(tokens, 'col')]
    transpose x3 -> x0, local copies, waits for them, and re-layouts: 156 us -> none  [dense_panel(): blocks.transpose(0, 2, 1, 3)]
    pallas_call x0 -> x10, Pallas kernels: none -> 121 us  [the longest x1 43.9 us: spread_down(): pl.pallas_call(functools.partial(spread_down_kernel, rows=rows, cols=cols...]
    dot_general x3 -> x0, matrix products: 72 us -> none  [the longest x1 24.9 us: shards(): jnp.dot(lax.all_gather(hidden, 'col', axis=1, tiled=True), down_dense, pr...]
    ppermute x0 -> x19, waiting for transfers between devices: none -> 71.6 us  [the longest x15 71.6 us: swap_tok(): return lax.ppermute(array, 'tok', [(i, i ^ step) for i in range(tok_size)])]
    another operation x2 -> x0, local copies, waits for them, and re-layouts: 39.2 us -> none
    ppermute x0 -> x19, starting transfers between devices: none -> 18.3 us  [the longest x15 17.8 us: swap_tok(): return lax.ppermute(array, 'tok', [(i, i ^ step) for i in range(tok_size)])]
  transfers between devices with their start and end apart: 4 -> 24, of which waited for: 3 -> 11; matrix products, arithmetic and copies ran while one was open for 40% -> 2% of each run, Pallas kernels for 0% -> 39%
where the time goes in v1:
time: 275 us; the launch traced here: 274 us
  Pallas kernels  121 us (44%)
  waiting for transfers between devices  105 us (38%)
  starting transfers between devices  18.5 us (7%)
  between operations  13.4 us (5%)
  other arithmetic  8.11 us (3%)
  local copies, waits for them, and re-layouts  7.04 us (3%)
    ppermute x15, waiting for transfers between devices, swap_tok(): return lax.ppermute(array, 'tok', [(i, i ^ step) for i in range(tok_size)])  71.6 us
    pallas_call x1, Pallas kernels, spread_down(): pl.pallas_call(functools.partial(spread_down_kernel, rows=rows, cols=cols...  43.9 us
    pallas_call x4, Pallas kernels, down(): pl.pallas_call(down_kernel, out_shape=jax.ShapeDtypeStruct((count, width)...  33.1 us
    all_gather x1, waiting for transfers between devices, shards(): gathered = lax.all_gather(tokens, 'col')  32.7 us
    pallas_call x4, Pallas kernels, gate_up(): pl.pallas_call(functools.partial(gate_up_kernel, parts=parts), out_shape=...  28.1 us
    ppermute x15, starting transfers between devices, swap_tok(): return lax.ppermute(array, 'tok', [(i, i ^ step) for i in range(tok_size)])  17.8 us
    pallas_call x1, Pallas kernels, spread_gate_up(): pl.pallas_call(functools.partial(spread_gate_up_kernel, rows=rows, cols=c...  16.4 us
    unnamed x14, local copies, waits for them, and re-layouts  5.62 us
  transfers between devices with their start and end apart: 24, of which 11 were waited for; matrix products, arithmetic and copies ran while one was open for 2% of the time, Pallas kernels for 39%

profile of v1, /device:TPU:0, one launch (start us, length us, event | category | flops | bytes accessed | tf_op | source)
XLA Modules:
  0.0 273.6 jit_solution(15286334264613783075)
XLA Ops:
  8.1 32.7 %all-gather.11.cloned.1.call-done = bf16[1024,1024]{1,0:T(8,128)(2,1)} async-done(((bf16[128,1024]{1,0:T(8,128)(2,1)}), bf16[1024,1024]{1,0:T(8,128)(2,1)}) %all-gather.11.cloned.1.call-update) | async-done | bytes 2097168 | tf_op jit(solution)/shard_map/all_gather | solution.py:210
  40.8 2.1 multiply_reduce_fusion
  42.9 1.6 fusion.1
  44.5 2.4 collective-permute-start.2
  48.7 5.9 %collective-permute-done.2.refs_3_ = bf16[128,1024]{1,0:T(8,128)(2,1)S(1)} collective-permute-done((bf16[128,1024]{1,0:T(8,128)(2,1)S(1)}, bf16[128,1024]{1,0:T(8,128)(2,1)S(1)}, u32[]{:S(2)}, u32[]{:S(2)}) %collective-permute-start.2) | collective-permute-done | bytes 262176 | tf_op jit(solution)/shard_map/ppermute | solution.py:196
  54.6 4.9 %collective-permute-done.1.refs_2_ = bf16[128,1024]{1,0:T(8,128)(2,1)S(1)} collective-permute-done((bf16[128,1024]{1,0:T(8,128)(2,1)S(1)}, bf16[128,1024]{1,0:T(8,128)(2,1)S(1)}, u32[]{:S(2)}, u32[]{:S(2)}) %collective-permute-start.1) | collective-permute-done | bytes 262176 | tf_op jit(solution)/shard_map/ppermute | solution.py:196
  60.2 16.4 %spread_gate_up.1.refs_8_ = bf16[4,2048,1536]{2,1,0:T(8,128)(2,1)} custom-call(s32[384]{0:T(512)S(1)} %get-tuple-element.38.gate_at, s32[384]{0:T(512)S(1)} %get-tuple-element.37.up_at, bf16[1,216,128,128]{3,2,1,0:T(8,128)(2,1)} %gate_ref.1, bf16[1,216,128,128]{3,2,1,0:T(8,128)(2,1)} %up_ref.1), custom_call_target="tpu_custom_call" | custom-call | bytes 39321600 | tf_op jit(solution)/shard_map/spread_gate_up/pallas_call | solution.py:45
  76.6 7.0 %gate_up_0.1 = (bf16[128,1536]{1,0:T(8,128)(2,1)S(1)}, bf16[128,1536]{1,0:T(8,128)(2,1)S(1)}, bf16[128,1536]{1,0:T(8,128)(2,1)S(1)}, bf16[128,1536]{1,0:T(8,128)(2,1)S(1)}) custom-call(bf16[128,1024]{1,0:T(8,128)(2,1)S(1)} %get-tuple-element.42.refs_0_, bf16[128,1024]{1,0:T(8,128)(2,1)S(1)} %collective-permute-done.refs_1_, ...), custom_call_target="tpu_custom_call" | custom-call | flops 3221225472 | bytes 9961472 | tf_op jit(solution)/shard_map/gate_up_0/pallas_call | solution.py:116
  83.6 1.5 collective-permute-start.16
  87.2 8.5 %collective-permute-done.16 = bf16[128,1536]{1,0:T(8,128)(2,1)S(1)} collective-permute-done((bf16[128,1536]{1,0:T(8,128)(2,1)S(1)}, bf16[128,1536]{1,0:T(8,128)(2,1)S(1)}, u32[]{:S(2)}, u32[]{:S(2)}) %collective-permute-start.16) | collective-permute-done | bytes 393248 | tf_op jit(solution)/shard_map/ppermute | solution.py:196
  95.7 8.7 %collective-permute-done.17 = bf16[128,1536]{1,0:T(8,128)(2,1)S(1)} collective-permute-done((bf16[128,1536]{1,0:T(8,128)(2,1)S(1)}, bf16[128,1536]{1,0:T(8,128)(2,1)S(1)}, u32[]{:S(2)}, u32[]{:S(2)}) %collective-permute-start.17) | collective-permute-done | bytes 393248 | tf_op jit(solution)/shard_map/ppermute | solution.py:196
  105.4 7.0 %gate_up_1.1 = (bf16[128,1536]{1,0:T(8,128)(2,1)S(1)}, bf16[128,1536]{1,0:T(8,128)(2,1)S(1)}, bf16[128,1536]{1,0:T(8,128)(2,1)S(1)}, bf16[128,1536]{1,0:T(8,128)(2,1)S(1)}) custom-call(bf16[128,1024]{1,0:T(8,128)(2,1)S(1)} %get-tuple-element.42.refs_0_, bf16[128,1024]{1,0:T(8,128)(2,1)S(1)} %collective-permute-done.refs_1_, ...), custom_call_target="tpu_custom_call" | custom-call | flops 3221225472 | bytes 9961472 | tf_op jit(solution)/shard_map/gate_up_1/pallas_call | solution.py:116
  113.0 1.4 collective-permute-start.14
  114.5 1.5 collective-permute-start.15
  116.0 8.6 %collective-permute-done.13 = bf16[128,1536]{1,0:T(8,128)(2,1)S(1)} collective-permute-done((bf16[128,1536]{1,0:T(8,128)(2,1)S(1)}, bf16[128,1536]{1,0:T(8,128)(2,1)S(1)}, u32[]{:S(2)}, u32[]{:S(2)}) %collective-permute-start.13) | collective-permute-done | bytes 393248 | tf_op jit(solution)/shard_map/ppermute | solution.py:196
  124.6 6.7 %collective-permute-done.14 = bf16[128,1536]{1,0:T(8,128)(2,1)S(1)} collective-permute-done((bf16[128,1536]{1,0:T(8,128)(2,1)S(1)}, bf16[128,1536]{1,0:T(8,128)(2,1)S(1)}, u32[]{:S(2)}, u32[]{:S(2)}) %collective-permute-start.14) | collective-permute-done | bytes 393248 | tf_op jit(solution)/shard_map/ppermute | solution.py:196
  132.4 7.0 %gate_up_2.1 = (bf16[128,1536]{1,0:T(8,128)(2,1)S(1)}, bf16[128,1536]{1,0:T(8,128)(2,1)S(1)}, bf16[128,1536]{1,0:T(8,128)(2,1)S(1)}, bf16[128,1536]{1,0:T(8,128)(2,1)S(1)}) custom-call(bf16[128,1024]{1,0:T(8,128)(2,1)S(1)} %get-tuple-element.42.refs_0_, bf16[128,1024]{1,0:T(8,128)(2,1)S(1)} %collective-permute-done.refs_1_, ...), custom_call_target="tpu_custom_call" | custom-call | flops 3221225472 | bytes 9961472 | tf_op jit(solution)/shard_map/gate_up_2/pallas_call | solution.py:116
  141.3 1.6 collective-permute-start.12
  143.0 8.6 %collective-permute-done.10 = bf16[128,1536]{1,0:T(8,128)(2,1)S(1)} collective-permute-done((bf16[128,1536]{1,0:T(8,128)(2,1)S(1)}, bf16[128,1536]{1,0:T(8,128)(2,1)S(1)}, u32[]{:S(2)}, u32[]{:S(2)}) %collective-permute-start.10) | collective-permute-done | bytes 393248 | tf_op jit(solution)/shard_map/ppermute | solution.py:196
  151.6 6.2 %collective-permute-done.11 = bf16[128,1536]{1,0:T(8,128)(2,1)S(1)} collective-permute-done((bf16[128,1536]{1,0:T(8,128)(2,1)S(1)}, bf16[128,1536]{1,0:T(8,128)(2,1)S(1)}, u32[]{:S(2)}, u32[]{:S(2)}) %collective-permute-start.11) | collective-permute-done | bytes 393248 | tf_op jit(solution)/shard_map/ppermute | solution.py:196
  158.9 7.0 %gate_up_3.1 = (bf16[128,1536]{1,0:T(8,128)(2,1)S(1)}, bf16[128,1536]{1,0:T(8,128)(2,1)S(1)}, bf16[128,1536]{1,0:T(8,128)(2,1)S(1)}, bf16[128,1536]{1,0:T(8,128)(2,1)S(1)}) custom-call(bf16[128,1024]{1,0:T(8,128)(2,1)S(1)} %get-tuple-element.42.refs_0_, bf16[128,1024]{1,0:T(8,128)(2,1)S(1)} %collective-permute-done.refs_1_, ...), custom_call_target="tpu_custom_call" | custom-call | flops 3221225472 | bytes 9961472 | tf_op jit(solution)/shard_map/gate_up_3/pallas_call | solution.py:116
  167.7 1.7 collective-permute-start.9
  169.5 8.0 %collective-permute-done.7 = bf16[128,1536]{1,0:T(8,128)(2,1)S(1)} collective-permute-done((bf16[128,1536]{1,0:T(8,128)(2,1)S(1)}, bf16[128,1536]{1,0:T(8,128)(2,1)S(1)}, u32[]{:S(2)}, u32[]{:S(2)}) %collective-permute-start.7) | collective-permute-done | bytes 393248 | tf_op jit(solution)/shard_map/ppermute | solution.py:196
  177.5 5.4 %collective-permute-done.8 = bf16[128,1536]{1,0:T(8,128)(2,1)S(1)} collective-permute-done((bf16[128,1536]{1,0:T(8,128)(2,1)S(1)}, bf16[128,1536]{1,0:T(8,128)(2,1)S(1)}, u32[]{:S(2)}, u32[]{:S(2)}) %collective-permute-start.8) | collective-permute-done | bytes 393248 | tf_op jit(solution)/shard_map/ppermute | solution.py:196
  184.4 43.9 %spread_down.1.weight_ref = bf16[4,8,768,1024]{3,2,1,0:T(8,128)(2,1)} custom-call(s32[1536]{0:T(1024)S(1)} %reshape.61.at_ref, bf16[8,108,128,128]{3,2,1,0:T(8,128)(2,1)} %values_ref.1), custom_call_target="tpu_custom_call" | custom-call | bytes 78643200 | tf_op jit(solution)/shard_map/spread_down/pallas_call | solution.py:75
  228.3 1.4 copy-done
  229.7 8.1 %down_0.1.before_ref = f32[128,1024]{1,0:T(8,128)S(1)} custom-call(bf16[8,128,768]{2,1,0:T(8,128)(2,1)S(1)} %bitcast.19, bf16[4,8,768,1024]{3,2,1,0:T(8,128)(2,1)} %spread_down.1.weight_ref, f32[128,1024]{1,0:T(8,128)S(1)} %broadcast_in_dim.55.before_ref), custom_call_target="tpu_custom_call" | custom-call | flops 1610612736 | bytes 14942208 | tf_op jit(solution)/shard_map/down_0/pallas_call | solution.py:151
  237.8 1.4 copy-done.1
  239.2 8.1 %down_1.1.before_ref = f32[128,1024]{1,0:T(8,128)S(1)} custom-call(bf16[8,128,768]{2,1,0:T(8,128)(2,1)S(1)} %bitcast.20, bf16[4,8,768,1024]{3,2,1,0:T(8,128)(2,1)} %spread_down.1.weight_ref, f32[128,1024]{1,0:T(8,128)S(1)} %down_0.1.before_ref), custom_call_target="tpu_custom_call" | custom-call | flops 1610612736 | bytes 14942208 | tf_op jit(solution)/shard_map/down_1/pallas_call | solution.py:151
  247.4 1.4 copy-done.2
  248.8 8.1 %down_2.1.before_ref = f32[128,1024]{1,0:T(8,128)S(1)} custom-call(bf16[8,128,768]{2,1,0:T(8,128)(2,1)S(1)} %bitcast.21, bf16[4,8,768,1024]{3,2,1,0:T(8,128)(2,1)} %spread_down.1.weight_ref, f32[128,1024]{1,0:T(8,128)S(1)} %down_1.1.before_ref), custom_call_target="tpu_custom_call" | custom-call | flops 1610612736 | bytes 14942208 | tf_op jit(solution)/shard_map/down_2/pallas_call | solution.py:151
  258.3 8.8 %down_3.1 = bf16[128,1024]{1,0:T(8,128)(2,1)} custom-call(bf16[8,128,768]{2,1,0:T(8,128)(2,1)S(1)} %bitcast.22, bf16[4,8,768,1024]{3,2,1,0:T(8,128)(2,1)} %spread_down.1.weight_ref, f32[128,1024]{1,0:T(8,128)S(1)} %down_2.1.before_ref), custom_call_target="tpu_custom_call" | custom-call | flops 1610612736 | bytes 14942208 | tf_op jit(solution)/shard_map/down_3/pallas_call | solution.py:151
  (70 shorter events, 16.4 us)
Async XLA Ops:
  6.5 53.5 %copy-start.5 = (s32[1,216]{1,0:T(1,128)S(1)}, s32[1,216]{1,0:T(1,128)}, u32[]{:S(2)}) copy-start(s32[1,216]{1,0:T(1,128)} %param.13) | copy-start | bytes 2596
  6.5 53.5 %copy-start.6 = (s32[1,216]{1,0:T(1,128)S(1)}, s32[1,216]{1,0:T(1,128)}, u32[]{:S(2)}) copy-start(s32[1,216]{1,0:T(1,128)} %param.11) | copy-start | bytes 2596
  6.5 34.3 %all-gather.11.cloned.1.call-start = ((), (), s32[]{:S(2)}) async-start(), calls=%async_computation | async-start | bytes 2359296 | tf_op jit(solution)/shard_map/all_gather | solution.py:210
  7.3 221.0 %all-gather.19.cloned.1.call-start = ((), (), s32[]{:S(2)}) async-start(), calls=%async_computation.4 | async-start | bytes 1769472 | tf_op jit(solution)/shard_map/all_gather | solution.py:242
  44.5 10.1 %collective-permute-start.2 = (bf16[128,1024]{1,0:T(8,128)(2,1)S(1)}, bf16[128,1024]{1,0:T(8,128)(2,1)S(1)}, u32[]{:S(2)}, u32[]{:S(2)}) collective-permute-start(bf16[128,1024]{1,0:T(8,128)(2,1)S(1)} %get-tuple-element.39), channel_id=1, source_target_pairs={{0,24},{8,16},{16,8},{24,0},{1,25},{9,17},{17,9},{25,1},{2,26},{10... | collective-permute-start | bytes 786440 | tf_op jit(solution)/shard_map/ppermute | solution.py:196
  46.9 12.6 %collective-permute-start.1 = (bf16[128,1024]{1,0:T(8,128)(2,1)S(1)}, bf16[128,1024]{1,0:T(8,128)(2,1)S(1)}, u32[]{:S(2)}, u32[]{:S(2)}) collective-permute-start(bf16[128,1024]{1,0:T(8,128)(2,1)S(1)} %get-tuple-element.40), channel_id=1, source_target_pairs={{0,16},{8,24},{16,0},{24,8},{1,17},{9,25},{17,1},{25,9},{2,18},{10... | collective-permute-start | bytes 786440 | tf_op jit(solution)/shard_map/ppermute | solution.py:196
  47.5 12.1 %collective-permute-start = (bf16[128,1024]{1,0:T(8,128)(2,1)S(1)}, bf16[128,1024]{1,0:T(8,128)(2,1)S(1)}, u32[]{:S(2)}, u32[]{:S(2)}) collective-permute-start(bf16[128,1024]{1,0:T(8,128)(2,1)S(1)} %get-tuple-element.41), channel_id=1, source_target_pairs={{0,8},{8,0},{16,24},{24,16},{1,9},{9,1},{17,25},{25,17},{2,10},{10... | collective-permute-start | bytes 786440 | tf_op jit(solution)/shard_map/ppermute | solution.py:196
  48.6 28.0 %collective-permute-start.3 = (bf16[128,1024]{1,0:T(8,128)(2,1)S(1)}, bf16[128,1024]{1,0:T(8,128)(2,1)S(1)}, u32[]{:S(2)}, u32[]{:S(2)}) collective-permute-start(bf16[128,1024]{1,0:T(8,128)(2,1)S(1)} %get-tuple-element.42.refs_0_), channel_id=1, source_target_pairs={{0,1},{1,0},{2,3},{3,2},{4,5},{5,4},{6,7},{7,6},{8,9},{9,8},{10,11... | collective-permute-start | bytes 786440 | tf_op jit(solution)/shard_map/ppermute | solution.py:199
  54.6 22.0 %collective-permute-start.6 = (bf16[128,1024]{1,0:T(8,128)(2,1)S(1)}, bf16[128,1024]{1,0:T(8,128)(2,1)S(1)}, u32[]{:S(2)}, u32[]{:S(2)}) collective-permute-start(bf16[128,1024]{1,0:T(8,128)(2,1)S(1)} %collective-permute-done.2.refs_3_), channel_id=1, source_target_pairs={{0,1},{1,0},{2,3},{3,2},{4,5},{5,4},{6,7},{7,6},{8,9},{9,8},{10,11... | collective-permute-start | bytes 786440 | tf_op jit(solution)/shard_map/ppermute | solution.py:199
  59.5 17.1 %collective-permute-start.5 = (bf16[128,1024]{1,0:T(8,128)(2,1)S(1)}, bf16[128,1024]{1,0:T(8,128)(2,1)S(1)}, u32[]{:S(2)}, u32[]{:S(2)}) collective-permute-start(bf16[128,1024]{1,0:T(8,128)(2,1)S(1)} %collective-permute-done.1.refs_2_), channel_id=1, source_target_pairs={{0,1},{1,0},{2,3},{3,2},{4,5},{5,4},{6,7},{7,6},{8,9},{9,8},{10,11... | collective-permute-start | bytes 786440 | tf_op jit(solution)/shard_map/ppermute | solution.py:199
  59.5 17.1 %collective-permute-start.4 = (bf16[128,1024]{1,0:T(8,128)(2,1)S(1)}, bf16[128,1024]{1,0:T(8,128)(2,1)S(1)}, u32[]{:S(2)}, u32[]{:S(2)}) collective-permute-start(bf16[128,1024]{1,0:T(8,128)(2,1)S(1)} %collective-permute-done.refs_1_), channel_id=1, source_target_pairs={{0,1},{1,0},{2,3},{3,2},{4,5},{5,4},{6,7},{7,6},{8,9},{9,8},{10,11... | collective-permute-start | bytes 786440 | tf_op jit(solution)/shard_map/ppermute | solution.py:199
  83.6 12.0 %collective-permute-start.16 = (bf16[128,1536]{1,0:T(8,128)(2,1)S(1)}, bf16[128,1536]{1,0:T(8,128)(2,1)S(1)}, u32[]{:S(2)}, u32[]{:S(2)}) collective-permute-start(bf16[128,1536]{1,0:T(8,128)(2,1)S(1)} %get-tuple-element.34), channel_id=1, source_target_pairs={{0,8},{8,0},{16,24},{24,16},{1,9},{9,1},{17,25},{25,17},{2,10},{10... | collective-permute-start | bytes 1179656 | tf_op jit(solution)/shard_map/ppermute | solution.py:196
  85.2 19.2 %collective-permute-start.17 = (bf16[128,1536]{1,0:T(8,128)(2,1)S(1)}, bf16[128,1536]{1,0:T(8,128)(2,1)S(1)}, u32[]{:S(2)}, u32[]{:S(2)}) collective-permute-start(bf16[128,1536]{1,0:T(8,128)(2,1)S(1)} %get-tuple-element.35), channel_id=1, source_target_pairs={{0,16},{8,24},{16,0},{24,8},{1,17},{9,25},{17,1},{25,9},{2,18},{10... | collective-permute-start | bytes 1179656 | tf_op jit(solution)/shard_map/ppermute | solution.py:196
  86.0 18.4 %collective-permute-start.18 = (bf16[128,1536]{1,0:T(8,128)(2,1)S(1)}, bf16[128,1536]{1,0:T(8,128)(2,1)S(1)}, u32[]{:S(2)}, u32[]{:S(2)}) collective-permute-start(bf16[128,1536]{1,0:T(8,128)(2,1)S(1)} %get-tuple-element.36), channel_id=1, source_target_pairs={{0,24},{8,16},{16,8},{24,0},{1,25},{9,17},{17,9},{25,1},{2,26},{10... | collective-permute-start | bytes 1179656 | tf_op jit(solution)/shard_map/ppermute | solution.py:196
  105.4 132.4 %all-gather.17.cloned.1.call-start = ((), (), s32[]{:S(2)}) async-start(), calls=%async_computation.3 | async-start | bytes 1769472 | tf_op jit(solution)/shard_map/all_gather | solution.py:242
  112.5 12.1 %collective-permute-start.13 = (bf16[128,1536]{1,0:T(8,128)(2,1)S(1)}, bf16[128,1536]{1,0:T(8,128)(2,1)S(1)}, u32[]{:S(2)}, u32[]{:S(2)}) collective-permute-start(bf16[128,1536]{1,0:T(8,128)(2,1)S(1)} %get-tuple-element.30), channel_id=1, source_target_pairs={{0,8},{8,0},{16,24},{24,16},{1,9},{9,1},{17,25},{25,17},{2,10},{10... | collective-permute-start | bytes 1179656 | tf_op jit(solution)/shard_map/ppermute | solution.py:196
  113.0 18.3 %collective-permute-start.14 = (bf16[128,1536]{1,0:T(8,128)(2,1)S(1)}, bf16[128,1536]{1,0:T(8,128)(2,1)S(1)}, u32[]{:S(2)}, u32[]{:S(2)}) collective-permute-start(bf16[128,1536]{1,0:T(8,128)(2,1)S(1)} %get-tuple-element.31), channel_id=1, source_target_pairs={{0,16},{8,24},{16,0},{24,8},{1,17},{9,25},{17,1},{25,9},{2,18},{10... | collective-permute-start | bytes 1179656 | tf_op jit(solution)/shard_map/ppermute | solution.py:196
  114.5 16.8 %collective-permute-start.15 = (bf16[128,1536]{1,0:T(8,128)(2,1)S(1)}, bf16[128,1536]{1,0:T(8,128)(2,1)S(1)}, u32[]{:S(2)}, u32[]{:S(2)}) collective-permute-start(bf16[128,1536]{1,0:T(8,128)(2,1)S(1)} %get-tuple-element.32), channel_id=1, source_target_pairs={{0,24},{8,16},{16,8},{24,0},{1,25},{9,17},{17,9},{25,1},{2,26},{10... | collective-permute-start | bytes 1179656 | tf_op jit(solution)/shard_map/ppermute | solution.py:196
  132.3 115.0 %all-gather.15.cloned.1.call-start = ((), (), s32[]{:S(2)}) async-start(), calls=%async_computation.2 | async-start | bytes 1769472 | tf_op jit(solution)/shard_map/all_gather | solution.py:242
  139.4 12.1 %collective-permute-start.10 = (bf16[128,1536]{1,0:T(8,128)(2,1)S(1)}, bf16[128,1536]{1,0:T(8,128)(2,1)S(1)}, u32[]{:S(2)}, u32[]{:S(2)}) collective-permute-start(bf16[128,1536]{1,0:T(8,128)(2,1)S(1)} %get-tuple-element.26), channel_id=1, source_target_pairs={{0,8},{8,0},{16,24},{24,16},{1,9},{9,1},{17,25},{25,17},{2,10},{10... | collective-permute-start | bytes 1179656 | tf_op jit(solution)/shard_map/ppermute | solution.py:196
  140.8 17.1 %collective-permute-start.11 = (bf16[128,1536]{1,0:T(8,128)(2,1)S(1)}, bf16[128,1536]{1,0:T(8,128)(2,1)S(1)}, u32[]{:S(2)}, u32[]{:S(2)}) collective-permute-start(bf16[128,1536]{1,0:T(8,128)(2,1)S(1)} %get-tuple-element.27), channel_id=1, source_target_pairs={{0,16},{8,24},{16,0},{24,8},{1,17},{9,25},{17,1},{25,9},{2,18},{10... | collective-permute-start | bytes 1179656 | tf_op jit(solution)/shard_map/ppermute | solution.py:196
  141.3 16.5 %collective-permute-start.12 = (bf16[128,1536]{1,0:T(8,128)(2,1)S(1)}, bf16[128,1536]{1,0:T(8,128)(2,1)S(1)}, u32[]{:S(2)}, u32[]{:S(2)}) collective-permute-start(bf16[128,1536]{1,0:T(8,128)(2,1)S(1)} %get-tuple-element.28), channel_id=1, source_target_pairs={{0,24},{8,16},{16,8},{24,0},{1,25},{9,17},{17,9},{25,1},{2,26},{10... | collective-permute-start | bytes 1179656 | tf_op jit(solution)/shard_map/ppermute | solution.py:196
  158.8 25.1 %copy-start.4 = (s32[8,108]{1,0:T(8,128)S(1)}, s32[8,108]{1,0:T(8,128)}, u32[]{:S(2)}) copy-start(s32[8,108]{1,0:T(8,128)} %param.15) | copy-start | bytes 10372
  158.8 98.1 %all-gather.13.cloned.1.call-start = ((), (), s32[]{:S(2)}) async-start(), calls=%async_computation.1 | async-start | bytes 1769472 | tf_op jit(solution)/shard_map/all_gather | solution.py:242
  165.9 11.6 %collective-permute-start.7 = (bf16[128,1536]{1,0:T(8,128)(2,1)S(1)}, bf16[128,1536]{1,0:T(8,128)(2,1)S(1)}, u32[]{:S(2)}, u32[]{:S(2)}) collective-permute-start(bf16[128,1536]{1,0:T(8,128)(2,1)S(1)} %get-tuple-element.22), channel_id=1, source_target_pairs={{0,8},{8,0},{16,24},{24,16},{1,9},{9,1},{17,25},{25,17},{2,10},{10... | collective-permute-start | bytes 1179656 | tf_op jit(solution)/shard_map/ppermute | solution.py:196
  166.5 16.4 %collective-permute-start.8 = (bf16[128,1536]{1,0:T(8,128)(2,1)S(1)}, bf16[128,1536]{1,0:T(8,128)(2,1)S(1)}, u32[]{:S(2)}, u32[]{:S(2)}) collective-permute-start(bf16[128,1536]{1,0:T(8,128)(2,1)S(1)} %get-tuple-element.23), channel_id=1, source_target_pairs={{0,16},{8,24},{16,0},{24,8},{1,17},{9,25},{17,1},{25,9},{2,18},{10... | collective-permute-start | bytes 1179656 | tf_op jit(solution)/shard_map/ppermute | solution.py:196
  167.7 15.2 %collective-permute-start.9 = (bf16[128,1536]{1,0:T(8,128)(2,1)S(1)}, bf16[128,1536]{1,0:T(8,128)(2,1)S(1)}, u32[]{:S(2)}, u32[]{:S(2)}) collective-permute-start(bf16[128,1536]{1,0:T(8,128)(2,1)S(1)} %get-tuple-element.24), channel_id=1, source_target_pairs={{0,24},{8,16},{16,8},{24,0},{1,25},{9,17},{17,9},{25,1},{2,26},{10... | collective-permute-start | bytes 1179656 | tf_op jit(solution)/shard_map/ppermute | solution.py:196
  228.3 1.4 copy-start
  237.8 1.4 copy-start.1
  247.4 1.4 copy-start.2
  256.9 1.4 copy-start.3
Sparse Core Ops, SparseCore 0:
  9.0 31.7 all-gather.10
  105.5 23.5 all-gather.18
  132.5 23.4 all-gather.16
  158.9 23.4 all-gather.14
  184.0 24.4 all-gather.12

commit v2 on v1

--- a/solution.py
+++ b/solution.py
@@ -169,7 +169,7 @@
     )(hidden, dense, before)
 
 
-def shards(
+def by_tokens(
     tokens,
     norm_gain,
     gate_block_entries,
@@ -244,6 +244,316 @@
         mixed = down(hidden, down_dense, mixed, chunk, jnp.bfloat16 if last else jnp.float32)
     return mixed
 
+def spread_shares_kernel(gate_at, up_at, gate_ref, up_ref, out_ref, *, rows, shares, cols):
+    chunk = pl.program_id(0)
+
+    @pl.loop(0, rows)
+    def _(row):
+        for share in range(shares):
+            for col in range(cols):
+                at = ((chunk * rows + row) * shares + share) * cols + col
+                put(out_ref, row, 2 * share * cols + col, gate_ref, gate_at[at])
+                put(out_ref, row, (2 * share + 1) * cols + col, up_ref, up_at[at])
+
+
+def spread_shares(gate_at, up_at, gate, up, chunks, rows, shares, cols):
+    edge = gate.shape[-1]
+    whole = pl.BlockSpec(gate.shape, lambda k, *_: (0, 0, 0, 0), pipeline_mode=pl.Buffered(1))
+    out = jax.ShapeDtypeStruct((chunks, rows * edge, 2 * shares * cols * edge), gate.dtype)
+    return pl.pallas_call(
+        functools.partial(spread_shares_kernel, rows=rows, shares=shares, cols=cols),
+        out_shape=out,
+        grid_spec=pltpu.PrefetchScalarGridSpec(
+            num_scalar_prefetch=2,
+            grid=(chunks,),
+            in_specs=[whole, whole],
+            out_specs=pl.BlockSpec((1,) + out.shape[1:], lambda k, *_: (k, 0, 0)),
+        ),
+        compiler_params=pltpu.CompilerParams(vmem_limit_bytes=48 * MIB),
+        cost_estimate=pl.CostEstimate(
+            flops=0, bytes_accessed=2 * (2 * gate.size + out.size), transcendentals=0
+        ),
+        name="spread_gate_up",
+    )(gate_at, up_at, gate, up)
+
+
+def spread_panels_kernel(at_ref, panels_ref, values_ref, out_ref, *, chunks, rows, cols):
+    panel = pl.program_id(0)
+    for chunk in range(chunks):
+        for row in range(rows):
+            for col in range(cols):
+                at = ((panel * chunks + chunk) * rows + row) * cols + col
+                put(out_ref.at[pl.ds(chunk, 1)], row, col, values_ref, at_ref[at])
+
+
+def spread_panels(at, panels, values, chunks, rows, cols):
+    count, _, edge, _ = values.shape
+    out = jax.ShapeDtypeStruct((chunks, count * rows * edge, cols * edge), values.dtype)
+    return pl.pallas_call(
+        functools.partial(spread_panels_kernel, chunks=chunks, rows=rows, cols=cols),
+        out_shape=out,
+        grid_spec=pltpu.PrefetchScalarGridSpec(
+            num_scalar_prefetch=2,
+            grid=(count,),
+            in_specs=[
+                pl.BlockSpec((1,) + values.shape[1:], lambda m, _, panels: (panels[m], 0, 0, 0))
+            ],
+            out_specs=pl.BlockSpec((chunks, rows * edge, cols * edge), lambda m, *_: (0, m, 0)),
+        ),
+        compiler_params=pltpu.CompilerParams(vmem_limit_bytes=48 * MIB),
+        cost_estimate=pl.CostEstimate(
+            flops=0, bytes_accessed=2 * (values.size + out.size), transcendentals=0
+        ),
+        name="spread_down",
+    )(at, panels, values)
+
+def pack_kernel(*refs, parts):
+    count = refs[0].shape[0]
+    for part in range(parts):
+        refs[-1][part * count:(part + 1) * count] = refs[part][...]
+
+
+def pack(pieces, after):
+    parts = len(pieces)
+    count, width = pieces[0].shape
+    return pl.pallas_call(
+        functools.partial(pack_kernel, parts=parts),
+        out_shape=jax.ShapeDtypeStruct((parts * count, width), pieces[0].dtype),
+        in_specs=[pl.BlockSpec(memory_space=pltpu.VMEM)] * parts
+        + [pl.BlockSpec(memory_space=pl.ANY)] * len(after),
+        out_specs=pl.BlockSpec(memory_space=pltpu.VMEM),
+        cost_estimate=pl.CostEstimate(
+            flops=0, bytes_accessed=4 * parts * count * width, transcendentals=0
+        ),
+        name="pack",
+    )(*pieces, *after)
+
+
+def pack_hidden_kernel(*refs, parts):
+    out = refs[-1]
+    count = out.shape[1] // parts
+    for step in range(parts):
+        for part in range(parts):
+            there = part ^ step
+            out[step, part * count:(part + 1) * count] = refs[step][there * count:(there + 1) * count]
+
+
+def pack_hidden(pieces):
+    parts = len(pieces)
+    return pl.pallas_call(
+        functools.partial(pack_hidden_kernel, parts=parts),
+        out_shape=jax.ShapeDtypeStruct((parts,) + pieces[0].shape, pieces[0].dtype),
+        in_specs=[pl.BlockSpec(memory_space=pltpu.VMEM)] * parts,
+        out_specs=pl.BlockSpec(memory_space=pltpu.VMEM),
+        cost_estimate=pl.CostEstimate(
+            flops=0, bytes_accessed=4 * parts * pieces[0].size, transcendentals=0
+        ),
+        name="pack_hidden",
+    )(*pieces)
+
+
+def combine_kernel(*refs, parts):
+    terms, scale, out = refs[:parts], refs[parts], refs[-1]
+    total = functools.reduce(jnp.add, [term[...].astype(jnp.float32) for term in terms])
+    total *= scale[...]
+    width = out.shape[-1]
+    gate_sum, up_sum = total[:, :width], total[:, width:]
+    out[...] = (gate_sum / (1.0 + jnp.exp(-gate_sum)) * up_sum).astype(out.dtype)
+
+
+def combine(terms, scale, after, chunk):
+    parts = len(terms)
+    count, width = terms[0].shape
+    rows = count // 4
+    return pl.pallas_call(
+        functools.partial(combine_kernel, parts=parts),
+        out_shape=jax.ShapeDtypeStruct((count, width // 2), terms[0].dtype),
+        grid=(count // rows,),
+        in_specs=[pl.BlockSpec((rows, width), lambda i: (i, 0))] * parts
+        + [pl.BlockSpec((rows, 1), lambda i: (i, 0)), pl.BlockSpec(memory_space=pl.ANY)],
+        out_specs=pl.BlockSpec((rows, width // 2), lambda i: (i, 0)),
+        compiler_params=pltpu.CompilerParams(vmem_limit_bytes=32 * MIB),
+        cost_estimate=pl.CostEstimate(
+            flops=8 * count * width,
+            bytes_accessed=2 * count * width * (parts + 1),
+            transcendentals=count * width // 2,
+        ),
+        name=f"combine_{chunk}",
+    )(*terms, scale, after)
+
+
+def panel_product_kernel(own, other, weight, *outs):
+    half = own.shape[1]
+    product = jnp.dot(own[...], weight[0, :half], preferred_element_type=jnp.float32)
+    product += jnp.dot(other[...], weight[0, half:], preferred_element_type=jnp.float32)
+    for part, out in enumerate(outs):
+
+        @pl.when(pl.program_id(0) == part)
+        def _():
+            out[...] = product.astype(out.dtype)
+
+
+def panel_product(own, other, dense, parts, chunk):
+    count, half = own.shape
+    _, depth, width = dense.shape
+    tile = width // parts
+    out = jax.ShapeDtypeStruct((count, tile), own.dtype)
+    return pl.pallas_call(
+        panel_product_kernel,
+        out_shape=[out] * parts,
+        grid=(parts,),
+        in_specs=[pl.BlockSpec((count, half), lambda n: (0, 0))] * 2
+        + [pl.BlockSpec((1, depth, tile), lambda n: (chunk, 0, n))],
+        out_specs=[pl.BlockSpec((count, tile), lambda n: (0, 0))] * parts,
+        compiler_params=pltpu.CompilerParams(vmem_limit_bytes=40 * MIB),
+        cost_estimate=pl.CostEstimate(
+            flops=2 * count * depth * width,
+            bytes_accessed=2 * (depth * width + count * (depth + width)),
+            transcendentals=0,
+        ),
+        name=f"gate_up_{chunk}",
+    )(own, other, dense)
+
+
+def down_product_kernel(own, other, weight, *refs):
+    before, out, held = refs[0] if len(refs) == 3 else None, refs[-2], refs[-1]
+    panels, _, depth = own.shape
+
+    @pl.when(pl.program_id(0) == 0)
+    def _():
+        for i in range(panels):
+            held[:, i * depth:(i + 1) * depth] = own[i]
+            held[:, (panels + i) * depth:(panels + i + 1) * depth] = other[i]
+
+    product = jnp.dot(held[...], weight[0], preferred_element_type=jnp.float32)
+    if before is not None:
+        product += before[...]
+    out[...] = product.astype(out.dtype)
+
+
+def down_product(own, other, dense, before, chunk, dtype):
+    panels, count, depth = own.shape
+    _, total, width = dense.shape
+    tile = width // 2
+    tiles = pl.BlockSpec((count, tile), lambda n: (0, n))
+    whole = pl.BlockSpec((panels, count, depth), lambda n: (0, 0, 0))
+    added = [] if before is None else [before]
+    return pl.pallas_call(
+        down_product_kernel,
+        out_shape=jax.ShapeDtypeStruct((count, width), dtype),
+        grid=(width // tile,),
+        in_specs=[whole, whole, pl.BlockSpec((1, total, tile), lambda n: (chunk, 0, n))]
+        + [tiles] * len(added),
+        out_specs=tiles,
+        scratch_shapes=[pltpu.VMEM((count, total), own.dtype)],
+        compiler_params=pltpu.CompilerParams(vmem_limit_bytes=40 * MIB),
+        cost_estimate=pl.CostEstimate(
+            flops=2 * count * total * width,
+            bytes_accessed=2 * total * (width + count) + 8 * count * width,
+            transcendentals=0,
+        ),
+        name=f"down_{chunk}",
+    )(own, other, dense, *added)
+
+
+def by_columns(
+    tokens,
+    norm_gain,
+    gate_block_entries,
+    gate_block_places,
+    up_block_entries,
+    up_block_places,
+    down_values,
+    down_slots,
+):
+    edge = gate_block_entries.shape[-1]
+    tok_size = lax.axis_size("tok")
+    col_size = lax.axis_size("col")
+    rows_per = MODEL_WIDTH // edge // tok_size
+    cols_per = HIDDEN_UNITS // edge // col_size
+    width_blocks = MODEL_WIDTH // edge // col_size
+    share = cols_per // tok_size
+    chunks = 3 if share % 3 == 0 else 1
+    cols = share // chunks
+    count, half = tokens.shape
+    tok, col = lax.axis_index("tok"), lax.axis_index("col")
+    chip, side = col // 2, col % 2
+    parts = range(tok_size)
+
+    def swap_tok(array, step):
+        return lax.ppermute(array, "tok", [(i, i ^ step) for i in parts])
+
+    def swap_chip(array, step):
+        return lax.ppermute(array, "col", [(i, i ^ (2 * step)) for i in range(col_size)])
+
+    def swap_core(array):
+        return lax.ppermute(array, "col", [(i, i ^ 1) for i in range(col_size)])
+
+    def to_users(array, part):
+        pairs = []
+        for i in parts:
+            for j in range(col_size):
+                user = (j // 2) * col_size + 2 * (i ^ part) + j % 2
+                pairs.append((i * col_size + j, user))
+        return lax.ppermute(array, ("tok", "col"), pairs)
+
+    widened = tokens.astype(jnp.float32)
+    gain = lax.dynamic_slice_in_dim(norm_gain, col * half, half, 0)
+    gained = (widened * gain).astype(jnp.bfloat16)
+    pieces = [to_users(gained, part) for part in parts]
+    squares = jnp.sum(widened * widened, axis=1)
+    squares = jnp.where(jnp.arange(tok_size)[:, None] == tok, squares[None], 0.0)
+    squares = lax.psum(squares, ("tok", "col"))
+
+    k, r, p, q = jnp.meshgrid(
+        jnp.arange(chunks), jnp.arange(rows_per), jnp.arange(tok_size), jnp.arange(cols),
+        indexing="ij",
+    )
+    row = (r + side * (rows_per // 2)) % rows_per
+    slots = (row * cols_per + (p ^ tok) * share + k * cols + q).reshape(-1).astype(jnp.int32)
+    gate_at = lookup(gate_block_places[0], slots)
+    up_at = lookup(up_block_places[0], slots)
+    m = jnp.arange(col_size, dtype=jnp.int32)
+    panels = 2 * ((m % tok_size) ^ chip) + (side ^ (m // tok_size))
+    slots = tok * share * width_blocks + jnp.arange(share * width_blocks, dtype=jnp.int32)
+    down_at = jnp.take(lookup(down_slots, slots), panels, axis=0).reshape(-1)
+
+    dense = spread_shares(
+        gate_at, up_at, gate_block_entries, up_block_entries, chunks, rows_per, tok_size, cols
+    )
+    down_dense = spread_panels(down_at, panels, down_values, chunks, cols, width_blocks)
+
+    own = pack(pieces, [dense, down_dense])
+    other = swap_core(own)
+
+    sums = [panel_product(own, other, dense, tok_size, chunk) for chunk in range(chunks)]
+    scale = lax.rsqrt(squares / MODEL_WIDTH + EPSILON)
+    scale = jnp.take(scale, jnp.arange(tok_size) ^ chip, axis=0).reshape(-1, 1)
+    mixed = None
+    for chunk in range(chunks):
+        terms = [sums[chunk][0]] + [swap_tok(sums[chunk][p], p) for p in parts[1:]]
+        hidden = combine(terms, scale, sums[-1][0], chunk)
+        held = pack_hidden([hidden] + [swap_chip(hidden, step) for step in parts[1:]])
+        last = chunk == chunks - 1
+        mixed = down_product(
+            held, swap_core(held), down_dense, mixed, chunk, jnp.bfloat16 if last else jnp.float32
+        )
+
+    mixed = mixed.reshape(tok_size, count, -1)
+    total = 0.0
+    for step in parts:
+        part = lax.dynamic_index_in_dim(mixed, chip ^ tok ^ step, 0, keepdims=False)
+        total += (swap_tok(part, step) if step else part).astype(jnp.float32)
+    return total.astype(jnp.bfloat16)
+
+
+def shards(*arrays):
+    tok_size = lax.axis_size("tok")
+    col_size = lax.axis_size("col")
+    blocks = HIDDEN_UNITS // arrays[2].shape[-1]
+    even = blocks % (col_size * tok_size) == 0 and col_size == 2 * tok_size == 8
+    return (by_columns if even else by_tokens)(*arrays)
+
 
 def solution(mesh):
     return jax.shard_map(

time: 275 us -> 257 us (0.935)
  waiting for transfers between devices: 105 us -> 64.3 us
  blocking collectives: 0 us -> 40.6 us
  Pallas kernels: 121 us -> 88.1 us
  starting transfers between devices: 18.5 us -> 40.7 us
  between operations: 13.4 us -> 0.46 us
  local copies, waits for them, and re-layouts: 7.04 us -> 18.3 us
  other arithmetic: 8.11 us -> 3.42 us
    psum x0 -> x1, blocking collectives: none -> 40.6 us  [by_columns(): squares = lax.psum(squares, ('tok', 'col'))]
    pallas_call x10 -> x15, Pallas kernels: 121 us -> 88.1 us  [the longest x3 24.3 us: panel_product(): pl.pallas_call(panel_product_kernel, out_shape=[out] * parts, grid=(parts...]
    all_gather x5 -> x0, waiting for transfers between devices: 32.7 us -> none  [the longest x1 32.7 us: shards(): gathered = lax.all_gather(tokens, 'col')]
    ppermute x15 -> x25, starting transfers between devices: 17.8 us -> 40.6 us  [the longest x12 16.2 us: swap_tok(): return lax.ppermute(array, 'tok', [(i, i ^ step) for i in parts])]
    unnamed x14 -> x66, local copies, waits for them, and re-layouts: 5.62 us -> 15.3 us
    ppermute x15 -> x25, waiting for transfers between devices: 71.6 us -> 64.3 us  [the longest x12 34.2 us: swap_tok(): return lax.ppermute(array, 'tok', [(i, i ^ step) for i in parts])]
    convert_element_type x5 -> x1, other arithmetic: 4.75 us -> 0.87 us  [by_columns(): return total.astype(jnp.bfloat16)]
  transfers between devices with their start and end apart: 24 -> 29, of which waited for: 11 -> 10; matrix products, arithmetic and copies ran while one was open for 2% -> 1% of each run, Pallas kernels for 39% -> 29%
where the time goes in v2:
time: 257 us; the launch traced here: 256 us
  Pallas kernels  88.1 us (34%)
  waiting for transfers between devices  64.3 us (25%)
  starting transfers between devices  40.7 us (16%)
  blocking collectives  40.6 us (16%)
  local copies, waits for them, and re-layouts  18.3 us (7%)
  other arithmetic  3.42 us (1%)
    psum x1, blocking collectives, by_columns(): squares = lax.psum(squares, ('tok', 'col'))  40.6 us
    ppermute x12, waiting for transfers between devices, swap_tok(): return lax.ppermute(array, 'tok', [(i, i ^ step) for i in parts])  34.2 us
    ppermute x9, waiting for transfers between devices, swap_chip(): lax.ppermute(array, 'col', [(i, i ^ 2 * step) for i in range(col_size)])  30 us
    pallas_call x3, Pallas kernels, panel_product(): pl.pallas_call(panel_product_kernel, out_shape=[out] * parts, grid=(parts...  24.3 us
    pallas_call x1, Pallas kernels, spread_shares(): pl.pallas_call(functools.partial(spread_shares_kernel, rows=rows, shares=...  17.3 us
    pallas_call x1, Pallas kernels, spread_panels(): pl.pallas_call(functools.partial(spread_panels_kernel, chunks=chunks, row...  16.3 us
    ppermute x12, starting transfers between devices, swap_tok(): return lax.ppermute(array, 'tok', [(i, i ^ step) for i in parts])  16.2 us
    unnamed x66, local copies, waits for them, and re-layouts  15.3 us
  transfers between devices with their start and end apart: 29, of which 10 were waited for; matrix products, arithmetic and copies ran while one was open for 1% of the time, Pallas kernels for 29%

profile of v2, /device:TPU:0, one launch (start us, length us, event | category | flops | bytes accessed | tf_op | source)
XLA Modules:
  0.0 255.8 jit_solution(5941237912549034355)
XLA Ops:
  2.5 5.7 %collective-permute-start.1 = (bf16[128,1024]{1,0:T(8,128)(2,1)S(1)}, bf16[128,1024]{1,0:T(8,128)(2,1)S(1)}, u32[]{:S(2)}, u32[]{:S(2)}) collective-permute-start(bf16[128,1024]{1,0:T(8,128)(2,1)S(1)} %get-tuple-element.37), channel_id=1, source_target_pairs={{0,2},{1,3},{2,10},{3,11},{4,18},{5,19},{6,26},{7,27},{8,0},{9,1},... | collective-permute-start | bytes 786440 | tf_op jit(solution)/shard_map/ppermute | solution.py:498
  8.2 3.5 %collective-permute-start.2 = (bf16[128,1024]{1,0:T(8,128)(2,1)S(1)}, bf16[128,1024]{1,0:T(8,128)(2,1)S(1)}, u32[]{:S(2)}, u32[]{:S(2)}) collective-permute-start(bf16[128,1024]{1,0:T(8,128)(2,1)S(1)} %get-tuple-element.37), channel_id=1, source_target_pairs={{0,4},{1,5},{2,12},{3,13},{4,20},{5,21},{6,28},{7,29},{8,6},{9,7},... | collective-permute-start | bytes 786440 | tf_op jit(solution)/shard_map/ppermute | solution.py:498
  16.2 16.3 %spread_down.1.refs_5_.weight = bf16[3,2048,1024]{2,1,0:T(8,128)(2,1)} custom-call(s32[384]{0:T(512)S(1)} %select_n.152.at_ref, s32[8]{0:T(128)S(1)} %get-tuple-element.32.panels_ref, bf16[8,108,128,128]{3,2,1,0:T(8,128)(2,1)} %values_ref.1), custom_call_target="tpu_custom_call" | custom-call | bytes 40894464 | tf_op jit(solution)/shard_map/spread_down/pallas_call | solution.py:292
  32.8 17.3 %spread_gate_up.1.refs_4_.weight = bf16[3,2048,2048]{2,1,0:T(8,128)(2,1)} custom-call(s32[384]{0:T(512)S(1)} %get-tuple-element.30.gate_at, s32[384]{0:T(512)S(1)} %get-tuple-element.29.up_at, bf16[1,216,128,128]{3,2,1,0:T(8,128)(2,1)} %gate_ref.1, bf16[1,216,128,128]{3,2,1,0:T(8,128)(2,1)} %up_ref.1), custom_call_target="tpu_custom_call" | custom-call | bytes 39321600 | tf_op jit(solution)/shard_map/spread_gate_up/pallas_call | solution.py:263
  51.7 2.2 pack.1.own
  54.0 40.6 %psum.7 = f32[4,128]{1,0:T(4,128)S(1)} all-reduce(f32[4,128]{1,0:T(4,128)S(1)} %broadcast_select_fusion.2), channel_id=1, replica_groups=mesh['tok'=4,'col'=8] {'tok','col'}, use_global_device_ids=true, to_apply=%region_4.5 | all-reduce | flops 512 | bytes 4096 | tf_op jit(solution)/shard_map/psum | solution.py:506
  95.8 8.0 %gate_up_0.1 = (bf16[512,512]{1,0:T(8,128)(2,1)S(1)}, bf16[512,512]{1,0:T(8,128)(2,1)S(1)}, bf16[512,512]{1,0:T(8,128)(2,1)S(1)}, bf16[512,512]{1,0:T(8,128)(2,1)}) custom-call(bf16[512,1024]{1,0:T(8,128)(2,1)S(1)} %copy-done, bf16[512,1024]{1,0:T(8,128)(2,1)S(1)} %collective-permute-done.4.other, bf16[3,2048,2048]{2,1,0:T(8,128)(2,1)} %spread_gate_up.1.refs_4_.weight), custom_call_target="tpu_custom_call" | custom-call | flops 4294967296 | bytes 12582912 | tf_op jit(solution)/shard_map/gate_up_0/pallas_call | solution.py:401
  104.6 2.3 collective-permute-start.19
  108.3 8.3 %gate_up_1.1 = (bf16[512,512]{1,0:T(8,128)(2,1)S(1)}, bf16[512,512]{1,0:T(8,128)(2,1)}, bf16[512,512]{1,0:T(8,128)(2,1)}, bf16[512,512]{1,0:T(8,128)(2,1)}) custom-call(bf16[512,1024]{1,0:T(8,128)(2,1)S(1)} %copy-done, bf16[512,1024]{1,0:T(8,128)(2,1)S(1)} %collective-permute-done.4.other, bf16[3,2048,2048]{2,1,0:T(8,128)(2,1)} %spread_gate_up.1.refs_4_.weight), custom_call_target="tpu_custom_call" | custom-call | flops 4294967296 | bytes 12582912 | tf_op jit(solution)/shard_map/gate_up_1/pallas_call | solution.py:401
  120.0 8.0 %gate_up_2.1 = (bf16[512,512]{1,0:T(8,128)(2,1)S(1)}, bf16[512,512]{1,0:T(8,128)(2,1)}, bf16[512,512]{1,0:T(8,128)(2,1)S(1)}, bf16[512,512]{1,0:T(8,128)(2,1)S(1)}) custom-call(bf16[512,1024]{1,0:T(8,128)(2,1)S(1)} %copy-done, bf16[512,1024]{1,0:T(8,128)(2,1)S(1)} %collective-permute-done.4.other, bf16[3,2048,2048]{2,1,0:T(8,128)(2,1)} %spread_gate_up.1.refs_4_.weight), custom_call_target="tpu_custom_call" | custom-call | flops 4294967296 | bytes 12582912 | tf_op jit(solution)/shard_map/gate_up_2/pallas_call | solution.py:401
  132.2 2.0 collective-permute-start.5
  135.6 6.6 %collective-permute-done.12.refs_1_ = bf16[512,512]{1,0:T(8,128)(2,1)S(1)} collective-permute-done((bf16[512,512]{1,0:T(8,128)(2,1)}, bf16[512,512]{1,0:T(8,128)(2,1)S(1)}, u32[]{:S(2)}, u32[]{:S(2)}) %collective-permute-start.12) | collective-permute-done | bytes 524320 | tf_op jit(solution)/shard_map/ppermute | solution.py:484
  147.4 2.2 combine_0.1.refs_0_
  149.6 2.5 collective-permute-done.13.refs_2_
  152.1 3.0 %collective-permute-done.14.refs_3_ = bf16[512,512]{1,0:T(8,128)(2,1)} collective-permute-done((bf16[512,512]{1,0:T(8,128)(2,1)}, bf16[512,512]{1,0:T(8,128)(2,1)}, u32[]{:S(2)}, u32[]{:S(2)}) %collective-permute-start.14) | collective-permute-done | bytes 524320 | tf_op jit(solution)/shard_map/ppermute | solution.py:484
  155.1 9.7 %collective-permute-done.5.refs_1_ = bf16[512,512]{1,0:T(8,128)(2,1)S(1)} collective-permute-done((bf16[512,512]{1,0:T(8,128)(2,1)}, bf16[512,512]{1,0:T(8,128)(2,1)S(1)}, u32[]{:S(2)}, u32[]{:S(2)}) %collective-permute-start.5) | collective-permute-done | bytes 524320 | tf_op jit(solution)/shard_map/ppermute | solution.py:484
  168.4 2.4 combine_1.1.refs_0_
  170.9 2.8 %collective-permute-start.16 = (bf16[512,256]{1,0:T(8,128)(2,1)S(1)}, bf16[512,256]{1,0:T(8,128)(2,1)}, u32[]{:S(2)}, u32[]{:S(2)}) collective-permute-start(bf16[512,256]{1,0:T(8,128)(2,1)S(1)} %combine_1.1.refs_0_), channel_id=1, source_target_pairs={{0,4},{1,5},{2,6},{3,7},{4,0},{5,1},{6,2},{7,3},{8,12},{9,13},{10,... | collective-permute-start | bytes 786440 | tf_op jit(solution)/shard_map/ppermute | solution.py:487
  177.9 2.2 pack_hidden.5.own
  181.4 2.4 combine_2.1.refs_0_
  183.8 2.3 collective-permute-start.10
  186.1 4.3 %collective-permute-start.8 = (bf16[512,256]{1,0:T(8,128)(2,1)S(1)}, bf16[512,256]{1,0:T(8,128)(2,1)S(1)}, u32[]{:S(2)}, u32[]{:S(2)}) collective-permute-start(bf16[512,256]{1,0:T(8,128)(2,1)S(1)} %combine_2.1.refs_0_), channel_id=1, source_target_pairs={{0,2},{1,3},{2,0},{3,1},{4,6},{5,7},{6,4},{7,5},{8,10},{9,11},{10,... | collective-permute-start | bytes 786440 | tf_op jit(solution)/shard_map/ppermute | solution.py:487
  190.5 10.3 %collective-permute-done.16.refs_2_ = bf16[512,256]{1,0:T(8,128)(2,1)} collective-permute-done((bf16[512,256]{1,0:T(8,128)(2,1)S(1)}, bf16[512,256]{1,0:T(8,128)(2,1)}, u32[]{:S(2)}, u32[]{:S(2)}) %collective-permute-start.16) | collective-permute-done | bytes 262176 | tf_op jit(solution)/shard_map/ppermute | solution.py:487
  200.8 2.2 pack_hidden.4.own
  203.8 16.9 %collective-permute-done.9.refs_2_ = bf16[512,256]{1,0:T(8,128)(2,1)S(1)} collective-permute-done((bf16[512,256]{1,0:T(8,128)(2,1)S(1)}, bf16[512,256]{1,0:T(8,128)(2,1)S(1)}, u32[]{:S(2)}, u32[]{:S(2)}) %collective-permute-start.9) | collective-permute-done | bytes 262176 | tf_op jit(solution)/shard_map/ppermute | solution.py:487
  221.5 2.2 pack_hidden.3.own
  223.7 4.6 %down_0.1.refs_0_ = f32[512,1024]{1,0:T(8,128)S(1)} custom-call(bf16[4,512,256]{2,1,0:T(8,128)(2,1)S(1)} %copy-done.1, bf16[4,512,256]{2,1,0:T(8,128)(2,1)S(1)} %collective-permute-done.25.other, bf16[3,2048,1024]{2,1,0:T(8,128)(2,1)} %spread_down.1.refs_5_.weight), custom_call_target="tpu_custom_call" | custom-call | flops 2147483648 | bytes 10485760 | tf_op jit(solution)/shard_map/down_0/pallas_call | solution.py:441
  228.4 4.9 %down_1.1.refs_0_ = f32[512,1024]{1,0:T(8,128)S(1)} custom-call(bf16[4,512,256]{2,1,0:T(8,128)(2,1)S(1)} %copy-done.2, bf16[4,512,256]{2,1,0:T(8,128)(2,1)} %collective-permute-done.18.other, bf16[3,2048,1024]{2,1,0:T(8,128)(2,1)} %spread_down.1.refs_5_.weight, f32[512,1024]{1,0:T(8,128)S(1)} %down_0.1.refs_0_), custom_call_target="tpu_custom_call" | custom-call | flops 2147483648 | bytes 10485760 | tf_op jit(solution)/shard_map/down_1/pallas_call | solution.py:441
  233.3 4.8 %down_2.1 = bf16[512,1024]{1,0:T(8,128)(2,1)S(1)} custom-call(bf16[4,512,256]{2,1,0:T(8,128)(2,1)S(1)} %copy-done.3, bf16[4,512,256]{2,1,0:T(8,128)(2,1)} %collective-permute-done.11.other, bf16[3,2048,1024]{2,1,0:T(8,128)(2,1)} %spread_down.1.refs_5_.weight, f32[512,1024]{1,0:T(8,128)S(1)} %down_1.1.refs_0_), custom_call_target="tpu_custom_call" | custom-call | flops 2147483648 | bytes 10485760 | tf_op jit(solution)/shard_map/down_2/pallas_call | solution.py:441
  238.2 2.8 %collective-permute-start.26 = (bf16[128,1024]{1,0:T(8,128)(2,1)S(1)}, bf16[128,1024]{1,0:T(8,128)(2,1)S(1)}, u32[]{:S(2)}, u32[]{:S(2)}) collective-permute-start(bf16[128,1024]{1,0:T(8,128)(2,1)S(1)} %get-tuple-element.33), channel_id=1, source_target_pairs={{0,8},{8,0},{16,24},{24,16},{1,9},{9,1},{17,25},{25,17},{2,10},{10... | collective-permute-start | bytes 786440 | tf_op jit(solution)/shard_map/ppermute | solution.py:484
  242.5 5.6 %collective-permute-done.26 = bf16[128,1024]{1,0:T(8,128)(2,1)S(1)} collective-permute-done((bf16[128,1024]{1,0:T(8,128)(2,1)S(1)}, bf16[128,1024]{1,0:T(8,128)(2,1)S(1)}, u32[]{:S(2)}, u32[]{:S(2)}) %collective-permute-start.26) | collective-permute-done | bytes 262176 | tf_op jit(solution)/shard_map/ppermute | solution.py:484
  248.1 6.9 %collective-permute-done.27 = bf16[128,1024]{1,0:T(8,128)(2,1)S(1)} collective-permute-done((bf16[128,1024]{1,0:T(8,128)(2,1)S(1)}, bf16[128,1024]{1,0:T(8,128)(2,1)S(1)}, u32[]{:S(2)}, u32[]{:S(2)}) %collective-permute-start.27) | collective-permute-done | bytes 262176 | tf_op jit(solution)/shard_map/ppermute | solution.py:484
  (142 shorter events, 39.5 us)
Async XLA Ops:
  1.8 48.3 %collective-permute-start = (bf16[128,1024]{1,0:T(8,128)(2,1)S(1)}, bf16[128,1024]{1,0:T(8,128)(2,1)S(1)}, u32[]{:S(2)}, u32[]{:S(2)}) collective-permute-start(bf16[128,1024]{1,0:T(8,128)(2,1)S(1)} %get-tuple-element.37), channel_id=1, source_target_pairs={{0,0},{1,1},{2,8},{3,9},{4,16},{5,17},{6,24},{7,25},{8,2},{9,3},{1... | collective-permute-start | bytes 786440 | tf_op jit(solution)/shard_map/ppermute | solution.py:498
  2.5 47.6 %collective-permute-start.1 = (bf16[128,1024]{1,0:T(8,128)(2,1)S(1)}, bf16[128,1024]{1,0:T(8,128)(2,1)S(1)}, u32[]{:S(2)}, u32[]{:S(2)}) collective-permute-start(bf16[128,1024]{1,0:T(8,128)(2,1)S(1)} %get-tuple-element.37), channel_id=1, source_target_pairs={{0,2},{1,3},{2,10},{3,11},{4,18},{5,19},{6,26},{7,27},{8,0},{9,1},... | collective-permute-start | bytes 786440 | tf_op jit(solution)/shard_map/ppermute | solution.py:498
  8.2 42.0 %collective-permute-start.2 = (bf16[128,1024]{1,0:T(8,128)(2,1)S(1)}, bf16[128,1024]{1,0:T(8,128)(2,1)S(1)}, u32[]{:S(2)}, u32[]{:S(2)}) collective-permute-start(bf16[128,1024]{1,0:T(8,128)(2,1)S(1)} %get-tuple-element.37), channel_id=1, source_target_pairs={{0,4},{1,5},{2,12},{3,13},{4,20},{5,21},{6,28},{7,29},{8,6},{9,7},... | collective-permute-start | bytes 786440 | tf_op jit(solution)/shard_map/ppermute | solution.py:498
  11.6 38.5 %collective-permute-start.3 = (bf16[128,1024]{1,0:T(8,128)(2,1)S(1)}, bf16[128,1024]{1,0:T(8,128)(2,1)S(1)}, u32[]{:S(2)}, u32[]{:S(2)}) collective-permute-start(bf16[128,1024]{1,0:T(8,128)(2,1)S(1)} %get-tuple-element.37), channel_id=1, source_target_pairs={{0,6},{1,7},{2,14},{3,15},{4,22},{5,23},{6,30},{7,31},{8,4},{9,5},... | collective-permute-start | bytes 786440 | tf_op jit(solution)/shard_map/ppermute | solution.py:498
  53.9 40.7 %collective-permute-start.4 = (bf16[512,1024]{1,0:T(8,128)(2,1)}, bf16[512,1024]{1,0:T(8,128)(2,1)S(1)}, u32[]{:S(2)}, u32[]{:S(2)}) collective-permute-start(bf16[512,1024]{1,0:T(8,128)(2,1)} %pack.1.own), channel_id=1, source_target_pairs={{0,1},{1,0},{2,3},{3,2},{4,5},{5,4},{6,7},{7,6},{8,9},{9,8},{10,11... | collective-permute-start | bytes 3145736 | tf_op jit(solution)/shard_map/ppermute | solution.py:490
  104.6 25.0 %collective-permute-start.19 = (bf16[512,512]{1,0:T(8,128)(2,1)S(1)}, bf16[512,512]{1,0:T(8,128)(2,1)S(1)}, u32[]{:S(2)}, u32[]{:S(2)}) collective-permute-start(bf16[512,512]{1,0:T(8,128)(2,1)S(1)} %get-tuple-element.26), channel_id=1, source_target_pairs={{0,8},{8,0},{16,24},{24,16},{1,9},{9,1},{17,25},{25,17},{2,10},{10... | collective-permute-start | bytes 1572872 | tf_op jit(solution)/shard_map/ppermute | solution.py:484
  106.9 24.5 %collective-permute-start.20 = (bf16[512,512]{1,0:T(8,128)(2,1)S(1)}, bf16[512,512]{1,0:T(8,128)(2,1)S(1)}, u32[]{:S(2)}, u32[]{:S(2)}) collective-permute-start(bf16[512,512]{1,0:T(8,128)(2,1)S(1)} %get-tuple-element.27), channel_id=1, source_target_pairs={{0,16},{8,24},{16,0},{24,8},{1,17},{9,25},{17,1},{25,9},{2,18},{10... | collective-permute-start | bytes 1572872 | tf_op jit(solution)/shard_map/ppermute | solution.py:484
  107.4 27.4 %collective-permute-start.21 = (bf16[512,512]{1,0:T(8,128)(2,1)}, bf16[512,512]{1,0:T(8,128)(2,1)}, u32[]{:S(2)}, u32[]{:S(2)}) collective-permute-start(bf16[512,512]{1,0:T(8,128)(2,1)} %get-tuple-element.28), channel_id=1, source_target_pairs={{0,24},{8,16},{16,8},{24,0},{1,25},{9,17},{17,9},{25,1},{2,26},{10... | collective-permute-start | bytes 1572872 | tf_op jit(solution)/shard_map/ppermute | solution.py:484
  117.5 24.8 %collective-permute-start.12 = (bf16[512,512]{1,0:T(8,128)(2,1)}, bf16[512,512]{1,0:T(8,128)(2,1)S(1)}, u32[]{:S(2)}, u32[]{:S(2)}) collective-permute-start(bf16[512,512]{1,0:T(8,128)(2,1)} %get-tuple-element.22), channel_id=1, source_target_pairs={{0,8},{8,0},{16,24},{24,16},{1,9},{9,1},{17,25},{25,17},{2,10},{10... | collective-permute-start | bytes 1572872 | tf_op jit(solution)/shard_map/ppermute | solution.py:484
  119.5 32.6 %collective-permute-start.13 = (bf16[512,512]{1,0:T(8,128)(2,1)}, bf16[512,512]{1,0:T(8,128)(2,1)}, u32[]{:S(2)}, u32[]{:S(2)}) collective-permute-start(bf16[512,512]{1,0:T(8,128)(2,1)} %get-tuple-element.23), channel_id=1, source_target_pairs={{0,16},{8,24},{16,0},{24,8},{1,17},{9,25},{17,1},{25,9},{2,18},{10... | collective-permute-start | bytes 1572872 | tf_op jit(solution)/shard_map/ppermute | solution.py:484
  130.4 24.6 %collective-permute-start.14 = (bf16[512,512]{1,0:T(8,128)(2,1)}, bf16[512,512]{1,0:T(8,128)(2,1)}, u32[]{:S(2)}, u32[]{:S(2)}) collective-permute-start(bf16[512,512]{1,0:T(8,128)(2,1)} %get-tuple-element.24), channel_id=1, source_target_pairs={{0,24},{8,16},{16,8},{24,0},{1,25},{9,17},{17,9},{25,1},{2,26},{10... | collective-permute-start | bytes 1572872 | tf_op jit(solution)/shard_map/ppermute | solution.py:484
  132.2 32.6 %collective-permute-start.5 = (bf16[512,512]{1,0:T(8,128)(2,1)}, bf16[512,512]{1,0:T(8,128)(2,1)S(1)}, u32[]{:S(2)}, u32[]{:S(2)}) collective-permute-start(bf16[512,512]{1,0:T(8,128)(2,1)} %get-tuple-element.18), channel_id=1, source_target_pairs={{0,8},{8,0},{16,24},{24,16},{1,9},{9,1},{17,25},{25,17},{2,10},{10... | collective-permute-start | bytes 1572872 | tf_op jit(solution)/shard_map/ppermute | solution.py:484
  134.8 45.4 %collective-permute-start.6 = (bf16[512,512]{1,0:T(8,128)(2,1)}, bf16[512,512]{1,0:T(8,128)(2,1)}, u32[]{:S(2)}, u32[]{:S(2)}) collective-permute-start(bf16[512,512]{1,0:T(8,128)(2,1)} %copy-done.20), channel_id=1, source_target_pairs={{0,16},{8,24},{16,0},{24,8},{1,17},{9,25},{17,1},{25,9},{2,18},{10... | collective-permute-start | bytes 1572872 | tf_op jit(solution)/shard_map/ppermute | solution.py:484
  142.2 38.0 %collective-permute-start.7 = (bf16[512,512]{1,0:T(8,128)(2,1)}, bf16[512,512]{1,0:T(8,128)(2,1)}, u32[]{:S(2)}, u32[]{:S(2)}) collective-permute-start(bf16[512,512]{1,0:T(8,128)(2,1)} %copy-done.19), channel_id=1, source_target_pairs={{0,24},{8,16},{16,8},{24,0},{1,25},{9,17},{17,9},{25,1},{2,26},{10... | collective-permute-start | bytes 1572872 | tf_op jit(solution)/shard_map/ppermute | solution.py:484
  152.1 18.7 %collective-permute-start.22 = (bf16[512,256]{1,0:T(8,128)(2,1)S(1)}, bf16[512,256]{1,0:T(8,128)(2,1)S(1)}, u32[]{:S(2)}, u32[]{:S(2)}) collective-permute-start(bf16[512,256]{1,0:T(8,128)(2,1)S(1)} %combine_0.1.refs_0_), channel_id=1, source_target_pairs={{0,2},{1,3},{2,0},{3,1},{4,6},{5,7},{6,4},{7,5},{8,10},{9,11},{10,... | collective-permute-start | bytes 786440 | tf_op jit(solution)/shard_map/ppermute | solution.py:487
  155.1 15.8 %collective-permute-start.23 = (bf16[512,256]{1,0:T(8,128)(2,1)S(1)}, bf16[512,256]{1,0:T(8,128)(2,1)S(1)}, u32[]{:S(2)}, u32[]{:S(2)}) collective-permute-start(bf16[512,256]{1,0:T(8,128)(2,1)S(1)} %combine_0.1.refs_0_), channel_id=1, source_target_pairs={{0,4},{1,5},{2,6},{3,7},{4,0},{5,1},{6,2},{7,3},{8,12},{9,13},{10,... | collective-permute-start | bytes 786440 | tf_op jit(solution)/shard_map/ppermute | solution.py:487
  164.8 10.9 %collective-permute-start.24 = (bf16[512,256]{1,0:T(8,128)(2,1)S(1)}, bf16[512,256]{1,0:T(8,128)(2,1)S(1)}, u32[]{:S(2)}, u32[]{:S(2)}) collective-permute-start(bf16[512,256]{1,0:T(8,128)(2,1)S(1)} %combine_0.1.refs_0_), channel_id=1, source_target_pairs={{0,6},{1,7},{2,4},{3,5},{4,2},{5,3},{6,0},{7,1},{8,14},{9,15},{10,... | collective-permute-start | bytes 786440 | tf_op jit(solution)/shard_map/ppermute | solution.py:487
  170.8 30.0 %copy-start.4 = (bf16[512,256]{1,0:T(8,128)(2,1)}, bf16[512,256]{1,0:T(8,128)(2,1)S(1)}, u32[]{:S(2)}) copy-start(bf16[512,256]{1,0:T(8,128)(2,1)S(1)} %combine_1.1.refs_0_) | copy-start | bytes 786436
  170.8 15.3 %collective-permute-start.15 = (bf16[512,256]{1,0:T(8,128)(2,1)S(1)}, bf16[512,256]{1,0:T(8,128)(2,1)}, u32[]{:S(2)}, u32[]{:S(2)}) collective-permute-start(bf16[512,256]{1,0:T(8,128)(2,1)S(1)} %combine_1.1.refs_0_), channel_id=1, source_target_pairs={{0,2},{1,3},{2,0},{3,1},{4,6},{5,7},{6,4},{7,5},{8,10},{9,11},{10,... | collective-permute-start | bytes 786440 | tf_op jit(solution)/shard_map/ppermute | solution.py:487
  170.9 29.9 %collective-permute-start.16 = (bf16[512,256]{1,0:T(8,128)(2,1)S(1)}, bf16[512,256]{1,0:T(8,128)(2,1)}, u32[]{:S(2)}, u32[]{:S(2)}) collective-permute-start(bf16[512,256]{1,0:T(8,128)(2,1)S(1)} %combine_1.1.refs_0_), channel_id=1, source_target_pairs={{0,4},{1,5},{2,6},{3,7},{4,0},{5,1},{6,2},{7,3},{8,12},{9,13},{10,... | collective-permute-start | bytes 786440 | tf_op jit(solution)/shard_map/ppermute | solution.py:487
  176.4 24.4 %collective-permute-start.17 = (bf16[512,256]{1,0:T(8,128)(2,1)S(1)}, bf16[512,256]{1,0:T(8,128)(2,1)}, u32[]{:S(2)}, u32[]{:S(2)}) collective-permute-start(bf16[512,256]{1,0:T(8,128)(2,1)S(1)} %combine_1.1.refs_0_), channel_id=1, source_target_pairs={{0,6},{1,7},{2,4},{3,5},{4,2},{5,3},{6,0},{7,1},{8,14},{9,15},{10,... | collective-permute-start | bytes 786440 | tf_op jit(solution)/shard_map/ppermute | solution.py:487
  180.2 43.5 %copy-start.1 = (bf16[4,512,256]{2,1,0:T(8,128)(2,1)S(1)}, bf16[4,512,256]{2,1,0:T(8,128)(2,1)}, u32[]{:S(2)}) copy-start(bf16[4,512,256]{2,1,0:T(8,128)(2,1)} %pack_hidden.5.own) | copy-start | bytes 3145732
  180.2 43.5 %collective-permute-start.25 = (bf16[4,512,256]{2,1,0:T(8,128)(2,1)}, bf16[4,512,256]{2,1,0:T(8,128)(2,1)S(1)}, u32[]{:S(2)}, u32[]{:S(2)}) collective-permute-start(bf16[4,512,256]{2,1,0:T(8,128)(2,1)} %pack_hidden.5.own), channel_id=1, source_target_pairs={{0,1},{1,0},{2,3},{3,2},{4,5},{5,4},{6,7},{7,6},{8,9},{9,8},{10,11... | collective-permute-start | bytes 3145736 | tf_op jit(solution)/shard_map/ppermute | solution.py:490
  183.8 37.0 %copy-start.6 = (bf16[512,256]{1,0:T(8,128)(2,1)}, bf16[512,256]{1,0:T(8,128)(2,1)S(1)}, u32[]{:S(2)}) copy-start(bf16[512,256]{1,0:T(8,128)(2,1)S(1)} %combine_2.1.refs_0_) | copy-start | bytes 786436
  183.8 19.2 %collective-permute-start.10 = (bf16[512,256]{1,0:T(8,128)(2,1)S(1)}, bf16[512,256]{1,0:T(8,128)(2,1)S(1)}, u32[]{:S(2)}, u32[]{:S(2)}) collective-permute-start(bf16[512,256]{1,0:T(8,128)(2,1)S(1)} %combine_2.1.refs_0_), channel_id=1, source_target_pairs={{0,6},{1,7},{2,4},{3,5},{4,2},{5,3},{6,0},{7,1},{8,14},{9,15},{10,... | collective-permute-start | bytes 786440 | tf_op jit(solution)/shard_map/ppermute | solution.py:487
  186.1 17.7 %collective-permute-start.8 = (bf16[512,256]{1,0:T(8,128)(2,1)S(1)}, bf16[512,256]{1,0:T(8,128)(2,1)S(1)}, u32[]{:S(2)}, u32[]{:S(2)}) collective-permute-start(bf16[512,256]{1,0:T(8,128)(2,1)S(1)} %combine_2.1.refs_0_), channel_id=1, source_target_pairs={{0,2},{1,3},{2,0},{3,1},{4,6},{5,7},{6,4},{7,5},{8,10},{9,11},{10,... | collective-permute-start | bytes 786440 | tf_op jit(solution)/shard_map/ppermute | solution.py:487
  200.8 20.0 %collective-permute-start.9 = (bf16[512,256]{1,0:T(8,128)(2,1)S(1)}, bf16[512,256]{1,0:T(8,128)(2,1)S(1)}, u32[]{:S(2)}, u32[]{:S(2)}) collective-permute-start(bf16[512,256]{1,0:T(8,128)(2,1)S(1)} %combine_2.1.refs_0_), channel_id=1, source_target_pairs={{0,4},{1,5},{2,6},{3,7},{4,0},{5,1},{6,2},{7,3},{8,12},{9,13},{10,... | collective-permute-start | bytes 786440 | tf_op jit(solution)/shard_map/ppermute | solution.py:487
  203.0 25.3 %collective-permute-start.18 = (bf16[4,512,256]{2,1,0:T(8,128)(2,1)}, bf16[4,512,256]{2,1,0:T(8,128)(2,1)}, u32[]{:S(2)}, u32[]{:S(2)}) collective-permute-start(bf16[4,512,256]{2,1,0:T(8,128)(2,1)} %pack_hidden.4.own), channel_id=1, source_target_pairs={{0,1},{1,0},{2,3},{3,2},{4,5},{5,4},{6,7},{7,6},{8,9},{9,8},{10,11... | collective-permute-start | bytes 3145736 | tf_op jit(solution)/shard_map/ppermute | solution.py:490
  223.7 9.6 %collective-permute-start.11 = (bf16[4,512,256]{2,1,0:T(8,128)(2,1)}, bf16[4,512,256]{2,1,0:T(8,128)(2,1)}, u32[]{:S(2)}, u32[]{:S(2)}) collective-permute-start(bf16[4,512,256]{2,1,0:T(8,128)(2,1)} %pack_hidden.3.own), channel_id=1, source_target_pairs={{0,1},{1,0},{2,3},{3,2},{4,5},{5,4},{6,7},{7,6},{8,9},{9,8},{10,11... | collective-permute-start | bytes 3145736 | tf_op jit(solution)/shard_map/ppermute | solution.py:490
  238.2 9.9 %collective-permute-start.26 = (bf16[128,1024]{1,0:T(8,128)(2,1)S(1)}, bf16[128,1024]{1,0:T(8,128)(2,1)S(1)}, u32[]{:S(2)}, u32[]{:S(2)}) collective-permute-start(bf16[128,1024]{1,0:T(8,128)(2,1)S(1)} %get-tuple-element.33), channel_id=1, source_target_pairs={{0,8},{8,0},{16,24},{24,16},{1,9},{9,1},{17,25},{25,17},{2,10},{10... | collective-permute-start | bytes 786440 | tf_op jit(solution)/shard_map/ppermute | solution.py:484
  240.9 14.0 %collective-permute-start.27 = (bf16[128,1024]{1,0:T(8,128)(2,1)S(1)}, bf16[128,1024]{1,0:T(8,128)(2,1)S(1)}, u32[]{:S(2)}, u32[]{:S(2)}) collective-permute-start(bf16[128,1024]{1,0:T(8,128)(2,1)S(1)} %get-tuple-element.35), channel_id=1, source_target_pairs={{0,16},{8,24},{16,0},{24,8},{1,17},{9,25},{17,1},{25,9},{2,18},{10... | collective-permute-start | bytes 786440 | tf_op jit(solution)/shard_map/ppermute | solution.py:484
  240.9 14.0 %collective-permute-start.28 = (bf16[128,1024]{1,0:T(8,128)(2,1)S(1)}, bf16[128,1024]{1,0:T(8,128)(2,1)S(1)}, u32[]{:S(2)}, u32[]{:S(2)}) collective-permute-start(bf16[128,1024]{1,0:T(8,128)(2,1)S(1)} %get-tuple-element.34), channel_id=1, source_target_pairs={{0,24},{8,16},{16,8},{24,0},{1,25},{9,17},{17,9},{25,1},{2,26},{10... | collective-permute-start | bytes 786440 | tf_op jit(solution)/shard_map/ppermute | solution.py:484
  (30 other events, 173.6 us)

commit v3 on v2

--- a/solution.py
+++ b/solution.py
@@ -229,7 +229,7 @@
     own = [own[0]] + [swap_tok(own[part], part) for part in range(1, tok_size)]
     other = [swap_core(part) for part in own]
 
-    hiddens = []
+    hiddens, halves = [], []
     for chunk in range(chunks):
         sums = gate_up(own, other, dense, chunk)
         terms = [sums[0]] + [swap_tok(sums[part], part) for part in range(1, tok_size)]
@@ -269,7 +269,7 @@
             in_specs=[whole, whole],
             out_specs=pl.BlockSpec((1,) + out.shape[1:], lambda k, *_: (k, 0, 0)),
         ),
-        compiler_params=pltpu.CompilerParams(vmem_limit_bytes=48 * MIB),
+        compiler_params=pltpu.CompilerParams(vmem_limit_bytes=54 * MIB),
         cost_estimate=pl.CostEstimate(
             flops=0, bytes_accessed=2 * (2 * gate.size + out.size), transcendentals=0
         ),
@@ -300,33 +300,53 @@
             ],
             out_specs=pl.BlockSpec((chunks, rows * edge, cols * edge), lambda m, *_: (0, m, 0)),
         ),
-        compiler_params=pltpu.CompilerParams(vmem_limit_bytes=48 * MIB),
+        compiler_params=pltpu.CompilerParams(vmem_limit_bytes=16 * MIB),
         cost_estimate=pl.CostEstimate(
             flops=0, bytes_accessed=2 * (values.size + out.size), transcendentals=0
         ),
         name="spread_down",
     )(at, panels, values)
 
+def sum_squares_kernel(tokens, _, out):
+    widened = tokens[...].astype(jnp.float32)
+    out[...] = jnp.sum(widened * widened, axis=1)[None]
+
+
+def sum_squares(tokens, after):
+    return pl.pallas_call(
+        sum_squares_kernel,
+        out_shape=jax.ShapeDtypeStruct((1, tokens.shape[0]), jnp.float32),
+        in_specs=[pl.BlockSpec(memory_space=pltpu.VMEM), pl.BlockSpec(memory_space=pl.ANY)],
+        out_specs=pl.BlockSpec(memory_space=pltpu.VMEM),
+        compiler_params=pltpu.CompilerParams(vmem_limit_bytes=4 * MIB),
+        name="sum_squares",
+    )(tokens, after)
+
+
 def pack_kernel(*refs, parts):
-    count = refs[0].shape[0]
+    pieces, scale, gain, out = refs[:parts], refs[parts], refs[parts + 1], refs[-1]
+    count = pieces[0].shape[0]
     for part in range(parts):
-        refs[-1][part * count:(part + 1) * count] = refs[part][...]
-
-
-def pack(pieces, after):
+        rows = slice(part * count, (part + 1) * count)
+        piece = pieces[part][...].astype(jnp.float32)
+        out[rows] = (piece * scale[rows] * gain[...]).astype(out.dtype)
+
+
+def pack(pieces, scale, gain, after):
     parts = len(pieces)
     count, width = pieces[0].shape
     return pl.pallas_call(
         functools.partial(pack_kernel, parts=parts),
         out_shape=jax.ShapeDtypeStruct((parts * count, width), pieces[0].dtype),
-        in_specs=[pl.BlockSpec(memory_space=pltpu.VMEM)] * parts
+        in_specs=[pl.BlockSpec(memory_space=pltpu.VMEM)] * (parts + 2)
         + [pl.BlockSpec(memory_space=pl.ANY)] * len(after),
         out_specs=pl.BlockSpec(memory_space=pltpu.VMEM),
+        compiler_params=pltpu.CompilerParams(vmem_limit_bytes=16 * MIB),
         cost_estimate=pl.CostEstimate(
             flops=0, bytes_accessed=4 * parts * count * width, transcendentals=0
         ),
         name="pack",
-    )(*pieces, *after)
+    )(*pieces, scale, gain, *after)
 
 
 def pack_hidden_kernel(*refs, parts):
@@ -338,74 +358,110 @@
             out[step, part * count:(part + 1) * count] = refs[step][there * count:(there + 1) * count]
 
 
-def pack_hidden(pieces):
+def pack_hidden(pieces, after):
     parts = len(pieces)
     return pl.pallas_call(
         functools.partial(pack_hidden_kernel, parts=parts),
         out_shape=jax.ShapeDtypeStruct((parts,) + pieces[0].shape, pieces[0].dtype),
-        in_specs=[pl.BlockSpec(memory_space=pltpu.VMEM)] * parts,
+        in_specs=[pl.BlockSpec(memory_space=pltpu.VMEM)] * parts
+        + [pl.BlockSpec(memory_space=pl.ANY)] * len(after),
         out_specs=pl.BlockSpec(memory_space=pltpu.VMEM),
+        compiler_params=pltpu.CompilerParams(vmem_limit_bytes=16 * MIB),
         cost_estimate=pl.CostEstimate(
             flops=0, bytes_accessed=4 * parts * pieces[0].size, transcendentals=0
         ),
         name="pack_hidden",
-    )(*pieces)
-
-
-def combine_kernel(*refs, parts):
-    terms, scale, out = refs[:parts], refs[parts], refs[-1]
-    total = functools.reduce(jnp.add, [term[...].astype(jnp.float32) for term in terms])
-    total *= scale[...]
-    width = out.shape[-1]
-    gate_sum, up_sum = total[:, :width], total[:, width:]
-    out[...] = (gate_sum / (1.0 + jnp.exp(-gate_sum)) * up_sum).astype(out.dtype)
-
-
-def combine(terms, scale, after, chunk):
-    parts = len(terms)
-    count, width = terms[0].shape
-    rows = count // 4
-    return pl.pallas_call(
-        functools.partial(combine_kernel, parts=parts),
-        out_shape=jax.ShapeDtypeStruct((count, width // 2), terms[0].dtype),
-        grid=(count // rows,),
-        in_specs=[pl.BlockSpec((rows, width), lambda i: (i, 0))] * parts
-        + [pl.BlockSpec((rows, 1), lambda i: (i, 0)), pl.BlockSpec(memory_space=pl.ANY)],
-        out_specs=pl.BlockSpec((rows, width // 2), lambda i: (i, 0)),
-        compiler_params=pltpu.CompilerParams(vmem_limit_bytes=32 * MIB),
+    )(*pieces, *after)
+
+
+def halfway_kernel(kept_a, came_a, kept_b, came_b, _, out_a, out_b):
+    for kept, came, out in ((kept_a, came_a, out_a), (kept_b, came_b, out_b)):
+        out[...] = (kept[0].astype(jnp.float32) + came[0].astype(jnp.float32)).astype(out.dtype)
+
+
+def halfway(kept_a, came_a, kept_b, came_b, after, chunk):
+    _, count, width = kept_a.shape
+    second = pl.BlockSpec((1, count, width), lambda i: (1, 0, 0))
+    whole = pl.BlockSpec((count, width), lambda i: (0, 0))
+    out = jax.ShapeDtypeStruct((count, width), kept_a.dtype)
+    return pl.pallas_call(
+        halfway_kernel,
+        out_shape=[out, out],
+        grid=(1,),
+        in_specs=[second] * 4 + [pl.BlockSpec(memory_space=pl.ANY)],
+        out_specs=[whole, whole],
+        compiler_params=pltpu.CompilerParams(vmem_limit_bytes=8 * MIB),
+        cost_estimate=pl.CostEstimate(
+            flops=2 * count * width, bytes_accessed=12 * count * width, transcendentals=0
+        ),
+        name=f"halfway_{chunk}",
+    )(kept_a, came_a, kept_b, came_b, after)
+
+
+def combine_kernel(*refs):
+    terms, out = refs[:6], refs[-1]
+    count = out.shape[0] // 2
+    width = out.shape[1]
+    for i in range(2):
+        kept, came, last = terms[3 * i:3 * i + 3]
+        total = kept[0].astype(jnp.float32) + came[0].astype(jnp.float32)
+        total += last[...].astype(jnp.float32)
+        gate_sum, up_sum = total[:, :width], total[:, width:]
+        hidden = gate_sum / (1.0 + jnp.exp(-gate_sum)) * up_sum
+        out[i * count:(i + 1) * count] = hidden.astype(out.dtype)
+
+
+def combine(kept_a, came_a, last_a, kept_b, came_b, last_b, after, chunk):
+    count, width = last_a.shape
+    first = pl.BlockSpec((1, count, width), lambda i: (0, 0, 0))
+    whole = pl.BlockSpec((count, width), lambda i: (0, 0))
+    return pl.pallas_call(
+        combine_kernel,
+        out_shape=jax.ShapeDtypeStruct((2 * count, width // 2), last_a.dtype),
+        grid=(1,),
+        in_specs=[first, first, whole] * 2 + [pl.BlockSpec(memory_space=pl.ANY)],
+        out_specs=pl.BlockSpec((2 * count, width // 2), lambda i: (0, 0)),
+        compiler_params=pltpu.CompilerParams(vmem_limit_bytes=10 * MIB),
         cost_estimate=pl.CostEstimate(
             flops=8 * count * width,
-            bytes_accessed=2 * count * width * (parts + 1),
+            bytes_accessed=14 * count * width,
             transcendentals=count * width // 2,
         ),
         name=f"combine_{chunk}",
-    )(*terms, scale, after)
-
-
-def panel_product_kernel(own, other, weight, *outs):
+    )(kept_a, came_a, last_a, kept_b, came_b, last_b, after)
+
+
+def panel_product_kernel(own, other, weight, kept_a, sent_a, kept_b, sent_b):
     half = own.shape[1]
     product = jnp.dot(own[...], weight[0, :half], preferred_element_type=jnp.float32)
     product += jnp.dot(other[...], weight[0, half:], preferred_element_type=jnp.float32)
-    for part, out in enumerate(outs):
-
-        @pl.when(pl.program_id(0) == part)
+    product = product.astype(kept_a.dtype)
+    count = product.shape[0] // 2
+    part = pl.program_id(0)
+    for flip in range(2):
+
+        @pl.when(part % 2 == flip)
         def _():
-            out[...] = product.astype(out.dtype)
-
-
-def panel_product(own, other, dense, parts, chunk):
+            (sent_a if flip else kept_a)[part // 2] = product[:count]
+
+        @pl.when(part // 2 == flip)
+        def _():
+            (sent_b if flip else kept_b)[part % 2] = product[count:]
+
+
+def panel_product(own, other, dense, chunk):
     count, half = own.shape
     _, depth, width = dense.shape
-    tile = width // parts
-    out = jax.ShapeDtypeStruct((count, tile), own.dtype)
+    tile = width // 4
+    out = jax.ShapeDtypeStruct((2, count // 2, tile), own.dtype)
     return pl.pallas_call(
         panel_product_kernel,
-        out_shape=[out] * parts,
-        grid=(parts,),
+        out_shape=[out] * 4,
+        grid=(4,),
         in_specs=[pl.BlockSpec((count, half), lambda n: (0, 0))] * 2
         + [pl.BlockSpec((1, depth, tile), lambda n: (chunk, 0, n))],
-        out_specs=[pl.BlockSpec((count, tile), lambda n: (0, 0))] * parts,
-        compiler_params=pltpu.CompilerParams(vmem_limit_bytes=40 * MIB),
+        out_specs=[pl.BlockSpec(out.shape, lambda n: (0, 0, 0))] * 4,
+        compiler_params=pltpu.CompilerParams(vmem_limit_bytes=42 * MIB),
         cost_estimate=pl.CostEstimate(
             flops=2 * count * depth * width,
             bytes_accessed=2 * (depth * width + count * (depth + width)),
@@ -415,8 +471,8 @@
     )(own, other, dense)
 
 
-def down_product_kernel(own, other, weight, *refs):
-    before, out, held = refs[0] if len(refs) == 3 else None, refs[-2], refs[-1]
+def down_product_kernel(flips, own, other, weight, *refs, added):
+    before, outs, held = refs[:added], refs[added:-1], refs[-1]
     panels, _, depth = own.shape
 
     @pl.when(pl.program_id(0) == 0)
@@ -425,35 +481,55 @@
             held[:, i * depth:(i + 1) * depth] = own[i]
             held[:, (panels + i) * depth:(panels + i + 1) * depth] = other[i]
 
-    product = jnp.dot(held[...], weight[0], preferred_element_type=jnp.float32)
-    if before is not None:
-        product += before[...]
-    out[...] = product.astype(out.dtype)
-
-
-def down_product(own, other, dense, before, chunk, dtype):
+    if len(outs) == 1:
+        product = jnp.dot(held[...], weight[0], preferred_element_type=jnp.float32)
+        for term in before:
+            product += term[...]
+        outs[0][...] = product
+        return
+    count = outs[0].shape[0]
+    order = []
+    for step, out in enumerate(outs):
+        at = pl.multiple_of((flips[0] ^ step) * count, count)
+        order.append(at)
+    for step, out in enumerate(outs):
+        rows = pl.ds(order[step], count)
+        product = jnp.dot(held[rows], weight[0], preferred_element_type=jnp.float32)
+        for term in before:
+            product += term[rows]
+        out[...] = product.astype(out.dtype)
+
+
+def down_product(own, other, dense, before, chunk, flips):
     panels, count, depth = own.shape
     _, total, width = dense.shape
     tile = width // 2
-    tiles = pl.BlockSpec((count, tile), lambda n: (0, n))
-    whole = pl.BlockSpec((panels, count, depth), lambda n: (0, 0, 0))
+    tiles = pl.BlockSpec((count, tile), lambda n, *_: (0, n))
+    whole = pl.BlockSpec((panels, count, depth), lambda n, *_: (0, 0, 0))
     added = [] if before is None else [before]
-    return pl.pallas_call(
-        down_product_kernel,
-        out_shape=jax.ShapeDtypeStruct((count, width), dtype),
-        grid=(width // tile,),
-        in_specs=[whole, whole, pl.BlockSpec((1, total, tile), lambda n: (chunk, 0, n))]
-        + [tiles] * len(added),
-        out_specs=tiles,
-        scratch_shapes=[pltpu.VMEM((count, total), own.dtype)],
-        compiler_params=pltpu.CompilerParams(vmem_limit_bytes=40 * MIB),
+    out, out_tiles = jax.ShapeDtypeStruct((count, width), jnp.float32), tiles
+    if flips is not None:
+        out = [jax.ShapeDtypeStruct((count // panels, width), own.dtype)] * panels
+        out_tiles = [pl.BlockSpec((count // panels, tile), lambda n, *_: (0, n))] * panels
+    return pl.pallas_call(
+        functools.partial(down_product_kernel, added=len(added)),
+        out_shape=out,
+        grid_spec=pltpu.PrefetchScalarGridSpec(
+            num_scalar_prefetch=1,
+            grid=(width // tile,),
+            in_specs=[whole, whole, pl.BlockSpec((1, total, tile), lambda n, *_: (chunk, 0, n))]
+            + [tiles] * len(added),
+            out_specs=out_tiles,
+            scratch_shapes=[pltpu.VMEM((count, total), own.dtype)],
+        ),
+        compiler_params=pltpu.CompilerParams(vmem_limit_bytes=24 * MIB),
         cost_estimate=pl.CostEstimate(
             flops=2 * count * total * width,
             bytes_accessed=2 * total * (width + count) + 8 * count * width,
             transcendentals=0,
         ),
         name=f"down_{chunk}",
-    )(own, other, dense, *added)
+    )(jnp.int32(0)[None] if flips is None else flips[None], own, other, dense, *added)
 
 
 def by_columns(
@@ -497,14 +573,7 @@
                 pairs.append((i * col_size + j, user))
         return lax.ppermute(array, ("tok", "col"), pairs)
 
-    widened = tokens.astype(jnp.float32)
-    gain = lax.dynamic_slice_in_dim(norm_gain, col * half, half, 0)
-    gained = (widened * gain).astype(jnp.bfloat16)
-    pieces = [to_users(gained, part) for part in parts]
-    squares = jnp.sum(widened * widened, axis=1)
-    squares = jnp.where(jnp.arange(tok_size)[:, None] == tok, squares[None], 0.0)
-    squares = lax.psum(squares, ("tok", "col"))
-
+    pieces = [to_users(tokens, part) for part in parts]
     k, r, p, q = jnp.meshgrid(
         jnp.arange(chunks), jnp.arange(rows_per), jnp.arange(tok_size), jnp.arange(cols),
         indexing="ij",
@@ -523,27 +592,43 @@
     )
     down_dense = spread_panels(down_at, panels, down_values, chunks, cols, width_blocks)
 
-    own = pack(pieces, [dense, down_dense])
+    squares = sum_squares(tokens, dense)
+    squares += swap_core(squares)
+    squares += swap_chip(squares, 1)
+    squares += swap_chip(squares, 2)
+    squares = jnp.concatenate([squares, swap_tok(squares, 1)])
+    squares = jnp.concatenate([squares, swap_tok(squares, 2)])
+
+    gain = lax.dynamic_slice_in_dim(norm_gain, (tok * 2 + side) * half, half, 0)[None]
+    scale = lax.rsqrt(squares / MODEL_WIDTH + EPSILON)
+    scale = jnp.take(scale, jnp.arange(tok_size) ^ chip ^ tok, axis=0).reshape(-1, 1)
+    own = pack(pieces, scale, gain, [down_dense])
     other = swap_core(own)
 
-    sums = [panel_product(own, other, dense, tok_size, chunk) for chunk in range(chunks)]
-    scale = lax.rsqrt(squares / MODEL_WIDTH + EPSILON)
-    scale = jnp.take(scale, jnp.arange(tok_size) ^ chip, axis=0).reshape(-1, 1)
+    sums = [panel_product(own, other, dense, chunk) for chunk in range(chunks)]
+    hiddens, halves = [], []
+    for chunk in range(chunks):
+        kept_a, sent_a, kept_b, sent_b = sums[chunk]
+        came_a, came_b = swap_tok(sent_a, 1), swap_tok(sent_b, 2)
+        ahead = sums[min(chunk + 1, chunks - 1)][0]
+        last_a, last_b = halfway(kept_a, came_a, kept_b, came_b, ahead, chunk)
+        halves.append(last_a)
+        last_a, last_b = swap_tok(last_a, 2), swap_tok(last_b, 1)
+        hidden = combine(kept_a, came_a, last_a, kept_b, came_b, last_b, sums[-1][0], chunk)
+        hiddens.append(hidden)
+
     mixed = None
     for chunk in range(chunks):
-        terms = [sums[chunk][0]] + [swap_tok(sums[chunk][p], p) for p in parts[1:]]
-        hidden = combine(terms, scale, sums[-1][0], chunk)
-        held = pack_hidden([hidden] + [swap_chip(hidden, step) for step in parts[1:]])
-        last = chunk == chunks - 1
-        mixed = down_product(
-            held, swap_core(held), down_dense, mixed, chunk, jnp.bfloat16 if last else jnp.float32
-        )
-
-    mixed = mixed.reshape(tok_size, count, -1)
-    total = 0.0
-    for step in parts:
-        part = lax.dynamic_index_in_dim(mixed, chip ^ tok ^ step, 0, keepdims=False)
-        total += (swap_tok(part, step) if step else part).astype(jnp.float32)
+        held = [hiddens[chunk]] + [swap_chip(hiddens[chunk], step) for step in parts[1:]]
+        ahead = hiddens[chunk + 1:chunk + 2] + halves[chunk + 2:chunk + 3]
+        ahead += [] if mixed is None else [mixed]
+        held = pack_hidden(held, ahead)
+        last = chip ^ tok if chunk == chunks - 1 else None
+        mixed = down_product(held, swap_core(held), down_dense, mixed, chunk, last)
+
+    total = mixed[0].astype(jnp.float32)
+    for step in parts[1:]:
+        total += swap_tok(mixed[step], step).astype(jnp.float32)
     return total.astype(jnp.bfloat16)
 
 

time: 257 us -> 248 us (0.965)
  blocking collectives: 40.6 us -> 0 us
  waiting for transfers between devices: 64.3 us -> 99 us
  Pallas kernels: 88.1 us -> 65.6 us
  starting transfers between devices: 40.7 us -> 51.4 us
  local copies, waits for them, and re-layouts: 18.3 us -> 25.2 us
    psum x1 -> x0, blocking collectives: 40.6 us -> none  [by_columns(): squares = lax.psum(squares, ('tok', 'col'))]
    ppermute x9 -> x11, waiting for transfers between devices: 30 us -> 49.8 us  [swap_chip(): lax.ppermute(array, 'col', [(i, i ^ 2 * step) for i in range(col_size)])]
    pallas_call x9 -> x13, Pallas kernels: 45.6 us -> 34.8 us  [the longest x3 22.4 us: panel_product(): pl.pallas_call(panel_product_kernel, out_shape=[out] * 4, grid=(4,), in_s...]
    ppermute x12 -> x17, waiting for transfers between devices: 34.2 us -> 43.8 us  [swap_tok(): return lax.ppermute(array, 'tok', [(i, i ^ step) for i in parts])]
    ppermute x9 -> x11, starting transfers between devices: 12.7 us -> 20.3 us  [swap_chip(): lax.ppermute(array, 'col', [(i, i ^ 2 * step) for i in range(col_size)])]
    unnamed x66 -> x18, local copies, waits for them, and re-layouts: 15.3 us -> 22.3 us
    pallas_call x3, Pallas kernels: 6.71 us -> 0.21 us  [pack_hidden(): pl.pallas_call(functools.partial(pack_hidden_kernel, parts=parts), out_sh...]
    ppermute x4 -> x5, waiting for transfers between devices: 0.01 us -> 5.43 us  [swap_core(): return lax.ppermute(array, 'col', [(i, i ^ 1) for i in range(col_size)])]
  transfers between devices with their start and end apart: 29 -> 37, of which waited for: 10 -> 16; matrix products, arithmetic and copies ran while one was open for 1% -> 2% of each run, Pallas kernels for 29% -> 22%
where the time goes in v3:
time: 248 us; the launch traced here: 245 us
  waiting for transfers between devices  99 us (40%)
  Pallas kernels  65.6 us (26%)
  starting transfers between devices  51.4 us (21%)
  local copies, waits for them, and re-layouts  25.2 us (10%)
  other arithmetic  2.85 us (1%)
    ppermute x11, waiting for transfers between devices, swap_chip(): lax.ppermute(array, 'col', [(i, i ^ 2 * step) for i in range(col_size)])  49.8 us
    ppermute x17, waiting for transfers between devices, swap_tok(): return lax.ppermute(array, 'tok', [(i, i ^ step) for i in parts])  43.8 us
    pallas_call x3, Pallas kernels, panel_product(): pl.pallas_call(panel_product_kernel, out_shape=[out] * 4, grid=(4,), in_s...  22.4 us
    unnamed x18, local copies, waits for them, and re-layouts  22.3 us
    ppermute x11, starting transfers between devices, swap_chip(): lax.ppermute(array, 'col', [(i, i ^ 2 * step) for i in range(col_size)])  20.3 us
    ppermute x17, starting transfers between devices, swap_tok(): return lax.ppermute(array, 'tok', [(i, i ^ step) for i in parts])  19 us
    pallas_call x1, Pallas kernels, spread_shares(): pl.pallas_call(functools.partial(spread_shares_kernel, rows=rows, shares=...  17.6 us
    pallas_call x1, Pallas kernels, spread_panels(): pl.pallas_call(functools.partial(spread_panels_kernel, chunks=chunks, row...  12.7 us
  transfers between devices with their start and end apart: 37, of which 16 were waited for; matrix products, arithmetic and copies ran while one was open for 2% of the time, Pallas kernels for 22%

profile of v3, /device:TPU:0, one launch (start us, length us, event | category | flops | bytes accessed | tf_op | source)
XLA Modules:
  0.0 244.5 jit_solution(18365068294013989123)
XLA Ops:
  1.6 4.8 %collective-permute-start.1 = (bf16[128,1024]{1,0:T(8,128)(2,1)}, bf16[128,1024]{1,0:T(8,128)(2,1)S(1)}, u32[]{:S(2)}, u32[]{:S(2)}) collective-permute-start(bf16[128,1024]{1,0:T(8,128)(2,1)} %tokens.1), channel_id=1, source_target_pairs={{0,2},{1,3},{2,10},{3,11},{4,18},{5,19},{6,26},{7,27},{8,0},{9,1},... | collective-permute-start | bytes 786440 | tf_op jit(solution)/shard_map/ppermute | solution.py:574
  6.4 3.5 %collective-permute-start.2 = (bf16[128,1024]{1,0:T(8,128)(2,1)}, bf16[128,1024]{1,0:T(8,128)(2,1)S(1)}, u32[]{:S(2)}, u32[]{:S(2)}) collective-permute-start(bf16[128,1024]{1,0:T(8,128)(2,1)} %tokens.1), channel_id=1, source_target_pairs={{0,4},{1,5},{2,12},{3,13},{4,20},{5,21},{6,28},{7,29},{8,6},{9,7},... | collective-permute-start | bytes 786440 | tf_op jit(solution)/shard_map/ppermute | solution.py:574
  14.1 17.6 %spread_gate_up.1._.weight = bf16[3,2048,2048]{2,1,0:T(8,128)(2,1)} custom-call(s32[384]{0:T(512)} %get-tuple-element.50.gate_at, s32[384]{0:T(512)} %get-tuple-element.49.up_at, bf16[1,216,128,128]{3,2,1,0:T(8,128)(2,1)} %gate_ref.1, bf16[1,216,128,128]{3,2,1,0:T(8,128)(2,1)} %up_ref.1), custom_call_target="tpu_custom_call" | custom-call | bytes 39321600 | tf_op jit(solution)/shard_map/spread_gate_up/pallas_call | solution.py:263
  31.7 8.2 %copy-done = bf16[3,2048,2048]{2,1,0:T(8,128)(2,1)S(1)} copy-done((bf16[3,2048,2048]{2,1,0:T(8,128)(2,1)S(1)}, bf16[3,2048,2048]{2,1,0:T(8,128)(2,1)}, u32[]{:S(2)}) %copy-start) | copy-done | bytes 25165848
  46.8 2.7 %collective-permute-done.6 = f32[1,128]{1,0:T(1,128)S(1)} collective-permute-done((f32[1,128]{1,0:T(1,128)S(1)}, f32[1,128]{1,0:T(1,128)S(1)}, u32[]{:S(2)}, u32[]{:S(2)}) %collective-permute-start.6) | collective-permute-done | bytes 544 | tf_op jit(solution)/shard_map/ppermute | solution.py:563
  55.3 12.7 %spread_down.1.refs_6_.weight = bf16[3,2048,1024]{2,1,0:T(8,128)(2,1)S(1)} custom-call(s32[384]{0:T(512)S(1)} %select_n.139.at_ref, s32[8]{0:T(128)S(1)} %get-tuple-element.52.panels_ref, bf16[8,108,128,128]{3,2,1,0:T(8,128)(2,1)} %values_ref.1), custom_call_target="tpu_custom_call" | custom-call | bytes 40894464 | tf_op jit(solution)/shard_map/spread_down/pallas_call | solution.py:292
  68.0 4.6 %copy-done.1 = bf16[3,2048,1024]{2,1,0:T(8,128)(2,1)} copy-done((bf16[3,2048,1024]{2,1,0:T(8,128)(2,1)}, bf16[3,2048,1024]{2,1,0:T(8,128)(2,1)S(1)}, u32[]{:S(2)}) %copy-start.1) | copy-done | bytes 12582936
  73.5 4.6 %copy-done.2 = bf16[3,2048,1024]{2,1,0:T(8,128)(2,1)S(1)} copy-done((bf16[3,2048,1024]{2,1,0:T(8,128)(2,1)S(1)}, bf16[3,2048,1024]{2,1,0:T(8,128)(2,1)}, u32[]{:S(2)}) %copy-start.2) | copy-done | bytes 12582936
  78.4 2.6 %collective-permute-done.9.other = bf16[512,1024]{1,0:T(8,128)(2,1)S(1)} collective-permute-done((bf16[512,1024]{1,0:T(8,128)(2,1)S(1)}, bf16[512,1024]{1,0:T(8,128)(2,1)S(1)}, u32[]{:S(2)}, u32[]{:S(2)}) %collective-permute-start.9) | collective-permute-done | bytes 1048608 | tf_op jit(solution)/shard_map/ppermute | solution.py:566
  81.1 7.2 %gate_up_0.1 = (bf16[2,256,512]{2,1,0:T(8,128)(2,1)S(1)}, bf16[2,256,512]{2,1,0:T(8,128)(2,1)S(1)}, bf16[2,256,512]{2,1,0:T(8,128)(2,1)S(1)}, bf16[2,256,512]{2,1,0:T(8,128)(2,1)S(1)}) custom-call(bf16[512,1024]{1,0:T(8,128)(2,1)S(1)} %pack.1.own, bf16[512,1024]{1,0:T(8,128)(2,1)S(1)} %collective-permute-done.9.other, ...), custom_call_target="tpu_custom_call" | custom-call | flops 4294967296 | bytes 12582912 | tf_op jit(solution)/shard_map/gate_up_0/pallas_call | solution.py:457
  89.8 7.2 %gate_up_1.1 = (bf16[2,256,512]{2,1,0:T(8,128)(2,1)S(1)}, bf16[2,256,512]{2,1,0:T(8,128)(2,1)S(1)}, bf16[2,256,512]{2,1,0:T(8,128)(2,1)S(1)}, bf16[2,256,512]{2,1,0:T(8,128)(2,1)S(1)}) custom-call(bf16[512,1024]{1,0:T(8,128)(2,1)S(1)} %pack.1.own, bf16[512,1024]{1,0:T(8,128)(2,1)S(1)} %collective-permute-done.9.other, ...), custom_call_target="tpu_custom_call" | custom-call | flops 4294967296 | bytes 12582912 | tf_op jit(solution)/shard_map/gate_up_1/pallas_call | solution.py:457
  99.7 8.0 %gate_up_2.1 = (bf16[2,256,512]{2,1,0:T(8,128)(2,1)S(1)}, bf16[2,256,512]{2,1,0:T(8,128)(2,1)S(1)}, bf16[2,256,512]{2,1,0:T(8,128)(2,1)S(1)}, bf16[2,256,512]{2,1,0:T(8,128)(2,1)S(1)}) custom-call(bf16[512,1024]{1,0:T(8,128)(2,1)S(1)} %pack.1.own, bf16[512,1024]{1,0:T(8,128)(2,1)S(1)} %collective-permute-done.9.other, ...), custom_call_target="tpu_custom_call" | custom-call | flops 4294967296 | bytes 12582912 | tf_op jit(solution)/shard_map/gate_up_2/pallas_call | solution.py:457
  109.8 13.9 %collective-permute-done.25.came_b.refs_4_ = bf16[2,256,512]{2,1,0:T(8,128)(2,1)S(1)} collective-permute-done((bf16[2,256,512]{2,1,0:T(8,128)(2,1)S(1)}, bf16[2,256,512]{2,1,0:T(8,128)(2,1)S(1)}, u32[]{:S(2)}, u32[]{:S(2)}) %collective-permute-start.25) | collective-permute-done | bytes 524320 | tf_op jit(solution)/shard_map/ppermute | solution.py:560
  127.7 12.9 %collective-permute-done.26.refs_2_ = bf16[256,512]{1,0:T(8,128)(2,1)S(1)} collective-permute-done((bf16[256,512]{1,0:T(8,128)(2,1)S(1)}, bf16[256,512]{1,0:T(8,128)(2,1)S(1)}, u32[]{:S(2)}, u32[]{:S(2)}) %collective-permute-start.26) | collective-permute-done | bytes 262176 | tf_op jit(solution)/shard_map/ppermute | solution.py:560
  144.5 2.4 collective-permute-start.30
  147.4 5.5 %collective-permute-done.28.refs_1_ = bf16[512,256]{1,0:T(8,128)(2,1)S(1)} collective-permute-done((bf16[512,256]{1,0:T(8,128)(2,1)S(1)}, bf16[512,256]{1,0:T(8,128)(2,1)S(1)}, u32[]{:S(2)}, u32[]{:S(2)}) %collective-permute-start.28) | collective-permute-done | bytes 262176 | tf_op jit(solution)/shard_map/ppermute | solution.py:563
  152.9 10.7 %collective-permute-done.29.refs_2_ = bf16[512,256]{1,0:T(8,128)(2,1)S(1)} collective-permute-done((bf16[512,256]{1,0:T(8,128)(2,1)S(1)}, bf16[512,256]{1,0:T(8,128)(2,1)S(1)}, u32[]{:S(2)}, u32[]{:S(2)}) %collective-permute-start.29) | collective-permute-done | bytes 262176 | tf_op jit(solution)/shard_map/ppermute | solution.py:563
  164.9 4.2 %collective-permute-start.21 = (bf16[512,256]{1,0:T(8,128)(2,1)S(1)}, bf16[512,256]{1,0:T(8,128)(2,1)S(1)}, u32[]{:S(2)}, u32[]{:S(2)}) collective-permute-start(bf16[512,256]{1,0:T(8,128)(2,1)S(1)} %combine_1.1.refs_4_.refs_0_), channel_id=1, source_target_pairs={{0,2},{1,3},{2,0},{3,1},{4,6},{5,7},{6,4},{7,5},{8,10},{9,11},{10,... | collective-permute-start | bytes 786440 | tf_op jit(solution)/shard_map/ppermute | solution.py:563
  169.1 3.4 %collective-permute-done.12.refs_2_ = bf16[256,512]{1,0:T(8,128)(2,1)S(1)} collective-permute-done((bf16[256,512]{1,0:T(8,128)(2,1)S(1)}, bf16[256,512]{1,0:T(8,128)(2,1)S(1)}, u32[]{:S(2)}, u32[]{:S(2)}) %collective-permute-start.12) | collective-permute-done | bytes 262176 | tf_op jit(solution)/shard_map/ppermute | solution.py:560
  173.9 3.2 %down_0.1.refs_5_.refs_0_ = f32[512,1024]{1,0:T(8,128)S(1)} custom-call(s32[1]{0:T(128)} %constant.131.clone.1.flips, bf16[4,512,256]{2,1,0:T(8,128)(2,1)S(1)} %pack_hidden.3.own, bf16[4,512,256]{2,1,0:T(8,128)(2,1)S(1)} %collective-permute-done.31.other, bf16[3,2048,1024]{2,1,0:T(8,128)(2,1)S(1)} %bitcast.10), custom_call_target="tpu_custom_call" | custom-call | flops 2147483648 | bytes 10485760 | tf_op jit(solution)/shard_map/down_0/pallas_call | solution.py:514
  177.1 2.5 %collective-permute-done.21.refs_1_ = bf16[512,256]{1,0:T(8,128)(2,1)S(1)} collective-permute-done((bf16[512,256]{1,0:T(8,128)(2,1)S(1)}, bf16[512,256]{1,0:T(8,128)(2,1)S(1)}, u32[]{:S(2)}, u32[]{:S(2)}) %collective-permute-start.21) | collective-permute-done | bytes 262176 | tf_op jit(solution)/shard_map/ppermute | solution.py:563
  179.6 10.9 %collective-permute-done.22.refs_2_ = bf16[512,256]{1,0:T(8,128)(2,1)S(1)} collective-permute-done((bf16[512,256]{1,0:T(8,128)(2,1)S(1)}, bf16[512,256]{1,0:T(8,128)(2,1)S(1)}, u32[]{:S(2)}, u32[]{:S(2)}) %collective-permute-start.22) | collective-permute-done | bytes 262176 | tf_op jit(solution)/shard_map/ppermute | solution.py:563
  190.6 4.9 %collective-permute-start.14 = (bf16[512,256]{1,0:T(8,128)(2,1)S(1)}, bf16[512,256]{1,0:T(8,128)(2,1)S(1)}, u32[]{:S(2)}, u32[]{:S(2)}) collective-permute-start(bf16[512,256]{1,0:T(8,128)(2,1)S(1)} %combine_2.1.refs_4_.refs_0_), channel_id=1, source_target_pairs={{0,2},{1,3},{2,0},{3,1},{4,6},{5,7},{6,4},{7,5},{8,10},{9,11},{10,... | collective-permute-start | bytes 786440 | tf_op jit(solution)/shard_map/ppermute | solution.py:563
  195.5 2.4 collective-permute-start.16
  197.9 3.4 %down_1.1.refs_4_.refs_0_ = f32[512,1024]{1,0:T(8,128)S(1)} custom-call(s32[1]{0:T(128)} %constant.131.clone.1.flips, bf16[4,512,256]{2,1,0:T(8,128)(2,1)S(1)} %pack_hidden.4.own, bf16[4,512,256]{2,1,0:T(8,128)(2,1)S(1)} %collective-permute-done.32.other, bf16[3,2048,1024]{2,1,0:T(8,128)(2,1)S(1)} %bitcast.10, f32[512,1024]{1,0:T(8,128)S(1)} %down_0.1.refs_5_.refs_0_), custom_call_target="tpu_custom_call" | custom-call | flops 2147483648 | bytes 10485760 | tf_op jit(solution)/shard_map/down_1/pallas_call | solution.py:514
  201.3 5.2 %collective-permute-done.14.refs_1_ = bf16[512,256]{1,0:T(8,128)(2,1)S(1)} collective-permute-done((bf16[512,256]{1,0:T(8,128)(2,1)S(1)}, bf16[512,256]{1,0:T(8,128)(2,1)S(1)}, u32[]{:S(2)}, u32[]{:S(2)}) %collective-permute-start.14) | collective-permute-done | bytes 262176 | tf_op jit(solution)/shard_map/ppermute | solution.py:563
  206.5 10.3 %collective-permute-done.15.refs_2_ = bf16[512,256]{1,0:T(8,128)(2,1)S(1)} collective-permute-done((bf16[512,256]{1,0:T(8,128)(2,1)S(1)}, bf16[512,256]{1,0:T(8,128)(2,1)S(1)}, u32[]{:S(2)}, u32[]{:S(2)}) %collective-permute-start.15) | collective-permute-done | bytes 262176 | tf_op jit(solution)/shard_map/ppermute | solution.py:563
  217.0 2.8 %collective-permute-done.33.other = bf16[4,512,256]{2,1,0:T(8,128)(2,1)} collective-permute-done((bf16[4,512,256]{2,1,0:T(8,128)(2,1)S(1)}, bf16[4,512,256]{2,1,0:T(8,128)(2,1)}, u32[]{:S(2)}, u32[]{:S(2)}) %collective-permute-start.33) | collective-permute-done | bytes 1048608 | tf_op jit(solution)/shard_map/ppermute | solution.py:566
  219.8 4.6 %copy-done.3 = bf16[3,2048,1024]{2,1,0:T(8,128)(2,1)S(1)} copy-done((bf16[3,2048,1024]{2,1,0:T(8,128)(2,1)S(1)}, bf16[3,2048,1024]{2,1,0:T(8,128)(2,1)}, u32[]{:S(2)}) %copy-start.3) | copy-done | bytes 12582936
  224.3 4.4 %down_2.1 = (bf16[128,1024]{1,0:T(8,128)(2,1)S(1)}, bf16[128,1024]{1,0:T(8,128)(2,1)S(1)}, bf16[128,1024]{1,0:T(8,128)(2,1)S(1)}, bf16[128,1024]{1,0:T(8,128)(2,1)S(1)}) custom-call(s32[1]{0:T(128)} %bitcast.flips, bf16[4,512,256]{2,1,0:T(8,128)(2,1)S(1)} %pack_hidden.5.own, bf16[4,512,256]{2,1,0:T(8,128)(2,1)} %collective-permute-done.33.other, ...), custom_call_target="tpu_custom_call" | custom-call | flops 2147483648 | bytes 10485760 | tf_op jit(solution)/shard_map/down_2/pallas_call | solution.py:514
  232.3 6.6 %collective-permute-done.36 = bf16[128,1024]{1,0:T(8,128)(2,1)S(1)} collective-permute-done((bf16[128,1024]{1,0:T(8,128)(2,1)S(1)}, bf16[128,1024]{1,0:T(8,128)(2,1)S(1)}, u32[]{:S(2)}, u32[]{:S(2)}) %collective-permute-start.36) | collective-permute-done | bytes 262176 | tf_op jit(solution)/shard_map/ppermute | solution.py:560
  238.9 4.8 %collective-permute-done.35 = bf16[128,1024]{1,0:T(8,128)(2,1)S(1)} collective-permute-done((bf16[128,1024]{1,0:T(8,128)(2,1)S(1)}, bf16[128,1024]{1,0:T(8,128)(2,1)S(1)}, u32[]{:S(2)}, u32[]{:S(2)}) %collective-permute-start.35) | collective-permute-done | bytes 262176 | tf_op jit(solution)/shard_map/ppermute | solution.py:560
  (114 shorter events, 41.4 us)
Async XLA Ops:
  0.0 73.4 %collective-permute-start = (bf16[128,1024]{1,0:T(8,128)(2,1)}, bf16[128,1024]{1,0:T(8,128)(2,1)S(1)}, u32[]{:S(2)}, u32[]{:S(2)}) collective-permute-start(bf16[128,1024]{1,0:T(8,128)(2,1)} %tokens.1), channel_id=1, source_target_pairs={{0,0},{1,1},{2,8},{3,9},{4,16},{5,17},{6,24},{7,25},{8,2},{9,3},{1... | collective-permute-start | bytes 786440 | tf_op jit(solution)/shard_map/ppermute | solution.py:574
  1.6 71.8 %collective-permute-start.1 = (bf16[128,1024]{1,0:T(8,128)(2,1)}, bf16[128,1024]{1,0:T(8,128)(2,1)S(1)}, u32[]{:S(2)}, u32[]{:S(2)}) collective-permute-start(bf16[128,1024]{1,0:T(8,128)(2,1)} %tokens.1), channel_id=1, source_target_pairs={{0,2},{1,3},{2,10},{3,11},{4,18},{5,19},{6,26},{7,27},{8,0},{9,1},... | collective-permute-start | bytes 786440 | tf_op jit(solution)/shard_map/ppermute | solution.py:574
  6.4 67.1 %collective-permute-start.2 = (bf16[128,1024]{1,0:T(8,128)(2,1)}, bf16[128,1024]{1,0:T(8,128)(2,1)S(1)}, u32[]{:S(2)}, u32[]{:S(2)}) collective-permute-start(bf16[128,1024]{1,0:T(8,128)(2,1)} %tokens.1), channel_id=1, source_target_pairs={{0,4},{1,5},{2,12},{3,13},{4,20},{5,21},{6,28},{7,29},{8,6},{9,7},... | collective-permute-start | bytes 786440 | tf_op jit(solution)/shard_map/ppermute | solution.py:574
  9.8 63.6 %collective-permute-start.3 = (bf16[128,1024]{1,0:T(8,128)(2,1)}, bf16[128,1024]{1,0:T(8,128)(2,1)S(1)}, u32[]{:S(2)}, u32[]{:S(2)}) collective-permute-start(bf16[128,1024]{1,0:T(8,128)(2,1)} %tokens.1), channel_id=1, source_target_pairs={{0,6},{1,7},{2,14},{3,15},{4,22},{5,23},{6,30},{7,31},{8,4},{9,5},... | collective-permute-start | bytes 786440 | tf_op jit(solution)/shard_map/ppermute | solution.py:574
  45.0 4.4 %collective-permute-start.6 = (f32[1,128]{1,0:T(1,128)S(1)}, f32[1,128]{1,0:T(1,128)S(1)}, u32[]{:S(2)}, u32[]{:S(2)}) collective-permute-start(f32[1,128]{1,0:T(1,128)S(1)} %add.154), channel_id=1, source_target_pairs={{0,4},{1,5},{2,6},{3,7},{4,0},{5,1},{6,2},{7,3},{8,12},{9,13},{10,... | collective-permute-start | bytes 1544 | tf_op jit(solution)/shard_map/ppermute | solution.py:563
  53.0 19.6 %collective-permute-start.8 = (f32[2,128]{1,0:T(2,128)S(1)}, f32[2,128]{1,0:T(2,128)S(1)}, u32[]{:S(2)}, u32[]{:S(2)}) collective-permute-start(f32[2,128]{1,0:T(2,128)S(1)} %pad_maximum_fusion), channel_id=1, source_target_pairs={{0,16},{8,24},{16,0},{24,8},{1,17},{9,25},{17,1},{25,9},{2,18},{10... | collective-permute-start | bytes 3080 | tf_op jit(solution)/shard_map/ppermute | solution.py:560
  88.3 21.0 %collective-permute-start.24 = (bf16[2,256,512]{2,1,0:T(8,128)(2,1)S(1)}, bf16[2,256,512]{2,1,0:T(8,128)(2,1)S(1)}, u32[]{:S(2)}, u32[]{:S(2)}) collective-permute-start(bf16[2,256,512]{2,1,0:T(8,128)(2,1)S(1)} %get-tuple-element.40), channel_id=1, source_target_pairs={{0,8},{8,0},{16,24},{24,16},{1,9},{9,1},{17,25},{25,17},{2,10},{10... | collective-permute-start | bytes 1572872 | tf_op jit(solution)/shard_map/ppermute | solution.py:560
  97.1 27.5 %collective-permute-start.17 = (bf16[2,256,512]{2,1,0:T(8,128)(2,1)S(1)}, bf16[2,256,512]{2,1,0:T(8,128)(2,1)S(1)}, u32[]{:S(2)}, u32[]{:S(2)}) collective-permute-start(bf16[2,256,512]{2,1,0:T(8,128)(2,1)S(1)} %get-tuple-element.34), channel_id=1, source_target_pairs={{0,8},{8,0},{16,24},{24,16},{1,9},{9,1},{17,25},{25,17},{2,10},{10... | collective-permute-start | bytes 1572872 | tf_op jit(solution)/shard_map/ppermute | solution.py:560
  97.7 28.3 %collective-permute-start.18 = (bf16[2,256,512]{2,1,0:T(8,128)(2,1)S(1)}, bf16[2,256,512]{2,1,0:T(8,128)(2,1)S(1)}, u32[]{:S(2)}, u32[]{:S(2)}) collective-permute-start(bf16[2,256,512]{2,1,0:T(8,128)(2,1)S(1)} %get-tuple-element.36), channel_id=1, source_target_pairs={{0,16},{8,24},{16,0},{24,8},{1,17},{9,25},{17,1},{25,9},{2,18},{10... | collective-permute-start | bytes 1572872 | tf_op jit(solution)/shard_map/ppermute | solution.py:560
  98.2 25.5 %collective-permute-start.25 = (bf16[2,256,512]{2,1,0:T(8,128)(2,1)S(1)}, bf16[2,256,512]{2,1,0:T(8,128)(2,1)S(1)}, u32[]{:S(2)}, u32[]{:S(2)}) collective-permute-start(bf16[2,256,512]{2,1,0:T(8,128)(2,1)S(1)} %get-tuple-element.42), channel_id=1, source_target_pairs={{0,16},{8,24},{16,0},{24,8},{1,17},{9,25},{17,1},{25,9},{2,18},{10... | collective-permute-start | bytes 1572872 | tf_op jit(solution)/shard_map/ppermute | solution.py:560
  107.7 36.8 %collective-permute-start.10 = (bf16[2,256,512]{2,1,0:T(8,128)(2,1)S(1)}, bf16[2,256,512]{2,1,0:T(8,128)(2,1)S(1)}, u32[]{:S(2)}, u32[]{:S(2)}) collective-permute-start(bf16[2,256,512]{2,1,0:T(8,128)(2,1)S(1)} %get-tuple-element.28), channel_id=1, source_target_pairs={{0,8},{8,0},{16,24},{24,16},{1,9},{9,1},{17,25},{25,17},{2,10},{10... | collective-permute-start | bytes 1572872 | tf_op jit(solution)/shard_map/ppermute | solution.py:560
  109.2 35.3 %collective-permute-start.11 = (bf16[2,256,512]{2,1,0:T(8,128)(2,1)S(1)}, bf16[2,256,512]{2,1,0:T(8,128)(2,1)S(1)}, u32[]{:S(2)}, u32[]{:S(2)}) collective-permute-start(bf16[2,256,512]{2,1,0:T(8,128)(2,1)S(1)} %get-tuple-element.30), channel_id=1, source_target_pairs={{0,16},{8,24},{16,0},{24,8},{1,17},{9,25},{17,1},{25,9},{2,18},{10... | collective-permute-start | bytes 1572872 | tf_op jit(solution)/shard_map/ppermute | solution.py:560
  123.9 16.7 %collective-permute-start.26 = (bf16[256,512]{1,0:T(8,128)(2,1)S(1)}, bf16[256,512]{1,0:T(8,128)(2,1)S(1)}, u32[]{:S(2)}, u32[]{:S(2)}) collective-permute-start(bf16[256,512]{1,0:T(8,128)(2,1)S(1)} %get-tuple-element.43), channel_id=1, source_target_pairs={{0,16},{8,24},{16,0},{24,8},{1,17},{9,25},{17,1},{25,9},{2,18},{10... | collective-permute-start | bytes 786440 | tf_op jit(solution)/shard_map/ppermute | solution.py:560
  124.5 17.6 %collective-permute-start.27 = (bf16[256,512]{1,0:T(8,128)(2,1)S(1)}, bf16[256,512]{1,0:T(8,128)(2,1)S(1)}, u32[]{:S(2)}, u32[]{:S(2)}) collective-permute-start(bf16[256,512]{1,0:T(8,128)(2,1)S(1)} %get-tuple-element.44), channel_id=1, source_target_pairs={{0,8},{8,0},{16,24},{24,16},{1,9},{9,1},{17,25},{25,17},{2,10},{10... | collective-permute-start | bytes 786440 | tf_op jit(solution)/shard_map/ppermute | solution.py:560
  126.1 20.9 %collective-permute-start.19 = (bf16[256,512]{1,0:T(8,128)(2,1)S(1)}, bf16[256,512]{1,0:T(8,128)(2,1)S(1)}, u32[]{:S(2)}, u32[]{:S(2)}) collective-permute-start(bf16[256,512]{1,0:T(8,128)(2,1)S(1)} %get-tuple-element.37), channel_id=1, source_target_pairs={{0,16},{8,24},{16,0},{24,8},{1,17},{9,25},{17,1},{25,9},{2,18},{10... | collective-permute-start | bytes 786440 | tf_op jit(solution)/shard_map/ppermute | solution.py:560
  140.6 6.5 %collective-permute-start.20 = (bf16[256,512]{1,0:T(8,128)(2,1)S(1)}, bf16[256,512]{1,0:T(8,128)(2,1)S(1)}, u32[]{:S(2)}, u32[]{:S(2)}) collective-permute-start(bf16[256,512]{1,0:T(8,128)(2,1)S(1)} %get-tuple-element.38), channel_id=1, source_target_pairs={{0,8},{8,0},{16,24},{24,16},{1,9},{9,1},{17,25},{25,17},{2,10},{10... | collective-permute-start | bytes 786440 | tf_op jit(solution)/shard_map/ppermute | solution.py:560
  142.4 10.5 %collective-permute-start.28 = (bf16[512,256]{1,0:T(8,128)(2,1)S(1)}, bf16[512,256]{1,0:T(8,128)(2,1)S(1)}, u32[]{:S(2)}, u32[]{:S(2)}) collective-permute-start(bf16[512,256]{1,0:T(8,128)(2,1)S(1)} %combine_0.1.refs_0_), channel_id=1, source_target_pairs={{0,2},{1,3},{2,0},{3,1},{4,6},{5,7},{6,4},{7,5},{8,10},{9,11},{10,... | collective-permute-start | bytes 786440 | tf_op jit(solution)/shard_map/ppermute | solution.py:563
  144.5 19.1 %collective-permute-start.29 = (bf16[512,256]{1,0:T(8,128)(2,1)S(1)}, bf16[512,256]{1,0:T(8,128)(2,1)S(1)}, u32[]{:S(2)}, u32[]{:S(2)}) collective-permute-start(bf16[512,256]{1,0:T(8,128)(2,1)S(1)} %combine_0.1.refs_0_), channel_id=1, source_target_pairs={{0,4},{1,5},{2,6},{3,7},{4,0},{5,1},{6,2},{7,3},{8,12},{9,13},{10,... | collective-permute-start | bytes 786440 | tf_op jit(solution)/shard_map/ppermute | solution.py:563
  144.5 19.1 %collective-permute-start.30 = (bf16[512,256]{1,0:T(8,128)(2,1)S(1)}, bf16[512,256]{1,0:T(8,128)(2,1)S(1)}, u32[]{:S(2)}, u32[]{:S(2)}) collective-permute-start(bf16[512,256]{1,0:T(8,128)(2,1)S(1)} %combine_0.1.refs_0_), channel_id=1, source_target_pairs={{0,6},{1,7},{2,4},{3,5},{4,2},{5,3},{6,0},{7,1},{8,14},{9,15},{10,... | collective-permute-start | bytes 786440 | tf_op jit(solution)/shard_map/ppermute | solution.py:563
  163.7 10.1 %collective-permute-start.31 = (bf16[4,512,256]{2,1,0:T(8,128)(2,1)S(1)}, bf16[4,512,256]{2,1,0:T(8,128)(2,1)S(1)}, u32[]{:S(2)}, u32[]{:S(2)}) collective-permute-start(bf16[4,512,256]{2,1,0:T(8,128)(2,1)S(1)} %pack_hidden.3.own), channel_id=1, source_target_pairs={{0,1},{1,0},{2,3},{3,2},{4,5},{5,4},{6,7},{7,6},{8,9},{9,8},{10,11... | collective-permute-start | bytes 3145736 | tf_op jit(solution)/shard_map/ppermute | solution.py:566
  163.8 8.7 %collective-permute-start.12 = (bf16[256,512]{1,0:T(8,128)(2,1)S(1)}, bf16[256,512]{1,0:T(8,128)(2,1)S(1)}, u32[]{:S(2)}, u32[]{:S(2)}) collective-permute-start(bf16[256,512]{1,0:T(8,128)(2,1)S(1)} %get-tuple-element.31.refs_5_), channel_id=1, source_target_pairs={{0,16},{8,24},{16,0},{24,8},{1,17},{9,25},{17,1},{25,9},{2,18},{10... | collective-permute-start | bytes 786440 | tf_op jit(solution)/shard_map/ppermute | solution.py:560
  164.3 9.2 %collective-permute-start.13 = (bf16[256,512]{1,0:T(8,128)(2,1)S(1)}, bf16[256,512]{1,0:T(8,128)(2,1)S(1)}, u32[]{:S(2)}, u32[]{:S(2)}) collective-permute-start(bf16[256,512]{1,0:T(8,128)(2,1)S(1)} %get-tuple-element.32), channel_id=1, source_target_pairs={{0,8},{8,0},{16,24},{24,16},{1,9},{9,1},{17,25},{25,17},{2,10},{10... | collective-permute-start | bytes 786440 | tf_op jit(solution)/shard_map/ppermute | solution.py:560
  164.9 14.7 %collective-permute-start.21 = (bf16[512,256]{1,0:T(8,128)(2,1)S(1)}, bf16[512,256]{1,0:T(8,128)(2,1)S(1)}, u32[]{:S(2)}, u32[]{:S(2)}) collective-permute-start(bf16[512,256]{1,0:T(8,128)(2,1)S(1)} %combine_1.1.refs_4_.refs_0_), channel_id=1, source_target_pairs={{0,2},{1,3},{2,0},{3,1},{4,6},{5,7},{6,4},{7,5},{8,10},{9,11},{10,... | collective-permute-start | bytes 786440 | tf_op jit(solution)/shard_map/ppermute | solution.py:563
  169.1 21.4 %collective-permute-start.22 = (bf16[512,256]{1,0:T(8,128)(2,1)S(1)}, bf16[512,256]{1,0:T(8,128)(2,1)S(1)}, u32[]{:S(2)}, u32[]{:S(2)}) collective-permute-start(bf16[512,256]{1,0:T(8,128)(2,1)S(1)} %combine_1.1.refs_4_.refs_0_), channel_id=1, source_target_pairs={{0,4},{1,5},{2,6},{3,7},{4,0},{5,1},{6,2},{7,3},{8,12},{9,13},{10,... | collective-permute-start | bytes 786440 | tf_op jit(solution)/shard_map/ppermute | solution.py:563
  172.5 17.9 %collective-permute-start.23 = (bf16[512,256]{1,0:T(8,128)(2,1)S(1)}, bf16[512,256]{1,0:T(8,128)(2,1)S(1)}, u32[]{:S(2)}, u32[]{:S(2)}) collective-permute-start(bf16[512,256]{1,0:T(8,128)(2,1)S(1)} %combine_1.1.refs_4_.refs_0_), channel_id=1, source_target_pairs={{0,6},{1,7},{2,4},{3,5},{4,2},{5,3},{6,0},{7,1},{8,14},{9,15},{10,... | collective-permute-start | bytes 786440 | tf_op jit(solution)/shard_map/ppermute | solution.py:563
  190.5 7.4 %collective-permute-start.32 = (bf16[4,512,256]{2,1,0:T(8,128)(2,1)S(1)}, bf16[4,512,256]{2,1,0:T(8,128)(2,1)S(1)}, u32[]{:S(2)}, u32[]{:S(2)}) collective-permute-start(bf16[4,512,256]{2,1,0:T(8,128)(2,1)S(1)} %pack_hidden.4.own), channel_id=1, source_target_pairs={{0,1},{1,0},{2,3},{3,2},{4,5},{5,4},{6,7},{7,6},{8,9},{9,8},{10,11... | collective-permute-start | bytes 3145736 | tf_op jit(solution)/shard_map/ppermute | solution.py:566
  190.6 15.9 %collective-permute-start.14 = (bf16[512,256]{1,0:T(8,128)(2,1)S(1)}, bf16[512,256]{1,0:T(8,128)(2,1)S(1)}, u32[]{:S(2)}, u32[]{:S(2)}) collective-permute-start(bf16[512,256]{1,0:T(8,128)(2,1)S(1)} %combine_2.1.refs_4_.refs_0_), channel_id=1, source_target_pairs={{0,2},{1,3},{2,0},{3,1},{4,6},{5,7},{6,4},{7,5},{8,10},{9,11},{10,... | collective-permute-start | bytes 786440 | tf_op jit(solution)/shard_map/ppermute | solution.py:563
  195.5 21.3 %collective-permute-start.15 = (bf16[512,256]{1,0:T(8,128)(2,1)S(1)}, bf16[512,256]{1,0:T(8,128)(2,1)S(1)}, u32[]{:S(2)}, u32[]{:S(2)}) collective-permute-start(bf16[512,256]{1,0:T(8,128)(2,1)S(1)} %combine_2.1.refs_4_.refs_0_), channel_id=1, source_target_pairs={{0,4},{1,5},{2,6},{3,7},{4,0},{5,1},{6,2},{7,3},{8,12},{9,13},{10,... | collective-permute-start | bytes 786440 | tf_op jit(solution)/shard_map/ppermute | solution.py:563
  195.5 21.3 %collective-permute-start.16 = (bf16[512,256]{1,0:T(8,128)(2,1)S(1)}, bf16[512,256]{1,0:T(8,128)(2,1)S(1)}, u32[]{:S(2)}, u32[]{:S(2)}) collective-permute-start(bf16[512,256]{1,0:T(8,128)(2,1)S(1)} %combine_2.1.refs_4_.refs_0_), channel_id=1, source_target_pairs={{0,6},{1,7},{2,4},{3,5},{4,2},{5,3},{6,0},{7,1},{8,14},{9,15},{10,... | collective-permute-start | bytes 786440 | tf_op jit(solution)/shard_map/ppermute | solution.py:563
  228.7 10.2 %collective-permute-start.36 = (bf16[128,1024]{1,0:T(8,128)(2,1)S(1)}, bf16[128,1024]{1,0:T(8,128)(2,1)S(1)}, u32[]{:S(2)}, u32[]{:S(2)}) collective-permute-start(bf16[128,1024]{1,0:T(8,128)(2,1)S(1)} %get-tuple-element.48), channel_id=1, source_target_pairs={{0,24},{8,16},{16,8},{24,0},{1,25},{9,17},{17,9},{25,1},{2,26},{10... | collective-permute-start | bytes 786440 | tf_op jit(solution)/shard_map/ppermute | solution.py:560
  231.1 12.5 %collective-permute-start.35 = (bf16[128,1024]{1,0:T(8,128)(2,1)S(1)}, bf16[128,1024]{1,0:T(8,128)(2,1)S(1)}, u32[]{:S(2)}, u32[]{:S(2)}) collective-permute-start(bf16[128,1024]{1,0:T(8,128)(2,1)S(1)} %get-tuple-element.47), channel_id=1, source_target_pairs={{0,16},{8,24},{16,0},{24,8},{1,17},{9,25},{17,1},{25,9},{2,18},{10... | collective-permute-start | bytes 786440 | tf_op jit(solution)/shard_map/ppermute | solution.py:560
  231.7 11.9 %collective-permute-start.34 = (bf16[128,1024]{1,0:T(8,128)(2,1)S(1)}, bf16[128,1024]{1,0:T(8,128)(2,1)S(1)}, u32[]{:S(2)}, u32[]{:S(2)}) collective-permute-start(bf16[128,1024]{1,0:T(8,128)(2,1)S(1)} %get-tuple-element.46), channel_id=1, source_target_pairs={{0,8},{8,0},{16,24},{24,16},{1,9},{9,1},{17,25},{25,17},{2,10},{10... | collective-permute-start | bytes 786440 | tf_op jit(solution)/shard_map/ppermute | solution.py:560
  (14 other events, 250.5 us)

commit v4 on v3

--- a/solution.py
+++ b/solution.py
@@ -12,6 +12,13 @@
 
 EPSILON = 1e-05
 MIB = 1 << 20
+MARK = jax.ShapeDtypeStruct((8, 128), jnp.float32)
+MARK_SPEC = pl.BlockSpec(MARK.shape, lambda *_: (0, 0))
+ANY_SPEC = pl.BlockSpec(memory_space=pl.ANY)
+
+
+def leave(mark):
+    mark[...] = jnp.zeros_like(mark)
 
 
 def lookup(places, slots):
@@ -244,41 +251,47 @@
         mixed = down(hidden, down_dense, mixed, chunk, jnp.bfloat16 if last else jnp.float32)
     return mixed
 
-def spread_shares_kernel(gate_at, up_at, gate_ref, up_ref, out_ref, *, rows, shares, cols):
-    chunk = pl.program_id(0)
+def spread_shares_kernel(gate_at, up_at, *refs, rows, shares, cols):
+    (gate_ref, up_ref), (out_ref, mark) = refs[:2], refs[-2:]
+    step = pl.program_id(0)
+    leave(mark)
 
     @pl.loop(0, rows)
     def _(row):
         for share in range(shares):
             for col in range(cols):
-                at = ((chunk * rows + row) * shares + share) * cols + col
+                at = ((step * rows + row) * shares + share) * cols + col
                 put(out_ref, row, 2 * share * cols + col, gate_ref, gate_at[at])
                 put(out_ref, row, (2 * share + 1) * cols + col, up_ref, up_at[at])
 
 
-def spread_shares(gate_at, up_at, gate, up, chunks, rows, shares, cols):
+def spread_shares(gate_at, up_at, gate, up, rows, shares, cols, after, chunk):
     edge = gate.shape[-1]
+    steps = 4
     whole = pl.BlockSpec(gate.shape, lambda k, *_: (0, 0, 0, 0), pipeline_mode=pl.Buffered(1))
-    out = jax.ShapeDtypeStruct((chunks, rows * edge, 2 * shares * cols * edge), gate.dtype)
-    return pl.pallas_call(
-        functools.partial(spread_shares_kernel, rows=rows, shares=shares, cols=cols),
-        out_shape=out,
+    out = jax.ShapeDtypeStruct((1, rows * edge, 2 * shares * cols * edge), gate.dtype)
+    block = (1, out.shape[1] // steps, out.shape[2])
+    return pl.pallas_call(
+        functools.partial(spread_shares_kernel, rows=rows // steps, shares=shares, cols=cols),
+        out_shape=[out, MARK],
         grid_spec=pltpu.PrefetchScalarGridSpec(
             num_scalar_prefetch=2,
-            grid=(chunks,),
-            in_specs=[whole, whole],
-            out_specs=pl.BlockSpec((1,) + out.shape[1:], lambda k, *_: (k, 0, 0)),
+            grid=(steps,),
+            in_specs=[whole, whole] + [ANY_SPEC] * len(after),
+            out_specs=[pl.BlockSpec(block, lambda k, *_: (0, k, 0)), MARK_SPEC],
         ),
         compiler_params=pltpu.CompilerParams(vmem_limit_bytes=54 * MIB),
         cost_estimate=pl.CostEstimate(
             flops=0, bytes_accessed=2 * (2 * gate.size + out.size), transcendentals=0
         ),
-        name="spread_gate_up",
-    )(gate_at, up_at, gate, up)
-
-
-def spread_panels_kernel(at_ref, panels_ref, values_ref, out_ref, *, chunks, rows, cols):
+        name=f"spread_gate_up_{chunk}",
+    )(gate_at, up_at, gate, up, *after)
+
+
+def spread_panels_kernel(at_ref, values_ref, *refs, chunks, rows, cols):
+    out_ref, mark = refs[-2:]
     panel = pl.program_id(0)
+    leave(mark)
     for chunk in range(chunks):
         for row in range(rows):
             for col in range(cols):
@@ -286,41 +299,45 @@
                 put(out_ref.at[pl.ds(chunk, 1)], row, col, values_ref, at_ref[at])
 
 
-def spread_panels(at, panels, values, chunks, rows, cols):
+def spread_panels(at, values, chunks, rows, cols, after):
     count, _, edge, _ = values.shape
     out = jax.ShapeDtypeStruct((chunks, count * rows * edge, cols * edge), values.dtype)
     return pl.pallas_call(
         functools.partial(spread_panels_kernel, chunks=chunks, rows=rows, cols=cols),
-        out_shape=out,
+        out_shape=[out, MARK],
         grid_spec=pltpu.PrefetchScalarGridSpec(
-            num_scalar_prefetch=2,
+            num_scalar_prefetch=1,
             grid=(count,),
             in_specs=[
-                pl.BlockSpec((1,) + values.shape[1:], lambda m, _, panels: (panels[m], 0, 0, 0))
+                pl.BlockSpec((1,) + values.shape[1:], lambda m, *_: (m, 0, 0, 0))
+            ]
+            + [ANY_SPEC] * len(after),
+            out_specs=[
+                pl.BlockSpec((chunks, rows * edge, cols * edge), lambda m, *_: (0, m, 0)),
+                MARK_SPEC,
             ],
-            out_specs=pl.BlockSpec((chunks, rows * edge, cols * edge), lambda m, *_: (0, m, 0)),
-        ),
-        compiler_params=pltpu.CompilerParams(vmem_limit_bytes=16 * MIB),
+        ),
+        compiler_params=pltpu.CompilerParams(vmem_limit_bytes=50 * MIB),
         cost_estimate=pl.CostEstimate(
             flops=0, bytes_accessed=2 * (values.size + out.size), transcendentals=0
         ),
         name="spread_down",
-    )(at, panels, values)
-
-def sum_squares_kernel(tokens, _, out):
+    )(at, values, *after)
+
+def sum_squares_kernel(tokens, out):
     widened = tokens[...].astype(jnp.float32)
     out[...] = jnp.sum(widened * widened, axis=1)[None]
 
 
-def sum_squares(tokens, after):
+def sum_squares(tokens):
     return pl.pallas_call(
         sum_squares_kernel,
         out_shape=jax.ShapeDtypeStruct((1, tokens.shape[0]), jnp.float32),
-        in_specs=[pl.BlockSpec(memory_space=pltpu.VMEM), pl.BlockSpec(memory_space=pl.ANY)],
+        in_specs=[pl.BlockSpec(memory_space=pltpu.VMEM)],
         out_specs=pl.BlockSpec(memory_space=pltpu.VMEM),
         compiler_params=pltpu.CompilerParams(vmem_limit_bytes=4 * MIB),
         name="sum_squares",
-    )(tokens, after)
+    )(tokens)
 
 
 def pack_kernel(*refs, parts):
@@ -349,32 +366,9 @@
     )(*pieces, scale, gain, *after)
 
 
-def pack_hidden_kernel(*refs, parts):
-    out = refs[-1]
-    count = out.shape[1] // parts
-    for step in range(parts):
-        for part in range(parts):
-            there = part ^ step
-            out[step, part * count:(part + 1) * count] = refs[step][there * count:(there + 1) * count]
-
-
-def pack_hidden(pieces, after):
-    parts = len(pieces)
-    return pl.pallas_call(
-        functools.partial(pack_hidden_kernel, parts=parts),
-        out_shape=jax.ShapeDtypeStruct((parts,) + pieces[0].shape, pieces[0].dtype),
-        in_specs=[pl.BlockSpec(memory_space=pltpu.VMEM)] * parts
-        + [pl.BlockSpec(memory_space=pl.ANY)] * len(after),
-        out_specs=pl.BlockSpec(memory_space=pltpu.VMEM),
-        compiler_params=pltpu.CompilerParams(vmem_limit_bytes=16 * MIB),
-        cost_estimate=pl.CostEstimate(
-            flops=0, bytes_accessed=4 * parts * pieces[0].size, transcendentals=0
-        ),
-        name="pack_hidden",
-    )(*pieces, *after)
-
-
-def halfway_kernel(kept_a, came_a, kept_b, came_b, _, out_a, out_b):
+def halfway_kernel(kept_a, came_a, kept_b, came_b, *refs):
+    out_a, out_b, mark = refs[-3:]
+    leave(mark)
     for kept, came, out in ((kept_a, came_a, out_a), (kept_b, came_b, out_b)):
         out[...] = (kept[0].astype(jnp.float32) + came[0].astype(jnp.float32)).astype(out.dtype)
 
@@ -386,20 +380,21 @@
     out = jax.ShapeDtypeStruct((count, width), kept_a.dtype)
     return pl.pallas_call(
         halfway_kernel,
-        out_shape=[out, out],
+        out_shape=[out, out, MARK],
         grid=(1,),
-        in_specs=[second] * 4 + [pl.BlockSpec(memory_space=pl.ANY)],
-        out_specs=[whole, whole],
+        in_specs=[second] * 4 + [ANY_SPEC] * len(after),
+        out_specs=[whole, whole, MARK_SPEC],
         compiler_params=pltpu.CompilerParams(vmem_limit_bytes=8 * MIB),
         cost_estimate=pl.CostEstimate(
             flops=2 * count * width, bytes_accessed=12 * count * width, transcendentals=0
         ),
         name=f"halfway_{chunk}",
-    )(kept_a, came_a, kept_b, came_b, after)
+    )(kept_a, came_a, kept_b, came_b, *after)
 
 
 def combine_kernel(*refs):
-    terms, out = refs[:6], refs[-1]
+    terms, out, mark = refs[:6], refs[-2], refs[-1]
+    leave(mark)
     count = out.shape[0] // 2
     width = out.shape[1]
     for i in range(2):
@@ -417,10 +412,10 @@
     whole = pl.BlockSpec((count, width), lambda i: (0, 0))
     return pl.pallas_call(
         combine_kernel,
-        out_shape=jax.ShapeDtypeStruct((2 * count, width // 2), last_a.dtype),
+        out_shape=[jax.ShapeDtypeStruct((2 * count, width // 2), last_a.dtype), MARK],
         grid=(1,),
-        in_specs=[first, first, whole] * 2 + [pl.BlockSpec(memory_space=pl.ANY)],
-        out_specs=pl.BlockSpec((2 * count, width // 2), lambda i: (0, 0)),
+        in_specs=[first, first, whole] * 2 + [ANY_SPEC] * len(after),
+        out_specs=[pl.BlockSpec((2 * count, width // 2), lambda i: (0, 0)), MARK_SPEC],
         compiler_params=pltpu.CompilerParams(vmem_limit_bytes=10 * MIB),
         cost_estimate=pl.CostEstimate(
             flops=8 * count * width,
@@ -428,10 +423,12 @@
             transcendentals=count * width // 2,
         ),
         name=f"combine_{chunk}",
-    )(kept_a, came_a, last_a, kept_b, came_b, last_b, after)
-
-
-def panel_product_kernel(own, other, weight, kept_a, sent_a, kept_b, sent_b):
+    )(kept_a, came_a, last_a, kept_b, came_b, last_b, *after)
+
+
+def panel_product_kernel(own, other, weight, *refs):
+    kept_a, sent_a, kept_b, sent_b, mark = refs[-5:]
+    leave(mark)
     half = own.shape[1]
     product = jnp.dot(own[...], weight[0, :half], preferred_element_type=jnp.float32)
     product += jnp.dot(other[...], weight[0, half:], preferred_element_type=jnp.float32)
@@ -449,37 +446,42 @@
             (sent_b if flip else kept_b)[part % 2] = product[count:]
 
 
-def panel_product(own, other, dense, chunk):
+def panel_product(own, other, dense, after, chunk):
     count, half = own.shape
     _, depth, width = dense.shape
     tile = width // 4
     out = jax.ShapeDtypeStruct((2, count // 2, tile), own.dtype)
     return pl.pallas_call(
         panel_product_kernel,
-        out_shape=[out] * 4,
+        out_shape=[out] * 4 + [MARK],
         grid=(4,),
         in_specs=[pl.BlockSpec((count, half), lambda n: (0, 0))] * 2
-        + [pl.BlockSpec((1, depth, tile), lambda n: (chunk, 0, n))],
-        out_specs=[pl.BlockSpec(out.shape, lambda n: (0, 0, 0))] * 4,
-        compiler_params=pltpu.CompilerParams(vmem_limit_bytes=42 * MIB),
+        + [pl.BlockSpec((1, depth, tile), lambda n: (0, 0, n))]
+        + [ANY_SPEC] * len(after),
+        out_specs=[pl.BlockSpec(out.shape, lambda n: (0, 0, 0))] * 4 + [MARK_SPEC],
+        compiler_params=pltpu.CompilerParams(vmem_limit_bytes=54 * MIB),
         cost_estimate=pl.CostEstimate(
             flops=2 * count * depth * width,
             bytes_accessed=2 * (depth * width + count * (depth + width)),
             transcendentals=0,
         ),
         name=f"gate_up_{chunk}",
-    )(own, other, dense)
-
-
-def down_product_kernel(flips, own, other, weight, *refs, added):
-    before, outs, held = refs[:added], refs[added:-1], refs[-1]
-    panels, _, depth = own.shape
+    )(own, other, dense, *after)
+
+
+def down_product_kernel(place, hidden, weight, *refs, added):
+    before, outs, mark, held = refs[:added], refs[added:-2], refs[-2], refs[-1]
+    leave(mark)
+    panels, parts, count, depth = hidden.shape
+    chip, flips = place[0], place[1]
 
     @pl.when(pl.program_id(0) == 0)
     def _():
-        for i in range(panels):
-            held[:, i * depth:(i + 1) * depth] = own[i]
-            held[:, (panels + i) * depth:(panels + i + 1) * depth] = other[i]
+        for panel in range(panels):
+            columns = slice(panel * depth, (panel + 1) * depth)
+            for part in range(parts):
+                there = part ^ chip ^ (panel // 2)
+                held[part * count:(part + 1) * count, columns] = hidden[panel, there]
 
     if len(outs) == 1:
         product = jnp.dot(held[...], weight[0], preferred_element_type=jnp.float32)
@@ -487,49 +489,47 @@
             product += term[...]
         outs[0][...] = product
         return
-    count = outs[0].shape[0]
-    order = []
     for step, out in enumerate(outs):
-        at = pl.multiple_of((flips[0] ^ step) * count, count)
-        order.append(at)
-    for step, out in enumerate(outs):
-        rows = pl.ds(order[step], count)
+        rows = pl.ds(pl.multiple_of((flips ^ step) * count, count), count)
         product = jnp.dot(held[rows], weight[0], preferred_element_type=jnp.float32)
         for term in before:
             product += term[rows]
         out[...] = product.astype(out.dtype)
 
 
-def down_product(own, other, dense, before, chunk, flips):
-    panels, count, depth = own.shape
+def down_product(place, hidden, dense, before, chunk, last):
+    panels, parts, count, depth = hidden.shape
     _, total, width = dense.shape
     tile = width // 2
-    tiles = pl.BlockSpec((count, tile), lambda n, *_: (0, n))
-    whole = pl.BlockSpec((panels, count, depth), lambda n, *_: (0, 0, 0))
+    tiles = pl.BlockSpec((parts * count, tile), lambda n, *_: (0, n))
     added = [] if before is None else [before]
-    out, out_tiles = jax.ShapeDtypeStruct((count, width), jnp.float32), tiles
-    if flips is not None:
-        out = [jax.ShapeDtypeStruct((count // panels, width), own.dtype)] * panels
-        out_tiles = [pl.BlockSpec((count // panels, tile), lambda n, *_: (0, n))] * panels
+    if last:
+        out = [jax.ShapeDtypeStruct((count, width), hidden.dtype)] * parts
+        out_tiles = [pl.BlockSpec((count, tile), lambda n, *_: (0, n))] * parts
+    else:
+        out, out_tiles = [jax.ShapeDtypeStruct((parts * count, width), jnp.float32)], [tiles]
     return pl.pallas_call(
         functools.partial(down_product_kernel, added=len(added)),
-        out_shape=out,
+        out_shape=out + [MARK],
         grid_spec=pltpu.PrefetchScalarGridSpec(
             num_scalar_prefetch=1,
             grid=(width // tile,),
-            in_specs=[whole, whole, pl.BlockSpec((1, total, tile), lambda n, *_: (chunk, 0, n))]
+            in_specs=[
+                pl.BlockSpec(hidden.shape, lambda n, *_: (0, 0, 0, 0)),
+                pl.BlockSpec((1, total, tile), lambda n, *_: (chunk, 0, n)),
+            ]
             + [tiles] * len(added),
-            out_specs=out_tiles,
-            scratch_shapes=[pltpu.VMEM((count, total), own.dtype)],
-        ),
-        compiler_params=pltpu.CompilerParams(vmem_limit_bytes=24 * MIB),
-        cost_estimate=pl.CostEstimate(
-            flops=2 * count * total * width,
-            bytes_accessed=2 * total * (width + count) + 8 * count * width,
+            out_specs=out_tiles + [MARK_SPEC],
+            scratch_shapes=[pltpu.VMEM((parts * count, total), hidden.dtype)],
+        ),
+        compiler_params=pltpu.CompilerParams(vmem_limit_bytes=50 * MIB),
+        cost_estimate=pl.CostEstimate(
+            flops=2 * parts * count * total * width,
+            bytes_accessed=2 * total * (width + parts * count) + 8 * parts * count * width,
             transcendentals=0,
         ),
         name=f"down_{chunk}",
-    )(jnp.int32(0)[None] if flips is None else flips[None], own, other, dense, *added)
+    )(place, hidden, dense, *added)
 
 
 def by_columns(
@@ -549,7 +549,7 @@
     cols_per = HIDDEN_UNITS // edge // col_size
     width_blocks = MODEL_WIDTH // edge // col_size
     share = cols_per // tok_size
-    chunks = 3 if share % 3 == 0 else 1
+    chunks = 2 if share % 2 == 0 else 1
     cols = share // chunks
     count, half = tokens.shape
     tok, col = lax.axis_index("tok"), lax.axis_index("col")
@@ -582,17 +582,17 @@
     slots = (row * cols_per + (p ^ tok) * share + k * cols + q).reshape(-1).astype(jnp.int32)
     gate_at = lookup(gate_block_places[0], slots)
     up_at = lookup(up_block_places[0], slots)
-    m = jnp.arange(col_size, dtype=jnp.int32)
-    panels = 2 * ((m % tok_size) ^ chip) + (side ^ (m // tok_size))
     slots = tok * share * width_blocks + jnp.arange(share * width_blocks, dtype=jnp.int32)
-    down_at = jnp.take(lookup(down_slots, slots), panels, axis=0).reshape(-1)
-
-    dense = spread_shares(
-        gate_at, up_at, gate_block_entries, up_block_entries, chunks, rows_per, tok_size, cols
-    )
-    down_dense = spread_panels(down_at, panels, down_values, chunks, cols, width_blocks)
-
-    squares = sum_squares(tokens, dense)
+    down_at = lookup(down_slots, slots).reshape(-1)
+    gate_at, up_at = gate_at.reshape(chunks, -1), up_at.reshape(chunks, -1)
+
+    def spread(chunk, after):
+        return spread_shares(
+            gate_at[chunk], up_at[chunk], gate_block_entries, up_block_entries,
+            rows_per, tok_size, cols, after, chunk,
+        )
+
+    squares = sum_squares(tokens)
     squares += swap_core(squares)
     squares += swap_chip(squares, 1)
     squares += swap_chip(squares, 2)
@@ -602,29 +602,35 @@
     gain = lax.dynamic_slice_in_dim(norm_gain, (tok * 2 + side) * half, half, 0)[None]
     scale = lax.rsqrt(squares / MODEL_WIDTH + EPSILON)
     scale = jnp.take(scale, jnp.arange(tok_size) ^ chip ^ tok, axis=0).reshape(-1, 1)
-    own = pack(pieces, scale, gain, [down_dense])
+    dense, mark = spread(0, [])
+    own = pack(pieces, scale, gain, [mark])
     other = swap_core(own)
 
-    sums = [panel_product(own, other, dense, chunk) for chunk in range(chunks)]
-    hiddens, halves = [], []
+    place = jnp.stack([chip, chip ^ tok])
+    hiddens = []
+    *sums, mark = panel_product(own, other, dense, [], 0)
+    if chunks > 1:
+        dense, mark = spread(1, [mark])
     for chunk in range(chunks):
-        kept_a, sent_a, kept_b, sent_b = sums[chunk]
+        kept_a, sent_a, kept_b, sent_b = sums
         came_a, came_b = swap_tok(sent_a, 1), swap_tok(sent_b, 2)
-        ahead = sums[min(chunk + 1, chunks - 1)][0]
-        last_a, last_b = halfway(kept_a, came_a, kept_b, came_b, ahead, chunk)
-        halves.append(last_a)
+        if chunk + 1 < chunks:
+            *sums, mark = panel_product(own, other, dense, [mark], chunk + 1)
+        last_a, last_b, mark = halfway(kept_a, came_a, kept_b, came_b, [mark], chunk)
         last_a, last_b = swap_tok(last_a, 2), swap_tok(last_b, 1)
-        hidden = combine(kept_a, came_a, last_a, kept_b, came_b, last_b, sums[-1][0], chunk)
-        hiddens.append(hidden)
-
-    mixed = None
+        if chunk + 2 < chunks:
+            dense, mark = spread(chunk + 2, [mark])
+        elif chunk == max(chunks - 2, 0):
+            down_dense, mark = spread_panels(
+                down_at, down_values, chunks, cols, width_blocks, [mark]
+            )
+        hidden, mark = combine(kept_a, came_a, last_a, kept_b, came_b, last_b, [mark], chunk)
+        hiddens.append(lax.all_gather(hidden.reshape(tok_size, count, -1), "col"))
+
+    mixed = [None]
     for chunk in range(chunks):
-        held = [hiddens[chunk]] + [swap_chip(hiddens[chunk], step) for step in parts[1:]]
-        ahead = hiddens[chunk + 1:chunk + 2] + halves[chunk + 2:chunk + 3]
-        ahead += [] if mixed is None else [mixed]
-        held = pack_hidden(held, ahead)
-        last = chip ^ tok if chunk == chunks - 1 else None
-        mixed = down_product(held, swap_core(held), down_dense, mixed, chunk, last)
+        last = chunk == chunks - 1
+        *mixed, _ = down_product(place, hiddens[chunk], down_dense, mixed[0], chunk, last)
 
     total = mixed[0].astype(jnp.float32)
     for step in parts[1:]:

time: 248 us -> 234 us (0.944); the launches traced: 245 us -> 234 us
  Pallas kernels: 65.6 us -> 84.6 us
  local copies, waits for them, and re-layouts: 25.2 us -> 8.34 us
  starting transfers between devices: 51.4 us -> 36.7 us
  between operations: 0.43 us -> 13.7 us
  waiting for transfers between devices: 99 us -> 88.1 us
    ppermute x11 -> x2, waiting for transfers between devices: 49.8 us -> 7.78 us  [swap_chip(): lax.ppermute(array, 'col', [(i, i ^ 2 * step) for i in range(col_size)])]
    all_gather x0 -> x2, waiting for transfers between devices: none -> 38.5 us  [by_columns(): hiddens.append(lax.all_gather(hidden.reshape(tok_size, count, -1), 'col'))]
    unnamed x18 -> x30, local copies, waits for them, and re-layouts: 22.3 us -> 5.11 us
    ppermute x11 -> x2, starting transfers between devices: 20.3 us -> 7.75 us  [swap_chip(): lax.ppermute(array, 'col', [(i, i ^ 2 * step) for i in range(col_size)])]
    pallas_call x13 -> x8, Pallas kernels: 41.5 us -> 51.6 us  [the longest x2 24 us: spread_shares(): pl.pallas_call(functools.partial(spread_shares_kernel, rows=rows // steps...]
    pallas_call x3 -> x2, Pallas kernels: 11 us -> 16 us  [down_product(): pl.pallas_call(functools.partial(down_product_kernel, added=len(added)),...]
    ppermute x17 -> x13, waiting for transfers between devices: 43.8 us -> 39.2 us  [swap_tok(): return lax.ppermute(array, 'tok', [(i, i ^ step) for i in parts])]
    pallas_call x1, Pallas kernels: 12.7 us -> 16.6 us  [spread_panels(): pl.pallas_call(functools.partial(spread_panels_kernel, chunks=chunks, row...]
  transfers between devices with their start and end apart: 37 -> 23, of which waited for: 16 -> 12; matrix products, arithmetic and copies ran while one was open for 2% -> 2% of each run, Pallas kernels for 22% -> 27%
where the time goes in v4:
time: 234 us
  waiting for transfers between devices  88.1 us (38%)
  Pallas kernels  84.6 us (36%)
  starting transfers between devices  36.7 us (16%)
  between operations  13.7 us (6%)
  local copies, waits for them, and re-layouts  8.34 us (4%)
    ppermute x13, waiting for transfers between devices, swap_tok(): return lax.ppermute(array, 'tok', [(i, i ^ step) for i in parts])  39.2 us
    all_gather x2, waiting for transfers between devices, by_columns(): hiddens.append(lax.all_gather(hidden.reshape(tok_size, count, -1), 'col'))  38.5 us
    pallas_call x2, Pallas kernels, spread_shares(): pl.pallas_call(functools.partial(spread_shares_kernel, rows=rows // steps...  24 us
    pallas_call x2, Pallas kernels, panel_product(): pl.pallas_call(panel_product_kernel, out_shape=[out] * 4 + [MARK], grid=(...  23.7 us
    ppermute x13, starting transfers between devices, swap_tok(): return lax.ppermute(array, 'tok', [(i, i ^ step) for i in parts])  16.9 us
    pallas_call x1, Pallas kernels, spread_panels(): pl.pallas_call(functools.partial(spread_panels_kernel, chunks=chunks, row...  16.6 us
    pallas_call x2, Pallas kernels, down_product(): pl.pallas_call(functools.partial(down_product_kernel, added=len(added)),...  16 us
    ppermute x4, starting transfers between devices, to_users(): return lax.ppermute(array, ('tok', 'col'), pairs)  11.8 us
  transfers between devices with their start and end apart: 23, of which 12 were waited for; matrix products, arithmetic and copies ran while one was open for 2% of the time, Pallas kernels for 27%

profile of v4, /device:TPU:0, one launch (start us, length us, event | category | flops | bytes accessed | tf_op | source)
XLA Modules:
  0.0 233.7 jit_solution(5399219692336216364)
XLA Ops:
  6.5 1.6 collective-permute-start
  8.1 4.8 %collective-permute-start.1 = (bf16[128,1024]{1,0:T(8,128)(2,1)}, bf16[128,1024]{1,0:T(8,128)(2,1)S(1)}, u32[]{:S(2)}, u32[]{:S(2)}) collective-permute-start(bf16[128,1024]{1,0:T(8,128)(2,1)} %tokens.1), channel_id=1, source_target_pairs={{0,2},{1,3},{2,10},{3,11},{4,18},{5,19},{6,26},{7,27},{8,0},{9,1},... | collective-permute-start | bytes 786440 | tf_op jit(solution)/shard_map/ppermute | solution.py:574
  12.9 3.5 %collective-permute-start.2 = (bf16[128,1024]{1,0:T(8,128)(2,1)}, bf16[128,1024]{1,0:T(8,128)(2,1)S(1)}, u32[]{:S(2)}, u32[]{:S(2)}) collective-permute-start(bf16[128,1024]{1,0:T(8,128)(2,1)} %tokens.1), channel_id=1, source_target_pairs={{0,4},{1,5},{2,12},{3,13},{4,20},{5,21},{6,28},{7,29},{8,6},{9,7},... | collective-permute-start | bytes 786440 | tf_op jit(solution)/shard_map/ppermute | solution.py:574
  16.4 1.9 collective-permute-start.3
  21.6 1.5 collective-permute-start.5
  23.7 6.1 %collective-permute-done.5 = f32[1,128]{1,0:T(1,128)S(1)} collective-permute-done((f32[1,128]{1,0:T(1,128)S(1)}, f32[1,128]{1,0:T(1,128)S(1)}, u32[]{:S(2)}, u32[]{:S(2)}) %collective-permute-start.5) | collective-permute-done | bytes 544 | tf_op jit(solution)/shard_map/ppermute | solution.py:563
  29.8 6.2 %collective-permute-start.6 = (f32[1,128]{1,0:T(1,128)S(1)}, f32[1,128]{1,0:T(1,128)S(1)}, u32[]{:S(2)}, u32[]{:S(2)}) collective-permute-start(f32[1,128]{1,0:T(1,128)S(1)} %add.100), channel_id=1, source_target_pairs={{0,4},{1,5},{2,6},{3,7},{4,0},{5,1},{6,2},{7,3},{8,12},{9,13},{10,... | collective-permute-start | bytes 1544 | tf_op jit(solution)/shard_map/ppermute | solution.py:563
  36.0 1.7 collective-permute-done.6
  37.8 2.7 %collective-permute-start.7 = (f32[1,128]{1,0:T(1,128)S(1)}, f32[1,128]{1,0:T(1,128)S(1)}, u32[]{:S(2)}, u32[]{:S(2)}) collective-permute-start(f32[1,128]{1,0:T(1,128)S(1)} %add.101), channel_id=1, source_target_pairs={{0,8},{8,0},{16,24},{24,16},{1,9},{9,1},{17,25},{25,17},{2,10},{10... | collective-permute-start | bytes 1544 | tf_op jit(solution)/shard_map/ppermute | solution.py:560
  40.4 1.5 collective-permute-done.7
  42.0 4.2 %collective-permute-start.8 = (f32[2,128]{1,0:T(2,128)S(1)}, f32[2,128]{1,0:T(2,128)S(1)}, u32[]{:S(2)}, u32[]{:S(2)}) collective-permute-start(f32[2,128]{1,0:T(2,128)S(1)} %pad_maximum_fusion), channel_id=1, source_target_pairs={{0,16},{8,24},{16,0},{24,8},{1,17},{9,25},{17,1},{25,9},{2,18},{10... | collective-permute-start | bytes 3080 | tf_op jit(solution)/shard_map/ppermute | solution.py:560
  46.9 12.0 %spread_gate_up_0.1 = (bf16[1,2048,3072]{2,1,0:T(8,128)(2,1)}, f32[8,128]{1,0:T(8,128)}) custom-call(s32[192]{0:T(256)} %get-tuple-element.71.gate_at, s32[192]{0:T(256)} %get-tuple-element.68.up_at, bf16[1,216,128,128]{3,2,1,0:T(8,128)(2,1)} %refs_0_.3, bf16[1,216,128,128]{3,2,1,0:T(8,128)(2,1)} %refs_1_.3), custom_call_target="tpu_custom_call" | custom-call | bytes 26738688 | tf_op jit(solution)/shard_map/spread_gate_up_0/pallas_call | solution.py:274
  60.8 2.6 %collective-permute-done.9.other = bf16[512,1024]{1,0:T(8,128)(2,1)S(1)} collective-permute-done((bf16[512,1024]{1,0:T(8,128)(2,1)S(1)}, bf16[512,1024]{1,0:T(8,128)(2,1)S(1)}, u32[]{:S(2)}, u32[]{:S(2)}) %collective-permute-start.9) | collective-permute-done | bytes 1048608 | tf_op jit(solution)/shard_map/ppermute | solution.py:566
  64.5 11.8 %gate_up_0.1 = (bf16[2,256,768]{2,1,0:T(8,128)(2,1)}, bf16[2,256,768]{2,1,0:T(8,128)(2,1)}, bf16[2,256,768]{2,1,0:T(8,128)(2,1)}, bf16[2,256,768]{2,1,0:T(8,128)(2,1)}, f32[8,128]{1,0:T(8,128)}) custom-call(bf16[512,1024]{1,0:T(8,128)(2,1)} %copy-done.8, bf16[512,1024]{1,0:T(8,128)(2,1)} %copy-done.14, bf16[1,2048,3072]{2,1,0:T(8,128)(2,1)} %get-tuple-element.36.weight), custom_call_target="tpu_custom_call" | custom-call | flops 6442450944 | bytes 17825792 | tf_op jit(solution)/shard_map/gate_up_0/pallas_call | solution.py:454
  77.0 12.0 %spread_gate_up_1.1 = (bf16[1,2048,3072]{2,1,0:T(8,128)(2,1)}, f32[8,128]{1,0:T(8,128)}) custom-call(s32[192]{0:T(256)} %get-tuple-element.72.gate_at, s32[192]{0:T(256)} %get-tuple-element.67.up_at, bf16[1,216,128,128]{3,2,1,0:T(8,128)(2,1)} %refs_0_.3, bf16[1,216,128,128]{3,2,1,0:T(8,128)(2,1)} %refs_1_.3, f32[8,128]{1,0:T(8,128)} %get-tuple-element.37.refs_2_), custom_call_target="tpu_custom_call" | custom-call | bytes 26738688 | tf_op jit(solution)/shard_map/spread_gate_up_1/pallas_call | solution.py:274
  89.0 11.9 %gate_up_1.1 = (bf16[2,256,768]{2,1,0:T(8,128)(2,1)}, bf16[2,256,768]{2,1,0:T(8,128)(2,1)}, bf16[2,256,768]{2,1,0:T(8,128)(2,1)}, bf16[2,256,768]{2,1,0:T(8,128)(2,1)}, f32[8,128]{1,0:T(8,128)}) custom-call(bf16[512,1024]{1,0:T(8,128)(2,1)} %copy-done.8, bf16[512,1024]{1,0:T(8,128)(2,1)} %copy-done.14, bf16[1,2048,3072]{2,1,0:T(8,128)(2,1)} %get-tuple-element.38.weight, ...), custom_call_target="tpu_custom_call" | custom-call | flops 6442450944 | bytes 17825792 | tf_op jit(solution)/shard_map/gate_up_1/pallas_call | solution.py:454
  103.5 2.0 collective-permute-start.14
  105.5 1.4 collective-permute-start.15
  107.3 16.6 %spread_down.1 = (bf16[2,3072,1024]{2,1,0:T(8,128)(2,1)}, f32[8,128]{1,0:T(8,128)S(1)}) custom-call(s32[384]{0:T(512)S(1)} %reshape.112.at_ref, bf16[8,108,128,128]{3,2,1,0:T(8,128)(2,1)} %values_ref.1, f32[8,128]{1,0:T(8,128)S(1)} %get-tuple-element.51.refs_0_), custom_call_target="tpu_custom_call" | custom-call | bytes 40894464 | tf_op jit(solution)/shard_map/spread_down/pallas_call | solution.py:305
  123.9 1.5 combine_0.1
  127.2 18.0 %collective-permute-done.10.came_a.refs_1_ = bf16[2,256,768]{2,1,0:T(8,128)(2,1)S(1)} collective-permute-done((bf16[2,256,768]{2,1,0:T(8,128)(2,1)}, bf16[2,256,768]{2,1,0:T(8,128)(2,1)S(1)}, u32[]{:S(2)}, u32[]{:S(2)}) %collective-permute-start.10) | collective-permute-done | bytes 786464 | tf_op jit(solution)/shard_map/ppermute | solution.py:560
  146.1 1.4 collective-permute-start.17
  147.5 7.3 %collective-permute-done.16.refs_2_ = bf16[256,768]{1,0:T(8,128)(2,1)S(1)} collective-permute-done((bf16[256,768]{1,0:T(8,128)(2,1)S(1)}, bf16[256,768]{1,0:T(8,128)(2,1)S(1)}, u32[]{:S(2)}, u32[]{:S(2)}) %collective-permute-start.16) | collective-permute-done | bytes 393248 | tf_op jit(solution)/shard_map/ppermute | solution.py:560
  155.0 1.2 combine_1.1
  156.3 7.6 %all-gather.5.cloned.1.call-done.hidden = bf16[8,4,128,384]{3,2,1,0:T(8,128)(2,1)} async-done(((bf16[1,4,128,384]{3,2,1,0:T(8,128)(2,1)}), bf16[8,4,128,384]{3,2,1,0:T(8,128)(2,1)}) %all-gather.5.cloned.1.call-update) | async-done | bytes 3145744 | tf_op jit(solution)/shard_map/all_gather | solution.py:628
  163.9 8.0 %down_0.1 = (f32[512,1024]{1,0:T(8,128)S(1)}, f32[8,128]{1,0:T(8,128)}) custom-call(s32[2]{0:T(128)S(1)} %pad_add_fusion.place, bf16[8,4,128,384]{3,2,1,0:T(8,128)(2,1)} %all-gather.5.cloned.1.call-done.hidden, bf16[2,3072,1024]{2,1,0:T(8,128)(2,1)} %get-tuple-element.58.weight), custom_call_target="tpu_custom_call" | custom-call | flops 3221225472 | bytes 13631488 | tf_op jit(solution)/shard_map/down_0/pallas_call | solution.py:511
  171.9 30.8 %all-gather.3.cloned.1.call-done.hidden = bf16[8,4,128,384]{3,2,1,0:T(8,128)(2,1)} async-done(((bf16[1,4,128,384]{3,2,1,0:T(8,128)(2,1)}), bf16[8,4,128,384]{3,2,1,0:T(8,128)(2,1)}) %all-gather.3.cloned.1.call-update) | async-done | bytes 3145744 | tf_op jit(solution)/shard_map/all_gather | solution.py:628
  202.7 8.0 %down_1.1 = (bf16[128,1024]{1,0:T(8,128)(2,1)S(1)}, bf16[128,1024]{1,0:T(8,128)(2,1)S(1)}, bf16[128,1024]{1,0:T(8,128)(2,1)S(1)}, bf16[128,1024]{1,0:T(8,128)(2,1)S(1)}, f32[8,128]{1,0:T(8,128)}) custom-call(s32[2]{0:T(128)S(1)} %pad_add_fusion.place, bf16[8,4,128,384]{3,2,1,0:T(8,128)(2,1)} %all-gather.3.cloned.1.call-done.hidden, ...), custom_call_target="tpu_custom_call" | custom-call | flops 3221225472 | bytes 13631488 | tf_op jit(solution)/shard_map/down_1/pallas_call | solution.py:511
  210.8 1.5 collective-permute-start.18
  212.2 1.5 collective-permute-start.19
  214.2 5.7 %collective-permute-done.18 = bf16[128,1024]{1,0:T(8,128)(2,1)S(1)} collective-permute-done((bf16[128,1024]{1,0:T(8,128)(2,1)S(1)}, bf16[128,1024]{1,0:T(8,128)(2,1)S(1)}, u32[]{:S(2)}, u32[]{:S(2)}) %collective-permute-start.18) | collective-permute-done | bytes 262176 | tf_op jit(solution)/shard_map/ppermute | solution.py:560
  219.9 6.1 %collective-permute-done.19 = bf16[128,1024]{1,0:T(8,128)(2,1)S(1)} collective-permute-done((bf16[128,1024]{1,0:T(8,128)(2,1)S(1)}, bf16[128,1024]{1,0:T(8,128)(2,1)S(1)}, u32[]{:S(2)}, u32[]{:S(2)}) %collective-permute-start.19) | collective-permute-done | bytes 262176 | tf_op jit(solution)/shard_map/ppermute | solution.py:560
  (90 shorter events, 15.5 us)
Async XLA Ops:
  6.5 157.4 %all-gather.5.cloned.1.call-start = ((), (), s32[]{:S(2)}) async-start(), calls=%async_computation.1 | async-start | bytes 3538944 | tf_op jit(solution)/shard_map/all_gather | solution.py:628
  6.5 53.1 %collective-permute-start = (bf16[128,1024]{1,0:T(8,128)(2,1)}, bf16[128,1024]{1,0:T(8,128)(2,1)S(1)}, u32[]{:S(2)}, u32[]{:S(2)}) collective-permute-start(bf16[128,1024]{1,0:T(8,128)(2,1)} %tokens.1), channel_id=1, source_target_pairs={{0,0},{1,1},{2,8},{3,9},{4,16},{5,17},{6,24},{7,25},{8,2},{9,3},{1... | collective-permute-start | bytes 786440 | tf_op jit(solution)/shard_map/ppermute | solution.py:574
  8.1 51.6 %collective-permute-start.1 = (bf16[128,1024]{1,0:T(8,128)(2,1)}, bf16[128,1024]{1,0:T(8,128)(2,1)S(1)}, u32[]{:S(2)}, u32[]{:S(2)}) collective-permute-start(bf16[128,1024]{1,0:T(8,128)(2,1)} %tokens.1), channel_id=1, source_target_pairs={{0,2},{1,3},{2,10},{3,11},{4,18},{5,19},{6,26},{7,27},{8,0},{9,1},... | collective-permute-start | bytes 786440 | tf_op jit(solution)/shard_map/ppermute | solution.py:574
  12.9 46.8 %collective-permute-start.2 = (bf16[128,1024]{1,0:T(8,128)(2,1)}, bf16[128,1024]{1,0:T(8,128)(2,1)S(1)}, u32[]{:S(2)}, u32[]{:S(2)}) collective-permute-start(bf16[128,1024]{1,0:T(8,128)(2,1)} %tokens.1), channel_id=1, source_target_pairs={{0,4},{1,5},{2,12},{3,13},{4,20},{5,21},{6,28},{7,29},{8,6},{9,7},... | collective-permute-start | bytes 786440 | tf_op jit(solution)/shard_map/ppermute | solution.py:574
  16.4 43.3 %collective-permute-start.3 = (bf16[128,1024]{1,0:T(8,128)(2,1)}, bf16[128,1024]{1,0:T(8,128)(2,1)S(1)}, u32[]{:S(2)}, u32[]{:S(2)}) collective-permute-start(bf16[128,1024]{1,0:T(8,128)(2,1)} %tokens.1), channel_id=1, source_target_pairs={{0,6},{1,7},{2,14},{3,15},{4,22},{5,23},{6,30},{7,31},{8,4},{9,5},... | collective-permute-start | bytes 786440 | tf_op jit(solution)/shard_map/ppermute | solution.py:574
  19.4 2.1 collective-permute-start.4
  21.6 8.2 %collective-permute-start.5 = (f32[1,128]{1,0:T(1,128)S(1)}, f32[1,128]{1,0:T(1,128)S(1)}, u32[]{:S(2)}, u32[]{:S(2)}) collective-permute-start(f32[1,128]{1,0:T(1,128)S(1)} %add.99), channel_id=1, source_target_pairs={{0,2},{1,3},{2,0},{3,1},{4,6},{5,7},{6,4},{7,5},{8,10},{9,11},{10,... | collective-permute-start | bytes 1544 | tf_op jit(solution)/shard_map/ppermute | solution.py:563
  29.8 8.0 %collective-permute-start.6 = (f32[1,128]{1,0:T(1,128)S(1)}, f32[1,128]{1,0:T(1,128)S(1)}, u32[]{:S(2)}, u32[]{:S(2)}) collective-permute-start(f32[1,128]{1,0:T(1,128)S(1)} %add.100), channel_id=1, source_target_pairs={{0,4},{1,5},{2,6},{3,7},{4,0},{5,1},{6,2},{7,3},{8,12},{9,13},{10,... | collective-permute-start | bytes 1544 | tf_op jit(solution)/shard_map/ppermute | solution.py:563
  37.8 4.2 %collective-permute-start.7 = (f32[1,128]{1,0:T(1,128)S(1)}, f32[1,128]{1,0:T(1,128)S(1)}, u32[]{:S(2)}, u32[]{:S(2)}) collective-permute-start(f32[1,128]{1,0:T(1,128)S(1)} %add.101), channel_id=1, source_target_pairs={{0,8},{8,0},{16,24},{24,16},{1,9},{9,1},{17,25},{25,17},{2,10},{10... | collective-permute-start | bytes 1544 | tf_op jit(solution)/shard_map/ppermute | solution.py:560
  42.0 16.9 %collective-permute-start.8 = (f32[2,128]{1,0:T(2,128)S(1)}, f32[2,128]{1,0:T(2,128)S(1)}, u32[]{:S(2)}, u32[]{:S(2)}) collective-permute-start(f32[2,128]{1,0:T(2,128)S(1)} %pad_maximum_fusion), channel_id=1, source_target_pairs={{0,16},{8,24},{16,0},{24,8},{1,17},{9,25},{17,1},{25,9},{2,18},{10... | collective-permute-start | bytes 3080 | tf_op jit(solution)/shard_map/ppermute | solution.py:560
  60.7 2.7 %copy-start.8 = (bf16[512,1024]{1,0:T(8,128)(2,1)}, bf16[512,1024]{1,0:T(8,128)(2,1)S(1)}, u32[]{:S(2)}) copy-start(bf16[512,1024]{1,0:T(8,128)(2,1)S(1)} %pack.1.own) | copy-start | bytes 3145732
  60.7 2.7 %collective-permute-start.9 = (bf16[512,1024]{1,0:T(8,128)(2,1)S(1)}, bf16[512,1024]{1,0:T(8,128)(2,1)S(1)}, u32[]{:S(2)}, u32[]{:S(2)}) collective-permute-start(bf16[512,1024]{1,0:T(8,128)(2,1)S(1)} %pack.1.own), channel_id=1, source_target_pairs={{0,1},{1,0},{2,3},{3,2},{4,5},{5,4},{6,7},{7,6},{8,9},{9,8},{10,11... | collective-permute-start | bytes 3145736 | tf_op jit(solution)/shard_map/ppermute | solution.py:566
  76.3 24.6 %collective-permute-start.12 = (bf16[2,256,768]{2,1,0:T(8,128)(2,1)}, bf16[2,256,768]{2,1,0:T(8,128)(2,1)S(1)}, u32[]{:S(2)}, u32[]{:S(2)}) collective-permute-start(bf16[2,256,768]{2,1,0:T(8,128)(2,1)} %get-tuple-element.45), channel_id=1, source_target_pairs={{0,8},{8,0},{16,24},{24,16},{1,9},{9,1},{17,25},{25,17},{2,10},{10... | collective-permute-start | bytes 2359304 | tf_op jit(solution)/shard_map/ppermute | solution.py:560
  76.9 23.9 %collective-permute-start.13 = (bf16[2,256,768]{2,1,0:T(8,128)(2,1)}, bf16[2,256,768]{2,1,0:T(8,128)(2,1)S(1)}, u32[]{:S(2)}, u32[]{:S(2)}) collective-permute-start(bf16[2,256,768]{2,1,0:T(8,128)(2,1)} %get-tuple-element.47), channel_id=1, source_target_pairs={{0,16},{8,24},{16,0},{24,8},{1,17},{9,25},{17,1},{25,9},{2,18},{10... | collective-permute-start | bytes 2359304 | tf_op jit(solution)/shard_map/ppermute | solution.py:560
  89.0 11.9 %copy-start.2 = (bf16[2,256,768]{2,1,0:T(8,128)(2,1)S(1)}, bf16[2,256,768]{2,1,0:T(8,128)(2,1)}, u32[]{:S(2)}) copy-start(bf16[2,256,768]{2,1,0:T(8,128)(2,1)} %get-tuple-element.44.kept_a.refs_0_) | copy-start | bytes 2359300
  89.0 11.9 %copy-start.3 = (bf16[2,256,768]{2,1,0:T(8,128)(2,1)S(1)}, bf16[2,256,768]{2,1,0:T(8,128)(2,1)}, u32[]{:S(2)}) copy-start(bf16[2,256,768]{2,1,0:T(8,128)(2,1)} %get-tuple-element.46.kept_b.refs_3_) | copy-start | bytes 2359300
  89.0 17.9 %copy-start.13 = (s32[8,108]{1,0:T(8,128)S(1)}, s32[8,108]{1,0:T(8,128)}, u32[]{:S(2)}) copy-start(s32[8,108]{1,0:T(8,128)} %param.15) | copy-start | bytes 10372
  100.9 1.7 copy-start.6
  103.5 20.4 %collective-permute-start.14 = (bf16[256,768]{1,0:T(8,128)(2,1)}, bf16[256,768]{1,0:T(8,128)(2,1)S(1)}, u32[]{:S(2)}, u32[]{:S(2)}) collective-permute-start(bf16[256,768]{1,0:T(8,128)(2,1)} %get-tuple-element.49), channel_id=1, source_target_pairs={{0,16},{8,24},{16,0},{24,8},{1,17},{9,25},{17,1},{25,9},{2,18},{10... | collective-permute-start | bytes 1179656 | tf_op jit(solution)/shard_map/ppermute | solution.py:560
  105.5 18.4 %collective-permute-start.15 = (bf16[256,768]{1,0:T(8,128)(2,1)}, bf16[256,768]{1,0:T(8,128)(2,1)}, u32[]{:S(2)}, u32[]{:S(2)}) collective-permute-start(bf16[256,768]{1,0:T(8,128)(2,1)} %get-tuple-element.50), channel_id=1, source_target_pairs={{0,8},{8,0},{16,24},{24,16},{1,9},{9,1},{17,25},{25,17},{2,10},{10... | collective-permute-start | bytes 1179656 | tf_op jit(solution)/shard_map/ppermute | solution.py:560
  107.3 16.7 %copy-start.5 = (bf16[2,256,768]{2,1,0:T(8,128)(2,1)S(1)}, bf16[2,256,768]{2,1,0:T(8,128)(2,1)}, u32[]{:S(2)}) copy-start(bf16[2,256,768]{2,1,0:T(8,128)(2,1)} %copy-done.4) | copy-start | bytes 2359300
  107.3 16.7 %copy-start.7 = (bf16[2,256,768]{2,1,0:T(8,128)(2,1)S(1)}, bf16[2,256,768]{2,1,0:T(8,128)(2,1)}, u32[]{:S(2)}) copy-start(bf16[2,256,768]{2,1,0:T(8,128)(2,1)} %copy-done.6) | copy-start | bytes 2359300
  107.3 38.2 %copy-start = (bf16[2,256,768]{2,1,0:T(8,128)(2,1)S(1)}, bf16[2,256,768]{2,1,0:T(8,128)(2,1)}, u32[]{:S(2)}) copy-start(bf16[2,256,768]{2,1,0:T(8,128)(2,1)} %get-tuple-element.40.kept_a.refs_0_) | copy-start | bytes 2359300
  107.3 38.2 %copy-start.1 = (bf16[2,256,768]{2,1,0:T(8,128)(2,1)S(1)}, bf16[2,256,768]{2,1,0:T(8,128)(2,1)}, u32[]{:S(2)}) copy-start(bf16[2,256,768]{2,1,0:T(8,128)(2,1)} %get-tuple-element.42.kept_b.refs_3_) | copy-start | bytes 2359300
  126.2 76.5 %all-gather.3.cloned.1.call-start = ((), (), s32[]{:S(2)}) async-start(), calls=%async_computation | async-start | bytes 3538944 | tf_op jit(solution)/shard_map/all_gather | solution.py:628
  126.4 18.7 %collective-permute-start.10 = (bf16[2,256,768]{2,1,0:T(8,128)(2,1)}, bf16[2,256,768]{2,1,0:T(8,128)(2,1)S(1)}, u32[]{:S(2)}, u32[]{:S(2)}) collective-permute-start(bf16[2,256,768]{2,1,0:T(8,128)(2,1)} %get-tuple-element.41), channel_id=1, source_target_pairs={{0,8},{8,0},{16,24},{24,16},{1,9},{9,1},{17,25},{25,17},{2,10},{10... | collective-permute-start | bytes 2359304 | tf_op jit(solution)/shard_map/ppermute | solution.py:560
  127.1 18.4 %collective-permute-start.11 = (bf16[2,256,768]{2,1,0:T(8,128)(2,1)}, bf16[2,256,768]{2,1,0:T(8,128)(2,1)S(1)}, u32[]{:S(2)}, u32[]{:S(2)}) collective-permute-start(bf16[2,256,768]{2,1,0:T(8,128)(2,1)} %get-tuple-element.43), channel_id=1, source_target_pairs={{0,16},{8,24},{16,0},{24,8},{1,17},{9,25},{17,1},{25,9},{2,18},{10... | collective-permute-start | bytes 2359304 | tf_op jit(solution)/shard_map/ppermute | solution.py:560
  145.7 9.0 %collective-permute-start.16 = (bf16[256,768]{1,0:T(8,128)(2,1)S(1)}, bf16[256,768]{1,0:T(8,128)(2,1)S(1)}, u32[]{:S(2)}, u32[]{:S(2)}) collective-permute-start(bf16[256,768]{1,0:T(8,128)(2,1)S(1)} %get-tuple-element.54), channel_id=1, source_target_pairs={{0,16},{8,24},{16,0},{24,8},{1,17},{9,25},{17,1},{25,9},{2,18},{10... | collective-permute-start | bytes 1179656 | tf_op jit(solution)/shard_map/ppermute | solution.py:560
  146.1 8.9 %collective-permute-start.17 = (bf16[256,768]{1,0:T(8,128)(2,1)S(1)}, bf16[256,768]{1,0:T(8,128)(2,1)S(1)}, u32[]{:S(2)}, u32[]{:S(2)}) collective-permute-start(bf16[256,768]{1,0:T(8,128)(2,1)S(1)} %get-tuple-element.55), channel_id=1, source_target_pairs={{0,8},{8,0},{16,24},{24,16},{1,9},{9,1},{17,25},{25,17},{2,10},{10... | collective-permute-start | bytes 1179656 | tf_op jit(solution)/shard_map/ppermute | solution.py:560
  210.8 9.1 %collective-permute-start.18 = (bf16[128,1024]{1,0:T(8,128)(2,1)S(1)}, bf16[128,1024]{1,0:T(8,128)(2,1)S(1)}, u32[]{:S(2)}, u32[]{:S(2)}) collective-permute-start(bf16[128,1024]{1,0:T(8,128)(2,1)S(1)} %get-tuple-element.62), channel_id=1, source_target_pairs={{0,8},{8,0},{16,24},{24,16},{1,9},{9,1},{17,25},{25,17},{2,10},{10... | collective-permute-start | bytes 786440 | tf_op jit(solution)/shard_map/ppermute | solution.py:560
  212.2 13.8 %collective-permute-start.19 = (bf16[128,1024]{1,0:T(8,128)(2,1)S(1)}, bf16[128,1024]{1,0:T(8,128)(2,1)S(1)}, u32[]{:S(2)}, u32[]{:S(2)}) collective-permute-start(bf16[128,1024]{1,0:T(8,128)(2,1)S(1)} %get-tuple-element.63), channel_id=1, source_target_pairs={{0,16},{8,24},{16,0},{24,8},{1,17},{9,25},{17,1},{25,9},{2,18},{10... | collective-permute-start | bytes 786440 | tf_op jit(solution)/shard_map/ppermute | solution.py:560
  213.7 12.3 %collective-permute-start.20 = (bf16[128,1024]{1,0:T(8,128)(2,1)S(1)}, bf16[128,1024]{1,0:T(8,128)(2,1)S(1)}, u32[]{:S(2)}, u32[]{:S(2)}) collective-permute-start(bf16[128,1024]{1,0:T(8,128)(2,1)S(1)} %get-tuple-element.64), channel_id=1, source_target_pairs={{0,24},{8,16},{16,8},{24,0},{1,25},{9,17},{17,9},{25,1},{2,26},{10... | collective-permute-start | bytes 786440 | tf_op jit(solution)/shard_map/ppermute | solution.py:560
  (6 other events, 5.1 us)
Sparse Core Ops, SparseCore 0:
  126.3 37.5 all-gather.4
  165.6 37.1 all-gather.2

commit v5 on v4

--- a/solution.py
+++ b/solution.py
@@ -594,6 +594,8 @@
 
     squares = sum_squares(tokens)
     squares += swap_core(squares)
+    dense, mark = spread(0, [])
+    squares += mark[:1, :1]
     squares += swap_chip(squares, 1)
     squares += swap_chip(squares, 2)
     squares = jnp.concatenate([squares, swap_tok(squares, 1)])
@@ -602,8 +604,7 @@
     gain = lax.dynamic_slice_in_dim(norm_gain, (tok * 2 + side) * half, half, 0)[None]
     scale = lax.rsqrt(squares / MODEL_WIDTH + EPSILON)
     scale = jnp.take(scale, jnp.arange(tok_size) ^ chip ^ tok, axis=0).reshape(-1, 1)
-    dense, mark = spread(0, [])
-    own = pack(pieces, scale, gain, [mark])
+    own = pack(pieces, scale, gain, [])
     other = swap_core(own)
 
     place = jnp.stack([chip, chip ^ tok])
@@ -614,17 +615,17 @@
     for chunk in range(chunks):
         kept_a, sent_a, kept_b, sent_b = sums
         came_a, came_b = swap_tok(sent_a, 1), swap_tok(sent_b, 2)
+        last_a, last_b, mark = halfway(kept_a, came_a, kept_b, came_b, [mark], chunk)
+        last_a, last_b = swap_tok(last_a, 2), swap_tok(last_b, 1)
         if chunk + 1 < chunks:
             *sums, mark = panel_product(own, other, dense, [mark], chunk + 1)
-        last_a, last_b, mark = halfway(kept_a, came_a, kept_b, came_b, [mark], chunk)
-        last_a, last_b = swap_tok(last_a, 2), swap_tok(last_b, 1)
+        hidden, mark = combine(kept_a, came_a, last_a, kept_b, came_b, last_b, [mark], chunk)
         if chunk + 2 < chunks:
             dense, mark = spread(chunk + 2, [mark])
         elif chunk == max(chunks - 2, 0):
             down_dense, mark = spread_panels(
                 down_at, down_values, chunks, cols, width_blocks, [mark]
             )
-        hidden, mark = combine(kept_a, came_a, last_a, kept_b, came_b, last_b, [mark], chunk)
         hiddens.append(lax.all_gather(hidden.reshape(tok_size, count, -1), "col"))
 
     mixed = [None]

time: 234 us -> 221 us (0.944)
  waiting for transfers between devices: 88.1 us -> 74.3 us
    ppermute x13, waiting for transfers between devices: 39.2 us -> 28.3 us  [swap_tok(): return lax.ppermute(array, 'tok', [(i, i ^ step) for i in parts])]
    ppermute x13, starting transfers between devices: 16.9 us -> 23 us  [swap_tok(): return lax.ppermute(array, 'tok', [(i, i ^ step) for i in parts])]
    ppermute x2, starting transfers between devices: 7.75 us -> 3.08 us  [swap_chip(): lax.ppermute(array, 'col', [(i, i ^ 2 * step) for i in range(col_size)])]
    ppermute x2, waiting for transfers between devices: 7.78 us -> 4.7 us  [swap_chip(): lax.ppermute(array, 'col', [(i, i ^ 2 * step) for i in range(col_size)])]
    unnamed x30 -> x24, local copies, waits for them, and re-layouts: 5.11 us -> 3.88 us
  transfers between devices with their start and end apart: 23 -> 23, of which waited for: 12 -> 14; matrix products, arithmetic and copies ran while one was open for 2% -> 3% of each run, Pallas kernels for 27% -> 28%
where the time goes in v5:
time: 221 us; the launch traced here: 220 us
  Pallas kernels  84.2 us (38%)
  waiting for transfers between devices  74.3 us (34%)
  starting transfers between devices  36.9 us (17%)
  between operations  13.7 us (6%)
  local copies, waits for them, and re-layouts  8.34 us (4%)
  other arithmetic  2.88 us (1%)
    all_gather x2, waiting for transfers between devices, by_columns(): hiddens.append(lax.all_gather(hidden.reshape(tok_size, count, -1), 'col'))  38.6 us
    ppermute x13, waiting for transfers between devices, swap_tok(): return lax.ppermute(array, 'tok', [(i, i ^ step) for i in parts])  28.3 us
    pallas_call x2, Pallas kernels, spread_shares(): pl.pallas_call(functools.partial(spread_shares_kernel, rows=rows // steps...  24.4 us
    pallas_call x2, Pallas kernels, panel_product(): pl.pallas_call(panel_product_kernel, out_shape=[out] * 4 + [MARK], grid=(...  24 us
    ppermute x13, starting transfers between devices, swap_tok(): return lax.ppermute(array, 'tok', [(i, i ^ step) for i in parts])  23 us
    pallas_call x1, Pallas kernels, spread_panels(): pl.pallas_call(functools.partial(spread_panels_kernel, chunks=chunks, row...  16.6 us
    pallas_call x2, Pallas kernels, down_product(): pl.pallas_call(functools.partial(down_product_kernel, added=len(added)),...  16 us
    ppermute x4, starting transfers between devices, to_users(): return lax.ppermute(array, ('tok', 'col'), pairs)  10.5 us
  transfers between devices with their start and end apart: 23, of which 14 were waited for; matrix products, arithmetic and copies ran while one was open for 3% of the time, Pallas kernels for 28%

profile of v5, /device:TPU:0, one launch (start us, length us, event | category | flops | bytes accessed | tf_op | source)
XLA Modules:
  0.0 220.3 jit_solution(15615503097125432142)
XLA Ops:
  6.5 1.6 collective-permute-start
  8.1 4.8 %collective-permute-start.1 = (bf16[128,1024]{1,0:T(8,128)(2,1)}, bf16[128,1024]{1,0:T(8,128)(2,1)S(1)}, u32[]{:S(2)}, u32[]{:S(2)}) collective-permute-start(bf16[128,1024]{1,0:T(8,128)(2,1)} %tokens.1), channel_id=1, source_target_pairs={{0,2},{1,3},{2,10},{3,11},{4,18},{5,19},{6,26},{7,27},{8,0},{9,1},... | collective-permute-start | bytes 786440 | tf_op jit(solution)/shard_map/ppermute | solution.py:574
  12.9 3.5 %collective-permute-start.2 = (bf16[128,1024]{1,0:T(8,128)(2,1)}, bf16[128,1024]{1,0:T(8,128)(2,1)S(1)}, u32[]{:S(2)}, u32[]{:S(2)}) collective-permute-start(bf16[128,1024]{1,0:T(8,128)(2,1)} %tokens.1), channel_id=1, source_target_pairs={{0,4},{1,5},{2,12},{3,13},{4,20},{5,21},{6,28},{7,29},{8,6},{9,7},... | collective-permute-start | bytes 786440 | tf_op jit(solution)/shard_map/ppermute | solution.py:574
  20.3 12.2 %spread_gate_up_0.1 = (bf16[1,2048,3072]{2,1,0:T(8,128)(2,1)}, f32[8,128]{1,0:T(8,128)}) custom-call(s32[192]{0:T(256)} %get-tuple-element.71.gate_at, s32[192]{0:T(256)} %get-tuple-element.68.up_at, bf16[1,216,128,128]{3,2,1,0:T(8,128)(2,1)} %refs_0_.3, bf16[1,216,128,128]{3,2,1,0:T(8,128)(2,1)} %refs_1_.3), custom_call_target="tpu_custom_call" | custom-call | bytes 26738688 | tf_op jit(solution)/shard_map/spread_gate_up_0/pallas_call | solution.py:274
  34.4 1.5 collective-permute-start.5
  36.5 1.5 collective-permute-done.5
  38.0 1.6 collective-permute-start.6
  39.6 3.2 %collective-permute-done.6 = f32[1,128]{1,0:T(1,128)S(1)} collective-permute-done((f32[1,128]{1,0:T(1,128)S(1)}, f32[1,128]{1,0:T(1,128)S(1)}, u32[]{:S(2)}, u32[]{:S(2)}) %collective-permute-start.6) | collective-permute-done | bytes 544 | tf_op jit(solution)/shard_map/ppermute | solution.py:563
  42.8 3.0 %collective-permute-start.7 = (f32[1,128]{1,0:T(1,128)S(1)}, f32[1,128]{1,0:T(1,128)S(1)}, u32[]{:S(2)}, u32[]{:S(2)}) collective-permute-start(f32[1,128]{1,0:T(1,128)S(1)} %add.121), channel_id=1, source_target_pairs={{0,8},{8,0},{16,24},{24,16},{1,9},{9,1},{17,25},{25,17},{2,10},{10... | collective-permute-start | bytes 1544 | tf_op jit(solution)/shard_map/ppermute | solution.py:560
  45.8 1.5 collective-permute-done.7
  47.3 7.1 %collective-permute-start.8 = (f32[2,128]{1,0:T(2,128)S(1)}, f32[2,128]{1,0:T(2,128)S(1)}, u32[]{:S(2)}, u32[]{:S(2)}) collective-permute-start(f32[2,128]{1,0:T(2,128)S(1)} %pad_maximum_fusion), channel_id=1, source_target_pairs={{0,16},{8,24},{16,0},{24,8},{1,17},{9,25},{17,1},{25,9},{2,18},{10... | collective-permute-start | bytes 3080 | tf_op jit(solution)/shard_map/ppermute | solution.py:560
  57.2 2.6 %collective-permute-done.9.other = bf16[512,1024]{1,0:T(8,128)(2,1)S(1)} collective-permute-done((bf16[512,1024]{1,0:T(8,128)(2,1)S(1)}, bf16[512,1024]{1,0:T(8,128)(2,1)S(1)}, u32[]{:S(2)}, u32[]{:S(2)}) %collective-permute-start.9) | collective-permute-done | bytes 1048608 | tf_op jit(solution)/shard_map/ppermute | solution.py:566
  60.8 12.0 %gate_up_0.1 = (bf16[2,256,768]{2,1,0:T(8,128)(2,1)}, bf16[2,256,768]{2,1,0:T(8,128)(2,1)}, bf16[2,256,768]{2,1,0:T(8,128)(2,1)}, bf16[2,256,768]{2,1,0:T(8,128)(2,1)}, f32[8,128]{1,0:T(8,128)}) custom-call(bf16[512,1024]{1,0:T(8,128)(2,1)} %copy-done.4, bf16[512,1024]{1,0:T(8,128)(2,1)} %copy-done.11, bf16[1,2048,3072]{2,1,0:T(8,128)(2,1)} %get-tuple-element.36.weight), custom_call_target="tpu_custom_call" | custom-call | flops 6442450944 | bytes 17825792 | tf_op jit(solution)/shard_map/gate_up_0/pallas_call | solution.py:454
  72.8 1.4 collective-permute-start.10
  74.3 2.0 collective-permute-start.11
  76.3 12.2 %spread_gate_up_1.1 = (bf16[1,2048,3072]{2,1,0:T(8,128)(2,1)}, f32[8,128]{1,0:T(8,128)}) custom-call(s32[192]{0:T(256)} %get-tuple-element.72.gate_at, s32[192]{0:T(256)} %get-tuple-element.67.up_at, bf16[1,216,128,128]{3,2,1,0:T(8,128)(2,1)} %refs_0_.3, bf16[1,216,128,128]{3,2,1,0:T(8,128)(2,1)} %refs_1_.3, f32[8,128]{1,0:T(8,128)} %get-tuple-element.37.refs_2_), custom_call_target="tpu_custom_call" | custom-call | bytes 26738688 | tf_op jit(solution)/shard_map/spread_gate_up_1/pallas_call | solution.py:274
  88.5 4.1 %collective-permute-done.10.came_a.refs_1_ = bf16[2,256,768]{2,1,0:T(8,128)(2,1)S(1)} collective-permute-done((bf16[2,256,768]{2,1,0:T(8,128)(2,1)}, bf16[2,256,768]{2,1,0:T(8,128)(2,1)S(1)}, u32[]{:S(2)}, u32[]{:S(2)}) %collective-permute-start.10) | collective-permute-done | bytes 786464 | tf_op jit(solution)/shard_map/ppermute | solution.py:560
  92.6 1.4 collective-permute-done.11.came_b.refs_4_
  95.5 1.7 collective-permute-start.14
  97.8 12.0 %gate_up_1.1 = (bf16[2,256,768]{2,1,0:T(8,128)(2,1)}, bf16[2,256,768]{2,1,0:T(8,128)(2,1)}, bf16[2,256,768]{2,1,0:T(8,128)(2,1)}, bf16[2,256,768]{2,1,0:T(8,128)(2,1)}, f32[8,128]{1,0:T(8,128)}) custom-call(bf16[512,1024]{1,0:T(8,128)(2,1)} %copy-done.4, bf16[512,1024]{1,0:T(8,128)(2,1)} %copy-done.11, bf16[1,2048,3072]{2,1,0:T(8,128)(2,1)} %get-tuple-element.38.weight, ...), custom_call_target="tpu_custom_call" | custom-call | flops 6442450944 | bytes 17825792 | tf_op jit(solution)/shard_map/gate_up_1/pallas_call | solution.py:454
  112.0 1.5 collective-permute-start.12
  114.2 16.6 %spread_down.1 = (bf16[2,3072,1024]{2,1,0:T(8,128)(2,1)}, f32[8,128]{1,0:T(8,128)S(1)}) custom-call(s32[384]{0:T(512)S(1)} %reshape.114.at_ref, bf16[8,108,128,128]{3,2,1,0:T(8,128)(2,1)} %values_ref.1, f32[8,128]{1,0:T(8,128)S(1)} %get-tuple-element.52.refs_0_), custom_call_target="tpu_custom_call" | custom-call | bytes 40894464 | tf_op jit(solution)/shard_map/spread_down/pallas_call | solution.py:305
  131.6 1.3 collective-permute-start.16
  133.4 6.9 %collective-permute-done.16.refs_2_ = bf16[256,768]{1,0:T(8,128)(2,1)S(1)} collective-permute-done((bf16[256,768]{1,0:T(8,128)(2,1)S(1)}, bf16[256,768]{1,0:T(8,128)(2,1)S(1)}, u32[]{:S(2)}, u32[]{:S(2)}) %collective-permute-start.16) | collective-permute-done | bytes 393248 | tf_op jit(solution)/shard_map/ppermute | solution.py:560
  142.7 7.8 %all-gather.5.cloned.1.call-done.hidden = bf16[8,4,128,384]{3,2,1,0:T(8,128)(2,1)} async-done(((bf16[1,4,128,384]{3,2,1,0:T(8,128)(2,1)}), bf16[8,4,128,384]{3,2,1,0:T(8,128)(2,1)}) %all-gather.5.cloned.1.call-update) | async-done | bytes 3145744 | tf_op jit(solution)/shard_map/all_gather | solution.py:629
  150.5 8.0 %down_0.1 = (f32[512,1024]{1,0:T(8,128)S(1)}, f32[8,128]{1,0:T(8,128)}) custom-call(s32[2]{0:T(128)S(1)} %pad_add_fusion.place, bf16[8,4,128,384]{3,2,1,0:T(8,128)(2,1)} %all-gather.5.cloned.1.call-done.hidden, bf16[2,3072,1024]{2,1,0:T(8,128)(2,1)} %get-tuple-element.58.weight), custom_call_target="tpu_custom_call" | custom-call | flops 3221225472 | bytes 13631488 | tf_op jit(solution)/shard_map/down_0/pallas_call | solution.py:511
  158.5 30.8 %all-gather.3.cloned.1.call-done.hidden = bf16[8,4,128,384]{3,2,1,0:T(8,128)(2,1)} async-done(((bf16[1,4,128,384]{3,2,1,0:T(8,128)(2,1)}), bf16[8,4,128,384]{3,2,1,0:T(8,128)(2,1)}) %all-gather.3.cloned.1.call-update) | async-done | bytes 3145744 | tf_op jit(solution)/shard_map/all_gather | solution.py:629
  189.3 8.0 %down_1.1 = (bf16[128,1024]{1,0:T(8,128)(2,1)S(1)}, bf16[128,1024]{1,0:T(8,128)(2,1)S(1)}, bf16[128,1024]{1,0:T(8,128)(2,1)S(1)}, bf16[128,1024]{1,0:T(8,128)(2,1)S(1)}, f32[8,128]{1,0:T(8,128)}) custom-call(s32[2]{0:T(128)S(1)} %pad_add_fusion.place, bf16[8,4,128,384]{3,2,1,0:T(8,128)(2,1)} %all-gather.3.cloned.1.call-done.hidden, ...), custom_call_target="tpu_custom_call" | custom-call | flops 3221225472 | bytes 13631488 | tf_op jit(solution)/shard_map/down_1/pallas_call | solution.py:511
  197.3 1.5 collective-permute-start.18
  198.8 1.5 collective-permute-start.19
  200.8 5.6 %collective-permute-done.18 = bf16[128,1024]{1,0:T(8,128)(2,1)S(1)} collective-permute-done((bf16[128,1024]{1,0:T(8,128)(2,1)S(1)}, bf16[128,1024]{1,0:T(8,128)(2,1)S(1)}, u32[]{:S(2)}, u32[]{:S(2)}) %collective-permute-start.18) | collective-permute-done | bytes 262176 | tf_op jit(solution)/shard_map/ppermute | solution.py:560
  206.4 6.1 %collective-permute-done.19 = bf16[128,1024]{1,0:T(8,128)(2,1)S(1)} collective-permute-done((bf16[128,1024]{1,0:T(8,128)(2,1)S(1)}, bf16[128,1024]{1,0:T(8,128)(2,1)S(1)}, u32[]{:S(2)}, u32[]{:S(2)}) %collective-permute-start.19) | collective-permute-done | bytes 262176 | tf_op jit(solution)/shard_map/ppermute | solution.py:560
  (85 shorter events, 20.0 us)
Async XLA Ops:
  6.5 143.9 %all-gather.5.cloned.1.call-start = ((), (), s32[]{:S(2)}) async-start(), calls=%async_computation.1 | async-start | bytes 3538944 | tf_op jit(solution)/shard_map/all_gather | solution.py:629
  6.5 50.3 %collective-permute-start = (bf16[128,1024]{1,0:T(8,128)(2,1)}, bf16[128,1024]{1,0:T(8,128)(2,1)S(1)}, u32[]{:S(2)}, u32[]{:S(2)}) collective-permute-start(bf16[128,1024]{1,0:T(8,128)(2,1)} %tokens.1), channel_id=1, source_target_pairs={{0,0},{1,1},{2,8},{3,9},{4,16},{5,17},{6,24},{7,25},{8,2},{9,3},{1... | collective-permute-start | bytes 786440 | tf_op jit(solution)/shard_map/ppermute | solution.py:574
  8.1 48.7 %collective-permute-start.1 = (bf16[128,1024]{1,0:T(8,128)(2,1)}, bf16[128,1024]{1,0:T(8,128)(2,1)S(1)}, u32[]{:S(2)}, u32[]{:S(2)}) collective-permute-start(bf16[128,1024]{1,0:T(8,128)(2,1)} %tokens.1), channel_id=1, source_target_pairs={{0,2},{1,3},{2,10},{3,11},{4,18},{5,19},{6,26},{7,27},{8,0},{9,1},... | collective-permute-start | bytes 786440 | tf_op jit(solution)/shard_map/ppermute | solution.py:574
  12.9 43.9 %collective-permute-start.2 = (bf16[128,1024]{1,0:T(8,128)(2,1)}, bf16[128,1024]{1,0:T(8,128)(2,1)S(1)}, u32[]{:S(2)}, u32[]{:S(2)}) collective-permute-start(bf16[128,1024]{1,0:T(8,128)(2,1)} %tokens.1), channel_id=1, source_target_pairs={{0,4},{1,5},{2,12},{3,13},{4,20},{5,21},{6,28},{7,29},{8,6},{9,7},... | collective-permute-start | bytes 786440 | tf_op jit(solution)/shard_map/ppermute | solution.py:574
  16.4 1.0 copy-start.5
  17.5 16.2 %collective-permute-start.4 = (f32[1,128]{1,0:T(1,128)S(1)}, f32[1,128]{1,0:T(1,128)S(1)}, u32[]{:S(2)}, u32[]{:S(2)}) collective-permute-start(f32[1,128]{1,0:T(1,128)S(1)} %sum_squares.1), channel_id=1, source_target_pairs={{0,1},{1,0},{2,3},{3,2},{4,5},{5,4},{6,7},{7,6},{8,9},{9,8},{10,11... | collective-permute-start | bytes 1544 | tf_op jit(solution)/shard_map/ppermute | solution.py:566
  20.3 15.6 %copy-start.6 = (bf16[128,1024]{1,0:T(8,128)(2,1)S(1)}, bf16[128,1024]{1,0:T(8,128)(2,1)}, u32[]{:S(2)}) copy-start(bf16[128,1024]{1,0:T(8,128)(2,1)} %tokens.1) | copy-start | bytes 786436
  34.4 3.6 %collective-permute-start.5 = (f32[1,128]{1,0:T(1,128)S(1)}, f32[1,128]{1,0:T(1,128)S(1)}, u32[]{:S(2)}, u32[]{:S(2)}) collective-permute-start(f32[1,128]{1,0:T(1,128)S(1)} %add_add_fusion), channel_id=1, source_target_pairs={{0,2},{1,3},{2,0},{3,1},{4,6},{5,7},{6,4},{7,5},{8,10},{9,11},{10,... | collective-permute-start | bytes 1544 | tf_op jit(solution)/shard_map/ppermute | solution.py:563
  35.9 21.0 %collective-permute-start.3 = (bf16[128,1024]{1,0:T(8,128)(2,1)S(1)}, bf16[128,1024]{1,0:T(8,128)(2,1)S(1)}, u32[]{:S(2)}, u32[]{:S(2)}) collective-permute-start(bf16[128,1024]{1,0:T(8,128)(2,1)S(1)} %copy-done.6), channel_id=1, source_target_pairs={{0,6},{1,7},{2,14},{3,15},{4,22},{5,23},{6,30},{7,31},{8,4},{9,5},... | collective-permute-start | bytes 786440 | tf_op jit(solution)/shard_map/ppermute | solution.py:574
  38.0 4.8 %collective-permute-start.6 = (f32[1,128]{1,0:T(1,128)S(1)}, f32[1,128]{1,0:T(1,128)S(1)}, u32[]{:S(2)}, u32[]{:S(2)}) collective-permute-start(f32[1,128]{1,0:T(1,128)S(1)} %add.120), channel_id=1, source_target_pairs={{0,4},{1,5},{2,6},{3,7},{4,0},{5,1},{6,2},{7,3},{8,12},{9,13},{10,... | collective-permute-start | bytes 1544 | tf_op jit(solution)/shard_map/ppermute | solution.py:563
  42.8 4.5 %collective-permute-start.7 = (f32[1,128]{1,0:T(1,128)S(1)}, f32[1,128]{1,0:T(1,128)S(1)}, u32[]{:S(2)}, u32[]{:S(2)}) collective-permute-start(f32[1,128]{1,0:T(1,128)S(1)} %add.121), channel_id=1, source_target_pairs={{0,8},{8,0},{16,24},{24,16},{1,9},{9,1},{17,25},{25,17},{2,10},{10... | collective-permute-start | bytes 1544 | tf_op jit(solution)/shard_map/ppermute | solution.py:560
  47.3 8.7 %collective-permute-start.8 = (f32[2,128]{1,0:T(2,128)S(1)}, f32[2,128]{1,0:T(2,128)S(1)}, u32[]{:S(2)}, u32[]{:S(2)}) collective-permute-start(f32[2,128]{1,0:T(2,128)S(1)} %pad_maximum_fusion), channel_id=1, source_target_pairs={{0,16},{8,24},{16,0},{24,8},{1,17},{9,25},{17,1},{25,9},{2,18},{10... | collective-permute-start | bytes 3080 | tf_op jit(solution)/shard_map/ppermute | solution.py:560
  57.1 2.7 %copy-start.4 = (bf16[512,1024]{1,0:T(8,128)(2,1)}, bf16[512,1024]{1,0:T(8,128)(2,1)S(1)}, u32[]{:S(2)}) copy-start(bf16[512,1024]{1,0:T(8,128)(2,1)S(1)} %pack.1.own) | copy-start | bytes 3145732
  57.2 2.7 %collective-permute-start.9 = (bf16[512,1024]{1,0:T(8,128)(2,1)S(1)}, bf16[512,1024]{1,0:T(8,128)(2,1)S(1)}, u32[]{:S(2)}, u32[]{:S(2)}) collective-permute-start(bf16[512,1024]{1,0:T(8,128)(2,1)S(1)} %pack.1.own), channel_id=1, source_target_pairs={{0,1},{1,0},{2,3},{3,2},{4,5},{5,4},{6,7},{7,6},{8,9},{9,8},{10,11... | collective-permute-start | bytes 3145736 | tf_op jit(solution)/shard_map/ppermute | solution.py:566
  59.9 1.0 copy-start.11
  72.8 19.8 %collective-permute-start.10 = (bf16[2,256,768]{2,1,0:T(8,128)(2,1)}, bf16[2,256,768]{2,1,0:T(8,128)(2,1)S(1)}, u32[]{:S(2)}, u32[]{:S(2)}) collective-permute-start(bf16[2,256,768]{2,1,0:T(8,128)(2,1)} %get-tuple-element.40), channel_id=1, source_target_pairs={{0,8},{8,0},{16,24},{24,16},{1,9},{9,1},{17,25},{25,17},{2,10},{10... | collective-permute-start | bytes 2359304 | tf_op jit(solution)/shard_map/ppermute | solution.py:560
  74.3 19.8 %collective-permute-start.11 = (bf16[2,256,768]{2,1,0:T(8,128)(2,1)}, bf16[2,256,768]{2,1,0:T(8,128)(2,1)S(1)}, u32[]{:S(2)}, u32[]{:S(2)}) collective-permute-start(bf16[2,256,768]{2,1,0:T(8,128)(2,1)} %get-tuple-element.42), channel_id=1, source_target_pairs={{0,16},{8,24},{16,0},{24,8},{1,17},{9,25},{17,1},{25,9},{2,18},{10... | collective-permute-start | bytes 2359304 | tf_op jit(solution)/shard_map/ppermute | solution.py:560
  76.3 17.8 %copy-start.2 = (bf16[2,256,768]{2,1,0:T(8,128)(2,1)S(1)}, bf16[2,256,768]{2,1,0:T(8,128)(2,1)}, u32[]{:S(2)}) copy-start(bf16[2,256,768]{2,1,0:T(8,128)(2,1)} %get-tuple-element.39.kept_a.refs_0_) | copy-start | bytes 2359300
  76.3 17.8 %copy-start.3 = (bf16[2,256,768]{2,1,0:T(8,128)(2,1)S(1)}, bf16[2,256,768]{2,1,0:T(8,128)(2,1)}, u32[]{:S(2)}) copy-start(bf16[2,256,768]{2,1,0:T(8,128)(2,1)} %get-tuple-element.41.kept_b.refs_3_) | copy-start | bytes 2359300
  95.5 14.4 %collective-permute-start.14 = (bf16[256,768]{1,0:T(8,128)(2,1)S(1)}, bf16[256,768]{1,0:T(8,128)(2,1)S(1)}, u32[]{:S(2)}, u32[]{:S(2)}) collective-permute-start(bf16[256,768]{1,0:T(8,128)(2,1)S(1)} %get-tuple-element.49), channel_id=1, source_target_pairs={{0,16},{8,24},{16,0},{24,8},{1,17},{9,25},{17,1},{25,9},{2,18},{10... | collective-permute-start | bytes 1179656 | tf_op jit(solution)/shard_map/ppermute | solution.py:560
  97.2 12.6 %collective-permute-start.15 = (bf16[256,768]{1,0:T(8,128)(2,1)S(1)}, bf16[256,768]{1,0:T(8,128)(2,1)S(1)}, u32[]{:S(2)}, u32[]{:S(2)}) collective-permute-start(bf16[256,768]{1,0:T(8,128)(2,1)S(1)} %get-tuple-element.50), channel_id=1, source_target_pairs={{0,8},{8,0},{16,24},{24,16},{1,9},{9,1},{17,25},{25,17},{2,10},{10... | collective-permute-start | bytes 1179656 | tf_op jit(solution)/shard_map/ppermute | solution.py:560
  97.8 16.0 %copy-start.10 = (s32[8,108]{1,0:T(8,128)S(1)}, s32[8,108]{1,0:T(8,128)}, u32[]{:S(2)}) copy-start(s32[8,108]{1,0:T(8,128)} %param.15) | copy-start | bytes 10372
  111.8 77.5 %all-gather.3.cloned.1.call-start = ((), (), s32[]{:S(2)}) async-start(), calls=%async_computation | async-start | bytes 3538944 | tf_op jit(solution)/shard_map/all_gather | solution.py:629
  112.0 18.8 %collective-permute-start.12 = (bf16[2,256,768]{2,1,0:T(8,128)(2,1)}, bf16[2,256,768]{2,1,0:T(8,128)(2,1)S(1)}, u32[]{:S(2)}, u32[]{:S(2)}) collective-permute-start(bf16[2,256,768]{2,1,0:T(8,128)(2,1)} %get-tuple-element.46), channel_id=1, source_target_pairs={{0,8},{8,0},{16,24},{24,16},{1,9},{9,1},{17,25},{25,17},{2,10},{10... | collective-permute-start | bytes 2359304 | tf_op jit(solution)/shard_map/ppermute | solution.py:560
  113.6 17.8 %collective-permute-start.13 = (bf16[2,256,768]{2,1,0:T(8,128)(2,1)}, bf16[2,256,768]{2,1,0:T(8,128)(2,1)S(1)}, u32[]{:S(2)}, u32[]{:S(2)}) collective-permute-start(bf16[2,256,768]{2,1,0:T(8,128)(2,1)} %get-tuple-element.48), channel_id=1, source_target_pairs={{0,16},{8,24},{16,0},{24,8},{1,17},{9,25},{17,1},{25,9},{2,18},{10... | collective-permute-start | bytes 2359304 | tf_op jit(solution)/shard_map/ppermute | solution.py:560
  114.2 17.2 %copy-start = (bf16[2,256,768]{2,1,0:T(8,128)(2,1)S(1)}, bf16[2,256,768]{2,1,0:T(8,128)(2,1)}, u32[]{:S(2)}) copy-start(bf16[2,256,768]{2,1,0:T(8,128)(2,1)} %get-tuple-element.45.kept_a.refs_0_) | copy-start | bytes 2359300
  114.2 17.2 %copy-start.1 = (bf16[2,256,768]{2,1,0:T(8,128)(2,1)S(1)}, bf16[2,256,768]{2,1,0:T(8,128)(2,1)}, u32[]{:S(2)}) copy-start(bf16[2,256,768]{2,1,0:T(8,128)(2,1)} %get-tuple-element.47.kept_b.refs_3_) | copy-start | bytes 2359300
  131.6 8.7 %collective-permute-start.16 = (bf16[256,768]{1,0:T(8,128)(2,1)S(1)}, bf16[256,768]{1,0:T(8,128)(2,1)S(1)}, u32[]{:S(2)}, u32[]{:S(2)}) collective-permute-start(bf16[256,768]{1,0:T(8,128)(2,1)S(1)} %get-tuple-element.54), channel_id=1, source_target_pairs={{0,16},{8,24},{16,0},{24,8},{1,17},{9,25},{17,1},{25,9},{2,18},{10... | collective-permute-start | bytes 1179656 | tf_op jit(solution)/shard_map/ppermute | solution.py:560
  132.8 8.5 %collective-permute-start.17 = (bf16[256,768]{1,0:T(8,128)(2,1)S(1)}, bf16[256,768]{1,0:T(8,128)(2,1)S(1)}, u32[]{:S(2)}, u32[]{:S(2)}) collective-permute-start(bf16[256,768]{1,0:T(8,128)(2,1)S(1)} %get-tuple-element.55), channel_id=1, source_target_pairs={{0,8},{8,0},{16,24},{24,16},{1,9},{9,1},{17,25},{25,17},{2,10},{10... | collective-permute-start | bytes 1179656 | tf_op jit(solution)/shard_map/ppermute | solution.py:560
  197.3 9.1 %collective-permute-start.18 = (bf16[128,1024]{1,0:T(8,128)(2,1)S(1)}, bf16[128,1024]{1,0:T(8,128)(2,1)S(1)}, u32[]{:S(2)}, u32[]{:S(2)}) collective-permute-start(bf16[128,1024]{1,0:T(8,128)(2,1)S(1)} %get-tuple-element.62), channel_id=1, source_target_pairs={{0,8},{8,0},{16,24},{24,16},{1,9},{9,1},{17,25},{25,17},{2,10},{10... | collective-permute-start | bytes 786440 | tf_op jit(solution)/shard_map/ppermute | solution.py:560
  198.8 13.8 %collective-permute-start.19 = (bf16[128,1024]{1,0:T(8,128)(2,1)S(1)}, bf16[128,1024]{1,0:T(8,128)(2,1)S(1)}, u32[]{:S(2)}, u32[]{:S(2)}) collective-permute-start(bf16[128,1024]{1,0:T(8,128)(2,1)S(1)} %get-tuple-element.63), channel_id=1, source_target_pairs={{0,16},{8,24},{16,0},{24,8},{1,17},{9,25},{17,1},{25,9},{2,18},{10... | collective-permute-start | bytes 786440 | tf_op jit(solution)/shard_map/ppermute | solution.py:560
  200.2 12.3 %collective-permute-start.20 = (bf16[128,1024]{1,0:T(8,128)(2,1)S(1)}, bf16[128,1024]{1,0:T(8,128)(2,1)S(1)}, u32[]{:S(2)}, u32[]{:S(2)}) collective-permute-start(bf16[128,1024]{1,0:T(8,128)(2,1)S(1)} %get-tuple-element.64), channel_id=1, source_target_pairs={{0,24},{8,16},{16,8},{24,0},{1,25},{9,17},{17,9},{25,1},{2,26},{10... | collective-permute-start | bytes 786440 | tf_op jit(solution)/shard_map/ppermute | solution.py:560
  (3 other events, 1.9 us)
Sparse Core Ops, SparseCore 0:
  111.9 38.4 all-gather.4
  152.1 37.1 all-gather.2

commit v6 on v5

--- a/solution.py
+++ b/solution.py
@@ -341,29 +341,51 @@
 
 
 def pack_kernel(*refs, parts):
-    pieces, scale, gain, out = refs[:parts], refs[parts], refs[parts + 1], refs[-1]
-    count = pieces[0].shape[0]
+    count = refs[0].shape[0]
     for part in range(parts):
-        rows = slice(part * count, (part + 1) * count)
-        piece = pieces[part][...].astype(jnp.float32)
-        out[rows] = (piece * scale[rows] * gain[...]).astype(out.dtype)
-
-
-def pack(pieces, scale, gain, after):
+        refs[-1][part * count:(part + 1) * count] = refs[part][...]
+
+
+def pack(pieces, after):
     parts = len(pieces)
     count, width = pieces[0].shape
     return pl.pallas_call(
         functools.partial(pack_kernel, parts=parts),
         out_shape=jax.ShapeDtypeStruct((parts * count, width), pieces[0].dtype),
-        in_specs=[pl.BlockSpec(memory_space=pltpu.VMEM)] * (parts + 2)
-        + [pl.BlockSpec(memory_space=pl.ANY)] * len(after),
+        in_specs=[pl.BlockSpec(memory_space=pltpu.VMEM)] * parts + [ANY_SPEC] * len(after),
         out_specs=pl.BlockSpec(memory_space=pltpu.VMEM),
         compiler_params=pltpu.CompilerParams(vmem_limit_bytes=16 * MIB),
         cost_estimate=pl.CostEstimate(
             flops=0, bytes_accessed=4 * parts * count * width, transcendentals=0
         ),
         name="pack",
-    )(*pieces, scale, gain, *after)
+    )(*pieces, *after)
+
+
+def pair_kernel(*refs, steps):
+    out = refs[-1]
+    count = out.shape[1] // 4
+    for i, step in enumerate(steps):
+        for part in range(4):
+            there = slice((part ^ step) * count, ((part ^ step) + 1) * count)
+            rows = refs[i][there]
+            if i == 1 and steps == (2, 3):
+                rows += refs[2][there]
+            out[i, part * count:(part + 1) * count] = rows
+
+
+def pair(pieces, steps, after):
+    return pl.pallas_call(
+        functools.partial(pair_kernel, steps=steps),
+        out_shape=jax.ShapeDtypeStruct((2,) + pieces[0].shape, pieces[0].dtype),
+        in_specs=[pl.BlockSpec(memory_space=pltpu.VMEM)] * len(pieces) + [ANY_SPEC],
+        out_specs=pl.BlockSpec(memory_space=pltpu.VMEM),
+        compiler_params=pltpu.CompilerParams(vmem_limit_bytes=16 * MIB),
+        cost_estimate=pl.CostEstimate(
+            flops=0, bytes_accessed=4 * len(pieces) * pieces[0].size, transcendentals=0
+        ),
+        name="pair",
+    )(*pieces, after)
 
 
 def halfway_kernel(kept_a, came_a, kept_b, came_b, *refs):
@@ -439,11 +461,11 @@
 
         @pl.when(part % 2 == flip)
         def _():
-            (sent_a if flip else kept_a)[part // 2] = product[:count]
+            (sent_a if flip else kept_a)[0] = product[:count]
 
         @pl.when(part // 2 == flip)
         def _():
-            (sent_b if flip else kept_b)[part % 2] = product[count:]
+            (sent_b if flip else kept_b)[0] = product[count:]
 
 
 def panel_product(own, other, dense, after, chunk):
@@ -458,7 +480,13 @@
         in_specs=[pl.BlockSpec((count, half), lambda n: (0, 0))] * 2
         + [pl.BlockSpec((1, depth, tile), lambda n: (0, 0, n))]
         + [ANY_SPEC] * len(after),
-        out_specs=[pl.BlockSpec(out.shape, lambda n: (0, 0, 0))] * 4 + [MARK_SPEC],
+        out_specs=[
+            pl.BlockSpec((1,) + out.shape[1:], lambda n: (n // 2, 0, 0)),
+            pl.BlockSpec((1,) + out.shape[1:], lambda n: (n // 2, 0, 0)),
+            pl.BlockSpec((1,) + out.shape[1:], lambda n: (jnp.minimum(n, 1), 0, 0)),
+            pl.BlockSpec((1,) + out.shape[1:], lambda n: (jnp.maximum(n - 2, 0), 0, 0)),
+            MARK_SPEC,
+        ],
         compiler_params=pltpu.CompilerParams(vmem_limit_bytes=54 * MIB),
         cost_estimate=pl.CostEstimate(
             flops=2 * count * depth * width,
@@ -522,7 +550,7 @@
             out_specs=out_tiles + [MARK_SPEC],
             scratch_shapes=[pltpu.VMEM((parts * count, total), hidden.dtype)],
         ),
-        compiler_params=pltpu.CompilerParams(vmem_limit_bytes=50 * MIB),
+        compiler_params=pltpu.CompilerParams(vmem_limit_bytes=42 * MIB),
         cost_estimate=pl.CostEstimate(
             flops=2 * parts * count * total * width,
             bytes_accessed=2 * total * (width + parts * count) + 8 * parts * count * width,
@@ -530,6 +558,60 @@
         ),
         name=f"down_{chunk}",
     )(place, hidden, dense, *added)
+
+
+def down_pair_kernel(place, own, other, *refs):
+    weights, before, outs, mark = refs[:4], refs[4], refs[5:-1], refs[-1]
+    leave(mark)
+    count = before.shape[0] // len(outs)
+    for step, out in enumerate(outs):
+        at = 0 if len(outs) == 1 else (place[1] ^ step) * count
+        rows = pl.ds(pl.multiple_of(at, count), count)
+        total = before[rows]
+        for i in range(2):
+            for j, side in enumerate((own, other)):
+                total += jnp.dot(
+                    side[i, rows], weights[2 * i + j][0, 0], preferred_element_type=jnp.float32
+                )
+        out[...] = total.astype(out.dtype)
+
+
+def down_pair(place, own, other, steps, dense, before, chunk, last):
+    _, count, depth = own.shape
+    width = dense.shape[-1]
+    dense = dense.reshape(dense.shape[0], -1, depth, width)
+    tile = width // 2
+    tiles = pl.BlockSpec((count, tile), lambda n, *_: (0, n))
+    whole = pl.BlockSpec(own.shape, lambda n, *_: (0, 0, 0))
+    weights = []
+    for step in steps:
+        for flip in range(2):
+
+            def at(n, place, step=step, flip=flip):
+                return chunk, 2 * (place[0] ^ step) + (place[2] ^ flip), 0, n
+
+            weights.append(pl.BlockSpec((1, 1, depth, tile), at))
+    out, out_tiles = [jax.ShapeDtypeStruct((count, width), jnp.float32)], [tiles]
+    if last:
+        out = [jax.ShapeDtypeStruct((count // 4, width), own.dtype)] * 4
+        out_tiles = [pl.BlockSpec((count // 4, tile), lambda n, *_: (0, n))] * 4
+    return pl.pallas_call(
+        down_pair_kernel,
+        out_shape=out + [MARK],
+        grid_spec=pltpu.PrefetchScalarGridSpec(
+            num_scalar_prefetch=1,
+            grid=(width // tile,),
+            in_specs=[whole, whole] + weights + [tiles],
+            out_specs=out_tiles + [MARK_SPEC],
+        ),
+        compiler_params=pltpu.CompilerParams(vmem_limit_bytes=42 * MIB),
+        cost_estimate=pl.CostEstimate(
+            flops=8 * count * depth * width,
+            bytes_accessed=8 * depth * (width + count) + 8 * count * width,
+            transcendentals=0,
+        ),
+        name=f"down_{chunk}_{steps[0]}",
+    )(place, own, other, *[dense] * 4, before)
 
 
 def by_columns(
@@ -549,7 +631,7 @@
     cols_per = HIDDEN_UNITS // edge // col_size
     width_blocks = MODEL_WIDTH // edge // col_size
     share = cols_per // tok_size
-    chunks = 2 if share % 2 == 0 else 1
+    chunks = 2
     cols = share // chunks
     count, half = tokens.shape
     tok, col = lax.axis_index("tok"), lax.axis_index("col")
@@ -573,7 +655,14 @@
                 pairs.append((i * col_size + j, user))
         return lax.ppermute(array, ("tok", "col"), pairs)
 
-    pieces = [to_users(tokens, part) for part in parts]
+    squares = sum_squares(tokens)
+    squares += swap_core(squares)
+    squares += functools.reduce(jnp.add, [swap_chip(squares, step) for step in parts[1:]])
+    scale = lax.rsqrt(squares.reshape(-1, 1) / MODEL_WIDTH + EPSILON)
+    gain = lax.dynamic_slice_in_dim(norm_gain, col * half, half, 0)
+    normed = (tokens.astype(jnp.float32) * scale * gain).astype(jnp.bfloat16)
+    pieces = [to_users(normed, part) for part in parts]
+
     k, r, p, q = jnp.meshgrid(
         jnp.arange(chunks), jnp.arange(rows_per), jnp.arange(tok_size), jnp.arange(cols),
         indexing="ij",
@@ -592,23 +681,13 @@
             rows_per, tok_size, cols, after, chunk,
         )
 
-    squares = sum_squares(tokens)
-    squares += swap_core(squares)
     dense, mark = spread(0, [])
-    squares += mark[:1, :1]
-    squares += swap_chip(squares, 1)
-    squares += swap_chip(squares, 2)
-    squares = jnp.concatenate([squares, swap_tok(squares, 1)])
-    squares = jnp.concatenate([squares, swap_tok(squares, 2)])
-
-    gain = lax.dynamic_slice_in_dim(norm_gain, (tok * 2 + side) * half, half, 0)[None]
-    scale = lax.rsqrt(squares / MODEL_WIDTH + EPSILON)
-    scale = jnp.take(scale, jnp.arange(tok_size) ^ chip ^ tok, axis=0).reshape(-1, 1)
-    own = pack(pieces, scale, gain, [])
+    own = pack(pieces, [mark])
     other = swap_core(own)
 
-    place = jnp.stack([chip, chip ^ tok])
-    hiddens = []
+    place = jnp.stack([chip, chip ^ tok, side])
+    mixed = [None]
+    gathered = []
     *sums, mark = panel_product(own, other, dense, [], 0)
     if chunks > 1:
         dense, mark = spread(1, [mark])
@@ -626,12 +705,20 @@
             down_dense, mark = spread_panels(
                 down_at, down_values, chunks, cols, width_blocks, [mark]
             )
-        hiddens.append(lax.all_gather(hidden.reshape(tok_size, count, -1), "col"))
-
-    mixed = [None]
-    for chunk in range(chunks):
-        last = chunk == chunks - 1
-        *mixed, _ = down_product(place, hiddens[chunk], down_dense, mixed[0], chunk, last)
+        if chunk + 1 < chunks:
+            gathered.append(lax.all_gather(hidden.reshape(tok_size, count, -1), "col"))
+
+    far = swap_chip(hidden, 2)
+    near = swap_chip(hidden, 1)
+    inner = lax.ppermute(hidden, "col", [(i, i ^ 6) for i in range(2, 6)])
+    ends = lax.ppermute(far, "col", [(i, i ^ 2) for i in range(2, 6)])
+    for chunk in range(chunks - 1):
+        *mixed, mark = down_product(place, gathered[chunk], down_dense, mixed[0], chunk, False)
+    for steps, pieces in (((0, 1), [hidden, near]), ((2, 3), [far, inner, ends])):
+        held = pair(pieces, steps, mark)
+        *mixed, mark = down_pair(
+            place, held, swap_core(held), steps, down_dense, mixed[0], chunks - 1, steps[0] == 2
+        )
 
     total = mixed[0].astype(jnp.float32)
     for step in parts[1:]:
@@ -643,7 +730,7 @@
     tok_size = lax.axis_size("tok")
     col_size = lax.axis_size("col")
     blocks = HIDDEN_UNITS // arrays[2].shape[-1]
-    even = blocks % (col_size * tok_size) == 0 and col_size == 2 * tok_size == 8
+    even = blocks % (2 * col_size * tok_size) == 0 and col_size == 2 * tok_size == 8
     return (by_columns if even else by_tokens)(*arrays)
 
 

time: 221 us -> 218 us (0.986)
  waiting for transfers between devices: 74.3 us -> 59.6 us
  starting transfers between devices: 36.9 us -> 45.2 us
    all_gather x2 -> x1, waiting for transfers between devices: 38.6 us -> 1.42 us  [by_columns(): gathered.append(lax.all_gather(hidden.reshape(tok_size, count, -1), 'col'))]
    ppermute x2 -> x5, waiting for transfers between devices: 4.7 us -> 20.9 us  [swap_chip(): lax.ppermute(array, 'col', [(i, i ^ 2 * step) for i in range(col_size)])]
    pallas_call x0 -> x4, Pallas kernels: none -> 11 us  [the longest x2 9.82 us: down_pair(): pl.pallas_call(down_pair_kernel, out_shape=out + [MARK], grid_spec=pltpu....]
    pallas_call x2 -> x1, Pallas kernels: 16 us -> 6.45 us  [down_product(): pl.pallas_call(functools.partial(down_product_kernel, added=len(added)),...]
    ppermute x2 -> x5, starting transfers between devices: 3.08 us -> 10.1 us  [swap_chip(): lax.ppermute(array, 'col', [(i, i ^ 2 * step) for i in range(col_size)])]
    ppermute x0 -> x2, waiting for transfers between devices: none -> 6.28 us  [the longest x1 6.28 us: by_columns(): ends = lax.ppermute(far, 'col', [(i, i ^ 2) for i in range(2, 6)])]
    unnamed x24 -> x26, local copies, waits for them, and re-layouts: 3.88 us -> 6.44 us
    ppermute x2 -> x4, waiting for transfers between devices: 2.65 us -> 4.92 us  [swap_core(): return lax.ppermute(array, 'col', [(i, i ^ 1) for i in range(col_size)])]
  transfers between devices with their start and end apart: 23 -> 27, of which waited for: 14 -> 16; matrix products, arithmetic and copies ran while one was open for 3% -> 2% of each run, Pallas kernels for 28% -> 31%
where the time goes in v6:
time: 218 us; the launch traced here: 217 us
  Pallas kernels  86.3 us (40%)
  waiting for transfers between devices  59.6 us (27%)
  starting transfers between devices  45.2 us (21%)
  between operations  13.7 us (6%)
  local copies, waits for them, and re-layouts  8.98 us (4%)
  other arithmetic  3.21 us (1%)
    ppermute x11, waiting for transfers between devices, swap_tok(): return lax.ppermute(array, 'tok', [(i, i ^ step) for i in parts])  26 us
    pallas_call x2, Pallas kernels, spread_shares(): pl.pallas_call(functools.partial(spread_shares_kernel, rows=rows // steps...  24.3 us
    ppermute x11, starting transfers between devices, swap_tok(): return lax.ppermute(array, 'tok', [(i, i ^ step) for i in parts])  23.8 us
    pallas_call x2, Pallas kernels, panel_product(): pl.pallas_call(panel_product_kernel, out_shape=[out] * 4 + [MARK], grid=(...  23.2 us
    ppermute x5, waiting for transfers between devices, swap_chip(): lax.ppermute(array, 'col', [(i, i ^ 2 * step) for i in range(col_size)])  20.9 us
    pallas_call x1, Pallas kernels, spread_panels(): pl.pallas_call(functools.partial(spread_panels_kernel, chunks=chunks, row...  16.6 us
    ppermute x5, starting transfers between devices, swap_chip(): lax.ppermute(array, 'col', [(i, i ^ 2 * step) for i in range(col_size)])  10.1 us
    pallas_call x2, Pallas kernels, down_pair(): pl.pallas_call(down_pair_kernel, out_shape=out + [MARK], grid_spec=pltpu....  9.82 us
  transfers between devices with their start and end apart: 27, of which 16 were waited for; matrix products, arithmetic and copies ran while one was open for 2% of the time, Pallas kernels for 31%

profile of v6, /device:TPU:0, one launch (start us, length us, event | category | flops | bytes accessed | tf_op | source)
XLA Modules:
  0.0 217.0 jit_solution(5000891132094989147)
XLA Ops:
  9.3 4.7 %collective-permute-start.3 = (f32[1,128]{1,0:T(1,128)S(1)}, f32[1,128]{1,0:T(1,128)S(1)}, u32[]{:S(2)}, u32[]{:S(2)}) collective-permute-start(f32[1,128]{1,0:T(1,128)S(1)} %add.90), channel_id=1, source_target_pairs={{0,6},{1,7},{2,4},{3,5},{4,2},{5,3},{6,0},{7,1},{8,14},{9,15},{10,... | collective-permute-start | bytes 1544 | tf_op jit(solution)/shard_map/ppermute | solution.py:645
  15.6 2.0 collective-permute-done.1
  20.3 4.2 %collective-permute-start.5 = (bf16[128,1024]{1,0:T(8,128)(2,1)S(1)}, bf16[128,1024]{1,0:T(8,128)(2,1)S(1)}, u32[]{:S(2)}, u32[]{:S(2)}) collective-permute-start(bf16[128,1024]{1,0:T(8,128)(2,1)S(1)} %multiply_convert_fusion), channel_id=1, source_target_pairs={{0,2},{1,3},{2,10},{3,11},{4,18},{5,19},{6,26},{7,27},{8,0},{9,1},... | collective-permute-start | bytes 786440 | tf_op jit(solution)/shard_map/ppermute | solution.py:656
  24.5 1.7 collective-permute-start.6
  26.2 1.6 collective-permute-start.7
  29.4 12.1 %spread_gate_up_0.1 = (bf16[1,2048,3072]{2,1,0:T(8,128)(2,1)}, f32[8,128]{1,0:T(8,128)}) custom-call(s32[192]{0:T(256)} %get-tuple-element.77.gate_at, s32[192]{0:T(256)} %get-tuple-element.74.up_at, bf16[1,216,128,128]{3,2,1,0:T(8,128)(2,1)} %refs_0_.3, bf16[1,216,128,128]{3,2,1,0:T(8,128)(2,1)} %refs_1_.3), custom_call_target="tpu_custom_call" | custom-call | bytes 26738688 | tf_op jit(solution)/shard_map/spread_gate_up_0/pallas_call | solution.py:274
  42.3 2.6 %collective-permute-done.8.other = bf16[512,1024]{1,0:T(8,128)(2,1)S(1)} collective-permute-done((bf16[512,1024]{1,0:T(8,128)(2,1)S(1)}, bf16[512,1024]{1,0:T(8,128)(2,1)S(1)}, u32[]{:S(2)}, u32[]{:S(2)}) %collective-permute-start.8) | collective-permute-done | bytes 1048608 | tf_op jit(solution)/shard_map/ppermute | solution.py:648
  45.9 11.6 %gate_up_0.1 = (bf16[2,256,768]{2,1,0:T(8,128)(2,1)}, bf16[2,256,768]{2,1,0:T(8,128)(2,1)}, bf16[2,256,768]{2,1,0:T(8,128)(2,1)}, bf16[2,256,768]{2,1,0:T(8,128)(2,1)}, f32[8,128]{1,0:T(8,128)}) custom-call(bf16[512,1024]{1,0:T(8,128)(2,1)} %copy-done.6, bf16[512,1024]{1,0:T(8,128)(2,1)} %copy-done.12, bf16[1,2048,3072]{2,1,0:T(8,128)(2,1)} %get-tuple-element.39.weight), custom_call_target="tpu_custom_call" | custom-call | flops 6442450944 | bytes 17825792 | tf_op jit(solution)/shard_map/gate_up_0/pallas_call | solution.py:476
  57.5 1.5 collective-permute-start.9
  59.0 11.4 %collective-permute-start.10 = (bf16[2,256,768]{2,1,0:T(8,128)(2,1)}, bf16[2,256,768]{2,1,0:T(8,128)(2,1)S(1)}, u32[]{:S(2)}, u32[]{:S(2)}) collective-permute-start(bf16[2,256,768]{2,1,0:T(8,128)(2,1)} %get-tuple-element.45), channel_id=1, source_target_pairs={{0,16},{8,24},{16,0},{24,8},{1,17},{9,25},{17,1},{25,9},{2,18},{10... | collective-permute-start | bytes 2359304 | tf_op jit(solution)/shard_map/ppermute | solution.py:642
  70.4 12.2 %spread_gate_up_1.1 = (bf16[1,2048,3072]{2,1,0:T(8,128)(2,1)}, f32[8,128]{1,0:T(8,128)}) custom-call(s32[192]{0:T(256)} %get-tuple-element.78.gate_at, s32[192]{0:T(256)} %get-tuple-element.73.up_at, bf16[1,216,128,128]{3,2,1,0:T(8,128)(2,1)} %refs_0_.3, bf16[1,216,128,128]{3,2,1,0:T(8,128)(2,1)} %refs_1_.3, f32[8,128]{1,0:T(8,128)} %get-tuple-element.40.refs_2_), custom_call_target="tpu_custom_call" | custom-call | bytes 26738688 | tf_op jit(solution)/shard_map/spread_gate_up_1/pallas_call | solution.py:274
  82.6 5.8 %collective-permute-done.10.came_b.refs_4_ = bf16[2,256,768]{2,1,0:T(8,128)(2,1)S(1)} collective-permute-done((bf16[2,256,768]{2,1,0:T(8,128)(2,1)}, bf16[2,256,768]{2,1,0:T(8,128)(2,1)S(1)}, u32[]{:S(2)}, u32[]{:S(2)}) %collective-permute-start.10) | collective-permute-done | bytes 786464 | tf_op jit(solution)/shard_map/ppermute | solution.py:642
  89.9 1.7 collective-permute-start.13
  91.6 1.7 collective-permute-start.14
  93.3 11.6 %gate_up_1.1 = (bf16[2,256,768]{2,1,0:T(8,128)(2,1)}, bf16[2,256,768]{2,1,0:T(8,128)(2,1)}, bf16[2,256,768]{2,1,0:T(8,128)(2,1)}, bf16[2,256,768]{2,1,0:T(8,128)(2,1)}, f32[8,128]{1,0:T(8,128)}) custom-call(bf16[512,1024]{1,0:T(8,128)(2,1)} %copy-done.6, bf16[512,1024]{1,0:T(8,128)(2,1)} %copy-done.12, bf16[1,2048,3072]{2,1,0:T(8,128)(2,1)} %get-tuple-element.41.weight, ...), custom_call_target="tpu_custom_call" | custom-call | flops 6442450944 | bytes 17825792 | tf_op jit(solution)/shard_map/gate_up_1/pallas_call | solution.py:476
  107.9 16.6 %spread_down.1 = (bf16[2,3072,1024]{2,1,0:T(8,128)(2,1)}, f32[8,128]{1,0:T(8,128)S(1)}) custom-call(s32[384]{0:T(512)S(1)} %reshape.88.at_ref, bf16[8,108,128,128]{3,2,1,0:T(8,128)(2,1)} %values_ref.1, f32[8,128]{1,0:T(8,128)S(1)} %get-tuple-element.55.refs_0_), custom_call_target="tpu_custom_call" | custom-call | bytes 40894464 | tf_op jit(solution)/shard_map/spread_down/pallas_call | solution.py:305
  127.3 1.7 collective-permute-start.16
  129.0 6.3 %collective-permute-done.15.refs_2_ = bf16[256,768]{1,0:T(8,128)(2,1)S(1)} collective-permute-done((bf16[256,768]{1,0:T(8,128)(2,1)}, bf16[256,768]{1,0:T(8,128)(2,1)S(1)}, u32[]{:S(2)}, u32[]{:S(2)}) %collective-permute-start.15) | collective-permute-done | bytes 393248 | tf_op jit(solution)/shard_map/ppermute | solution.py:642
  136.7 2.2 %combine_1.1 = (bf16[512,384]{1,0:T(8,128)(2,1)}, f32[8,128]{1,0:T(8,128)}) custom-call(bf16[2,256,768]{2,1,0:T(8,128)(2,1)S(1)} %copy-done.1, bf16[2,256,768]{2,1,0:T(8,128)(2,1)S(1)} %collective-permute-done.11.came_a.refs_1_, bf16[256,768]{1,0:T(8,128)(2,1)S(1)} %collective-permute-done.15.refs_2_, bf16[2,256,768]{2,1,0:T(8,128)(2,1)S(1)} %copy-done.2, ...), custom_call_target="tpu_custom_call" | custom-call | flops 1572864 | bytes 2752512 | tf_op jit(solution)/shard_map/combine_1/pallas_call | solution.py:435
  139.0 1.4 all-gather.2.cloned.1.call-done.hidden
  140.4 1.9 copy-done
  142.3 6.4 %down_0.1 = (f32[512,1024]{1,0:T(8,128)S(1)}, f32[8,128]{1,0:T(8,128)S(1)}) custom-call(s32[3]{0:T(128)S(1)} %pad_add_fusion.place, bf16[8,4,128,384]{3,2,1,0:T(8,128)(2,1)S(1)} %copy-done, bf16[2,3072,1024]{2,1,0:T(8,128)(2,1)} %get-tuple-element.62.weight), custom_call_target="tpu_custom_call" | custom-call | flops 3221225472 | bytes 13631488 | tf_op jit(solution)/shard_map/down_0/pallas_call | solution.py:539
  150.1 4.8 %collective-permute-start.17 = (bf16[512,384]{1,0:T(8,128)(2,1)}, bf16[512,384]{1,0:T(8,128)(2,1)S(1)}, u32[]{:S(2)}, u32[]{:S(2)}) collective-permute-start(bf16[512,384]{1,0:T(8,128)(2,1)} %get-tuple-element.60.refs_0_), channel_id=1, source_target_pairs={{0,4},{1,5},{2,6},{3,7},{4,0},{5,1},{6,2},{7,3},{8,12},{9,13},{10,... | collective-permute-start | bytes 1179656 | tf_op jit(solution)/shard_map/ppermute | solution.py:645
  155.6 17.8 %collective-permute-done.17.refs_0_ = bf16[512,384]{1,0:T(8,128)(2,1)S(1)} collective-permute-done((bf16[512,384]{1,0:T(8,128)(2,1)}, bf16[512,384]{1,0:T(8,128)(2,1)S(1)}, u32[]{:S(2)}, u32[]{:S(2)}) %collective-permute-start.17) | collective-permute-done | bytes 393248 | tf_op jit(solution)/shard_map/ppermute | solution.py:645
  173.4 1.5 collective-permute-start.19
  174.8 4.6 %down_1_0.1 = (f32[512,1024]{1,0:T(8,128)S(1)}, f32[8,128]{1,0:T(8,128)S(1)}) custom-call(s32[3]{0:T(128)S(1)} %pad_add_fusion.place, bf16[2,512,384]{2,1,0:T(8,128)(2,1)S(1)} %pair.2.own, bf16[2,512,384]{2,1,0:T(8,128)(2,1)S(1)} %collective-permute-done.21.other, bf16[2,8,384,1024]{3,2,1,0:T(8,128)(2,1)} %bitcast.9, bf16[2,8,384,1024]{3,2,1,0:T(8,128)(2,1)} %bitcast.10, ...), custom_call_target="tpu_custom_call" | custom-call | flops 1610612736 | bytes 8912896 | tf_op jit(solution)/shard_map/down_1_0/pallas_call | solution.py:598
  179.5 6.3 %collective-permute-done.19.refs_2_ = bf16[512,384]{1,0:T(8,128)(2,1)S(1)} collective-permute-done((bf16[512,384]{1,0:T(8,128)(2,1)S(1)}, bf16[512,384]{1,0:T(8,128)(2,1)S(1)}, u32[]{:S(2)}, u32[]{:S(2)}) %collective-permute-start.19) | collective-permute-done | bytes 393248 | tf_op jit(solution)/shard_map/ppermute | solution.py:714
  186.0 2.3 %collective-permute-done.22.other = bf16[2,512,384]{2,1,0:T(8,128)(2,1)S(1)} collective-permute-done((bf16[2,512,384]{2,1,0:T(8,128)(2,1)S(1)}, bf16[2,512,384]{2,1,0:T(8,128)(2,1)S(1)}, u32[]{:S(2)}, u32[]{:S(2)}) %collective-permute-start.22) | collective-permute-done | bytes 786464 | tf_op jit(solution)/shard_map/ppermute | solution.py:648
  188.2 5.2 %down_1_2.1 = (bf16[128,1024]{1,0:T(8,128)(2,1)S(1)}, bf16[128,1024]{1,0:T(8,128)(2,1)S(1)}, bf16[128,1024]{1,0:T(8,128)(2,1)S(1)}, bf16[128,1024]{1,0:T(8,128)(2,1)S(1)}, f32[8,128]{1,0:T(8,128)}) custom-call(s32[3]{0:T(128)S(1)} %pad_add_fusion.place, bf16[2,512,384]{2,1,0:T(8,128)(2,1)S(1)} %pair.3.own, ...), custom_call_target="tpu_custom_call" | custom-call | flops 1610612736 | bytes 8912896 | tf_op jit(solution)/shard_map/down_1_2/pallas_call | solution.py:598
  193.4 3.6 %collective-permute-start.25 = (bf16[128,1024]{1,0:T(8,128)(2,1)S(1)}, bf16[128,1024]{1,0:T(8,128)(2,1)S(1)}, u32[]{:S(2)}, u32[]{:S(2)}) collective-permute-start(bf16[128,1024]{1,0:T(8,128)(2,1)S(1)} %get-tuple-element.70), channel_id=1, source_target_pairs={{0,24},{8,16},{16,8},{24,0},{1,25},{9,17},{17,9},{25,1},{2,26},{10... | collective-permute-start | bytes 786440 | tf_op jit(solution)/shard_map/ppermute | solution.py:642
  197.6 6.6 %collective-permute-done.25 = bf16[128,1024]{1,0:T(8,128)(2,1)S(1)} collective-permute-done((bf16[128,1024]{1,0:T(8,128)(2,1)S(1)}, bf16[128,1024]{1,0:T(8,128)(2,1)S(1)}, u32[]{:S(2)}, u32[]{:S(2)}) %collective-permute-start.25) | collective-permute-done | bytes 262176 | tf_op jit(solution)/shard_map/ppermute | solution.py:642
  204.1 5.1 %collective-permute-done.24 = bf16[128,1024]{1,0:T(8,128)(2,1)S(1)} collective-permute-done((bf16[128,1024]{1,0:T(8,128)(2,1)S(1)}, bf16[128,1024]{1,0:T(8,128)(2,1)S(1)}, u32[]{:S(2)}, u32[]{:S(2)}) %collective-permute-start.24) | collective-permute-done | bytes 262176 | tf_op jit(solution)/shard_map/ppermute | solution.py:642
  (88 shorter events, 22.6 us)
Async XLA Ops:
  6.5 133.9 %all-gather.2.cloned.1.call-start = ((), (), s32[]{:S(2)}) async-start(), calls=%async_computation | async-start | bytes 3538944 | tf_op jit(solution)/shard_map/all_gather | solution.py:709
  7.6 1.7 collective-permute-start
  9.3 6.2 %collective-permute-start.3 = (f32[1,128]{1,0:T(1,128)S(1)}, f32[1,128]{1,0:T(1,128)S(1)}, u32[]{:S(2)}, u32[]{:S(2)}) collective-permute-start(f32[1,128]{1,0:T(1,128)S(1)} %add.90), channel_id=1, source_target_pairs={{0,6},{1,7},{2,4},{3,5},{4,2},{5,3},{6,0},{7,1},{8,14},{9,15},{10,... | collective-permute-start | bytes 1544 | tf_op jit(solution)/shard_map/ppermute | solution.py:645
  14.0 3.5 %collective-permute-start.1 = (f32[1,128]{1,0:T(1,128)S(1)}, f32[1,128]{1,0:T(1,128)S(1)}, u32[]{:S(2)}, u32[]{:S(2)}) collective-permute-start(f32[1,128]{1,0:T(1,128)S(1)} %add.90), channel_id=1, source_target_pairs={{0,2},{1,3},{2,0},{3,1},{4,6},{5,7},{6,4},{7,5},{8,10},{9,11},{10,... | collective-permute-start | bytes 1544 | tf_op jit(solution)/shard_map/ppermute | solution.py:645
  14.0 4.4 %collective-permute-start.2 = (f32[1,128]{1,0:T(1,128)S(1)}, f32[1,128]{1,0:T(1,128)S(1)}, u32[]{:S(2)}, u32[]{:S(2)}) collective-permute-start(f32[1,128]{1,0:T(1,128)S(1)} %add.90), channel_id=1, source_target_pairs={{0,4},{1,5},{2,6},{3,7},{4,0},{5,1},{6,2},{7,3},{8,12},{9,13},{10,... | collective-permute-start | bytes 1544 | tf_op jit(solution)/shard_map/ppermute | solution.py:645
  19.6 21.9 %collective-permute-start.4 = (bf16[128,1024]{1,0:T(8,128)(2,1)S(1)}, bf16[128,1024]{1,0:T(8,128)(2,1)S(1)}, u32[]{:S(2)}, u32[]{:S(2)}) collective-permute-start(bf16[128,1024]{1,0:T(8,128)(2,1)S(1)} %multiply_convert_fusion), channel_id=1, source_target_pairs={{0,0},{1,1},{2,8},{3,9},{4,16},{5,17},{6,24},{7,25},{8,2},{9,3},{1... | collective-permute-start | bytes 786440 | tf_op jit(solution)/shard_map/ppermute | solution.py:656
  20.3 21.2 %collective-permute-start.5 = (bf16[128,1024]{1,0:T(8,128)(2,1)S(1)}, bf16[128,1024]{1,0:T(8,128)(2,1)S(1)}, u32[]{:S(2)}, u32[]{:S(2)}) collective-permute-start(bf16[128,1024]{1,0:T(8,128)(2,1)S(1)} %multiply_convert_fusion), channel_id=1, source_target_pairs={{0,2},{1,3},{2,10},{3,11},{4,18},{5,19},{6,26},{7,27},{8,0},{9,1},... | collective-permute-start | bytes 786440 | tf_op jit(solution)/shard_map/ppermute | solution.py:656
  24.5 16.9 %collective-permute-start.6 = (bf16[128,1024]{1,0:T(8,128)(2,1)S(1)}, bf16[128,1024]{1,0:T(8,128)(2,1)S(1)}, u32[]{:S(2)}, u32[]{:S(2)}) collective-permute-start(bf16[128,1024]{1,0:T(8,128)(2,1)S(1)} %multiply_convert_fusion), channel_id=1, source_target_pairs={{0,4},{1,5},{2,12},{3,13},{4,20},{5,21},{6,28},{7,29},{8,6},{9,7},... | collective-permute-start | bytes 786440 | tf_op jit(solution)/shard_map/ppermute | solution.py:656
  26.2 15.3 %collective-permute-start.7 = (bf16[128,1024]{1,0:T(8,128)(2,1)S(1)}, bf16[128,1024]{1,0:T(8,128)(2,1)S(1)}, u32[]{:S(2)}, u32[]{:S(2)}) collective-permute-start(bf16[128,1024]{1,0:T(8,128)(2,1)S(1)} %multiply_convert_fusion), channel_id=1, source_target_pairs={{0,6},{1,7},{2,14},{3,15},{4,22},{5,23},{6,30},{7,31},{8,4},{9,5},... | collective-permute-start | bytes 786440 | tf_op jit(solution)/shard_map/ppermute | solution.py:656
  42.2 2.7 %collective-permute-start.8 = (bf16[512,1024]{1,0:T(8,128)(2,1)S(1)}, bf16[512,1024]{1,0:T(8,128)(2,1)S(1)}, u32[]{:S(2)}, u32[]{:S(2)}) collective-permute-start(bf16[512,1024]{1,0:T(8,128)(2,1)S(1)} %pack.1.own), channel_id=1, source_target_pairs={{0,1},{1,0},{2,3},{3,2},{4,5},{5,4},{6,7},{7,6},{8,9},{9,8},{10,11... | collective-permute-start | bytes 3145736 | tf_op jit(solution)/shard_map/ppermute | solution.py:648
  57.5 25.1 %collective-permute-start.9 = (bf16[2,256,768]{2,1,0:T(8,128)(2,1)}, bf16[2,256,768]{2,1,0:T(8,128)(2,1)S(1)}, u32[]{:S(2)}, u32[]{:S(2)}) collective-permute-start(bf16[2,256,768]{2,1,0:T(8,128)(2,1)} %get-tuple-element.43), channel_id=1, source_target_pairs={{0,8},{8,0},{16,24},{24,16},{1,9},{9,1},{17,25},{25,17},{2,10},{10... | collective-permute-start | bytes 2359304 | tf_op jit(solution)/shard_map/ppermute | solution.py:642
  59.0 29.4 %collective-permute-start.10 = (bf16[2,256,768]{2,1,0:T(8,128)(2,1)}, bf16[2,256,768]{2,1,0:T(8,128)(2,1)S(1)}, u32[]{:S(2)}, u32[]{:S(2)}) collective-permute-start(bf16[2,256,768]{2,1,0:T(8,128)(2,1)} %get-tuple-element.45), channel_id=1, source_target_pairs={{0,16},{8,24},{16,0},{24,8},{1,17},{9,25},{17,1},{25,9},{2,18},{10... | collective-permute-start | bytes 2359304 | tf_op jit(solution)/shard_map/ppermute | solution.py:642
  70.4 18.1 %copy-start.3 = (bf16[2,256,768]{2,1,0:T(8,128)(2,1)S(1)}, bf16[2,256,768]{2,1,0:T(8,128)(2,1)}, u32[]{:S(2)}) copy-start(bf16[2,256,768]{2,1,0:T(8,128)(2,1)} %get-tuple-element.42.kept_a.refs_0_) | copy-start | bytes 2359300
  70.4 18.1 %copy-start.4 = (bf16[2,256,768]{2,1,0:T(8,128)(2,1)S(1)}, bf16[2,256,768]{2,1,0:T(8,128)(2,1)}, u32[]{:S(2)}) copy-start(bf16[2,256,768]{2,1,0:T(8,128)(2,1)} %get-tuple-element.44.kept_b.refs_3_) | copy-start | bytes 2359300
  89.9 15.0 %collective-permute-start.13 = (bf16[256,768]{1,0:T(8,128)(2,1)S(1)}, bf16[256,768]{1,0:T(8,128)(2,1)S(1)}, u32[]{:S(2)}, u32[]{:S(2)}) collective-permute-start(bf16[256,768]{1,0:T(8,128)(2,1)S(1)} %get-tuple-element.52), channel_id=1, source_target_pairs={{0,16},{8,24},{16,0},{24,8},{1,17},{9,25},{17,1},{25,9},{2,18},{10... | collective-permute-start | bytes 1179656 | tf_op jit(solution)/shard_map/ppermute | solution.py:642
  91.6 13.3 %collective-permute-start.14 = (bf16[256,768]{1,0:T(8,128)(2,1)S(1)}, bf16[256,768]{1,0:T(8,128)(2,1)S(1)}, u32[]{:S(2)}, u32[]{:S(2)}) collective-permute-start(bf16[256,768]{1,0:T(8,128)(2,1)S(1)} %get-tuple-element.53), channel_id=1, source_target_pairs={{0,8},{8,0},{16,24},{24,16},{1,9},{9,1},{17,25},{25,17},{2,10},{10... | collective-permute-start | bytes 1179656 | tf_op jit(solution)/shard_map/ppermute | solution.py:642
  93.3 14.3 %copy-start.11 = (s32[8,108]{1,0:T(8,128)S(1)}, s32[8,108]{1,0:T(8,128)}, u32[]{:S(2)}) copy-start(s32[8,108]{1,0:T(8,128)} %param.15) | copy-start | bytes 10372
  106.8 18.1 %collective-permute-start.11 = (bf16[2,256,768]{2,1,0:T(8,128)(2,1)}, bf16[2,256,768]{2,1,0:T(8,128)(2,1)S(1)}, u32[]{:S(2)}, u32[]{:S(2)}) collective-permute-start(bf16[2,256,768]{2,1,0:T(8,128)(2,1)} %get-tuple-element.49), channel_id=1, source_target_pairs={{0,8},{8,0},{16,24},{24,16},{1,9},{9,1},{17,25},{25,17},{2,10},{10... | collective-permute-start | bytes 2359304 | tf_op jit(solution)/shard_map/ppermute | solution.py:642
  107.3 18.1 %collective-permute-start.12 = (bf16[2,256,768]{2,1,0:T(8,128)(2,1)}, bf16[2,256,768]{2,1,0:T(8,128)(2,1)S(1)}, u32[]{:S(2)}, u32[]{:S(2)}) collective-permute-start(bf16[2,256,768]{2,1,0:T(8,128)(2,1)} %get-tuple-element.51), channel_id=1, source_target_pairs={{0,16},{8,24},{16,0},{24,8},{1,17},{9,25},{17,1},{25,9},{2,18},{10... | collective-permute-start | bytes 2359304 | tf_op jit(solution)/shard_map/ppermute | solution.py:642
  107.9 17.5 %copy-start.1 = (bf16[2,256,768]{2,1,0:T(8,128)(2,1)S(1)}, bf16[2,256,768]{2,1,0:T(8,128)(2,1)}, u32[]{:S(2)}) copy-start(bf16[2,256,768]{2,1,0:T(8,128)(2,1)} %get-tuple-element.48.kept_a.refs_0_) | copy-start | bytes 2359300
  107.9 17.5 %copy-start.2 = (bf16[2,256,768]{2,1,0:T(8,128)(2,1)S(1)}, bf16[2,256,768]{2,1,0:T(8,128)(2,1)}, u32[]{:S(2)}) copy-start(bf16[2,256,768]{2,1,0:T(8,128)(2,1)} %get-tuple-element.50.kept_b.refs_3_) | copy-start | bytes 2359300
  126.4 8.9 %collective-permute-start.15 = (bf16[256,768]{1,0:T(8,128)(2,1)}, bf16[256,768]{1,0:T(8,128)(2,1)S(1)}, u32[]{:S(2)}, u32[]{:S(2)}) collective-permute-start(bf16[256,768]{1,0:T(8,128)(2,1)} %get-tuple-element.57), channel_id=1, source_target_pairs={{0,16},{8,24},{16,0},{24,8},{1,17},{9,25},{17,1},{25,9},{2,18},{10... | collective-permute-start | bytes 1179656 | tf_op jit(solution)/shard_map/ppermute | solution.py:642
  127.3 9.4 %collective-permute-start.16 = (bf16[256,768]{1,0:T(8,128)(2,1)}, bf16[256,768]{1,0:T(8,128)(2,1)}, u32[]{:S(2)}, u32[]{:S(2)}) collective-permute-start(bf16[256,768]{1,0:T(8,128)(2,1)} %get-tuple-element.58), channel_id=1, source_target_pairs={{0,8},{8,0},{16,24},{24,16},{1,9},{9,1},{17,25},{25,17},{2,10},{10... | collective-permute-start | bytes 1179656 | tf_op jit(solution)/shard_map/ppermute | solution.py:642
  138.9 9.8 %collective-permute-start.20 = (bf16[512,384]{1,0:T(8,128)(2,1)}, bf16[512,384]{1,0:T(8,128)(2,1)S(1)}, u32[]{:S(2)}, u32[]{:S(2)}) collective-permute-start(bf16[512,384]{1,0:T(8,128)(2,1)} %get-tuple-element.60.refs_0_), channel_id=1, source_target_pairs={{0,2},{1,3},{2,0},{3,1},{4,6},{5,7},{6,4},{7,5},{8,10},{9,11},{10,... | collective-permute-start | bytes 1179656 | tf_op jit(solution)/shard_map/ppermute | solution.py:645
  149.8 25.0 %collective-permute-start.21 = (bf16[2,512,384]{2,1,0:T(8,128)(2,1)S(1)}, bf16[2,512,384]{2,1,0:T(8,128)(2,1)S(1)}, u32[]{:S(2)}, u32[]{:S(2)}) collective-permute-start(bf16[2,512,384]{2,1,0:T(8,128)(2,1)S(1)} %pair.2.own), channel_id=1, source_target_pairs={{0,1},{1,0},{2,3},{3,2},{4,5},{5,4},{6,7},{7,6},{8,9},{9,8},{10,11... | collective-permute-start | bytes 2359304 | tf_op jit(solution)/shard_map/ppermute | solution.py:648
  150.1 23.2 %collective-permute-start.17 = (bf16[512,384]{1,0:T(8,128)(2,1)}, bf16[512,384]{1,0:T(8,128)(2,1)S(1)}, u32[]{:S(2)}, u32[]{:S(2)}) collective-permute-start(bf16[512,384]{1,0:T(8,128)(2,1)} %get-tuple-element.60.refs_0_), channel_id=1, source_target_pairs={{0,4},{1,5},{2,6},{3,7},{4,0},{5,1},{6,2},{7,3},{8,12},{9,13},{10,... | collective-permute-start | bytes 1179656 | tf_op jit(solution)/shard_map/ppermute | solution.py:645
  154.9 24.6 %collective-permute-start.18 = (bf16[512,384]{1,0:T(8,128)(2,1)}, bf16[512,384]{1,0:T(8,128)(2,1)S(1)}, u32[]{:S(2)}, u32[]{:S(2)}) collective-permute-start(bf16[512,384]{1,0:T(8,128)(2,1)} %get-tuple-element.60.refs_0_), channel_id=1, source_target_pairs={{2,4},{3,5},{4,2},{5,3},{10,12},{11,13},{12,10},{13,11},{18,20},{1... | collective-permute-start | bytes 1179656 | tf_op jit(solution)/shard_map/ppermute | solution.py:713
  173.4 12.4 %collective-permute-start.19 = (bf16[512,384]{1,0:T(8,128)(2,1)S(1)}, bf16[512,384]{1,0:T(8,128)(2,1)S(1)}, u32[]{:S(2)}, u32[]{:S(2)}) collective-permute-start(bf16[512,384]{1,0:T(8,128)(2,1)S(1)} %collective-permute-done.17.refs_0_), channel_id=1, source_target_pairs={{2,0},{3,1},{4,6},{5,7},{10,8},{11,9},{12,14},{13,15},{18,16},{19,... | collective-permute-start | bytes 1179656 | tf_op jit(solution)/shard_map/ppermute | solution.py:714
  185.9 2.4 %collective-permute-start.22 = (bf16[2,512,384]{2,1,0:T(8,128)(2,1)S(1)}, bf16[2,512,384]{2,1,0:T(8,128)(2,1)S(1)}, u32[]{:S(2)}, u32[]{:S(2)}) collective-permute-start(bf16[2,512,384]{2,1,0:T(8,128)(2,1)S(1)} %pair.3.own), channel_id=1, source_target_pairs={{0,1},{1,0},{2,3},{3,2},{4,5},{5,4},{6,7},{7,6},{8,9},{9,8},{10,11... | collective-permute-start | bytes 2359304 | tf_op jit(solution)/shard_map/ppermute | solution.py:648
  193.4 10.7 %collective-permute-start.25 = (bf16[128,1024]{1,0:T(8,128)(2,1)S(1)}, bf16[128,1024]{1,0:T(8,128)(2,1)S(1)}, u32[]{:S(2)}, u32[]{:S(2)}) collective-permute-start(bf16[128,1024]{1,0:T(8,128)(2,1)S(1)} %get-tuple-element.70), channel_id=1, source_target_pairs={{0,24},{8,16},{16,8},{24,0},{1,25},{9,17},{17,9},{25,1},{2,26},{10... | collective-permute-start | bytes 786440 | tf_op jit(solution)/shard_map/ppermute | solution.py:642
  197.0 12.2 %collective-permute-start.24 = (bf16[128,1024]{1,0:T(8,128)(2,1)S(1)}, bf16[128,1024]{1,0:T(8,128)(2,1)S(1)}, u32[]{:S(2)}, u32[]{:S(2)}) collective-permute-start(bf16[128,1024]{1,0:T(8,128)(2,1)S(1)} %get-tuple-element.69), channel_id=1, source_target_pairs={{0,16},{8,24},{16,0},{24,8},{1,17},{9,25},{17,1},{25,9},{2,18},{10... | collective-permute-start | bytes 786440 | tf_op jit(solution)/shard_map/ppermute | solution.py:642
  197.0 12.3 %collective-permute-start.23 = (bf16[128,1024]{1,0:T(8,128)(2,1)S(1)}, bf16[128,1024]{1,0:T(8,128)(2,1)S(1)}, u32[]{:S(2)}, u32[]{:S(2)}) collective-permute-start(bf16[128,1024]{1,0:T(8,128)(2,1)S(1)} %get-tuple-element.68), channel_id=1, source_target_pairs={{0,8},{8,0},{16,24},{24,16},{1,9},{9,1},{17,25},{25,17},{2,10},{10... | collective-permute-start | bytes 786440 | tf_op jit(solution)/shard_map/ppermute | solution.py:642
  (8 other events, 9.2 us)
Sparse Core Ops, SparseCore 0:
  107.0 33.3 all-gather.1

commit v7 on v6

--- a/solution.py
+++ b/solution.py
@@ -362,29 +362,29 @@
     )(*pieces, *after)
 
 
-def pair_kernel(*refs, steps):
-    out = refs[-1]
+def stack_kernel(*refs, steps):
+    pieces, out = refs[:-2], refs[-1]
     count = out.shape[1] // 4
     for i, step in enumerate(steps):
         for part in range(4):
             there = slice((part ^ step) * count, ((part ^ step) + 1) * count)
-            rows = refs[i][there]
-            if i == 1 and steps == (2, 3):
-                rows += refs[2][there]
+            rows = pieces[i][there]
+            if i + 1 == len(steps) < len(pieces):
+                rows += pieces[i + 1][there]
             out[i, part * count:(part + 1) * count] = rows
 
 
-def pair(pieces, steps, after):
-    return pl.pallas_call(
-        functools.partial(pair_kernel, steps=steps),
-        out_shape=jax.ShapeDtypeStruct((2,) + pieces[0].shape, pieces[0].dtype),
+def stack(pieces, steps, after):
+    return pl.pallas_call(
+        functools.partial(stack_kernel, steps=steps),
+        out_shape=jax.ShapeDtypeStruct((len(steps),) + pieces[0].shape, pieces[0].dtype),
         in_specs=[pl.BlockSpec(memory_space=pltpu.VMEM)] * len(pieces) + [ANY_SPEC],
         out_specs=pl.BlockSpec(memory_space=pltpu.VMEM),
         compiler_params=pltpu.CompilerParams(vmem_limit_bytes=16 * MIB),
         cost_estimate=pl.CostEstimate(
             flops=0, bytes_accessed=4 * len(pieces) * pieces[0].size, transcendentals=0
         ),
-        name="pair",
+        name="stack",
     )(*pieces, after)
 
 
@@ -560,15 +560,16 @@
     )(place, hidden, dense, *added)
 
 
-def down_pair_kernel(place, own, other, *refs):
-    weights, before, outs, mark = refs[:4], refs[4], refs[5:-1], refs[-1]
+def down_steps_kernel(place, own, other, *refs):
+    pieces = 2 * own.shape[0]
+    weights, before, outs, mark = refs[:pieces], refs[pieces], refs[pieces + 1:-1], refs[-1]
     leave(mark)
     count = before.shape[0] // len(outs)
     for step, out in enumerate(outs):
         at = 0 if len(outs) == 1 else (place[1] ^ step) * count
         rows = pl.ds(pl.multiple_of(at, count), count)
         total = before[rows]
-        for i in range(2):
+        for i in range(pieces // 2):
             for j, side in enumerate((own, other)):
                 total += jnp.dot(
                     side[i, rows], weights[2 * i + j][0, 0], preferred_element_type=jnp.float32
@@ -576,7 +577,7 @@
         out[...] = total.astype(out.dtype)
 
 
-def down_pair(place, own, other, steps, dense, before, chunk, last):
+def down_steps(place, own, other, steps, dense, before, chunk, last):
     _, count, depth = own.shape
     width = dense.shape[-1]
     dense = dense.reshape(dense.shape[0], -1, depth, width)
@@ -596,7 +597,7 @@
         out = [jax.ShapeDtypeStruct((count // 4, width), own.dtype)] * 4
         out_tiles = [pl.BlockSpec((count // 4, tile), lambda n, *_: (0, n))] * 4
     return pl.pallas_call(
-        down_pair_kernel,
+        down_steps_kernel,
         out_shape=out + [MARK],
         grid_spec=pltpu.PrefetchScalarGridSpec(
             num_scalar_prefetch=1,
@@ -606,12 +607,12 @@
         ),
         compiler_params=pltpu.CompilerParams(vmem_limit_bytes=42 * MIB),
         cost_estimate=pl.CostEstimate(
-            flops=8 * count * depth * width,
-            bytes_accessed=8 * depth * (width + count) + 8 * count * width,
+            flops=4 * len(steps) * count * depth * width,
+            bytes_accessed=4 * len(steps) * depth * (width + count) + 8 * count * width,
             transcendentals=0,
         ),
         name=f"down_{chunk}_{steps[0]}",
-    )(place, own, other, *[dense] * 4, before)
+    )(place, own, other, *[dense] * len(weights), before)
 
 
 def by_columns(
@@ -714,10 +715,10 @@
     ends = lax.ppermute(far, "col", [(i, i ^ 2) for i in range(2, 6)])
     for chunk in range(chunks - 1):
         *mixed, mark = down_product(place, gathered[chunk], down_dense, mixed[0], chunk, False)
-    for steps, pieces in (((0, 1), [hidden, near]), ((2, 3), [far, inner, ends])):
-        held = pair(pieces, steps, mark)
-        *mixed, mark = down_pair(
-            place, held, swap_core(held), steps, down_dense, mixed[0], chunks - 1, steps[0] == 2
+    for steps, pieces in (((0, 1, 2), [hidden, near, far]), ((3,), [inner, ends])):
+        held = stack(pieces, steps, mark)
+        *mixed, mark = down_steps(
+            place, held, swap_core(held), steps, down_dense, mixed[0], chunks - 1, steps == (3,)
         )
 
     total = mixed[0].astype(jnp.float32)

time: 218 us -> 201 us (0.922)
  waiting for transfers between devices: 59.6 us -> 47.8 us
  starting transfers between devices: 45.2 us -> 39.6 us
    ppermute x5, waiting for transfers between devices: 20.9 us -> 8.91 us  [swap_chip(): lax.ppermute(array, 'col', [(i, i ^ 2 * step) for i in range(col_size)])]
    ppermute x5, starting transfers between devices: 10.1 us -> 5.36 us  [swap_chip(): lax.ppermute(array, 'col', [(i, i ^ 2 * step) for i in range(col_size)])]
    unnamed x26 -> x30, local copies, waits for them, and re-layouts: 6.44 us -> 8.18 us
  transfers between devices with their start and end apart: 27 -> 27, of which waited for: 16 -> 16; matrix products, arithmetic and copies ran while one was open for 2% -> 2% of each run, Pallas kernels for 31% -> 34%
where the time goes in v7:
time: 201 us; the launch traced here: 200 us
  Pallas kernels  84.8 us (42%)
  waiting for transfers between devices  47.8 us (24%)
  starting transfers between devices  39.6 us (20%)
  between operations  13.7 us (7%)
  local copies, waits for them, and re-layouts  10.7 us (5%)
  other arithmetic  3.22 us (2%)
    ppermute x11, waiting for transfers between devices, swap_tok(): return lax.ppermute(array, 'tok', [(i, i ^ step) for i in parts])  25 us
    pallas_call x2, Pallas kernels, spread_shares(): pl.pallas_call(functools.partial(spread_shares_kernel, rows=rows // steps...  24.3 us
    pallas_call x2, Pallas kernels, panel_product(): pl.pallas_call(panel_product_kernel, out_shape=[out] * 4 + [MARK], grid=(...  23.3 us
    ppermute x11, starting transfers between devices, swap_tok(): return lax.ppermute(array, 'tok', [(i, i ^ step) for i in parts])  23.1 us
    pallas_call x1, Pallas kernels, spread_panels(): pl.pallas_call(functools.partial(spread_panels_kernel, chunks=chunks, row...  16.6 us
    pallas_call x2, Pallas kernels, down_steps(): pl.pallas_call(down_steps_kernel, out_shape=out + [MARK], grid_spec=pltpu...  9.82 us
    ppermute x5, waiting for transfers between devices, swap_chip(): lax.ppermute(array, 'col', [(i, i ^ 2 * step) for i in range(col_size)])  8.91 us
    ppermute x4, starting transfers between devices, to_users(): return lax.ppermute(array, ('tok', 'col'), pairs)  8.24 us
  transfers between devices with their start and end apart: 27, of which 16 were waited for; matrix products, arithmetic and copies ran while one was open for 2% of the time, Pallas kernels for 34%

profile of v7, /device:TPU:0, one launch (start us, length us, event | category | flops | bytes accessed | tf_op | source)
XLA Modules:
  0.0 199.8 jit_solution(3364954049136108111)
XLA Ops:
  9.3 4.7 %collective-permute-start.3 = (f32[1,128]{1,0:T(1,128)S(1)}, f32[1,128]{1,0:T(1,128)S(1)}, u32[]{:S(2)}, u32[]{:S(2)}) collective-permute-start(f32[1,128]{1,0:T(1,128)S(1)} %add.90), channel_id=1, source_target_pairs={{0,6},{1,7},{2,4},{3,5},{4,2},{5,3},{6,0},{7,1},{8,14},{9,15},{10,... | collective-permute-start | bytes 1544 | tf_op jit(solution)/shard_map/ppermute | solution.py:646
  15.6 2.0 %collective-permute-done.1 = f32[1,128]{1,0:T(1,128)S(1)} collective-permute-done((f32[1,128]{1,0:T(1,128)S(1)}, f32[1,128]{1,0:T(1,128)S(1)}, u32[]{:S(2)}, u32[]{:S(2)}) %collective-permute-start.1) | collective-permute-done | bytes 544 | tf_op jit(solution)/shard_map/ppermute | solution.py:646
  20.3 4.2 %collective-permute-start.5 = (bf16[128,1024]{1,0:T(8,128)(2,1)S(1)}, bf16[128,1024]{1,0:T(8,128)(2,1)S(1)}, u32[]{:S(2)}, u32[]{:S(2)}) collective-permute-start(bf16[128,1024]{1,0:T(8,128)(2,1)S(1)} %multiply_convert_fusion), channel_id=1, source_target_pairs={{0,2},{1,3},{2,10},{3,11},{4,18},{5,19},{6,26},{7,27},{8,0},{9,1},... | collective-permute-start | bytes 786440 | tf_op jit(solution)/shard_map/ppermute | solution.py:657
  24.5 1.7 collective-permute-start.6
  26.2 1.6 collective-permute-start.7
  29.4 12.1 %spread_gate_up_0.1 = (bf16[1,2048,3072]{2,1,0:T(8,128)(2,1)}, f32[8,128]{1,0:T(8,128)}) custom-call(s32[192]{0:T(256)} %get-tuple-element.77.gate_at, s32[192]{0:T(256)} %get-tuple-element.74.up_at, bf16[1,216,128,128]{3,2,1,0:T(8,128)(2,1)} %refs_0_.3, bf16[1,216,128,128]{3,2,1,0:T(8,128)(2,1)} %refs_1_.3), custom_call_target="tpu_custom_call" | custom-call | bytes 26738688 | tf_op jit(solution)/shard_map/spread_gate_up_0/pallas_call | solution.py:274
  42.3 2.6 %collective-permute-done.8.other = bf16[512,1024]{1,0:T(8,128)(2,1)S(1)} collective-permute-done((bf16[512,1024]{1,0:T(8,128)(2,1)S(1)}, bf16[512,1024]{1,0:T(8,128)(2,1)S(1)}, u32[]{:S(2)}, u32[]{:S(2)}) %collective-permute-start.8) | collective-permute-done | bytes 1048608 | tf_op jit(solution)/shard_map/ppermute | solution.py:649
  45.9 11.6 %gate_up_0.1 = (bf16[2,256,768]{2,1,0:T(8,128)(2,1)}, bf16[2,256,768]{2,1,0:T(8,128)(2,1)}, bf16[2,256,768]{2,1,0:T(8,128)(2,1)}, bf16[2,256,768]{2,1,0:T(8,128)(2,1)}, f32[8,128]{1,0:T(8,128)}) custom-call(bf16[512,1024]{1,0:T(8,128)(2,1)} %copy-done.6, bf16[512,1024]{1,0:T(8,128)(2,1)} %copy-done.14, bf16[1,2048,3072]{2,1,0:T(8,128)(2,1)} %get-tuple-element.39.weight), custom_call_target="tpu_custom_call" | custom-call | flops 6442450944 | bytes 17825792 | tf_op jit(solution)/shard_map/gate_up_0/pallas_call | solution.py:476
  57.6 1.5 collective-permute-start.9
  59.1 11.4 %collective-permute-start.10 = (bf16[2,256,768]{2,1,0:T(8,128)(2,1)}, bf16[2,256,768]{2,1,0:T(8,128)(2,1)S(1)}, u32[]{:S(2)}, u32[]{:S(2)}) collective-permute-start(bf16[2,256,768]{2,1,0:T(8,128)(2,1)} %get-tuple-element.45), channel_id=1, source_target_pairs={{0,16},{8,24},{16,0},{24,8},{1,17},{9,25},{17,1},{25,9},{2,18},{10... | collective-permute-start | bytes 2359304 | tf_op jit(solution)/shard_map/ppermute | solution.py:643
  70.4 12.2 %spread_gate_up_1.1 = (bf16[1,2048,3072]{2,1,0:T(8,128)(2,1)}, f32[8,128]{1,0:T(8,128)}) custom-call(s32[192]{0:T(256)} %get-tuple-element.78.gate_at, s32[192]{0:T(256)} %get-tuple-element.73.up_at, bf16[1,216,128,128]{3,2,1,0:T(8,128)(2,1)} %refs_0_.3, bf16[1,216,128,128]{3,2,1,0:T(8,128)(2,1)} %refs_1_.3, f32[8,128]{1,0:T(8,128)} %get-tuple-element.40.refs_2_), custom_call_target="tpu_custom_call" | custom-call | bytes 26738688 | tf_op jit(solution)/shard_map/spread_gate_up_1/pallas_call | solution.py:274
  82.7 5.8 %collective-permute-done.10.came_b.refs_4_ = bf16[2,256,768]{2,1,0:T(8,128)(2,1)S(1)} collective-permute-done((bf16[2,256,768]{2,1,0:T(8,128)(2,1)}, bf16[2,256,768]{2,1,0:T(8,128)(2,1)S(1)}, u32[]{:S(2)}, u32[]{:S(2)}) %collective-permute-start.10) | collective-permute-done | bytes 786464 | tf_op jit(solution)/shard_map/ppermute | solution.py:643
  90.0 1.7 collective-permute-start.13
  91.7 1.7 collective-permute-start.14
  93.4 11.6 %gate_up_1.1 = (bf16[2,256,768]{2,1,0:T(8,128)(2,1)}, bf16[2,256,768]{2,1,0:T(8,128)(2,1)}, bf16[2,256,768]{2,1,0:T(8,128)(2,1)}, bf16[2,256,768]{2,1,0:T(8,128)(2,1)}, f32[8,128]{1,0:T(8,128)}) custom-call(bf16[512,1024]{1,0:T(8,128)(2,1)} %copy-done.6, bf16[512,1024]{1,0:T(8,128)(2,1)} %copy-done.14, bf16[1,2048,3072]{2,1,0:T(8,128)(2,1)} %get-tuple-element.41.weight, ...), custom_call_target="tpu_custom_call" | custom-call | flops 6442450944 | bytes 17825792 | tf_op jit(solution)/shard_map/gate_up_1/pallas_call | solution.py:476
  105.7 1.2 combine_0.1
  108.0 16.6 %spread_down.1 = (bf16[2,3072,1024]{2,1,0:T(8,128)(2,1)}, f32[8,128]{1,0:T(8,128)S(1)}) custom-call(s32[384]{0:T(512)S(1)} %reshape.88.at_ref, bf16[8,108,128,128]{3,2,1,0:T(8,128)(2,1)} %values_ref.1, f32[8,128]{1,0:T(8,128)S(1)} %get-tuple-element.55.refs_0_), custom_call_target="tpu_custom_call" | custom-call | bytes 40894464 | tf_op jit(solution)/shard_map/spread_down/pallas_call | solution.py:305
  127.4 1.7 collective-permute-start.16
  129.1 6.2 %collective-permute-done.15.refs_2_ = bf16[256,768]{1,0:T(8,128)(2,1)S(1)} collective-permute-done((bf16[256,768]{1,0:T(8,128)(2,1)}, bf16[256,768]{1,0:T(8,128)(2,1)S(1)}, u32[]{:S(2)}, u32[]{:S(2)}) %collective-permute-start.15) | collective-permute-done | bytes 393248 | tf_op jit(solution)/shard_map/ppermute | solution.py:643
  137.8 1.6 combine_1.1
  139.5 3.2 %all-gather.2.cloned.1.call-done.hidden = bf16[8,4,128,384]{3,2,1,0:T(8,128)(2,1)} async-done(((bf16[1,4,128,384]{3,2,1,0:T(8,128)(2,1)}), bf16[8,4,128,384]{3,2,1,0:T(8,128)(2,1)}) %all-gather.2.cloned.1.call-update) | async-done | bytes 3145744 | tf_op jit(solution)/shard_map/all_gather | solution.py:710
  142.7 1.9 copy-done
  144.6 6.4 %down_0.1 = (f32[512,1024]{1,0:T(8,128)S(1)}, f32[8,128]{1,0:T(8,128)S(1)}) custom-call(s32[3]{0:T(128)S(1)} %pad_add_fusion.place, bf16[8,4,128,384]{3,2,1,0:T(8,128)(2,1)S(1)} %copy-done, bf16[2,3072,1024]{2,1,0:T(8,128)(2,1)} %get-tuple-element.62.weight), custom_call_target="tpu_custom_call" | custom-call | flops 3221225472 | bytes 13631488 | tf_op jit(solution)/shard_map/down_0/pallas_call | solution.py:539
  151.0 5.8 %collective-permute-done.18.refs_2_ = bf16[512,384]{1,0:T(8,128)(2,1)S(1)} collective-permute-done((bf16[512,384]{1,0:T(8,128)(2,1)S(1)}, bf16[512,384]{1,0:T(8,128)(2,1)S(1)}, u32[]{:S(2)}, u32[]{:S(2)}) %collective-permute-start.18) | collective-permute-done | bytes 393248 | tf_op jit(solution)/shard_map/ppermute | solution.py:646
  157.7 1.5 collective-permute-start.19
  159.8 6.0 %down_1_0.1 = (f32[512,1024]{1,0:T(8,128)S(1)}, f32[8,128]{1,0:T(8,128)S(1)}) custom-call(s32[3]{0:T(128)S(1)} %pad_add_fusion.place, bf16[3,512,384]{2,1,0:T(8,128)(2,1)S(1)} %stack.18.own, bf16[3,512,384]{2,1,0:T(8,128)(2,1)S(1)} %collective-permute-done.21.other, bf16[2,8,384,1024]{3,2,1,0:T(8,128)(2,1)} %bitcast.9, bf16[2,8,384,1024]{3,2,1,0:T(8,128)(2,1)} %bitcast.10, ...), custom_call_target="tpu_custom_call" | custom-call | flops 2415919104 | bytes 11272192 | tf_op jit(solution)/shard_map/down_1_0/pallas_call | solution.py:599
  165.9 5.7 %collective-permute-done.19.refs_1_ = bf16[512,384]{1,0:T(8,128)(2,1)S(1)} collective-permute-done((bf16[512,384]{1,0:T(8,128)(2,1)S(1)}, bf16[512,384]{1,0:T(8,128)(2,1)S(1)}, u32[]{:S(2)}, u32[]{:S(2)}) %collective-permute-start.19) | collective-permute-done | bytes 393248 | tf_op jit(solution)/shard_map/ppermute | solution.py:715
  171.6 1.7 collective-permute-done.22.other
  173.4 3.8 %down_1_3.1 = (bf16[128,1024]{1,0:T(8,128)(2,1)S(1)}, bf16[128,1024]{1,0:T(8,128)(2,1)S(1)}, bf16[128,1024]{1,0:T(8,128)(2,1)S(1)}, bf16[128,1024]{1,0:T(8,128)(2,1)S(1)}, f32[8,128]{1,0:T(8,128)}) custom-call(s32[3]{0:T(128)S(1)} %pad_add_fusion.place, bf16[1,512,384]{2,1,0:T(8,128)(2,1)S(1)} %stack.19.own, ...), custom_call_target="tpu_custom_call" | custom-call | flops 805306368 | bytes 6553600 | tf_op jit(solution)/shard_map/down_1_3/pallas_call | solution.py:599
  177.2 2.4 %collective-permute-start.25 = (bf16[128,1024]{1,0:T(8,128)(2,1)S(1)}, bf16[128,1024]{1,0:T(8,128)(2,1)S(1)}, u32[]{:S(2)}, u32[]{:S(2)}) collective-permute-start(bf16[128,1024]{1,0:T(8,128)(2,1)S(1)} %get-tuple-element.70), channel_id=1, source_target_pairs={{0,24},{8,16},{16,8},{24,0},{1,25},{9,17},{17,9},{25,1},{2,26},{10... | collective-permute-start | bytes 786440 | tf_op jit(solution)/shard_map/ppermute | solution.py:643
  180.7 6.6 %collective-permute-done.25 = bf16[128,1024]{1,0:T(8,128)(2,1)S(1)} collective-permute-done((bf16[128,1024]{1,0:T(8,128)(2,1)S(1)}, bf16[128,1024]{1,0:T(8,128)(2,1)S(1)}, u32[]{:S(2)}, u32[]{:S(2)}) %collective-permute-start.25) | collective-permute-done | bytes 262176 | tf_op jit(solution)/shard_map/ppermute | solution.py:643
  187.3 4.8 %collective-permute-done.24 = bf16[128,1024]{1,0:T(8,128)(2,1)S(1)} collective-permute-done((bf16[128,1024]{1,0:T(8,128)(2,1)S(1)}, bf16[128,1024]{1,0:T(8,128)(2,1)S(1)}, u32[]{:S(2)}, u32[]{:S(2)}) %collective-permute-start.24) | collective-permute-done | bytes 262176 | tf_op jit(solution)/shard_map/ppermute | solution.py:643
  (92 shorter events, 22.3 us)
Async XLA Ops:
  6.5 136.1 %all-gather.2.cloned.1.call-start = ((), (), s32[]{:S(2)}) async-start(), calls=%async_computation | async-start | bytes 3538944 | tf_op jit(solution)/shard_map/all_gather | solution.py:710
  7.6 1.7 collective-permute-start
  9.3 6.2 %collective-permute-start.3 = (f32[1,128]{1,0:T(1,128)S(1)}, f32[1,128]{1,0:T(1,128)S(1)}, u32[]{:S(2)}, u32[]{:S(2)}) collective-permute-start(f32[1,128]{1,0:T(1,128)S(1)} %add.90), channel_id=1, source_target_pairs={{0,6},{1,7},{2,4},{3,5},{4,2},{5,3},{6,0},{7,1},{8,14},{9,15},{10,... | collective-permute-start | bytes 1544 | tf_op jit(solution)/shard_map/ppermute | solution.py:646
  14.0 3.5 %collective-permute-start.1 = (f32[1,128]{1,0:T(1,128)S(1)}, f32[1,128]{1,0:T(1,128)S(1)}, u32[]{:S(2)}, u32[]{:S(2)}) collective-permute-start(f32[1,128]{1,0:T(1,128)S(1)} %add.90), channel_id=1, source_target_pairs={{0,2},{1,3},{2,0},{3,1},{4,6},{5,7},{6,4},{7,5},{8,10},{9,11},{10,... | collective-permute-start | bytes 1544 | tf_op jit(solution)/shard_map/ppermute | solution.py:646
  14.0 4.4 %collective-permute-start.2 = (f32[1,128]{1,0:T(1,128)S(1)}, f32[1,128]{1,0:T(1,128)S(1)}, u32[]{:S(2)}, u32[]{:S(2)}) collective-permute-start(f32[1,128]{1,0:T(1,128)S(1)} %add.90), channel_id=1, source_target_pairs={{0,4},{1,5},{2,6},{3,7},{4,0},{5,1},{6,2},{7,3},{8,12},{9,13},{10,... | collective-permute-start | bytes 1544 | tf_op jit(solution)/shard_map/ppermute | solution.py:646
  19.6 21.9 %collective-permute-start.4 = (bf16[128,1024]{1,0:T(8,128)(2,1)S(1)}, bf16[128,1024]{1,0:T(8,128)(2,1)S(1)}, u32[]{:S(2)}, u32[]{:S(2)}) collective-permute-start(bf16[128,1024]{1,0:T(8,128)(2,1)S(1)} %multiply_convert_fusion), channel_id=1, source_target_pairs={{0,0},{1,1},{2,8},{3,9},{4,16},{5,17},{6,24},{7,25},{8,2},{9,3},{1... | collective-permute-start | bytes 786440 | tf_op jit(solution)/shard_map/ppermute | solution.py:657
  20.3 21.2 %collective-permute-start.5 = (bf16[128,1024]{1,0:T(8,128)(2,1)S(1)}, bf16[128,1024]{1,0:T(8,128)(2,1)S(1)}, u32[]{:S(2)}, u32[]{:S(2)}) collective-permute-start(bf16[128,1024]{1,0:T(8,128)(2,1)S(1)} %multiply_convert_fusion), channel_id=1, source_target_pairs={{0,2},{1,3},{2,10},{3,11},{4,18},{5,19},{6,26},{7,27},{8,0},{9,1},... | collective-permute-start | bytes 786440 | tf_op jit(solution)/shard_map/ppermute | solution.py:657
  24.5 17.0 %collective-permute-start.6 = (bf16[128,1024]{1,0:T(8,128)(2,1)S(1)}, bf16[128,1024]{1,0:T(8,128)(2,1)S(1)}, u32[]{:S(2)}, u32[]{:S(2)}) collective-permute-start(bf16[128,1024]{1,0:T(8,128)(2,1)S(1)} %multiply_convert_fusion), channel_id=1, source_target_pairs={{0,4},{1,5},{2,12},{3,13},{4,20},{5,21},{6,28},{7,29},{8,6},{9,7},... | collective-permute-start | bytes 786440 | tf_op jit(solution)/shard_map/ppermute | solution.py:657
  26.2 15.3 %collective-permute-start.7 = (bf16[128,1024]{1,0:T(8,128)(2,1)S(1)}, bf16[128,1024]{1,0:T(8,128)(2,1)S(1)}, u32[]{:S(2)}, u32[]{:S(2)}) collective-permute-start(bf16[128,1024]{1,0:T(8,128)(2,1)S(1)} %multiply_convert_fusion), channel_id=1, source_target_pairs={{0,6},{1,7},{2,14},{3,15},{4,22},{5,23},{6,30},{7,31},{8,4},{9,5},... | collective-permute-start | bytes 786440 | tf_op jit(solution)/shard_map/ppermute | solution.py:657
  42.2 2.7 %collective-permute-start.8 = (bf16[512,1024]{1,0:T(8,128)(2,1)S(1)}, bf16[512,1024]{1,0:T(8,128)(2,1)S(1)}, u32[]{:S(2)}, u32[]{:S(2)}) collective-permute-start(bf16[512,1024]{1,0:T(8,128)(2,1)S(1)} %pack.1.own), channel_id=1, source_target_pairs={{0,1},{1,0},{2,3},{3,2},{4,5},{5,4},{6,7},{7,6},{8,9},{9,8},{10,11... | collective-permute-start | bytes 3145736 | tf_op jit(solution)/shard_map/ppermute | solution.py:649
  57.6 25.1 %collective-permute-start.9 = (bf16[2,256,768]{2,1,0:T(8,128)(2,1)}, bf16[2,256,768]{2,1,0:T(8,128)(2,1)S(1)}, u32[]{:S(2)}, u32[]{:S(2)}) collective-permute-start(bf16[2,256,768]{2,1,0:T(8,128)(2,1)} %get-tuple-element.43), channel_id=1, source_target_pairs={{0,8},{8,0},{16,24},{24,16},{1,9},{9,1},{17,25},{25,17},{2,10},{10... | collective-permute-start | bytes 2359304 | tf_op jit(solution)/shard_map/ppermute | solution.py:643
  59.1 29.4 %collective-permute-start.10 = (bf16[2,256,768]{2,1,0:T(8,128)(2,1)}, bf16[2,256,768]{2,1,0:T(8,128)(2,1)S(1)}, u32[]{:S(2)}, u32[]{:S(2)}) collective-permute-start(bf16[2,256,768]{2,1,0:T(8,128)(2,1)} %get-tuple-element.45), channel_id=1, source_target_pairs={{0,16},{8,24},{16,0},{24,8},{1,17},{9,25},{17,1},{25,9},{2,18},{10... | collective-permute-start | bytes 2359304 | tf_op jit(solution)/shard_map/ppermute | solution.py:643
  70.4 18.1 %copy-start.3 = (bf16[2,256,768]{2,1,0:T(8,128)(2,1)S(1)}, bf16[2,256,768]{2,1,0:T(8,128)(2,1)}, u32[]{:S(2)}) copy-start(bf16[2,256,768]{2,1,0:T(8,128)(2,1)} %get-tuple-element.42.kept_a.refs_0_) | copy-start | bytes 2359300
  70.4 18.1 %copy-start.4 = (bf16[2,256,768]{2,1,0:T(8,128)(2,1)S(1)}, bf16[2,256,768]{2,1,0:T(8,128)(2,1)}, u32[]{:S(2)}) copy-start(bf16[2,256,768]{2,1,0:T(8,128)(2,1)} %get-tuple-element.44.kept_b.refs_3_) | copy-start | bytes 2359300
  90.0 15.1 %collective-permute-start.13 = (bf16[256,768]{1,0:T(8,128)(2,1)S(1)}, bf16[256,768]{1,0:T(8,128)(2,1)S(1)}, u32[]{:S(2)}, u32[]{:S(2)}) collective-permute-start(bf16[256,768]{1,0:T(8,128)(2,1)S(1)} %get-tuple-element.52), channel_id=1, source_target_pairs={{0,16},{8,24},{16,0},{24,8},{1,17},{9,25},{17,1},{25,9},{2,18},{10... | collective-permute-start | bytes 1179656 | tf_op jit(solution)/shard_map/ppermute | solution.py:643
  91.7 13.3 %collective-permute-start.14 = (bf16[256,768]{1,0:T(8,128)(2,1)S(1)}, bf16[256,768]{1,0:T(8,128)(2,1)S(1)}, u32[]{:S(2)}, u32[]{:S(2)}) collective-permute-start(bf16[256,768]{1,0:T(8,128)(2,1)S(1)} %get-tuple-element.53), channel_id=1, source_target_pairs={{0,8},{8,0},{16,24},{24,16},{1,9},{9,1},{17,25},{25,17},{2,10},{10... | collective-permute-start | bytes 1179656 | tf_op jit(solution)/shard_map/ppermute | solution.py:643
  93.4 14.3 %copy-start.13 = (s32[8,108]{1,0:T(8,128)S(1)}, s32[8,108]{1,0:T(8,128)}, u32[]{:S(2)}) copy-start(s32[8,108]{1,0:T(8,128)} %param.15) | copy-start | bytes 10372
  107.0 18.1 %collective-permute-start.11 = (bf16[2,256,768]{2,1,0:T(8,128)(2,1)}, bf16[2,256,768]{2,1,0:T(8,128)(2,1)S(1)}, u32[]{:S(2)}, u32[]{:S(2)}) collective-permute-start(bf16[2,256,768]{2,1,0:T(8,128)(2,1)} %get-tuple-element.49), channel_id=1, source_target_pairs={{0,8},{8,0},{16,24},{24,16},{1,9},{9,1},{17,25},{25,17},{2,10},{10... | collective-permute-start | bytes 2359304 | tf_op jit(solution)/shard_map/ppermute | solution.py:643
  107.4 18.1 %collective-permute-start.12 = (bf16[2,256,768]{2,1,0:T(8,128)(2,1)}, bf16[2,256,768]{2,1,0:T(8,128)(2,1)S(1)}, u32[]{:S(2)}, u32[]{:S(2)}) collective-permute-start(bf16[2,256,768]{2,1,0:T(8,128)(2,1)} %get-tuple-element.51), channel_id=1, source_target_pairs={{0,16},{8,24},{16,0},{24,8},{1,17},{9,25},{17,1},{25,9},{2,18},{10... | collective-permute-start | bytes 2359304 | tf_op jit(solution)/shard_map/ppermute | solution.py:643
  108.0 17.5 %copy-start.1 = (bf16[2,256,768]{2,1,0:T(8,128)(2,1)S(1)}, bf16[2,256,768]{2,1,0:T(8,128)(2,1)}, u32[]{:S(2)}) copy-start(bf16[2,256,768]{2,1,0:T(8,128)(2,1)} %get-tuple-element.48.kept_a.refs_0_) | copy-start | bytes 2359300
  108.0 17.5 %copy-start.2 = (bf16[2,256,768]{2,1,0:T(8,128)(2,1)S(1)}, bf16[2,256,768]{2,1,0:T(8,128)(2,1)}, u32[]{:S(2)}) copy-start(bf16[2,256,768]{2,1,0:T(8,128)(2,1)} %get-tuple-element.50.kept_b.refs_3_) | copy-start | bytes 2359300
  126.5 8.9 %collective-permute-start.15 = (bf16[256,768]{1,0:T(8,128)(2,1)}, bf16[256,768]{1,0:T(8,128)(2,1)S(1)}, u32[]{:S(2)}, u32[]{:S(2)}) collective-permute-start(bf16[256,768]{1,0:T(8,128)(2,1)} %get-tuple-element.57), channel_id=1, source_target_pairs={{0,16},{8,24},{16,0},{24,8},{1,17},{9,25},{17,1},{25,9},{2,18},{10... | collective-permute-start | bytes 1179656 | tf_op jit(solution)/shard_map/ppermute | solution.py:643
  127.4 9.4 %collective-permute-start.16 = (bf16[256,768]{1,0:T(8,128)(2,1)}, bf16[256,768]{1,0:T(8,128)(2,1)}, u32[]{:S(2)}, u32[]{:S(2)}) collective-permute-start(bf16[256,768]{1,0:T(8,128)(2,1)} %get-tuple-element.58), channel_id=1, source_target_pairs={{0,8},{8,0},{16,24},{24,16},{1,9},{9,1},{17,25},{25,17},{2,10},{10... | collective-permute-start | bytes 1179656 | tf_op jit(solution)/shard_map/ppermute | solution.py:643
  139.4 17.4 %collective-permute-start.18 = (bf16[512,384]{1,0:T(8,128)(2,1)S(1)}, bf16[512,384]{1,0:T(8,128)(2,1)S(1)}, u32[]{:S(2)}, u32[]{:S(2)}) collective-permute-start(bf16[512,384]{1,0:T(8,128)(2,1)S(1)} %get-tuple-element.60.refs_0_), channel_id=1, source_target_pairs={{0,4},{1,5},{2,6},{3,7},{4,0},{5,1},{6,2},{7,3},{8,12},{9,13},{10,... | collective-permute-start | bytes 1179656 | tf_op jit(solution)/shard_map/ppermute | solution.py:646
  139.4 17.4 %collective-permute-start.20 = (bf16[512,384]{1,0:T(8,128)(2,1)S(1)}, bf16[512,384]{1,0:T(8,128)(2,1)S(1)}, u32[]{:S(2)}, u32[]{:S(2)}) collective-permute-start(bf16[512,384]{1,0:T(8,128)(2,1)S(1)} %get-tuple-element.60.refs_0_), channel_id=1, source_target_pairs={{0,2},{1,3},{2,0},{3,1},{4,6},{5,7},{6,4},{7,5},{8,10},{9,11},{10,... | collective-permute-start | bytes 1179656 | tf_op jit(solution)/shard_map/ppermute | solution.py:646
  156.9 2.9 %collective-permute-start.21 = (bf16[3,512,384]{2,1,0:T(8,128)(2,1)S(1)}, bf16[3,512,384]{2,1,0:T(8,128)(2,1)S(1)}, u32[]{:S(2)}, u32[]{:S(2)}) collective-permute-start(bf16[3,512,384]{2,1,0:T(8,128)(2,1)S(1)} %stack.18.own), channel_id=1, source_target_pairs={{0,1},{1,0},{2,3},{3,2},{4,5},{5,4},{6,7},{7,6},{8,9},{9,8},{10,11... | collective-permute-start | bytes 3538952 | tf_op jit(solution)/shard_map/ppermute | solution.py:649
  157.0 8.9 %collective-permute-start.17 = (bf16[512,384]{1,0:T(8,128)(2,1)S(1)}, bf16[512,384]{1,0:T(8,128)(2,1)S(1)}, u32[]{:S(2)}, u32[]{:S(2)}) collective-permute-start(bf16[512,384]{1,0:T(8,128)(2,1)S(1)} %get-tuple-element.60.refs_0_), channel_id=1, source_target_pairs={{2,4},{3,5},{4,2},{5,3},{10,12},{11,13},{12,10},{13,11},{18,20},{1... | collective-permute-start | bytes 1179656 | tf_op jit(solution)/shard_map/ppermute | solution.py:714
  157.7 13.8 %collective-permute-start.19 = (bf16[512,384]{1,0:T(8,128)(2,1)S(1)}, bf16[512,384]{1,0:T(8,128)(2,1)S(1)}, u32[]{:S(2)}, u32[]{:S(2)}) collective-permute-start(bf16[512,384]{1,0:T(8,128)(2,1)S(1)} %collective-permute-done.18.refs_2_), channel_id=1, source_target_pairs={{2,0},{3,1},{4,6},{5,7},{10,8},{11,9},{12,14},{13,15},{18,16},{19,... | collective-permute-start | bytes 1179656 | tf_op jit(solution)/shard_map/ppermute | solution.py:715
  171.6 1.8 collective-permute-start.22
  177.2 10.1 %collective-permute-start.25 = (bf16[128,1024]{1,0:T(8,128)(2,1)S(1)}, bf16[128,1024]{1,0:T(8,128)(2,1)S(1)}, u32[]{:S(2)}, u32[]{:S(2)}) collective-permute-start(bf16[128,1024]{1,0:T(8,128)(2,1)S(1)} %get-tuple-element.70), channel_id=1, source_target_pairs={{0,24},{8,16},{16,8},{24,0},{1,25},{9,17},{17,9},{25,1},{2,26},{10... | collective-permute-start | bytes 786440 | tf_op jit(solution)/shard_map/ppermute | solution.py:643
  179.5 12.5 %collective-permute-start.24 = (bf16[128,1024]{1,0:T(8,128)(2,1)S(1)}, bf16[128,1024]{1,0:T(8,128)(2,1)S(1)}, u32[]{:S(2)}, u32[]{:S(2)}) collective-permute-start(bf16[128,1024]{1,0:T(8,128)(2,1)S(1)} %get-tuple-element.69), channel_id=1, source_target_pairs={{0,16},{8,24},{16,0},{24,8},{1,17},{9,25},{17,1},{25,9},{2,18},{10... | collective-permute-start | bytes 786440 | tf_op jit(solution)/shard_map/ppermute | solution.py:643
  180.1 12.0 %collective-permute-start.23 = (bf16[128,1024]{1,0:T(8,128)(2,1)S(1)}, bf16[128,1024]{1,0:T(8,128)(2,1)S(1)}, u32[]{:S(2)}, u32[]{:S(2)}) collective-permute-start(bf16[128,1024]{1,0:T(8,128)(2,1)S(1)} %get-tuple-element.68), channel_id=1, source_target_pairs={{0,8},{8,0},{16,24},{24,16},{1,9},{9,1},{17,25},{25,17},{2,10},{10... | collective-permute-start | bytes 786440 | tf_op jit(solution)/shard_map/ppermute | solution.py:643
  (10 other events, 10.9 us)
Sparse Core Ops, SparseCore 0:
  107.1 35.5 all-gather.1

commit v8 on v7

--- a/solution.py
+++ b/solution.py
@@ -15,6 +15,7 @@
 MARK = jax.ShapeDtypeStruct((8, 128), jnp.float32)
 MARK_SPEC = pl.BlockSpec(MARK.shape, lambda *_: (0, 0))
 ANY_SPEC = pl.BlockSpec(memory_space=pl.ANY)
+LITTLE = pl.CostEstimate(flops=1, bytes_accessed=1, transcendentals=0)
 
 
 def leave(mark):
@@ -281,9 +282,7 @@
             out_specs=[pl.BlockSpec(block, lambda k, *_: (0, k, 0)), MARK_SPEC],
         ),
         compiler_params=pltpu.CompilerParams(vmem_limit_bytes=54 * MIB),
-        cost_estimate=pl.CostEstimate(
-            flops=0, bytes_accessed=2 * (2 * gate.size + out.size), transcendentals=0
-        ),
+        cost_estimate=LITTLE,
         name=f"spread_gate_up_{chunk}",
     )(gate_at, up_at, gate, up, *after)
 
@@ -318,9 +317,7 @@
             ],
         ),
         compiler_params=pltpu.CompilerParams(vmem_limit_bytes=50 * MIB),
-        cost_estimate=pl.CostEstimate(
-            flops=0, bytes_accessed=2 * (values.size + out.size), transcendentals=0
-        ),
+        cost_estimate=LITTLE,
         name="spread_down",
     )(at, values, *after)
 
@@ -355,9 +352,7 @@
         in_specs=[pl.BlockSpec(memory_space=pltpu.VMEM)] * parts + [ANY_SPEC] * len(after),
         out_specs=pl.BlockSpec(memory_space=pltpu.VMEM),
         compiler_params=pltpu.CompilerParams(vmem_limit_bytes=16 * MIB),
-        cost_estimate=pl.CostEstimate(
-            flops=0, bytes_accessed=4 * parts * count * width, transcendentals=0
-        ),
+        cost_estimate=LITTLE,
         name="pack",
     )(*pieces, *after)
 
@@ -381,9 +376,7 @@
         in_specs=[pl.BlockSpec(memory_space=pltpu.VMEM)] * len(pieces) + [ANY_SPEC],
         out_specs=pl.BlockSpec(memory_space=pltpu.VMEM),
         compiler_params=pltpu.CompilerParams(vmem_limit_bytes=16 * MIB),
-        cost_estimate=pl.CostEstimate(
-            flops=0, bytes_accessed=4 * len(pieces) * pieces[0].size, transcendentals=0
-        ),
+        cost_estimate=LITTLE,
         name="stack",
     )(*pieces, after)
 
@@ -407,9 +400,7 @@
         in_specs=[second] * 4 + [ANY_SPEC] * len(after),
         out_specs=[whole, whole, MARK_SPEC],
         compiler_params=pltpu.CompilerParams(vmem_limit_bytes=8 * MIB),
-        cost_estimate=pl.CostEstimate(
-            flops=2 * count * width, bytes_accessed=12 * count * width, transcendentals=0
-        ),
+        cost_estimate=LITTLE,
         name=f"halfway_{chunk}",
     )(kept_a, came_a, kept_b, came_b, *after)
 
@@ -439,11 +430,7 @@
         in_specs=[first, first, whole] * 2 + [ANY_SPEC] * len(after),
         out_specs=[pl.BlockSpec((2 * count, width // 2), lambda i: (0, 0)), MARK_SPEC],
         compiler_params=pltpu.CompilerParams(vmem_limit_bytes=10 * MIB),
-        cost_estimate=pl.CostEstimate(
-            flops=8 * count * width,
-            bytes_accessed=14 * count * width,
-            transcendentals=count * width // 2,
-        ),
+        cost_estimate=LITTLE,
         name=f"combine_{chunk}",
     )(kept_a, came_a, last_a, kept_b, came_b, last_b, *after)
 
@@ -488,12 +475,49 @@
             MARK_SPEC,
         ],
         compiler_params=pltpu.CompilerParams(vmem_limit_bytes=54 * MIB),
-        cost_estimate=pl.CostEstimate(
-            flops=2 * count * depth * width,
-            bytes_accessed=2 * (depth * width + count * (depth + width)),
-            transcendentals=0,
-        ),
+        cost_estimate=LITTLE,
         name=f"gate_up_{chunk}",
+    )(own, other, dense, *after)
+
+
+def panel_half_kernel(own, other, weight, *refs, first):
+    out_a, out_b, mark = refs[-3:]
+    leave(mark)
+    half = own.shape[1]
+    count = own.shape[0] // 2
+    part = pl.program_id(0) + first
+
+    def product(rows):
+        total = jnp.dot(own[rows], weight[0, :half], preferred_element_type=jnp.float32)
+        total += jnp.dot(other[rows], weight[0, half:], preferred_element_type=jnp.float32)
+        return total.astype(out_a.dtype)
+
+    @pl.when(part % 2 == first)
+    def _():
+        out_a[0] = product(slice(0, count))
+
+    @pl.when(part // 2 == first)
+    def _():
+        out_b[0] = product(slice(count, 2 * count))
+
+
+def panel_half(own, other, dense, first, after, chunk):
+    count, half = own.shape
+    _, depth, width = dense.shape
+    tile = width // 4
+    out = jax.ShapeDtypeStruct((2, count // 2, tile), own.dtype)
+    at = pl.BlockSpec((1,) + out.shape[1:], lambda n: ((n // 2 if first else (n + 1) // 2), 0, 0))
+    return pl.pallas_call(
+        functools.partial(panel_half_kernel, first=first),
+        out_shape=[out, out, MARK],
+        grid=(3,),
+        in_specs=[pl.BlockSpec((count, half), lambda n: (0, 0))] * 2
+        + [pl.BlockSpec((1, depth, tile), lambda n: (0, 0, n + first))]
+        + [ANY_SPEC] * len(after),
+        out_specs=[at, at, MARK_SPEC],
+        compiler_params=pltpu.CompilerParams(vmem_limit_bytes=54 * MIB),
+        cost_estimate=LITTLE,
+        name=f"{'sent' if first else 'kept'}_{chunk}",
     )(own, other, dense, *after)
 
 
@@ -551,11 +575,7 @@
             scratch_shapes=[pltpu.VMEM((parts * count, total), hidden.dtype)],
         ),
         compiler_params=pltpu.CompilerParams(vmem_limit_bytes=42 * MIB),
-        cost_estimate=pl.CostEstimate(
-            flops=2 * parts * count * total * width,
-            bytes_accessed=2 * total * (width + parts * count) + 8 * parts * count * width,
-            transcendentals=0,
-        ),
+        cost_estimate=LITTLE,
         name=f"down_{chunk}",
     )(place, hidden, dense, *added)
 
@@ -606,11 +626,7 @@
             out_specs=out_tiles + [MARK_SPEC],
         ),
         compiler_params=pltpu.CompilerParams(vmem_limit_bytes=42 * MIB),
-        cost_estimate=pl.CostEstimate(
-            flops=4 * len(steps) * count * depth * width,
-            bytes_accessed=4 * len(steps) * depth * (width + count) + 8 * count * width,
-            transcendentals=0,
-        ),
+        cost_estimate=LITTLE,
         name=f"down_{chunk}_{steps[0]}",
     )(place, own, other, *[dense] * len(weights), before)
 
@@ -689,7 +705,9 @@
     place = jnp.stack([chip, chip ^ tok, side])
     mixed = [None]
     gathered = []
-    *sums, mark = panel_product(own, other, dense, [], 0)
+    sent_a, sent_b, mark = panel_half(own, other, dense, 1, [], 0)
+    kept_a, kept_b, mark = panel_half(own, other, dense, 0, [mark], 0)
+    sums = kept_a, sent_a, kept_b, sent_b
     if chunks > 1:
         dense, mark = spread(1, [mark])
     for chunk in range(chunks):

time: 201 us -> 202 us (level)
  Pallas kernels: 84.8 us -> 88.4 us
    pallas_call x0 -> x2, Pallas kernels: none -> 17 us  [panel_half(): pl.pallas_call(functools.partial(panel_half_kernel, first=first), out_sha...]
    pallas_call x2 -> x1, Pallas kernels: 23.3 us -> 11.6 us  [panel_product(): pl.pallas_call(panel_product_kernel, out_shape=[out] * 4 + [MARK], grid=(...]
    all_gather x1, waiting for transfers between devices: 3.2 us -> 14.5 us  [by_columns(): gathered.append(lax.all_gather(hidden.reshape(tok_size, count, -1), 'col'))]
    ppermute x11, waiting for transfers between devices: 25 us -> 19.1 us  [swap_tok(): return lax.ppermute(array, 'tok', [(i, i ^ step) for i in parts])]
    ppermute x5, waiting for transfers between devices: 8.91 us -> 3.12 us  [swap_chip(): lax.ppermute(array, 'col', [(i, i ^ 2 * step) for i in range(col_size)])]
    unnamed x30 -> x26, local copies, waits for them, and re-layouts: 8.18 us -> 6.45 us
  transfers between devices with their start and end apart: 27 -> 27, of which waited for: 16 -> 13; matrix products, arithmetic and copies ran while one was open for 2% -> 2% of each run, Pallas kernels for 34% -> 37%
where the time goes in v8:
time: 202 us
  Pallas kernels  88.4 us (44%)
  waiting for transfers between devices  46.8 us (23%)
  starting transfers between devices  40.6 us (20%)
  between operations  13.7 us (7%)
  local copies, waits for them, and re-layouts  8.98 us (4%)
  other arithmetic  3.21 us (2%)
    pallas_call x2, Pallas kernels, spread_shares(): pl.pallas_call(functools.partial(spread_shares_kernel, rows=rows // steps...  24.3 us
    ppermute x11, starting transfers between devices, swap_tok(): return lax.ppermute(array, 'tok', [(i, i ^ step) for i in parts])  23.9 us
    ppermute x11, waiting for transfers between devices, swap_tok(): return lax.ppermute(array, 'tok', [(i, i ^ step) for i in parts])  19.1 us
    pallas_call x2, Pallas kernels, panel_half(): pl.pallas_call(functools.partial(panel_half_kernel, first=first), out_sha...  17 us
    pallas_call x1, Pallas kernels, spread_panels(): pl.pallas_call(functools.partial(spread_panels_kernel, chunks=chunks, row...  16.5 us
    all_gather x1, waiting for transfers between devices, by_columns(): gathered.append(lax.all_gather(hidden.reshape(tok_size, count, -1), 'col'))  14.5 us
    pallas_call x1, Pallas kernels, panel_product(): pl.pallas_call(panel_product_kernel, out_shape=[out] * 4 + [MARK], grid=(...  11.6 us
    pallas_call x2, Pallas kernels, down_steps(): pl.pallas_call(down_steps_kernel, out_shape=out + [MARK], grid_spec=pltpu...  9.82 us
  transfers between devices with their start and end apart: 27, of which 13 were waited for; matrix products, arithmetic and copies ran while one was open for 2% of the time, Pallas kernels for 37%

profile of v8, /device:TPU:0, one launch (start us, length us, event | category | flops | bytes accessed | tf_op | source)
XLA Modules:
  0.0 201.7 jit_solution(14828426173244960688)
XLA Ops:
  9.3 4.7 %collective-permute-start.3 = (f32[1,128]{1,0:T(1,128)S(1)}, f32[1,128]{1,0:T(1,128)S(1)}, u32[]{:S(2)}, u32[]{:S(2)}) collective-permute-start(f32[1,128]{1,0:T(1,128)S(1)} %add.90), channel_id=1, source_target_pairs={{0,6},{1,7},{2,4},{3,5},{4,2},{5,3},{6,0},{7,1},{8,14},{9,15},{10,... | collective-permute-start | bytes 1544 | tf_op jit(solution)/shard_map/ppermute | solution.py:662
  15.6 2.0 %collective-permute-done.1 = f32[1,128]{1,0:T(1,128)S(1)} collective-permute-done((f32[1,128]{1,0:T(1,128)S(1)}, f32[1,128]{1,0:T(1,128)S(1)}, u32[]{:S(2)}, u32[]{:S(2)}) %collective-permute-start.1) | collective-permute-done | bytes 544 | tf_op jit(solution)/shard_map/ppermute | solution.py:662
  18.5 1.1 multiply_convert_fusion
  20.3 4.2 %collective-permute-start.5 = (bf16[128,1024]{1,0:T(8,128)(2,1)S(1)}, bf16[128,1024]{1,0:T(8,128)(2,1)S(1)}, u32[]{:S(2)}, u32[]{:S(2)}) collective-permute-start(bf16[128,1024]{1,0:T(8,128)(2,1)S(1)} %multiply_convert_fusion), channel_id=1, source_target_pairs={{0,2},{1,3},{2,10},{3,11},{4,18},{5,19},{6,26},{7,27},{8,0},{9,1},... | collective-permute-start | bytes 786440 | tf_op jit(solution)/shard_map/ppermute | solution.py:673
  24.5 1.7 collective-permute-start.6
  26.2 1.6 collective-permute-start.7
  29.3 12.1 %spread_gate_up_0.1 = (bf16[1,2048,3072]{2,1,0:T(8,128)(2,1)}, f32[8,128]{1,0:T(8,128)}) custom-call(s32[192]{0:T(256)} %get-tuple-element.79.gate_at, s32[192]{0:T(256)} %get-tuple-element.76.up_at, bf16[1,216,128,128]{3,2,1,0:T(8,128)(2,1)} %refs_0_.3, bf16[1,216,128,128]{3,2,1,0:T(8,128)(2,1)} %refs_1_.3), custom_call_target="tpu_custom_call" | custom-call | flops 1 | bytes 1 | tf_op jit(solution)/shard_map/spread_gate_up_0/pallas_call | solution.py:275
  42.3 2.6 %collective-permute-done.8.other = bf16[512,1024]{1,0:T(8,128)(2,1)S(1)} collective-permute-done((bf16[512,1024]{1,0:T(8,128)(2,1)S(1)}, bf16[512,1024]{1,0:T(8,128)(2,1)S(1)}, u32[]{:S(2)}, u32[]{:S(2)}) %collective-permute-start.8) | collective-permute-done | bytes 1048608 | tf_op jit(solution)/shard_map/ppermute | solution.py:665
  45.9 8.3 %sent_0.1 = (bf16[2,256,768]{2,1,0:T(8,128)(2,1)}, bf16[2,256,768]{2,1,0:T(8,128)(2,1)}, f32[8,128]{1,0:T(8,128)}) custom-call(bf16[512,1024]{1,0:T(8,128)(2,1)} %copy-done, bf16[512,1024]{1,0:T(8,128)(2,1)} %copy-done.11, bf16[1,2048,3072]{2,1,0:T(8,128)(2,1)} %get-tuple-element.40.weight), custom_call_target="tpu_custom_call" | custom-call | flops 1 | bytes 1 | tf_op jit(solution)/shard_map/sent_0/pallas_call | solution.py:510
  54.3 1.5 collective-permute-start.9
  55.7 11.3 %collective-permute-start.10 = (bf16[2,256,768]{2,1,0:T(8,128)(2,1)}, bf16[2,256,768]{2,1,0:T(8,128)(2,1)S(1)}, u32[]{:S(2)}, u32[]{:S(2)}) collective-permute-start(bf16[2,256,768]{2,1,0:T(8,128)(2,1)} %get-tuple-element.47), channel_id=1, source_target_pairs={{0,16},{8,24},{16,0},{24,8},{1,17},{9,25},{17,1},{25,9},{2,18},{10... | collective-permute-start | bytes 2359304 | tf_op jit(solution)/shard_map/ppermute | solution.py:659
  67.1 8.6 %kept_0.1 = (bf16[2,256,768]{2,1,0:T(8,128)(2,1)}, bf16[2,256,768]{2,1,0:T(8,128)(2,1)}, f32[8,128]{1,0:T(8,128)}) custom-call(bf16[512,1024]{1,0:T(8,128)(2,1)} %copy-done, bf16[512,1024]{1,0:T(8,128)(2,1)} %copy-done.11, bf16[1,2048,3072]{2,1,0:T(8,128)(2,1)} %get-tuple-element.40.weight, f32[8,128]{1,0:T(8,128)} %get-tuple-element.41.refs_0_), custom_call_target="tpu_custom_call" | custom-call | flops 1 | bytes 1 | tf_op jit(solution)/shard_map/kept_0/pallas_call | solution.py:510
  75.7 12.2 %spread_gate_up_1.1 = (bf16[1,2048,3072]{2,1,0:T(8,128)(2,1)}, f32[8,128]{1,0:T(8,128)}) custom-call(s32[192]{0:T(256)} %get-tuple-element.80.gate_at, s32[192]{0:T(256)} %get-tuple-element.75.up_at, bf16[1,216,128,128]{3,2,1,0:T(8,128)(2,1)} %refs_0_.3, bf16[1,216,128,128]{3,2,1,0:T(8,128)(2,1)} %refs_1_.3, f32[8,128]{1,0:T(8,128)} %get-tuple-element.42.refs_2_), custom_call_target="tpu_custom_call" | custom-call | flops 1 | bytes 1 | tf_op jit(solution)/shard_map/spread_gate_up_1/pallas_call | solution.py:275
  89.5 2.0 collective-permute-start.14
  91.4 11.6 %gate_up_1.1 = (bf16[2,256,768]{2,1,0:T(8,128)(2,1)}, bf16[2,256,768]{2,1,0:T(8,128)(2,1)}, bf16[2,256,768]{2,1,0:T(8,128)(2,1)}, bf16[2,256,768]{2,1,0:T(8,128)(2,1)}, f32[8,128]{1,0:T(8,128)}) custom-call(bf16[512,1024]{1,0:T(8,128)(2,1)} %copy-done, bf16[512,1024]{1,0:T(8,128)(2,1)} %copy-done.11, bf16[1,2048,3072]{2,1,0:T(8,128)(2,1)} %get-tuple-element.43.weight, ...), custom_call_target="tpu_custom_call" | custom-call | flops 1 | bytes 1 | tf_op jit(solution)/shard_map/gate_up_1/pallas_call | solution.py:463
  103.8 1.2 combine_0.1
  105.1 2.0 %collective-permute-start.12 = (bf16[2,256,768]{2,1,0:T(8,128)(2,1)}, bf16[2,256,768]{2,1,0:T(8,128)(2,1)S(1)}, u32[]{:S(2)}, u32[]{:S(2)}) collective-permute-start(bf16[2,256,768]{2,1,0:T(8,128)(2,1)} %get-tuple-element.53), channel_id=1, source_target_pairs={{0,16},{8,24},{16,0},{24,8},{1,17},{9,25},{17,1},{25,9},{2,18},{10... | collective-permute-start | bytes 2359304 | tf_op jit(solution)/shard_map/ppermute | solution.py:659
  107.5 16.5 %spread_down.1 = (bf16[2,3072,1024]{2,1,0:T(8,128)(2,1)}, f32[8,128]{1,0:T(8,128)S(1)}) custom-call(s32[384]{0:T(512)S(1)} %reshape.88.at_ref, bf16[8,108,128,128]{3,2,1,0:T(8,128)(2,1)} %values_ref.1, f32[8,128]{1,0:T(8,128)S(1)} %get-tuple-element.57.refs_0_), custom_call_target="tpu_custom_call" | custom-call | flops 1 | bytes 1 | tf_op jit(solution)/shard_map/spread_down/pallas_call | solution.py:304
  124.3 1.8 collective-permute-start.15
  126.1 1.7 collective-permute-start.16
  127.7 6.4 %collective-permute-done.15.refs_2_ = bf16[256,768]{1,0:T(8,128)(2,1)S(1)} collective-permute-done((bf16[256,768]{1,0:T(8,128)(2,1)S(1)}, bf16[256,768]{1,0:T(8,128)(2,1)S(1)}, u32[]{:S(2)}, u32[]{:S(2)}) %collective-permute-start.15) | collective-permute-done | bytes 393248 | tf_op jit(solution)/shard_map/ppermute | solution.py:659
  135.9 14.5 %all-gather.2.cloned.1.call-done.hidden = bf16[8,4,128,384]{3,2,1,0:T(8,128)(2,1)} async-done(((bf16[1,4,128,384]{3,2,1,0:T(8,128)(2,1)}), bf16[8,4,128,384]{3,2,1,0:T(8,128)(2,1)}) %all-gather.2.cloned.1.call-update) | async-done | bytes 3145744 | tf_op jit(solution)/shard_map/all_gather | solution.py:728
  150.4 1.9 copy-done.1
  152.3 6.4 %down_0.1 = (f32[512,1024]{1,0:T(8,128)S(1)}, f32[8,128]{1,0:T(8,128)S(1)}) custom-call(s32[3]{0:T(128)S(1)} %pad_add_fusion.place, bf16[8,4,128,384]{3,2,1,0:T(8,128)(2,1)S(1)} %copy-done.1, bf16[2,3072,1024]{2,1,0:T(8,128)(2,1)} %get-tuple-element.64.weight), custom_call_target="tpu_custom_call" | custom-call | flops 1 | bytes 1 | tf_op jit(solution)/shard_map/down_0/pallas_call | solution.py:563
  159.9 1.5 collective-permute-start.19
  161.8 6.0 %down_1_0.1 = (f32[512,1024]{1,0:T(8,128)S(1)}, f32[8,128]{1,0:T(8,128)S(1)}) custom-call(s32[3]{0:T(128)S(1)} %pad_add_fusion.place, bf16[3,512,384]{2,1,0:T(8,128)(2,1)S(1)} %stack.18.own, bf16[3,512,384]{2,1,0:T(8,128)(2,1)S(1)} %collective-permute-done.21.other, bf16[2,8,384,1024]{3,2,1,0:T(8,128)(2,1)} %bitcast.9, bf16[2,8,384,1024]{3,2,1,0:T(8,128)(2,1)} %bitcast.10, ...), custom_call_target="tpu_custom_call" | custom-call | flops 1 | bytes 1 | tf_op jit(solution)/shard_map/down_1_0/pallas_call | solution.py:619
  167.8 5.2 %collective-permute-done.19.refs_1_ = bf16[512,384]{1,0:T(8,128)(2,1)S(1)} collective-permute-done((bf16[512,384]{1,0:T(8,128)(2,1)S(1)}, bf16[512,384]{1,0:T(8,128)(2,1)S(1)}, u32[]{:S(2)}, u32[]{:S(2)}) %collective-permute-start.19) | collective-permute-done | bytes 393248 | tf_op jit(solution)/shard_map/ppermute | solution.py:733
  173.2 1.7 collective-permute-done.22.other
  174.9 3.8 %down_1_3.1 = (bf16[128,1024]{1,0:T(8,128)(2,1)S(1)}, bf16[128,1024]{1,0:T(8,128)(2,1)S(1)}, bf16[128,1024]{1,0:T(8,128)(2,1)S(1)}, bf16[128,1024]{1,0:T(8,128)(2,1)S(1)}, f32[8,128]{1,0:T(8,128)}) custom-call(s32[3]{0:T(128)S(1)} %pad_add_fusion.place, bf16[1,512,384]{2,1,0:T(8,128)(2,1)S(1)} %stack.19.own, ...), custom_call_target="tpu_custom_call" | custom-call | flops 1 | bytes 1 | tf_op jit(solution)/shard_map/down_1_3/pallas_call | solution.py:619
  178.7 2.8 %collective-permute-start.25 = (bf16[128,1024]{1,0:T(8,128)(2,1)S(1)}, bf16[128,1024]{1,0:T(8,128)(2,1)S(1)}, u32[]{:S(2)}, u32[]{:S(2)}) collective-permute-start(bf16[128,1024]{1,0:T(8,128)(2,1)S(1)} %get-tuple-element.72), channel_id=1, source_target_pairs={{0,24},{8,16},{16,8},{24,0},{1,25},{9,17},{17,9},{25,1},{2,26},{10... | collective-permute-start | bytes 786440 | tf_op jit(solution)/shard_map/ppermute | solution.py:659
  182.2 6.6 %collective-permute-done.25 = bf16[128,1024]{1,0:T(8,128)(2,1)S(1)} collective-permute-done((bf16[128,1024]{1,0:T(8,128)(2,1)S(1)}, bf16[128,1024]{1,0:T(8,128)(2,1)S(1)}, u32[]{:S(2)}, u32[]{:S(2)}) %collective-permute-start.25) | collective-permute-done | bytes 262176 | tf_op jit(solution)/shard_map/ppermute | solution.py:659
  188.8 4.9 %collective-permute-done.24 = bf16[128,1024]{1,0:T(8,128)(2,1)S(1)} collective-permute-done((bf16[128,1024]{1,0:T(8,128)(2,1)S(1)}, bf16[128,1024]{1,0:T(8,128)(2,1)S(1)}, u32[]{:S(2)}, u32[]{:S(2)}) %collective-permute-start.24) | collective-permute-done | bytes 262176 | tf_op jit(solution)/shard_map/ppermute | solution.py:659
  (89 shorter events, 17.4 us)
Async XLA Ops:
  6.5 143.9 %all-gather.2.cloned.1.call-start = ((), (), s32[]{:S(2)}) async-start(), calls=%async_computation | async-start | bytes 3538944 | tf_op jit(solution)/shard_map/all_gather | solution.py:728
  7.6 1.7 collective-permute-start
  9.3 6.2 %collective-permute-start.3 = (f32[1,128]{1,0:T(1,128)S(1)}, f32[1,128]{1,0:T(1,128)S(1)}, u32[]{:S(2)}, u32[]{:S(2)}) collective-permute-start(f32[1,128]{1,0:T(1,128)S(1)} %add.90), channel_id=1, source_target_pairs={{0,6},{1,7},{2,4},{3,5},{4,2},{5,3},{6,0},{7,1},{8,14},{9,15},{10,... | collective-permute-start | bytes 1544 | tf_op jit(solution)/shard_map/ppermute | solution.py:662
  14.0 3.5 %collective-permute-start.1 = (f32[1,128]{1,0:T(1,128)S(1)}, f32[1,128]{1,0:T(1,128)S(1)}, u32[]{:S(2)}, u32[]{:S(2)}) collective-permute-start(f32[1,128]{1,0:T(1,128)S(1)} %add.90), channel_id=1, source_target_pairs={{0,2},{1,3},{2,0},{3,1},{4,6},{5,7},{6,4},{7,5},{8,10},{9,11},{10,... | collective-permute-start | bytes 1544 | tf_op jit(solution)/shard_map/ppermute | solution.py:662
  14.0 4.4 %collective-permute-start.2 = (f32[1,128]{1,0:T(1,128)S(1)}, f32[1,128]{1,0:T(1,128)S(1)}, u32[]{:S(2)}, u32[]{:S(2)}) collective-permute-start(f32[1,128]{1,0:T(1,128)S(1)} %add.90), channel_id=1, source_target_pairs={{0,4},{1,5},{2,6},{3,7},{4,0},{5,1},{6,2},{7,3},{8,12},{9,13},{10,... | collective-permute-start | bytes 1544 | tf_op jit(solution)/shard_map/ppermute | solution.py:662
  19.6 21.9 %collective-permute-start.4 = (bf16[128,1024]{1,0:T(8,128)(2,1)S(1)}, bf16[128,1024]{1,0:T(8,128)(2,1)S(1)}, u32[]{:S(2)}, u32[]{:S(2)}) collective-permute-start(bf16[128,1024]{1,0:T(8,128)(2,1)S(1)} %multiply_convert_fusion), channel_id=1, source_target_pairs={{0,0},{1,1},{2,8},{3,9},{4,16},{5,17},{6,24},{7,25},{8,2},{9,3},{1... | collective-permute-start | bytes 786440 | tf_op jit(solution)/shard_map/ppermute | solution.py:673
  20.3 21.2 %collective-permute-start.5 = (bf16[128,1024]{1,0:T(8,128)(2,1)S(1)}, bf16[128,1024]{1,0:T(8,128)(2,1)S(1)}, u32[]{:S(2)}, u32[]{:S(2)}) collective-permute-start(bf16[128,1024]{1,0:T(8,128)(2,1)S(1)} %multiply_convert_fusion), channel_id=1, source_target_pairs={{0,2},{1,3},{2,10},{3,11},{4,18},{5,19},{6,26},{7,27},{8,0},{9,1},... | collective-permute-start | bytes 786440 | tf_op jit(solution)/shard_map/ppermute | solution.py:673
  24.5 16.9 %collective-permute-start.6 = (bf16[128,1024]{1,0:T(8,128)(2,1)S(1)}, bf16[128,1024]{1,0:T(8,128)(2,1)S(1)}, u32[]{:S(2)}, u32[]{:S(2)}) collective-permute-start(bf16[128,1024]{1,0:T(8,128)(2,1)S(1)} %multiply_convert_fusion), channel_id=1, source_target_pairs={{0,4},{1,5},{2,12},{3,13},{4,20},{5,21},{6,28},{7,29},{8,6},{9,7},... | collective-permute-start | bytes 786440 | tf_op jit(solution)/shard_map/ppermute | solution.py:673
  26.2 15.3 %collective-permute-start.7 = (bf16[128,1024]{1,0:T(8,128)(2,1)S(1)}, bf16[128,1024]{1,0:T(8,128)(2,1)S(1)}, u32[]{:S(2)}, u32[]{:S(2)}) collective-permute-start(bf16[128,1024]{1,0:T(8,128)(2,1)S(1)} %multiply_convert_fusion), channel_id=1, source_target_pairs={{0,6},{1,7},{2,14},{3,15},{4,22},{5,23},{6,30},{7,31},{8,4},{9,5},... | collective-permute-start | bytes 786440 | tf_op jit(solution)/shard_map/ppermute | solution.py:673
  42.2 2.7 %collective-permute-start.8 = (bf16[512,1024]{1,0:T(8,128)(2,1)S(1)}, bf16[512,1024]{1,0:T(8,128)(2,1)S(1)}, u32[]{:S(2)}, u32[]{:S(2)}) collective-permute-start(bf16[512,1024]{1,0:T(8,128)(2,1)S(1)} %pack.1.own), channel_id=1, source_target_pairs={{0,1},{1,0},{2,3},{3,2},{4,5},{5,4},{6,7},{7,6},{8,9},{9,8},{10,11... | collective-permute-start | bytes 3145736 | tf_op jit(solution)/shard_map/ppermute | solution.py:665
  54.3 33.7 %collective-permute-start.9 = (bf16[2,256,768]{2,1,0:T(8,128)(2,1)}, bf16[2,256,768]{2,1,0:T(8,128)(2,1)S(1)}, u32[]{:S(2)}, u32[]{:S(2)}) collective-permute-start(bf16[2,256,768]{2,1,0:T(8,128)(2,1)} %get-tuple-element.45), channel_id=1, source_target_pairs={{0,8},{8,0},{16,24},{24,16},{1,9},{9,1},{17,25},{25,17},{2,10},{10... | collective-permute-start | bytes 2359304 | tf_op jit(solution)/shard_map/ppermute | solution.py:659
  55.7 32.2 %collective-permute-start.10 = (bf16[2,256,768]{2,1,0:T(8,128)(2,1)}, bf16[2,256,768]{2,1,0:T(8,128)(2,1)S(1)}, u32[]{:S(2)}, u32[]{:S(2)}) collective-permute-start(bf16[2,256,768]{2,1,0:T(8,128)(2,1)} %get-tuple-element.47), channel_id=1, source_target_pairs={{0,16},{8,24},{16,0},{24,8},{1,17},{9,25},{17,1},{25,9},{2,18},{10... | collective-permute-start | bytes 2359304 | tf_op jit(solution)/shard_map/ppermute | solution.py:659
  75.7 12.2 %copy-start.4 = (bf16[2,256,768]{2,1,0:T(8,128)(2,1)S(1)}, bf16[2,256,768]{2,1,0:T(8,128)(2,1)}, u32[]{:S(2)}) copy-start(bf16[2,256,768]{2,1,0:T(8,128)(2,1)} %get-tuple-element.44.kept_a.refs_0_) | copy-start | bytes 2359300
  75.7 12.2 %copy-start.5 = (bf16[2,256,768]{2,1,0:T(8,128)(2,1)S(1)}, bf16[2,256,768]{2,1,0:T(8,128)(2,1)}, u32[]{:S(2)}) copy-start(bf16[2,256,768]{2,1,0:T(8,128)(2,1)} %get-tuple-element.46.kept_b.refs_3_) | copy-start | bytes 2359300
  89.4 13.7 %collective-permute-start.13 = (bf16[256,768]{1,0:T(8,128)(2,1)S(1)}, bf16[256,768]{1,0:T(8,128)(2,1)S(1)}, u32[]{:S(2)}, u32[]{:S(2)}) collective-permute-start(bf16[256,768]{1,0:T(8,128)(2,1)S(1)} %get-tuple-element.54), channel_id=1, source_target_pairs={{0,16},{8,24},{16,0},{24,8},{1,17},{9,25},{17,1},{25,9},{2,18},{10... | collective-permute-start | bytes 1179656 | tf_op jit(solution)/shard_map/ppermute | solution.py:659
  89.5 13.6 %collective-permute-start.14 = (bf16[256,768]{1,0:T(8,128)(2,1)S(1)}, bf16[256,768]{1,0:T(8,128)(2,1)S(1)}, u32[]{:S(2)}, u32[]{:S(2)}) collective-permute-start(bf16[256,768]{1,0:T(8,128)(2,1)S(1)} %get-tuple-element.55), channel_id=1, source_target_pairs={{0,8},{8,0},{16,24},{24,16},{1,9},{9,1},{17,25},{25,17},{2,10},{10... | collective-permute-start | bytes 1179656 | tf_op jit(solution)/shard_map/ppermute | solution.py:659
  91.4 15.7 %copy-start.12 = (s32[8,108]{1,0:T(8,128)S(1)}, s32[8,108]{1,0:T(8,128)}, u32[]{:S(2)}) copy-start(s32[8,108]{1,0:T(8,128)} %param.15) | copy-start | bytes 10372
  105.0 19.1 %collective-permute-start.11 = (bf16[2,256,768]{2,1,0:T(8,128)(2,1)}, bf16[2,256,768]{2,1,0:T(8,128)(2,1)S(1)}, u32[]{:S(2)}, u32[]{:S(2)}) collective-permute-start(bf16[2,256,768]{2,1,0:T(8,128)(2,1)} %get-tuple-element.51), channel_id=1, source_target_pairs={{0,8},{8,0},{16,24},{24,16},{1,9},{9,1},{17,25},{25,17},{2,10},{10... | collective-permute-start | bytes 2359304 | tf_op jit(solution)/shard_map/ppermute | solution.py:659
  105.1 19.0 %collective-permute-start.12 = (bf16[2,256,768]{2,1,0:T(8,128)(2,1)}, bf16[2,256,768]{2,1,0:T(8,128)(2,1)S(1)}, u32[]{:S(2)}, u32[]{:S(2)}) collective-permute-start(bf16[2,256,768]{2,1,0:T(8,128)(2,1)} %get-tuple-element.53), channel_id=1, source_target_pairs={{0,16},{8,24},{16,0},{24,8},{1,17},{9,25},{17,1},{25,9},{2,18},{10... | collective-permute-start | bytes 2359304 | tf_op jit(solution)/shard_map/ppermute | solution.py:659
  107.5 16.6 %copy-start.2 = (bf16[2,256,768]{2,1,0:T(8,128)(2,1)S(1)}, bf16[2,256,768]{2,1,0:T(8,128)(2,1)}, u32[]{:S(2)}) copy-start(bf16[2,256,768]{2,1,0:T(8,128)(2,1)} %get-tuple-element.50.kept_a.refs_0_) | copy-start | bytes 2359300
  107.5 16.6 %copy-start.3 = (bf16[2,256,768]{2,1,0:T(8,128)(2,1)S(1)}, bf16[2,256,768]{2,1,0:T(8,128)(2,1)}, u32[]{:S(2)}) copy-start(bf16[2,256,768]{2,1,0:T(8,128)(2,1)} %get-tuple-element.52.kept_b.refs_3_) | copy-start | bytes 2359300
  124.3 9.9 %collective-permute-start.15 = (bf16[256,768]{1,0:T(8,128)(2,1)S(1)}, bf16[256,768]{1,0:T(8,128)(2,1)S(1)}, u32[]{:S(2)}, u32[]{:S(2)}) collective-permute-start(bf16[256,768]{1,0:T(8,128)(2,1)S(1)} %get-tuple-element.59), channel_id=1, source_target_pairs={{0,16},{8,24},{16,0},{24,8},{1,17},{9,25},{17,1},{25,9},{2,18},{10... | collective-permute-start | bytes 1179656 | tf_op jit(solution)/shard_map/ppermute | solution.py:659
  126.1 8.9 %collective-permute-start.16 = (bf16[256,768]{1,0:T(8,128)(2,1)S(1)}, bf16[256,768]{1,0:T(8,128)(2,1)S(1)}, u32[]{:S(2)}, u32[]{:S(2)}) collective-permute-start(bf16[256,768]{1,0:T(8,128)(2,1)S(1)} %get-tuple-element.60), channel_id=1, source_target_pairs={{0,8},{8,0},{16,24},{24,16},{1,9},{9,1},{17,25},{25,17},{2,10},{10... | collective-permute-start | bytes 1179656 | tf_op jit(solution)/shard_map/ppermute | solution.py:659
  135.8 22.9 %collective-permute-start.18 = (bf16[512,384]{1,0:T(8,128)(2,1)S(1)}, bf16[512,384]{1,0:T(8,128)(2,1)S(1)}, u32[]{:S(2)}, u32[]{:S(2)}) collective-permute-start(bf16[512,384]{1,0:T(8,128)(2,1)S(1)} %get-tuple-element.62.refs_0_), channel_id=1, source_target_pairs={{0,4},{1,5},{2,6},{3,7},{4,0},{5,1},{6,2},{7,3},{8,12},{9,13},{10,... | collective-permute-start | bytes 1179656 | tf_op jit(solution)/shard_map/ppermute | solution.py:662
  135.8 22.9 %collective-permute-start.20 = (bf16[512,384]{1,0:T(8,128)(2,1)S(1)}, bf16[512,384]{1,0:T(8,128)(2,1)S(1)}, u32[]{:S(2)}, u32[]{:S(2)}) collective-permute-start(bf16[512,384]{1,0:T(8,128)(2,1)S(1)} %get-tuple-element.62.refs_0_), channel_id=1, source_target_pairs={{0,2},{1,3},{2,0},{3,1},{4,6},{5,7},{6,4},{7,5},{8,10},{9,11},{10,... | collective-permute-start | bytes 1179656 | tf_op jit(solution)/shard_map/ppermute | solution.py:662
  158.9 2.9 %collective-permute-start.21 = (bf16[3,512,384]{2,1,0:T(8,128)(2,1)S(1)}, bf16[3,512,384]{2,1,0:T(8,128)(2,1)S(1)}, u32[]{:S(2)}, u32[]{:S(2)}) collective-permute-start(bf16[3,512,384]{2,1,0:T(8,128)(2,1)S(1)} %stack.18.own), channel_id=1, source_target_pairs={{0,1},{1,0},{2,3},{3,2},{4,5},{5,4},{6,7},{7,6},{8,9},{9,8},{10,11... | collective-permute-start | bytes 3538952 | tf_op jit(solution)/shard_map/ppermute | solution.py:665
  159.2 8.6 %collective-permute-start.17 = (bf16[512,384]{1,0:T(8,128)(2,1)S(1)}, bf16[512,384]{1,0:T(8,128)(2,1)S(1)}, u32[]{:S(2)}, u32[]{:S(2)}) collective-permute-start(bf16[512,384]{1,0:T(8,128)(2,1)S(1)} %get-tuple-element.62.refs_0_), channel_id=1, source_target_pairs={{2,4},{3,5},{4,2},{5,3},{10,12},{11,13},{12,10},{13,11},{18,20},{1... | collective-permute-start | bytes 1179656 | tf_op jit(solution)/shard_map/ppermute | solution.py:732
  159.9 13.2 %collective-permute-start.19 = (bf16[512,384]{1,0:T(8,128)(2,1)S(1)}, bf16[512,384]{1,0:T(8,128)(2,1)S(1)}, u32[]{:S(2)}, u32[]{:S(2)}) collective-permute-start(bf16[512,384]{1,0:T(8,128)(2,1)S(1)} %collective-permute-done.18.refs_2_), channel_id=1, source_target_pairs={{2,0},{3,1},{4,6},{5,7},{10,8},{11,9},{12,14},{13,15},{18,16},{19,... | collective-permute-start | bytes 1179656 | tf_op jit(solution)/shard_map/ppermute | solution.py:733
  173.1 1.8 collective-permute-start.22
  178.7 10.1 %collective-permute-start.25 = (bf16[128,1024]{1,0:T(8,128)(2,1)S(1)}, bf16[128,1024]{1,0:T(8,128)(2,1)S(1)}, u32[]{:S(2)}, u32[]{:S(2)}) collective-permute-start(bf16[128,1024]{1,0:T(8,128)(2,1)S(1)} %get-tuple-element.72), channel_id=1, source_target_pairs={{0,24},{8,16},{16,8},{24,0},{1,25},{9,17},{17,9},{25,1},{2,26},{10... | collective-permute-start | bytes 786440 | tf_op jit(solution)/shard_map/ppermute | solution.py:659
  181.5 12.2 %collective-permute-start.24 = (bf16[128,1024]{1,0:T(8,128)(2,1)S(1)}, bf16[128,1024]{1,0:T(8,128)(2,1)S(1)}, u32[]{:S(2)}, u32[]{:S(2)}) collective-permute-start(bf16[128,1024]{1,0:T(8,128)(2,1)S(1)} %get-tuple-element.71), channel_id=1, source_target_pairs={{0,16},{8,24},{16,0},{24,8},{1,17},{9,25},{17,1},{25,9},{2,18},{10... | collective-permute-start | bytes 786440 | tf_op jit(solution)/shard_map/ppermute | solution.py:659
  181.8 12.2 %collective-permute-start.23 = (bf16[128,1024]{1,0:T(8,128)(2,1)S(1)}, bf16[128,1024]{1,0:T(8,128)(2,1)S(1)}, u32[]{:S(2)}, u32[]{:S(2)}) collective-permute-start(bf16[128,1024]{1,0:T(8,128)(2,1)S(1)} %get-tuple-element.70), channel_id=1, source_target_pairs={{0,8},{8,0},{16,24},{24,16},{1,9},{9,1},{17,25},{25,17},{2,10},{10... | collective-permute-start | bytes 786440 | tf_op jit(solution)/shard_map/ppermute | solution.py:659
  (8 other events, 9.2 us)
Sparse Core Ops, SparseCore 0:
  105.1 45.2 all-gather.1

commit v9 on v8

--- a/solution.py
+++ b/solution.py
@@ -358,7 +358,8 @@
 
 
 def stack_kernel(*refs, steps):
-    pieces, out = refs[:-2], refs[-1]
+    pieces, out, mark = refs[:-3], refs[-2], refs[-1]
+    leave(mark)
     count = out.shape[1] // 4
     for i, step in enumerate(steps):
         for part in range(4):
@@ -372,9 +373,9 @@
 def stack(pieces, steps, after):
     return pl.pallas_call(
         functools.partial(stack_kernel, steps=steps),
-        out_shape=jax.ShapeDtypeStruct((len(steps),) + pieces[0].shape, pieces[0].dtype),
+        out_shape=[jax.ShapeDtypeStruct((len(steps),) + pieces[0].shape, pieces[0].dtype), MARK],
         in_specs=[pl.BlockSpec(memory_space=pltpu.VMEM)] * len(pieces) + [ANY_SPEC],
-        out_specs=pl.BlockSpec(memory_space=pltpu.VMEM),
+        out_specs=[pl.BlockSpec(memory_space=pltpu.VMEM)] * 2,
         compiler_params=pltpu.CompilerParams(vmem_limit_bytes=16 * MIB),
         cost_estimate=LITTLE,
         name="stack",
@@ -480,115 +481,18 @@
     )(own, other, dense, *after)
 
 
-def panel_half_kernel(own, other, weight, *refs, first):
-    out_a, out_b, mark = refs[-3:]
+def down_steps_kernel(place, own, other, *refs, added, outputs):
+    pieces = 2 * own.shape[0]
+    weights, before = refs[:pieces], refs[pieces:pieces + added]
+    outs, mark = refs[-1 - outputs:-1], refs[-1]
     leave(mark)
-    half = own.shape[1]
-    count = own.shape[0] // 2
-    part = pl.program_id(0) + first
-
-    def product(rows):
-        total = jnp.dot(own[rows], weight[0, :half], preferred_element_type=jnp.float32)
-        total += jnp.dot(other[rows], weight[0, half:], preferred_element_type=jnp.float32)
-        return total.astype(out_a.dtype)
-
-    @pl.when(part % 2 == first)
-    def _():
-        out_a[0] = product(slice(0, count))
-
-    @pl.when(part // 2 == first)
-    def _():
-        out_b[0] = product(slice(count, 2 * count))
-
-
-def panel_half(own, other, dense, first, after, chunk):
-    count, half = own.shape
-    _, depth, width = dense.shape
-    tile = width // 4
-    out = jax.ShapeDtypeStruct((2, count // 2, tile), own.dtype)
-    at = pl.BlockSpec((1,) + out.shape[1:], lambda n: ((n // 2 if first else (n + 1) // 2), 0, 0))
-    return pl.pallas_call(
-        functools.partial(panel_half_kernel, first=first),
-        out_shape=[out, out, MARK],
-        grid=(3,),
-        in_specs=[pl.BlockSpec((count, half), lambda n: (0, 0))] * 2
-        + [pl.BlockSpec((1, depth, tile), lambda n: (0, 0, n + first))]
-        + [ANY_SPEC] * len(after),
-        out_specs=[at, at, MARK_SPEC],
-        compiler_params=pltpu.CompilerParams(vmem_limit_bytes=54 * MIB),
-        cost_estimate=LITTLE,
-        name=f"{'sent' if first else 'kept'}_{chunk}",
-    )(own, other, dense, *after)
-
-
-def down_product_kernel(place, hidden, weight, *refs, added):
-    before, outs, mark, held = refs[:added], refs[added:-2], refs[-2], refs[-1]
-    leave(mark)
-    panels, parts, count, depth = hidden.shape
-    chip, flips = place[0], place[1]
-
-    @pl.when(pl.program_id(0) == 0)
-    def _():
-        for panel in range(panels):
-            columns = slice(panel * depth, (panel + 1) * depth)
-            for part in range(parts):
-                there = part ^ chip ^ (panel // 2)
-                held[part * count:(part + 1) * count, columns] = hidden[panel, there]
-
-    if len(outs) == 1:
-        product = jnp.dot(held[...], weight[0], preferred_element_type=jnp.float32)
-        for term in before:
-            product += term[...]
-        outs[0][...] = product
-        return
-    for step, out in enumerate(outs):
-        rows = pl.ds(pl.multiple_of((flips ^ step) * count, count), count)
-        product = jnp.dot(held[rows], weight[0], preferred_element_type=jnp.float32)
-        for term in before:
-            product += term[rows]
-        out[...] = product.astype(out.dtype)
-
-
-def down_product(place, hidden, dense, before, chunk, last):
-    panels, parts, count, depth = hidden.shape
-    _, total, width = dense.shape
-    tile = width // 2
-    tiles = pl.BlockSpec((parts * count, tile), lambda n, *_: (0, n))
-    added = [] if before is None else [before]
-    if last:
-        out = [jax.ShapeDtypeStruct((count, width), hidden.dtype)] * parts
-        out_tiles = [pl.BlockSpec((count, tile), lambda n, *_: (0, n))] * parts
-    else:
-        out, out_tiles = [jax.ShapeDtypeStruct((parts * count, width), jnp.float32)], [tiles]
-    return pl.pallas_call(
-        functools.partial(down_product_kernel, added=len(added)),
-        out_shape=out + [MARK],
-        grid_spec=pltpu.PrefetchScalarGridSpec(
-            num_scalar_prefetch=1,
-            grid=(width // tile,),
-            in_specs=[
-                pl.BlockSpec(hidden.shape, lambda n, *_: (0, 0, 0, 0)),
-                pl.BlockSpec((1, total, tile), lambda n, *_: (chunk, 0, n)),
-            ]
-            + [tiles] * len(added),
-            out_specs=out_tiles + [MARK_SPEC],
-            scratch_shapes=[pltpu.VMEM((parts * count, total), hidden.dtype)],
-        ),
-        compiler_params=pltpu.CompilerParams(vmem_limit_bytes=42 * MIB),
-        cost_estimate=LITTLE,
-        name=f"down_{chunk}",
-    )(place, hidden, dense, *added)
-
-
-def down_steps_kernel(place, own, other, *refs):
-    pieces = 2 * own.shape[0]
-    weights, before, outs, mark = refs[:pieces], refs[pieces], refs[pieces + 1:-1], refs[-1]
-    leave(mark)
-    count = before.shape[0] // len(outs)
+    count = own.shape[1] // len(outs)
     for step, out in enumerate(outs):
         at = 0 if len(outs) == 1 else (place[1] ^ step) * count
         rows = pl.ds(pl.multiple_of(at, count), count)
-        total = before[rows]
+        total = 0.0
+        for term in before:
+            total += term[rows]
         for i in range(pieces // 2):
             for j, side in enumerate((own, other)):
                 total += jnp.dot(
@@ -597,7 +501,7 @@
         out[...] = total.astype(out.dtype)
 
 
-def down_steps(place, own, other, steps, dense, before, chunk, last):
+def down_steps(place, own, other, steps, dense, before, chunk, last, after):
     _, count, depth = own.shape
     width = dense.shape[-1]
     dense = dense.reshape(dense.shape[0], -1, depth, width)
@@ -612,23 +516,24 @@
                 return chunk, 2 * (place[0] ^ step) + (place[2] ^ flip), 0, n
 
             weights.append(pl.BlockSpec((1, 1, depth, tile), at))
+    added = [] if before is None else [before]
     out, out_tiles = [jax.ShapeDtypeStruct((count, width), jnp.float32)], [tiles]
     if last:
         out = [jax.ShapeDtypeStruct((count // 4, width), own.dtype)] * 4
         out_tiles = [pl.BlockSpec((count // 4, tile), lambda n, *_: (0, n))] * 4
     return pl.pallas_call(
-        down_steps_kernel,
+        functools.partial(down_steps_kernel, added=len(added), outputs=len(out)),
         out_shape=out + [MARK],
         grid_spec=pltpu.PrefetchScalarGridSpec(
             num_scalar_prefetch=1,
             grid=(width // tile,),
-            in_specs=[whole, whole] + weights + [tiles],
+            in_specs=[whole, whole] + weights + [tiles] * len(added) + [ANY_SPEC],
             out_specs=out_tiles + [MARK_SPEC],
         ),
         compiler_params=pltpu.CompilerParams(vmem_limit_bytes=42 * MIB),
         cost_estimate=LITTLE,
         name=f"down_{chunk}_{steps[0]}",
-    )(place, own, other, *[dense] * len(weights), before)
+    )(place, own, other, *[dense] * len(weights), *added, after)
 
 
 def by_columns(
@@ -703,41 +608,46 @@
     other = swap_core(own)
 
     place = jnp.stack([chip, chip ^ tok, side])
-    mixed = [None]
-    gathered = []
-    sent_a, sent_b, mark = panel_half(own, other, dense, 1, [], 0)
-    kept_a, kept_b, mark = panel_half(own, other, dense, 0, [mark], 0)
-    sums = kept_a, sent_a, kept_b, sent_b
-    if chunks > 1:
-        dense, mark = spread(1, [mark])
-    for chunk in range(chunks):
+
+    def send(hidden):
+        far = swap_chip(hidden, 2)
+        near = swap_chip(hidden, 1)
+        inner = lax.ppermute(hidden, "col", [(i, i ^ 6) for i in range(2, 6)])
+        ends = lax.ppermute(far, "col", [(i, i ^ 2) for i in range(2, 6)])
+        return [hidden, near, far], [inner, ends]
+
+    *sums, mark = panel_product(own, other, dense, [], 0)
+    dense, mark = spread(1, [mark])
+    mixed = None
+    for chunk in range(2):
         kept_a, sent_a, kept_b, sent_b = sums
         came_a, came_b = swap_tok(sent_a, 1), swap_tok(sent_b, 2)
+        if not chunk:
+            *sums, mark = panel_product(own, other, dense, [mark], 1)
         last_a, last_b, mark = halfway(kept_a, came_a, kept_b, came_b, [mark], chunk)
         last_a, last_b = swap_tok(last_a, 2), swap_tok(last_b, 1)
-        if chunk + 1 < chunks:
-            *sums, mark = panel_product(own, other, dense, [mark], chunk + 1)
+        if chunk:
+            held, mark = stack(early, (0, 1, 2), mark)
+            mixed, mark = down_steps(
+                place, held, swap_core(held), (0, 1, 2), down_dense, None, 0, False, mark
+            )
+            held, mark = stack(late, (3,), mark)
         hidden, mark = combine(kept_a, came_a, last_a, kept_b, came_b, last_b, [mark], chunk)
-        if chunk + 2 < chunks:
-            dense, mark = spread(chunk + 2, [mark])
-        elif chunk == max(chunks - 2, 0):
+        if chunk:
+            mixed, mark = down_steps(
+                place, held, swap_core(held), (3,), down_dense, mixed, 0, False, mark
+            )
+        else:
             down_dense, mark = spread_panels(
                 down_at, down_values, chunks, cols, width_blocks, [mark]
             )
-        if chunk + 1 < chunks:
-            gathered.append(lax.all_gather(hidden.reshape(tok_size, count, -1), "col"))
-
-    far = swap_chip(hidden, 2)
-    near = swap_chip(hidden, 1)
-    inner = lax.ppermute(hidden, "col", [(i, i ^ 6) for i in range(2, 6)])
-    ends = lax.ppermute(far, "col", [(i, i ^ 2) for i in range(2, 6)])
-    for chunk in range(chunks - 1):
-        *mixed, mark = down_product(place, gathered[chunk], down_dense, mixed[0], chunk, False)
-    for steps, pieces in (((0, 1, 2), [hidden, near, far]), ((3,), [inner, ends])):
-        held = stack(pieces, steps, mark)
-        *mixed, mark = down_steps(
-            place, held, swap_core(held), steps, down_dense, mixed[0], chunks - 1, steps == (3,)
-        )
+        early, late = send(hidden)
+    held, mark = stack(early, (0, 1, 2), mark)
+    mixed, mark = down_steps(
+        place, held, swap_core(held), (0, 1, 2), down_dense, mixed, 1, False, mark
+    )
+    held, mark = stack(late, (3,), mark)
+    *mixed, _ = down_steps(place, held, swap_core(held), (3,), down_dense, mixed, 1, True, mark)
 
     total = mixed[0].astype(jnp.float32)
     for step in parts[1:]:

time: 202 us -> 212 us (1.050)
  waiting for transfers between devices: 46.8 us -> 66.9 us
  between operations: 13.7 us -> 0.32 us
  Pallas kernels: 88.4 us -> 91.6 us
  local copies, waits for them, and re-layouts: 8.98 us -> 5.84 us
  starting transfers between devices: 40.6 us -> 43.7 us
    ppermute x11, waiting for transfers between devices: 19.1 us -> 36 us  [swap_tok(): return lax.ppermute(array, 'tok', [(i, i ^ step) for i in parts])]
    ppermute x5 -> x7, waiting for transfers between devices: 3.12 us -> 18.7 us  [swap_chip(): lax.ppermute(array, 'col', [(i, i ^ 2 * step) for i in range(col_size)])]
    all_gather x1 -> x0, waiting for transfers between devices: 14.5 us -> none  [by_columns(): gathered.append(lax.all_gather(hidden.reshape(tok_size, count, -1), 'col'))]
    pallas_call x1 -> x2, Pallas kernels: 11.6 us -> 23.3 us  [panel_product(): pl.pallas_call(panel_product_kernel, out_shape=[out] * 4 + [MARK], grid=(...]
    pallas_call x7 -> x8, Pallas kernels: 33.4 us -> 23.7 us  [the longest x4 20.1 us: down_steps(): pl.pallas_call(functools.partial(down_steps_kernel, added=len(added), out...]
    ppermute x5 -> x7, starting transfers between devices: 5.35 us -> 10.4 us  [swap_chip(): lax.ppermute(array, 'col', [(i, i ^ 2 * step) for i in range(col_size)])]
    unnamed x26 -> x20, local copies, waits for them, and re-layouts: 6.45 us -> 3.31 us
    ppermute x2 -> x4, starting transfers between devices: 2.15 us -> 4.85 us  [the longest x2 2.75 us: send(): ends = lax.ppermute(far, 'col', [(i, i ^ 2) for i in range(2, 6)])]
  transfers between devices with their start and end apart: 27 -> 32, of which waited for: 13 -> 12; matrix products, arithmetic and copies ran while one was open for 2% -> 2% of each run, Pallas kernels for 37% -> 35%
where the time goes in v9:
time: 212 us; the launch traced here: 211 us
  Pallas kernels  91.6 us (43%)
  waiting for transfers between devices  66.9 us (32%)
  starting transfers between devices  43.7 us (21%)
  local copies, waits for them, and re-layouts  5.84 us (3%)
  other arithmetic  3.21 us (2%)
    ppermute x11, waiting for transfers between devices, swap_tok(): return lax.ppermute(array, 'tok', [(i, i ^ step) for i in parts])  36 us
    pallas_call x2, Pallas kernels, spread_shares(): pl.pallas_call(functools.partial(spread_shares_kernel, rows=rows // steps...  24.1 us
    pallas_call x2, Pallas kernels, panel_product(): pl.pallas_call(panel_product_kernel, out_shape=[out] * 4 + [MARK], grid=(...  23.3 us
    ppermute x11, starting transfers between devices, swap_tok(): return lax.ppermute(array, 'tok', [(i, i ^ step) for i in parts])  21.9 us
    pallas_call x4, Pallas kernels, down_steps(): pl.pallas_call(functools.partial(down_steps_kernel, added=len(added), out...  20.1 us
    ppermute x7, waiting for transfers between devices, swap_chip(): lax.ppermute(array, 'col', [(i, i ^ 2 * step) for i in range(col_size)])  18.7 us
    pallas_call x1, Pallas kernels, spread_panels(): pl.pallas_call(functools.partial(spread_panels_kernel, chunks=chunks, row...  16.3 us
    ppermute x7, starting transfers between devices, swap_chip(): lax.ppermute(array, 'col', [(i, i ^ 2 * step) for i in range(col_size)])  10.4 us
  transfers between devices with their start and end apart: 32, of which 12 were waited for; matrix products, arithmetic and copies ran while one was open for 2% of the time, Pallas kernels for 35%

profile of v9, /device:TPU:0, one launch (start us, length us, event | category | flops | bytes accessed | tf_op | source)
XLA Modules:
  0.0 211.5 jit_solution(11172380705662063076)
XLA Ops:
  2.8 4.7 %collective-permute-start.3 = (f32[1,128]{1,0:T(1,128)S(1)}, f32[1,128]{1,0:T(1,128)S(1)}, u32[]{:S(2)}, u32[]{:S(2)}) collective-permute-start(f32[1,128]{1,0:T(1,128)S(1)} %add.90), channel_id=1, source_target_pairs={{0,6},{1,7},{2,4},{3,5},{4,2},{5,3},{6,0},{7,1},{8,14},{9,15},{10,... | collective-permute-start | bytes 1544 | tf_op jit(solution)/shard_map/ppermute | solution.py:567
  9.0 2.9 %collective-permute-done.2 = f32[1,128]{1,0:T(1,128)S(1)} collective-permute-done((f32[1,128]{1,0:T(1,128)S(1)}, f32[1,128]{1,0:T(1,128)S(1)}, u32[]{:S(2)}, u32[]{:S(2)}) %collective-permute-start.2) | collective-permute-done | bytes 544 | tf_op jit(solution)/shard_map/ppermute | solution.py:567
  13.0 1.5 collective-permute-start.7
  14.6 1.5 collective-permute-start.6
  16.1 2.0 collective-permute-start.5
  20.3 12.1 %spread_gate_up_0.1 = (bf16[1,2048,3072]{2,1,0:T(8,128)(2,1)}, f32[8,128]{1,0:T(8,128)}) custom-call(s32[192]{0:T(256)} %get-tuple-element.99.gate_at, s32[192]{0:T(256)} %get-tuple-element.96.up_at, bf16[1,216,128,128]{3,2,1,0:T(8,128)(2,1)} %refs_0_.3, bf16[1,216,128,128]{3,2,1,0:T(8,128)(2,1)} %refs_1_.3), custom_call_target="tpu_custom_call" | custom-call | flops 1 | bytes 1 | tf_op jit(solution)/shard_map/spread_gate_up_0/pallas_call | solution.py:275
  33.3 2.6 %collective-permute-done.8.other = bf16[512,1024]{1,0:T(8,128)(2,1)S(1)} collective-permute-done((bf16[512,1024]{1,0:T(8,128)(2,1)S(1)}, bf16[512,1024]{1,0:T(8,128)(2,1)S(1)}, u32[]{:S(2)}, u32[]{:S(2)}) %collective-permute-start.8) | collective-permute-done | bytes 1048608 | tf_op jit(solution)/shard_map/ppermute | solution.py:570
  36.9 11.6 %gate_up_0.1 = (bf16[2,256,768]{2,1,0:T(8,128)(2,1)}, bf16[2,256,768]{2,1,0:T(8,128)(2,1)}, bf16[2,256,768]{2,1,0:T(8,128)(2,1)}, bf16[2,256,768]{2,1,0:T(8,128)(2,1)}, f32[8,128]{1,0:T(8,128)}) custom-call(bf16[512,1024]{1,0:T(8,128)(2,1)} %copy-done, bf16[512,1024]{1,0:T(8,128)(2,1)} %copy-done.8, bf16[1,2048,3072]{2,1,0:T(8,128)(2,1)} %get-tuple-element.50.weight), custom_call_target="tpu_custom_call" | custom-call | flops 1 | bytes 1 | tf_op jit(solution)/shard_map/gate_up_0/pallas_call | solution.py:464
  48.5 4.2 %collective-permute-start.11 = (bf16[2,256,768]{2,1,0:T(8,128)(2,1)}, bf16[2,256,768]{2,1,0:T(8,128)(2,1)S(1)}, u32[]{:S(2)}, u32[]{:S(2)}) collective-permute-start(bf16[2,256,768]{2,1,0:T(8,128)(2,1)} %get-tuple-element.59), channel_id=1, source_target_pairs={{0,8},{8,0},{16,24},{24,16},{1,9},{9,1},{17,25},{25,17},{2,10},{10... | collective-permute-start | bytes 2359304 | tf_op jit(solution)/shard_map/ppermute | solution.py:564
  52.7 6.6 %collective-permute-start.12 = (bf16[2,256,768]{2,1,0:T(8,128)(2,1)}, bf16[2,256,768]{2,1,0:T(8,128)(2,1)S(1)}, u32[]{:S(2)}, u32[]{:S(2)}) collective-permute-start(bf16[2,256,768]{2,1,0:T(8,128)(2,1)} %get-tuple-element.61), channel_id=1, source_target_pairs={{0,16},{8,24},{16,0},{24,8},{1,17},{9,25},{17,1},{25,9},{2,18},{10... | collective-permute-start | bytes 2359304 | tf_op jit(solution)/shard_map/ppermute | solution.py:564
  59.3 12.1 %spread_gate_up_1.1 = (bf16[1,2048,3072]{2,1,0:T(8,128)(2,1)}, f32[8,128]{1,0:T(8,128)}) custom-call(s32[192]{0:T(256)} %get-tuple-element.100.gate_at, s32[192]{0:T(256)} %get-tuple-element.95.up_at, bf16[1,216,128,128]{3,2,1,0:T(8,128)(2,1)} %refs_0_.3, bf16[1,216,128,128]{3,2,1,0:T(8,128)(2,1)} %refs_1_.3, f32[8,128]{1,0:T(8,128)} %get-tuple-element.51.refs_2_), custom_call_target="tpu_custom_call" | custom-call | flops 1 | bytes 1 | tf_op jit(solution)/shard_map/spread_gate_up_1/pallas_call | solution.py:275
  71.4 11.7 %gate_up_1.1 = (bf16[2,256,768]{2,1,0:T(8,128)(2,1)}, bf16[2,256,768]{2,1,0:T(8,128)(2,1)}, bf16[2,256,768]{2,1,0:T(8,128)(2,1)}, bf16[2,256,768]{2,1,0:T(8,128)(2,1)}, f32[8,128]{1,0:T(8,128)}) custom-call(bf16[512,1024]{1,0:T(8,128)(2,1)} %copy-done, bf16[512,1024]{1,0:T(8,128)(2,1)} %copy-done.8, bf16[1,2048,3072]{2,1,0:T(8,128)(2,1)} %get-tuple-element.52.weight, ...), custom_call_target="tpu_custom_call" | custom-call | flops 1 | bytes 1 | tf_op jit(solution)/shard_map/gate_up_1/pallas_call | solution.py:464
  83.1 2.0 collective-permute-start.9
  86.0 2.1 collective-permute-start.13
  88.2 24.3 %collective-permute-done.13.refs_2_ = bf16[256,768]{1,0:T(8,128)(2,1)S(1)} collective-permute-done((bf16[256,768]{1,0:T(8,128)(2,1)S(1)}, bf16[256,768]{1,0:T(8,128)(2,1)S(1)}, u32[]{:S(2)}, u32[]{:S(2)}) %collective-permute-start.13) | collective-permute-done | bytes 393248 | tf_op jit(solution)/shard_map/ppermute | solution.py:564
  113.9 1.5 collective-permute-start.18
  115.8 16.3 %spread_down.1 = (bf16[2,3072,1024]{2,1,0:T(8,128)(2,1)}, f32[8,128]{1,0:T(8,128)S(1)}) custom-call(s32[384]{0:T(512)S(1)} %reshape.90.at_ref, bf16[8,108,128,128]{3,2,1,0:T(8,128)(2,1)} %values_ref.1, f32[8,128]{1,0:T(8,128)S(1)} %get-tuple-element.66.refs_0_), custom_call_target="tpu_custom_call" | custom-call | flops 1 | bytes 1 | tf_op jit(solution)/shard_map/spread_down/pallas_call | solution.py:304
  133.2 2.2 %stack.20 = (bf16[3,512,384]{2,1,0:T(8,128)(2,1)}, f32[8,128]{1,0:T(8,128)S(1)}) custom-call(bf16[512,384]{1,0:T(8,128)(2,1)} %get-tuple-element.70.refs_0_, bf16[512,384]{1,0:T(8,128)(2,1)S(1)} %collective-permute-done.20.refs_1_, bf16[512,384]{1,0:T(8,128)(2,1)} %collective-permute-done.18.refs_2_, f32[8,128]{1,0:T(8,128)S(1)} %get-tuple-element.71.refs_3_), custom_call_target="tpu_custom_call" | custom-call | flops 1 | bytes 1 | tf_op jit(solution)/shard_map/stack/pallas_call | solution.py:374
  138.1 1.8 collective-permute-start.15
  139.9 1.7 collective-permute-start.16
  141.7 7.0 %down_0_0.1 = (f32[512,1024]{1,0:T(8,128)S(1)}, f32[8,128]{1,0:T(8,128)S(1)}) custom-call(s32[3]{0:T(128)S(1)} %pad_add_fusion.place, bf16[3,512,384]{2,1,0:T(8,128)(2,1)} %get-tuple-element.72.own, bf16[3,512,384]{2,1,0:T(8,128)(2,1)} %collective-permute-done.21.other, bf16[2,8,384,1024]{3,2,1,0:T(8,128)(2,1)} %bitcast.8, ...), custom_call_target="tpu_custom_call" | custom-call | flops 1 | bytes 1 | tf_op jit(solution)/shard_map/down_0_0/pallas_call | solution.py:524
  148.7 1.9 collective-permute-done.19.refs_1_
  153.3 2.8 %collective-permute-start.25 = (bf16[512,384]{1,0:T(8,128)(2,1)S(1)}, bf16[512,384]{1,0:T(8,128)(2,1)S(1)}, u32[]{:S(2)}, u32[]{:S(2)}) collective-permute-start(bf16[512,384]{1,0:T(8,128)(2,1)S(1)} %get-tuple-element.77.refs_0_), channel_id=1, source_target_pairs={{0,2},{1,3},{2,0},{3,1},{4,6},{5,7},{6,4},{7,5},{8,10},{9,11},{10,... | collective-permute-start | bytes 1179656 | tf_op jit(solution)/shard_map/ppermute | solution.py:567
  156.6 3.3 %down_0_3.1 = (f32[512,1024]{1,0:T(8,128)S(1)}, f32[8,128]{1,0:T(8,128)S(1)}) custom-call(s32[3]{0:T(128)S(1)} %pad_add_fusion.place, bf16[1,512,384]{2,1,0:T(8,128)(2,1)S(1)} %get-tuple-element.78.own, bf16[1,512,384]{2,1,0:T(8,128)(2,1)S(1)} %collective-permute-done.26.other, bf16[2,8,384,1024]{3,2,1,0:T(8,128)(2,1)} %bitcast.14, ...), custom_call_target="tpu_custom_call" | custom-call | flops 1 | bytes 1 | tf_op jit(solution)/shard_map/down_0_3/pallas_call | solution.py:524
  159.9 12.7 %collective-permute-done.25.refs_1_ = bf16[512,384]{1,0:T(8,128)(2,1)S(1)} collective-permute-done((bf16[512,384]{1,0:T(8,128)(2,1)S(1)}, bf16[512,384]{1,0:T(8,128)(2,1)S(1)}, u32[]{:S(2)}, u32[]{:S(2)}) %collective-permute-start.25) | collective-permute-done | bytes 393248 | tf_op jit(solution)/shard_map/ppermute | solution.py:567
  172.6 2.9 %collective-permute-done.23.refs_2_ = bf16[512,384]{1,0:T(8,128)(2,1)S(1)} collective-permute-done((bf16[512,384]{1,0:T(8,128)(2,1)S(1)}, bf16[512,384]{1,0:T(8,128)(2,1)S(1)}, u32[]{:S(2)}, u32[]{:S(2)}) %collective-permute-start.23) | collective-permute-done | bytes 393248 | tf_op jit(solution)/shard_map/ppermute | solution.py:567
  178.5 6.0 %down_1_0.1 = (f32[512,1024]{1,0:T(8,128)S(1)}, f32[8,128]{1,0:T(8,128)S(1)}) custom-call(s32[3]{0:T(128)S(1)} %pad_add_fusion.place, bf16[3,512,384]{2,1,0:T(8,128)(2,1)S(1)} %get-tuple-element.82.own, bf16[3,512,384]{2,1,0:T(8,128)(2,1)S(1)} %collective-permute-done.27.other, bf16[2,8,384,1024]{3,2,1,0:T(8,128)(2,1)} %bitcast.16, ...), custom_call_target="tpu_custom_call" | custom-call | flops 1 | bytes 1 | tf_op jit(solution)/shard_map/down_1_0/pallas_call | solution.py:524
  184.5 5.2 %collective-permute-done.24.refs_1_ = bf16[512,384]{1,0:T(8,128)(2,1)S(1)} collective-permute-done((bf16[512,384]{1,0:T(8,128)(2,1)S(1)}, bf16[512,384]{1,0:T(8,128)(2,1)S(1)}, u32[]{:S(2)}, u32[]{:S(2)}) %collective-permute-start.24) | collective-permute-done | bytes 393248 | tf_op jit(solution)/shard_map/ppermute | solution.py:616
  189.9 1.7 collective-permute-done.28.other
  191.6 3.8 %down_1_3.1 = (bf16[128,1024]{1,0:T(8,128)(2,1)S(1)}, bf16[128,1024]{1,0:T(8,128)(2,1)S(1)}, bf16[128,1024]{1,0:T(8,128)(2,1)S(1)}, bf16[128,1024]{1,0:T(8,128)(2,1)S(1)}, f32[8,128]{1,0:T(8,128)}) custom-call(s32[3]{0:T(128)S(1)} %pad_add_fusion.place, bf16[1,512,384]{2,1,0:T(8,128)(2,1)S(1)} %get-tuple-element.86.own, ...), custom_call_target="tpu_custom_call" | custom-call | flops 1 | bytes 1 | tf_op jit(solution)/shard_map/down_1_3/pallas_call | solution.py:524
  198.9 5.7 %collective-permute-done.29 = bf16[128,1024]{1,0:T(8,128)(2,1)S(1)} collective-permute-done((bf16[128,1024]{1,0:T(8,128)(2,1)S(1)}, bf16[128,1024]{1,0:T(8,128)(2,1)S(1)}, u32[]{:S(2)}, u32[]{:S(2)}) %collective-permute-start.29) | collective-permute-done | bytes 262176 | tf_op jit(solution)/shard_map/ppermute | solution.py:564
  204.6 6.0 %collective-permute-done.30 = bf16[128,1024]{1,0:T(8,128)(2,1)S(1)} collective-permute-done((bf16[128,1024]{1,0:T(8,128)(2,1)S(1)}, bf16[128,1024]{1,0:T(8,128)(2,1)S(1)}, u32[]{:S(2)}, u32[]{:S(2)}) %collective-permute-start.30) | collective-permute-done | bytes 262176 | tf_op jit(solution)/shard_map/ppermute | solution.py:564
  (94 shorter events, 26.6 us)
Async XLA Ops:
  1.1 1.7 collective-permute-start
  2.8 6.2 %collective-permute-start.3 = (f32[1,128]{1,0:T(1,128)S(1)}, f32[1,128]{1,0:T(1,128)S(1)}, u32[]{:S(2)}, u32[]{:S(2)}) collective-permute-start(f32[1,128]{1,0:T(1,128)S(1)} %add.90), channel_id=1, source_target_pairs={{0,6},{1,7},{2,4},{3,5},{4,2},{5,3},{6,0},{7,1},{8,14},{9,15},{10,... | collective-permute-start | bytes 1544 | tf_op jit(solution)/shard_map/ppermute | solution.py:567
  7.5 4.4 %collective-permute-start.2 = (f32[1,128]{1,0:T(1,128)S(1)}, f32[1,128]{1,0:T(1,128)S(1)}, u32[]{:S(2)}, u32[]{:S(2)}) collective-permute-start(f32[1,128]{1,0:T(1,128)S(1)} %add.90), channel_id=1, source_target_pairs={{0,4},{1,5},{2,6},{3,7},{4,0},{5,1},{6,2},{7,3},{8,12},{9,13},{10,... | collective-permute-start | bytes 1544 | tf_op jit(solution)/shard_map/ppermute | solution.py:567
  7.5 4.4 %collective-permute-start.1 = (f32[1,128]{1,0:T(1,128)S(1)}, f32[1,128]{1,0:T(1,128)S(1)}, u32[]{:S(2)}, u32[]{:S(2)}) collective-permute-start(f32[1,128]{1,0:T(1,128)S(1)} %add.90), channel_id=1, source_target_pairs={{0,2},{1,3},{2,0},{3,1},{4,6},{5,7},{6,4},{7,5},{8,10},{9,11},{10,... | collective-permute-start | bytes 1544 | tf_op jit(solution)/shard_map/ppermute | solution.py:567
  13.0 19.3 %collective-permute-start.7 = (bf16[128,1024]{1,0:T(8,128)(2,1)S(1)}, bf16[128,1024]{1,0:T(8,128)(2,1)S(1)}, u32[]{:S(2)}, u32[]{:S(2)}) collective-permute-start(bf16[128,1024]{1,0:T(8,128)(2,1)S(1)} %multiply_convert_fusion), channel_id=1, source_target_pairs={{0,6},{1,7},{2,14},{3,15},{4,22},{5,23},{6,30},{7,31},{8,4},{9,5},... | collective-permute-start | bytes 786440 | tf_op jit(solution)/shard_map/ppermute | solution.py:578
  14.6 17.8 %collective-permute-start.6 = (bf16[128,1024]{1,0:T(8,128)(2,1)S(1)}, bf16[128,1024]{1,0:T(8,128)(2,1)S(1)}, u32[]{:S(2)}, u32[]{:S(2)}) collective-permute-start(bf16[128,1024]{1,0:T(8,128)(2,1)S(1)} %multiply_convert_fusion), channel_id=1, source_target_pairs={{0,4},{1,5},{2,12},{3,13},{4,20},{5,21},{6,28},{7,29},{8,6},{9,7},... | collective-permute-start | bytes 786440 | tf_op jit(solution)/shard_map/ppermute | solution.py:578
  16.1 16.3 %collective-permute-start.5 = (bf16[128,1024]{1,0:T(8,128)(2,1)S(1)}, bf16[128,1024]{1,0:T(8,128)(2,1)S(1)}, u32[]{:S(2)}, u32[]{:S(2)}) collective-permute-start(bf16[128,1024]{1,0:T(8,128)(2,1)S(1)} %multiply_convert_fusion), channel_id=1, source_target_pairs={{0,2},{1,3},{2,10},{3,11},{4,18},{5,19},{6,26},{7,27},{8,0},{9,1},... | collective-permute-start | bytes 786440 | tf_op jit(solution)/shard_map/ppermute | solution.py:578
  18.1 14.3 %collective-permute-start.4 = (bf16[128,1024]{1,0:T(8,128)(2,1)S(1)}, bf16[128,1024]{1,0:T(8,128)(2,1)S(1)}, u32[]{:S(2)}, u32[]{:S(2)}) collective-permute-start(bf16[128,1024]{1,0:T(8,128)(2,1)S(1)} %multiply_convert_fusion), channel_id=1, source_target_pairs={{0,0},{1,1},{2,8},{3,9},{4,16},{5,17},{6,24},{7,25},{8,2},{9,3},{1... | collective-permute-start | bytes 786440 | tf_op jit(solution)/shard_map/ppermute | solution.py:578
  33.2 2.7 %collective-permute-start.8 = (bf16[512,1024]{1,0:T(8,128)(2,1)S(1)}, bf16[512,1024]{1,0:T(8,128)(2,1)S(1)}, u32[]{:S(2)}, u32[]{:S(2)}) collective-permute-start(bf16[512,1024]{1,0:T(8,128)(2,1)S(1)} %pack.1.own), channel_id=1, source_target_pairs={{0,1},{1,0},{2,3},{3,2},{4,5},{5,4},{6,7},{7,6},{8,9},{9,8},{10,11... | collective-permute-start | bytes 3145736 | tf_op jit(solution)/shard_map/ppermute | solution.py:570
  48.5 36.6 %collective-permute-start.11 = (bf16[2,256,768]{2,1,0:T(8,128)(2,1)}, bf16[2,256,768]{2,1,0:T(8,128)(2,1)S(1)}, u32[]{:S(2)}, u32[]{:S(2)}) collective-permute-start(bf16[2,256,768]{2,1,0:T(8,128)(2,1)} %get-tuple-element.59), channel_id=1, source_target_pairs={{0,8},{8,0},{16,24},{24,16},{1,9},{9,1},{17,25},{25,17},{2,10},{10... | collective-permute-start | bytes 2359304 | tf_op jit(solution)/shard_map/ppermute | solution.py:564
  52.7 32.4 %collective-permute-start.12 = (bf16[2,256,768]{2,1,0:T(8,128)(2,1)}, bf16[2,256,768]{2,1,0:T(8,128)(2,1)S(1)}, u32[]{:S(2)}, u32[]{:S(2)}) collective-permute-start(bf16[2,256,768]{2,1,0:T(8,128)(2,1)} %get-tuple-element.61), channel_id=1, source_target_pairs={{0,16},{8,24},{16,0},{24,8},{1,17},{9,25},{17,1},{25,9},{2,18},{10... | collective-permute-start | bytes 2359304 | tf_op jit(solution)/shard_map/ppermute | solution.py:564
  83.1 49.0 %collective-permute-start.9 = (bf16[2,256,768]{2,1,0:T(8,128)(2,1)}, bf16[2,256,768]{2,1,0:T(8,128)(2,1)S(1)}, u32[]{:S(2)}, u32[]{:S(2)}) collective-permute-start(bf16[2,256,768]{2,1,0:T(8,128)(2,1)} %get-tuple-element.55), channel_id=1, source_target_pairs={{0,8},{8,0},{16,24},{24,16},{1,9},{9,1},{17,25},{25,17},{2,10},{10... | collective-permute-start | bytes 2359304 | tf_op jit(solution)/shard_map/ppermute | solution.py:564
  85.1 47.1 %collective-permute-start.10 = (bf16[2,256,768]{2,1,0:T(8,128)(2,1)}, bf16[2,256,768]{2,1,0:T(8,128)(2,1)S(1)}, u32[]{:S(2)}, u32[]{:S(2)}) collective-permute-start(bf16[2,256,768]{2,1,0:T(8,128)(2,1)} %get-tuple-element.57), channel_id=1, source_target_pairs={{0,16},{8,24},{16,0},{24,8},{1,17},{9,25},{17,1},{25,9},{2,18},{10... | collective-permute-start | bytes 2359304 | tf_op jit(solution)/shard_map/ppermute | solution.py:564
  86.0 26.5 %collective-permute-start.13 = (bf16[256,768]{1,0:T(8,128)(2,1)S(1)}, bf16[256,768]{1,0:T(8,128)(2,1)S(1)}, u32[]{:S(2)}, u32[]{:S(2)}) collective-permute-start(bf16[256,768]{1,0:T(8,128)(2,1)S(1)} %get-tuple-element.63), channel_id=1, source_target_pairs={{0,16},{8,24},{16,0},{24,8},{1,17},{9,25},{17,1},{25,9},{2,18},{10... | collective-permute-start | bytes 1179656 | tf_op jit(solution)/shard_map/ppermute | solution.py:564
  88.1 24.4 %collective-permute-start.14 = (bf16[256,768]{1,0:T(8,128)(2,1)S(1)}, bf16[256,768]{1,0:T(8,128)(2,1)S(1)}, u32[]{:S(2)}, u32[]{:S(2)}) collective-permute-start(bf16[256,768]{1,0:T(8,128)(2,1)S(1)} %get-tuple-element.64), channel_id=1, source_target_pairs={{0,8},{8,0},{16,24},{24,16},{1,9},{9,1},{17,25},{25,17},{2,10},{10... | collective-permute-start | bytes 1179656 | tf_op jit(solution)/shard_map/ppermute | solution.py:564
  113.7 19.5 %collective-permute-start.20 = (bf16[512,384]{1,0:T(8,128)(2,1)}, bf16[512,384]{1,0:T(8,128)(2,1)S(1)}, u32[]{:S(2)}, u32[]{:S(2)}) collective-permute-start(bf16[512,384]{1,0:T(8,128)(2,1)} %get-tuple-element.70.refs_0_), channel_id=1, source_target_pairs={{0,2},{1,3},{2,0},{3,1},{4,6},{5,7},{6,4},{7,5},{8,10},{9,11},{10,... | collective-permute-start | bytes 1179656 | tf_op jit(solution)/shard_map/ppermute | solution.py:567
  113.9 19.3 %collective-permute-start.18 = (bf16[512,384]{1,0:T(8,128)(2,1)}, bf16[512,384]{1,0:T(8,128)(2,1)}, u32[]{:S(2)}, u32[]{:S(2)}) collective-permute-start(bf16[512,384]{1,0:T(8,128)(2,1)} %get-tuple-element.70.refs_0_), channel_id=1, source_target_pairs={{0,4},{1,5},{2,6},{3,7},{4,0},{5,1},{6,2},{7,3},{8,12},{9,13},{10,... | collective-permute-start | bytes 1179656 | tf_op jit(solution)/shard_map/ppermute | solution.py:567
  135.4 6.2 %collective-permute-start.21 = (bf16[3,512,384]{2,1,0:T(8,128)(2,1)}, bf16[3,512,384]{2,1,0:T(8,128)(2,1)}, u32[]{:S(2)}, u32[]{:S(2)}) collective-permute-start(bf16[3,512,384]{2,1,0:T(8,128)(2,1)} %get-tuple-element.72.own), channel_id=1, source_target_pairs={{0,1},{1,0},{2,3},{3,2},{4,5},{5,4},{6,7},{7,6},{8,9},{9,8},{10,11... | collective-permute-start | bytes 3538952 | tf_op jit(solution)/shard_map/ppermute | solution.py:570
  135.4 13.3 %collective-permute-start.17 = (bf16[512,384]{1,0:T(8,128)(2,1)}, bf16[512,384]{1,0:T(8,128)(2,1)}, u32[]{:S(2)}, u32[]{:S(2)}) collective-permute-start(bf16[512,384]{1,0:T(8,128)(2,1)} %get-tuple-element.70.refs_0_), channel_id=1, source_target_pairs={{2,4},{3,5},{4,2},{5,3},{10,12},{11,13},{12,10},{13,11},{18,20},{1... | collective-permute-start | bytes 1179656 | tf_op jit(solution)/shard_map/ppermute | solution.py:615
  136.8 13.7 %collective-permute-start.19 = (bf16[512,384]{1,0:T(8,128)(2,1)}, bf16[512,384]{1,0:T(8,128)(2,1)}, u32[]{:S(2)}, u32[]{:S(2)}) collective-permute-start(bf16[512,384]{1,0:T(8,128)(2,1)} %collective-permute-done.18.refs_2_), channel_id=1, source_target_pairs={{2,0},{3,1},{4,6},{5,7},{10,8},{11,9},{12,14},{13,15},{18,16},{19,... | collective-permute-start | bytes 1179656 | tf_op jit(solution)/shard_map/ppermute | solution.py:616
  138.1 13.7 %collective-permute-start.15 = (bf16[256,768]{1,0:T(8,128)(2,1)}, bf16[256,768]{1,0:T(8,128)(2,1)S(1)}, u32[]{:S(2)}, u32[]{:S(2)}) collective-permute-start(bf16[256,768]{1,0:T(8,128)(2,1)} %get-tuple-element.68), channel_id=1, source_target_pairs={{0,16},{8,24},{16,0},{24,8},{1,17},{9,25},{17,1},{25,9},{2,18},{10... | collective-permute-start | bytes 1179656 | tf_op jit(solution)/shard_map/ppermute | solution.py:564
  139.9 11.9 %collective-permute-start.16 = (bf16[256,768]{1,0:T(8,128)(2,1)}, bf16[256,768]{1,0:T(8,128)(2,1)}, u32[]{:S(2)}, u32[]{:S(2)}) collective-permute-start(bf16[256,768]{1,0:T(8,128)(2,1)} %get-tuple-element.69), channel_id=1, source_target_pairs={{0,8},{8,0},{16,24},{24,16},{1,9},{9,1},{17,25},{25,17},{2,10},{10... | collective-permute-start | bytes 1179656 | tf_op jit(solution)/shard_map/ppermute | solution.py:564
  151.7 4.8 %collective-permute-start.26 = (bf16[1,512,384]{2,1,0:T(8,128)(2,1)S(1)}, bf16[1,512,384]{2,1,0:T(8,128)(2,1)S(1)}, u32[]{:S(2)}, u32[]{:S(2)}) collective-permute-start(bf16[1,512,384]{2,1,0:T(8,128)(2,1)S(1)} %get-tuple-element.78.own), channel_id=1, source_target_pairs={{0,1},{1,0},{2,3},{3,2},{4,5},{5,4},{6,7},{7,6},{8,9},{9,8},{10,11... | collective-permute-start | bytes 1179656 | tf_op jit(solution)/shard_map/ppermute | solution.py:570
  153.3 19.2 %collective-permute-start.25 = (bf16[512,384]{1,0:T(8,128)(2,1)S(1)}, bf16[512,384]{1,0:T(8,128)(2,1)S(1)}, u32[]{:S(2)}, u32[]{:S(2)}) collective-permute-start(bf16[512,384]{1,0:T(8,128)(2,1)S(1)} %get-tuple-element.77.refs_0_), channel_id=1, source_target_pairs={{0,2},{1,3},{2,0},{3,1},{4,6},{5,7},{6,4},{7,5},{8,10},{9,11},{10,... | collective-permute-start | bytes 1179656 | tf_op jit(solution)/shard_map/ppermute | solution.py:567
  156.1 19.4 %collective-permute-start.23 = (bf16[512,384]{1,0:T(8,128)(2,1)S(1)}, bf16[512,384]{1,0:T(8,128)(2,1)S(1)}, u32[]{:S(2)}, u32[]{:S(2)}) collective-permute-start(bf16[512,384]{1,0:T(8,128)(2,1)S(1)} %get-tuple-element.77.refs_0_), channel_id=1, source_target_pairs={{0,4},{1,5},{2,6},{3,7},{4,0},{5,1},{6,2},{7,3},{8,12},{9,13},{10,... | collective-permute-start | bytes 1179656 | tf_op jit(solution)/shard_map/ppermute | solution.py:567
  175.6 2.9 %collective-permute-start.27 = (bf16[3,512,384]{2,1,0:T(8,128)(2,1)S(1)}, bf16[3,512,384]{2,1,0:T(8,128)(2,1)S(1)}, u32[]{:S(2)}, u32[]{:S(2)}) collective-permute-start(bf16[3,512,384]{2,1,0:T(8,128)(2,1)S(1)} %get-tuple-element.82.own), channel_id=1, source_target_pairs={{0,1},{1,0},{2,3},{3,2},{4,5},{5,4},{6,7},{7,6},{8,9},{9,8},{10,11... | collective-permute-start | bytes 3538952 | tf_op jit(solution)/shard_map/ppermute | solution.py:570
  175.6 8.9 %collective-permute-start.22 = (bf16[512,384]{1,0:T(8,128)(2,1)S(1)}, bf16[512,384]{1,0:T(8,128)(2,1)S(1)}, u32[]{:S(2)}, u32[]{:S(2)}) collective-permute-start(bf16[512,384]{1,0:T(8,128)(2,1)S(1)} %get-tuple-element.77.refs_0_), channel_id=1, source_target_pairs={{2,4},{3,5},{4,2},{5,3},{10,12},{11,13},{12,10},{13,11},{18,20},{1... | collective-permute-start | bytes 1179656 | tf_op jit(solution)/shard_map/ppermute | solution.py:615
  176.3 13.4 %collective-permute-start.24 = (bf16[512,384]{1,0:T(8,128)(2,1)S(1)}, bf16[512,384]{1,0:T(8,128)(2,1)S(1)}, u32[]{:S(2)}, u32[]{:S(2)}) collective-permute-start(bf16[512,384]{1,0:T(8,128)(2,1)S(1)} %collective-permute-done.23.refs_2_), channel_id=1, source_target_pairs={{2,0},{3,1},{4,6},{5,7},{10,8},{11,9},{12,14},{13,15},{18,16},{19,... | collective-permute-start | bytes 1179656 | tf_op jit(solution)/shard_map/ppermute | solution.py:616
  189.8 1.8 collective-permute-start.28
  195.4 9.2 %collective-permute-start.29 = (bf16[128,1024]{1,0:T(8,128)(2,1)S(1)}, bf16[128,1024]{1,0:T(8,128)(2,1)S(1)}, u32[]{:S(2)}, u32[]{:S(2)}) collective-permute-start(bf16[128,1024]{1,0:T(8,128)(2,1)S(1)} %get-tuple-element.90), channel_id=1, source_target_pairs={{0,8},{8,0},{16,24},{24,16},{1,9},{9,1},{17,25},{25,17},{2,10},{10... | collective-permute-start | bytes 786440 | tf_op jit(solution)/shard_map/ppermute | solution.py:564
  196.9 13.7 %collective-permute-start.30 = (bf16[128,1024]{1,0:T(8,128)(2,1)S(1)}, bf16[128,1024]{1,0:T(8,128)(2,1)S(1)}, u32[]{:S(2)}, u32[]{:S(2)}) collective-permute-start(bf16[128,1024]{1,0:T(8,128)(2,1)S(1)} %get-tuple-element.91), channel_id=1, source_target_pairs={{0,16},{8,24},{16,0},{24,8},{1,17},{9,25},{17,1},{25,9},{2,18},{10... | collective-permute-start | bytes 786440 | tf_op jit(solution)/shard_map/ppermute | solution.py:564
  197.7 12.9 %collective-permute-start.31 = (bf16[128,1024]{1,0:T(8,128)(2,1)S(1)}, bf16[128,1024]{1,0:T(8,128)(2,1)S(1)}, u32[]{:S(2)}, u32[]{:S(2)}) collective-permute-start(bf16[128,1024]{1,0:T(8,128)(2,1)S(1)} %get-tuple-element.92), channel_id=1, source_target_pairs={{0,24},{8,16},{16,8},{24,0},{1,25},{9,17},{17,9},{25,1},{2,26},{10... | collective-permute-start | bytes 786440 | tf_op jit(solution)/shard_map/ppermute | solution.py:564
  (10 other events, 95.6 us)

commit v10 on v9

--- a/solution.py
+++ b/solution.py
@@ -355,6 +355,24 @@
         cost_estimate=LITTLE,
         name="pack",
     )(*pieces, *after)
+
+
+def hold_kernel(*refs):
+    leave(refs[-1])
+
+
+def hold(arrays, after):
+    count = len(arrays)
+    *arrays, _ = pl.pallas_call(
+        hold_kernel,
+        out_shape=[jax.ShapeDtypeStruct(array.shape, array.dtype) for array in arrays] + [MARK],
+        in_specs=[ANY_SPEC] * (count + len(after)),
+        out_specs=[ANY_SPEC] * count + [pl.BlockSpec(memory_space=pltpu.VMEM)],
+        input_output_aliases={i: i for i in range(count)},
+        cost_estimate=LITTLE,
+        name="hold",
+    )(*arrays, *after)
+    return arrays
 
 
 def stack_kernel(*refs, steps):
@@ -622,8 +640,6 @@
     for chunk in range(2):
         kept_a, sent_a, kept_b, sent_b = sums
         came_a, came_b = swap_tok(sent_a, 1), swap_tok(sent_b, 2)
-        if not chunk:
-            *sums, mark = panel_product(own, other, dense, [mark], 1)
         last_a, last_b, mark = halfway(kept_a, came_a, kept_b, came_b, [mark], chunk)
         last_a, last_b = swap_tok(last_a, 2), swap_tok(last_b, 1)
         if chunk:
@@ -632,12 +648,17 @@
                 place, held, swap_core(held), (0, 1, 2), down_dense, None, 0, False, mark
             )
             held, mark = stack(late, (3,), mark)
+        else:
+            *sums, mark = panel_product(own, other, dense, [mark], 1)
         hidden, mark = combine(kept_a, came_a, last_a, kept_b, came_b, last_b, [mark], chunk)
         if chunk:
             mixed, mark = down_steps(
                 place, held, swap_core(held), (3,), down_dense, mixed, 0, False, mark
             )
         else:
+            kept_a, sent_a, kept_b, sent_b = sums
+            sent_a, sent_b = hold([sent_a, sent_b], [mark])
+            sums = kept_a, sent_a, kept_b, sent_b
             down_dense, mark = spread_panels(
                 down_at, down_values, chunks, cols, width_blocks, [mark]
             )

time: 212 us -> 201 us (0.948)
  waiting for transfers between devices: 66.9 us -> 48.3 us
  starting transfers between devices: 43.7 us -> 47.5 us
  local copies, waits for them, and re-layouts: 5.84 us -> 8.38 us
    ppermute x11, waiting for transfers between devices: 36 us -> 17.2 us  [swap_tok(): return lax.ppermute(array, 'tok', [(i, i ^ step) for i in parts])]
    ppermute x4, starting transfers between devices: 5.72 us -> 8.24 us  [to_users(): return lax.ppermute(array, ('tok', 'col'), pairs)]
    unnamed x20 -> x28, local copies, waits for them, and re-layouts: 3.31 us -> 5.83 us
  transfers between devices with their start and end apart: 32 -> 32, of which waited for: 12 -> 13; matrix products, arithmetic and copies ran while one was open for 2% -> 2% of each run, Pallas kernels for 35% -> 36%
where the time goes in v10:
time: 201 us; the launch traced here: 200 us
  Pallas kernels  92.3 us (46%)
  waiting for transfers between devices  48.3 us (24%)
  starting transfers between devices  47.5 us (24%)
  local copies, waits for them, and re-layouts  8.38 us (4%)
  other arithmetic  3.21 us (2%)
    pallas_call x2, Pallas kernels, spread_shares(): pl.pallas_call(functools.partial(spread_shares_kernel, rows=rows // steps...  24.3 us
    ppermute x11, starting transfers between devices, swap_tok(): return lax.ppermute(array, 'tok', [(i, i ^ step) for i in parts])  23.3 us
    pallas_call x2, Pallas kernels, panel_product(): pl.pallas_call(panel_product_kernel, out_shape=[out] * 4 + [MARK], grid=(...  23.2 us
    pallas_call x4, Pallas kernels, down_steps(): pl.pallas_call(functools.partial(down_steps_kernel, added=len(added), out...  20.1 us
    ppermute x7, waiting for transfers between devices, swap_chip(): lax.ppermute(array, 'col', [(i, i ^ 2 * step) for i in range(col_size)])  17.7 us
    ppermute x11, waiting for transfers between devices, swap_tok(): return lax.ppermute(array, 'tok', [(i, i ^ step) for i in parts])  17.2 us
    pallas_call x1, Pallas kernels, spread_panels(): pl.pallas_call(functools.partial(spread_panels_kernel, chunks=chunks, row...  16.4 us
    ppermute x7, starting transfers between devices, swap_chip(): lax.ppermute(array, 'col', [(i, i ^ 2 * step) for i in range(col_size)])  10.2 us
  transfers between devices with their start and end apart: 32, of which 13 were waited for; matrix products, arithmetic and copies ran while one was open for 2% of the time, Pallas kernels for 36%

profile of v10, /device:TPU:0, one launch (start us, length us, event | category | flops | bytes accessed | tf_op | source)
XLA Modules:
  0.0 200.0 jit_solution(977544198064072839)
XLA Ops:
  2.8 4.7 %collective-permute-start.3 = (f32[1,128]{1,0:T(1,128)S(1)}, f32[1,128]{1,0:T(1,128)S(1)}, u32[]{:S(2)}, u32[]{:S(2)}) collective-permute-start(f32[1,128]{1,0:T(1,128)S(1)} %add.90), channel_id=1, source_target_pairs={{0,6},{1,7},{2,4},{3,5},{4,2},{5,3},{6,0},{7,1},{8,14},{9,15},{10,... | collective-permute-start | bytes 1544 | tf_op jit(solution)/shard_map/ppermute | solution.py:585
  9.0 2.0 %collective-permute-done.1 = f32[1,128]{1,0:T(1,128)S(1)} collective-permute-done((f32[1,128]{1,0:T(1,128)S(1)}, f32[1,128]{1,0:T(1,128)S(1)}, u32[]{:S(2)}, u32[]{:S(2)}) %collective-permute-start.1) | collective-permute-done | bytes 544 | tf_op jit(solution)/shard_map/ppermute | solution.py:585
  13.7 4.2 %collective-permute-start.5 = (bf16[128,1024]{1,0:T(8,128)(2,1)S(1)}, bf16[128,1024]{1,0:T(8,128)(2,1)S(1)}, u32[]{:S(2)}, u32[]{:S(2)}) collective-permute-start(bf16[128,1024]{1,0:T(8,128)(2,1)S(1)} %multiply_convert_fusion), channel_id=1, source_target_pairs={{0,2},{1,3},{2,10},{3,11},{4,18},{5,19},{6,26},{7,27},{8,0},{9,1},... | collective-permute-start | bytes 786440 | tf_op jit(solution)/shard_map/ppermute | solution.py:596
  18.0 1.7 collective-permute-start.6
  19.6 1.6 collective-permute-start.7
  22.8 12.1 %spread_gate_up_0.1 = (bf16[1,2048,3072]{2,1,0:T(8,128)(2,1)}, f32[8,128]{1,0:T(8,128)}) custom-call(s32[192]{0:T(256)} %get-tuple-element.103.gate_at, s32[192]{0:T(256)} %get-tuple-element.100.up_at, bf16[1,216,128,128]{3,2,1,0:T(8,128)(2,1)} %refs_0_.3, bf16[1,216,128,128]{3,2,1,0:T(8,128)(2,1)} %refs_1_.3), custom_call_target="tpu_custom_call" | custom-call | flops 1 | bytes 1 | tf_op jit(solution)/shard_map/spread_gate_up_0/pallas_call | solution.py:275
  35.8 2.6 %collective-permute-done.8.other = bf16[512,1024]{1,0:T(8,128)(2,1)S(1)} collective-permute-done((bf16[512,1024]{1,0:T(8,128)(2,1)S(1)}, bf16[512,1024]{1,0:T(8,128)(2,1)S(1)}, u32[]{:S(2)}, u32[]{:S(2)}) %collective-permute-start.8) | collective-permute-done | bytes 1048608 | tf_op jit(solution)/shard_map/ppermute | solution.py:588
  39.4 11.6 %gate_up_0.1 = (bf16[2,256,768]{2,1,0:T(8,128)(2,1)}, bf16[2,256,768]{2,1,0:T(8,128)(2,1)}, bf16[2,256,768]{2,1,0:T(8,128)(2,1)}, bf16[2,256,768]{2,1,0:T(8,128)(2,1)}, f32[8,128]{1,0:T(8,128)}) custom-call(bf16[512,1024]{1,0:T(8,128)(2,1)} %copy-done, bf16[512,1024]{1,0:T(8,128)(2,1)} %copy-done.12, bf16[1,2048,3072]{2,1,0:T(8,128)(2,1)} %get-tuple-element.52.weight), custom_call_target="tpu_custom_call" | custom-call | flops 1 | bytes 1 | tf_op jit(solution)/shard_map/gate_up_0/pallas_call | solution.py:482
  51.0 1.5 collective-permute-start.9
  52.5 11.3 %collective-permute-start.10 = (bf16[2,256,768]{2,1,0:T(8,128)(2,1)}, bf16[2,256,768]{2,1,0:T(8,128)(2,1)S(1)}, u32[]{:S(2)}, u32[]{:S(2)}) collective-permute-start(bf16[2,256,768]{2,1,0:T(8,128)(2,1)} %get-tuple-element.58), channel_id=1, source_target_pairs={{0,16},{8,24},{16,0},{24,8},{1,17},{9,25},{17,1},{25,9},{2,18},{10... | collective-permute-start | bytes 2359304 | tf_op jit(solution)/shard_map/ppermute | solution.py:582
  63.9 12.2 %spread_gate_up_1.1 = (bf16[1,2048,3072]{2,1,0:T(8,128)(2,1)}, f32[8,128]{1,0:T(8,128)}) custom-call(s32[192]{0:T(256)} %get-tuple-element.104.gate_at, s32[192]{0:T(256)} %get-tuple-element.99.up_at, bf16[1,216,128,128]{3,2,1,0:T(8,128)(2,1)} %refs_0_.3, bf16[1,216,128,128]{3,2,1,0:T(8,128)(2,1)} %refs_1_.3, f32[8,128]{1,0:T(8,128)} %get-tuple-element.53.refs_2_), custom_call_target="tpu_custom_call" | custom-call | flops 1 | bytes 1 | tf_op jit(solution)/shard_map/spread_gate_up_1/pallas_call | solution.py:275
  76.1 5.8 %collective-permute-done.10.came_b.refs_4_ = bf16[2,256,768]{2,1,0:T(8,128)(2,1)S(1)} collective-permute-done((bf16[2,256,768]{2,1,0:T(8,128)(2,1)}, bf16[2,256,768]{2,1,0:T(8,128)(2,1)S(1)}, u32[]{:S(2)}, u32[]{:S(2)}) %collective-permute-start.10) | collective-permute-done | bytes 786464 | tf_op jit(solution)/shard_map/ppermute | solution.py:582
  83.4 1.7 collective-permute-start.11
  85.1 1.7 collective-permute-start.12
  86.8 11.6 %gate_up_1.1 = (bf16[2,256,768]{2,1,0:T(8,128)(2,1)}, bf16[2,256,768]{2,1,0:T(8,128)(2,1)}, bf16[2,256,768]{2,1,0:T(8,128)(2,1)}, bf16[2,256,768]{2,1,0:T(8,128)(2,1)}, f32[8,128]{1,0:T(8,128)}) custom-call(bf16[512,1024]{1,0:T(8,128)(2,1)} %copy-done, bf16[512,1024]{1,0:T(8,128)(2,1)} %copy-done.12, bf16[1,2048,3072]{2,1,0:T(8,128)(2,1)} %get-tuple-element.54.weight, ...), custom_call_target="tpu_custom_call" | custom-call | flops 1 | bytes 1 | tf_op jit(solution)/shard_map/gate_up_1/pallas_call | solution.py:482
  103.8 16.4 %spread_down.1 = (bf16[2,3072,1024]{2,1,0:T(8,128)(2,1)}, f32[8,128]{1,0:T(8,128)S(1)}) custom-call(s32[384]{0:T(512)S(1)} %reshape.90.at_ref, bf16[8,108,128,128]{3,2,1,0:T(8,128)(2,1)} %values_ref.1, f32[8,128]{1,0:T(8,128)S(1)} %copy-done.7), custom_call_target="tpu_custom_call" | custom-call | flops 1 | bytes 1 | tf_op jit(solution)/shard_map/spread_down/pallas_call | solution.py:304
  121.2 2.2 %stack.20 = (bf16[3,512,384]{2,1,0:T(8,128)(2,1)}, f32[8,128]{1,0:T(8,128)S(1)}) custom-call(bf16[512,384]{1,0:T(8,128)(2,1)} %get-tuple-element.74.refs_0_, bf16[512,384]{1,0:T(8,128)(2,1)S(1)} %collective-permute-done.20.refs_1_, bf16[512,384]{1,0:T(8,128)(2,1)} %collective-permute-done.18.refs_2_, f32[8,128]{1,0:T(8,128)S(1)} %get-tuple-element.75.refs_3_), custom_call_target="tpu_custom_call" | custom-call | flops 1 | bytes 1 | tf_op jit(solution)/shard_map/stack/pallas_call | solution.py:392
  127.4 1.7 collective-permute-start.16
  129.2 7.0 %down_0_0.1 = (f32[512,1024]{1,0:T(8,128)S(1)}, f32[8,128]{1,0:T(8,128)S(1)}) custom-call(s32[3]{0:T(128)S(1)} %pad_add_fusion.place, bf16[3,512,384]{2,1,0:T(8,128)(2,1)} %get-tuple-element.76.own, bf16[3,512,384]{2,1,0:T(8,128)(2,1)} %collective-permute-done.21.other, bf16[2,8,384,1024]{3,2,1,0:T(8,128)(2,1)} %bitcast.8, ...), custom_call_target="tpu_custom_call" | custom-call | flops 1 | bytes 1 | tf_op jit(solution)/shard_map/down_0_0/pallas_call | solution.py:542
  136.2 3.2 %collective-permute-done.19.refs_1_ = bf16[512,384]{1,0:T(8,128)(2,1)} collective-permute-done((bf16[512,384]{1,0:T(8,128)(2,1)}, bf16[512,384]{1,0:T(8,128)(2,1)}, u32[]{:S(2)}, u32[]{:S(2)}) %collective-permute-start.19) | collective-permute-done | bytes 393248 | tf_op jit(solution)/shard_map/ppermute | solution.py:634
  140.7 1.5 combine_1.1
  142.1 4.3 %collective-permute-start.23 = (bf16[512,384]{1,0:T(8,128)(2,1)S(1)}, bf16[512,384]{1,0:T(8,128)(2,1)S(1)}, u32[]{:S(2)}, u32[]{:S(2)}) collective-permute-start(bf16[512,384]{1,0:T(8,128)(2,1)S(1)} %get-tuple-element.81.refs_0_), channel_id=1, source_target_pairs={{0,4},{1,5},{2,6},{3,7},{4,0},{5,1},{6,2},{7,3},{8,12},{9,13},{10,... | collective-permute-start | bytes 1179656 | tf_op jit(solution)/shard_map/ppermute | solution.py:585
  146.5 3.3 %down_0_3.1 = (f32[512,1024]{1,0:T(8,128)S(1)}, f32[8,128]{1,0:T(8,128)S(1)}) custom-call(s32[3]{0:T(128)S(1)} %pad_add_fusion.place, bf16[1,512,384]{2,1,0:T(8,128)(2,1)S(1)} %get-tuple-element.82.own, bf16[1,512,384]{2,1,0:T(8,128)(2,1)S(1)} %collective-permute-done.26.other, bf16[2,8,384,1024]{3,2,1,0:T(8,128)(2,1)} %bitcast.14, ...), custom_call_target="tpu_custom_call" | custom-call | flops 1 | bytes 1 | tf_op jit(solution)/shard_map/down_0_3/pallas_call | solution.py:542
  149.7 13.8 %collective-permute-done.23.refs_2_ = bf16[512,384]{1,0:T(8,128)(2,1)S(1)} collective-permute-done((bf16[512,384]{1,0:T(8,128)(2,1)S(1)}, bf16[512,384]{1,0:T(8,128)(2,1)S(1)}, u32[]{:S(2)}, u32[]{:S(2)}) %collective-permute-start.23) | collective-permute-done | bytes 393248 | tf_op jit(solution)/shard_map/ppermute | solution.py:585
  165.2 1.5 collective-permute-start.24
  167.3 6.0 %down_1_0.1 = (f32[512,1024]{1,0:T(8,128)S(1)}, f32[8,128]{1,0:T(8,128)S(1)}) custom-call(s32[3]{0:T(128)S(1)} %pad_add_fusion.place, bf16[3,512,384]{2,1,0:T(8,128)(2,1)S(1)} %get-tuple-element.86.own, bf16[3,512,384]{2,1,0:T(8,128)(2,1)S(1)} %collective-permute-done.27.other, bf16[2,8,384,1024]{3,2,1,0:T(8,128)(2,1)} %bitcast.16, ...), custom_call_target="tpu_custom_call" | custom-call | flops 1 | bytes 1 | tf_op jit(solution)/shard_map/down_1_0/pallas_call | solution.py:542
  173.3 5.2 %collective-permute-done.24.refs_1_ = bf16[512,384]{1,0:T(8,128)(2,1)S(1)} collective-permute-done((bf16[512,384]{1,0:T(8,128)(2,1)S(1)}, bf16[512,384]{1,0:T(8,128)(2,1)S(1)}, u32[]{:S(2)}, u32[]{:S(2)}) %collective-permute-start.24) | collective-permute-done | bytes 393248 | tf_op jit(solution)/shard_map/ppermute | solution.py:634
  178.7 1.7 collective-permute-done.28.other
  180.4 3.8 %down_1_3.1 = (bf16[128,1024]{1,0:T(8,128)(2,1)S(1)}, bf16[128,1024]{1,0:T(8,128)(2,1)S(1)}, bf16[128,1024]{1,0:T(8,128)(2,1)S(1)}, bf16[128,1024]{1,0:T(8,128)(2,1)S(1)}, f32[8,128]{1,0:T(8,128)}) custom-call(s32[3]{0:T(128)S(1)} %pad_add_fusion.place, bf16[1,512,384]{2,1,0:T(8,128)(2,1)S(1)} %get-tuple-element.90.own, ...), custom_call_target="tpu_custom_call" | custom-call | flops 1 | bytes 1 | tf_op jit(solution)/shard_map/down_1_3/pallas_call | solution.py:542
  184.2 1.8 collective-permute-start.31
  187.7 6.6 %collective-permute-done.31 = bf16[128,1024]{1,0:T(8,128)(2,1)S(1)} collective-permute-done((bf16[128,1024]{1,0:T(8,128)(2,1)S(1)}, bf16[128,1024]{1,0:T(8,128)(2,1)S(1)}, u32[]{:S(2)}, u32[]{:S(2)}) %collective-permute-start.31) | collective-permute-done | bytes 262176 | tf_op jit(solution)/shard_map/ppermute | solution.py:582
  194.4 4.8 %collective-permute-done.30 = bf16[128,1024]{1,0:T(8,128)(2,1)S(1)} collective-permute-done((bf16[128,1024]{1,0:T(8,128)(2,1)S(1)}, bf16[128,1024]{1,0:T(8,128)(2,1)S(1)}, u32[]{:S(2)}, u32[]{:S(2)}) %collective-permute-start.30) | collective-permute-done | bytes 262176 | tf_op jit(solution)/shard_map/ppermute | solution.py:582
  (103 shorter events, 28.4 us)
Async XLA Ops:
  1.1 1.7 collective-permute-start
  2.8 6.2 %collective-permute-start.3 = (f32[1,128]{1,0:T(1,128)S(1)}, f32[1,128]{1,0:T(1,128)S(1)}, u32[]{:S(2)}, u32[]{:S(2)}) collective-permute-start(f32[1,128]{1,0:T(1,128)S(1)} %add.90), channel_id=1, source_target_pairs={{0,6},{1,7},{2,4},{3,5},{4,2},{5,3},{6,0},{7,1},{8,14},{9,15},{10,... | collective-permute-start | bytes 1544 | tf_op jit(solution)/shard_map/ppermute | solution.py:585
  7.5 3.5 %collective-permute-start.1 = (f32[1,128]{1,0:T(1,128)S(1)}, f32[1,128]{1,0:T(1,128)S(1)}, u32[]{:S(2)}, u32[]{:S(2)}) collective-permute-start(f32[1,128]{1,0:T(1,128)S(1)} %add.90), channel_id=1, source_target_pairs={{0,2},{1,3},{2,0},{3,1},{4,6},{5,7},{6,4},{7,5},{8,10},{9,11},{10,... | collective-permute-start | bytes 1544 | tf_op jit(solution)/shard_map/ppermute | solution.py:585
  7.5 4.4 %collective-permute-start.2 = (f32[1,128]{1,0:T(1,128)S(1)}, f32[1,128]{1,0:T(1,128)S(1)}, u32[]{:S(2)}, u32[]{:S(2)}) collective-permute-start(f32[1,128]{1,0:T(1,128)S(1)} %add.90), channel_id=1, source_target_pairs={{0,4},{1,5},{2,6},{3,7},{4,0},{5,1},{6,2},{7,3},{8,12},{9,13},{10,... | collective-permute-start | bytes 1544 | tf_op jit(solution)/shard_map/ppermute | solution.py:585
  13.0 21.9 %collective-permute-start.4 = (bf16[128,1024]{1,0:T(8,128)(2,1)S(1)}, bf16[128,1024]{1,0:T(8,128)(2,1)S(1)}, u32[]{:S(2)}, u32[]{:S(2)}) collective-permute-start(bf16[128,1024]{1,0:T(8,128)(2,1)S(1)} %multiply_convert_fusion), channel_id=1, source_target_pairs={{0,0},{1,1},{2,8},{3,9},{4,16},{5,17},{6,24},{7,25},{8,2},{9,3},{1... | collective-permute-start | bytes 786440 | tf_op jit(solution)/shard_map/ppermute | solution.py:596
  13.7 21.2 %collective-permute-start.5 = (bf16[128,1024]{1,0:T(8,128)(2,1)S(1)}, bf16[128,1024]{1,0:T(8,128)(2,1)S(1)}, u32[]{:S(2)}, u32[]{:S(2)}) collective-permute-start(bf16[128,1024]{1,0:T(8,128)(2,1)S(1)} %multiply_convert_fusion), channel_id=1, source_target_pairs={{0,2},{1,3},{2,10},{3,11},{4,18},{5,19},{6,26},{7,27},{8,0},{9,1},... | collective-permute-start | bytes 786440 | tf_op jit(solution)/shard_map/ppermute | solution.py:596
  18.0 17.0 %collective-permute-start.6 = (bf16[128,1024]{1,0:T(8,128)(2,1)S(1)}, bf16[128,1024]{1,0:T(8,128)(2,1)S(1)}, u32[]{:S(2)}, u32[]{:S(2)}) collective-permute-start(bf16[128,1024]{1,0:T(8,128)(2,1)S(1)} %multiply_convert_fusion), channel_id=1, source_target_pairs={{0,4},{1,5},{2,12},{3,13},{4,20},{5,21},{6,28},{7,29},{8,6},{9,7},... | collective-permute-start | bytes 786440 | tf_op jit(solution)/shard_map/ppermute | solution.py:596
  19.6 15.3 %collective-permute-start.7 = (bf16[128,1024]{1,0:T(8,128)(2,1)S(1)}, bf16[128,1024]{1,0:T(8,128)(2,1)S(1)}, u32[]{:S(2)}, u32[]{:S(2)}) collective-permute-start(bf16[128,1024]{1,0:T(8,128)(2,1)S(1)} %multiply_convert_fusion), channel_id=1, source_target_pairs={{0,6},{1,7},{2,14},{3,15},{4,22},{5,23},{6,30},{7,31},{8,4},{9,5},... | collective-permute-start | bytes 786440 | tf_op jit(solution)/shard_map/ppermute | solution.py:596
  35.7 2.7 %collective-permute-start.8 = (bf16[512,1024]{1,0:T(8,128)(2,1)S(1)}, bf16[512,1024]{1,0:T(8,128)(2,1)S(1)}, u32[]{:S(2)}, u32[]{:S(2)}) collective-permute-start(bf16[512,1024]{1,0:T(8,128)(2,1)S(1)} %pack.1.own), channel_id=1, source_target_pairs={{0,1},{1,0},{2,3},{3,2},{4,5},{5,4},{6,7},{7,6},{8,9},{9,8},{10,11... | collective-permute-start | bytes 3145736 | tf_op jit(solution)/shard_map/ppermute | solution.py:588
  51.0 25.1 %collective-permute-start.9 = (bf16[2,256,768]{2,1,0:T(8,128)(2,1)}, bf16[2,256,768]{2,1,0:T(8,128)(2,1)S(1)}, u32[]{:S(2)}, u32[]{:S(2)}) collective-permute-start(bf16[2,256,768]{2,1,0:T(8,128)(2,1)} %get-tuple-element.56), channel_id=1, source_target_pairs={{0,8},{8,0},{16,24},{24,16},{1,9},{9,1},{17,25},{25,17},{2,10},{10... | collective-permute-start | bytes 2359304 | tf_op jit(solution)/shard_map/ppermute | solution.py:582
  52.5 29.4 %collective-permute-start.10 = (bf16[2,256,768]{2,1,0:T(8,128)(2,1)}, bf16[2,256,768]{2,1,0:T(8,128)(2,1)S(1)}, u32[]{:S(2)}, u32[]{:S(2)}) collective-permute-start(bf16[2,256,768]{2,1,0:T(8,128)(2,1)} %get-tuple-element.58), channel_id=1, source_target_pairs={{0,16},{8,24},{16,0},{24,8},{1,17},{9,25},{17,1},{25,9},{2,18},{10... | collective-permute-start | bytes 2359304 | tf_op jit(solution)/shard_map/ppermute | solution.py:582
  83.4 15.0 %collective-permute-start.11 = (bf16[256,768]{1,0:T(8,128)(2,1)S(1)}, bf16[256,768]{1,0:T(8,128)(2,1)S(1)}, u32[]{:S(2)}, u32[]{:S(2)}) collective-permute-start(bf16[256,768]{1,0:T(8,128)(2,1)S(1)} %get-tuple-element.64), channel_id=1, source_target_pairs={{0,16},{8,24},{16,0},{24,8},{1,17},{9,25},{17,1},{25,9},{2,18},{10... | collective-permute-start | bytes 1179656 | tf_op jit(solution)/shard_map/ppermute | solution.py:582
  85.1 13.3 %collective-permute-start.12 = (bf16[256,768]{1,0:T(8,128)(2,1)S(1)}, bf16[256,768]{1,0:T(8,128)(2,1)S(1)}, u32[]{:S(2)}, u32[]{:S(2)}) collective-permute-start(bf16[256,768]{1,0:T(8,128)(2,1)S(1)} %get-tuple-element.65), channel_id=1, source_target_pairs={{0,8},{8,0},{16,24},{24,16},{1,9},{9,1},{17,25},{25,17},{2,10},{10... | collective-permute-start | bytes 1179656 | tf_op jit(solution)/shard_map/ppermute | solution.py:582
  101.5 18.6 %collective-permute-start.13 = (bf16[2,256,768]{2,1,0:T(8,128)(2,1)}, bf16[2,256,768]{2,1,0:T(8,128)(2,1)S(1)}, u32[]{:S(2)}, u32[]{:S(2)}) collective-permute-start(bf16[2,256,768]{2,1,0:T(8,128)(2,1)} %get-tuple-element.68), channel_id=1, source_target_pairs={{0,8},{8,0},{16,24},{24,16},{1,9},{9,1},{17,25},{25,17},{2,10},{10... | collective-permute-start | bytes 2359304 | tf_op jit(solution)/shard_map/ppermute | solution.py:582
  101.9 18.3 %collective-permute-start.14 = (bf16[2,256,768]{2,1,0:T(8,128)(2,1)}, bf16[2,256,768]{2,1,0:T(8,128)(2,1)S(1)}, u32[]{:S(2)}, u32[]{:S(2)}) collective-permute-start(bf16[2,256,768]{2,1,0:T(8,128)(2,1)} %get-tuple-element.70), channel_id=1, source_target_pairs={{0,16},{8,24},{16,0},{24,8},{1,17},{9,25},{17,1},{25,9},{2,18},{10... | collective-permute-start | bytes 2359304 | tf_op jit(solution)/shard_map/ppermute | solution.py:582
  102.2 19.0 %collective-permute-start.18 = (bf16[512,384]{1,0:T(8,128)(2,1)}, bf16[512,384]{1,0:T(8,128)(2,1)}, u32[]{:S(2)}, u32[]{:S(2)}) collective-permute-start(bf16[512,384]{1,0:T(8,128)(2,1)} %get-tuple-element.74.refs_0_), channel_id=1, source_target_pairs={{0,4},{1,5},{2,6},{3,7},{4,0},{5,1},{6,2},{7,3},{8,12},{9,13},{10,... | collective-permute-start | bytes 1179656 | tf_op jit(solution)/shard_map/ppermute | solution.py:585
  102.2 19.0 %collective-permute-start.20 = (bf16[512,384]{1,0:T(8,128)(2,1)}, bf16[512,384]{1,0:T(8,128)(2,1)S(1)}, u32[]{:S(2)}, u32[]{:S(2)}) collective-permute-start(bf16[512,384]{1,0:T(8,128)(2,1)} %get-tuple-element.74.refs_0_), channel_id=1, source_target_pairs={{0,2},{1,3},{2,0},{3,1},{4,6},{5,7},{6,4},{7,5},{8,10},{9,11},{10,... | collective-permute-start | bytes 1179656 | tf_op jit(solution)/shard_map/ppermute | solution.py:585
  123.5 5.7 %collective-permute-start.21 = (bf16[3,512,384]{2,1,0:T(8,128)(2,1)}, bf16[3,512,384]{2,1,0:T(8,128)(2,1)}, u32[]{:S(2)}, u32[]{:S(2)}) collective-permute-start(bf16[3,512,384]{2,1,0:T(8,128)(2,1)} %get-tuple-element.76.own), channel_id=1, source_target_pairs={{0,1},{1,0},{2,3},{3,2},{4,5},{5,4},{6,7},{7,6},{8,9},{9,8},{10,11... | collective-permute-start | bytes 3538952 | tf_op jit(solution)/shard_map/ppermute | solution.py:588
  123.5 12.7 %collective-permute-start.17 = (bf16[512,384]{1,0:T(8,128)(2,1)}, bf16[512,384]{1,0:T(8,128)(2,1)}, u32[]{:S(2)}, u32[]{:S(2)}) collective-permute-start(bf16[512,384]{1,0:T(8,128)(2,1)} %get-tuple-element.74.refs_0_), channel_id=1, source_target_pairs={{2,4},{3,5},{4,2},{5,3},{10,12},{11,13},{12,10},{13,11},{18,20},{1... | collective-permute-start | bytes 1179656 | tf_op jit(solution)/shard_map/ppermute | solution.py:633
  124.9 14.5 %collective-permute-start.19 = (bf16[512,384]{1,0:T(8,128)(2,1)}, bf16[512,384]{1,0:T(8,128)(2,1)}, u32[]{:S(2)}, u32[]{:S(2)}) collective-permute-start(bf16[512,384]{1,0:T(8,128)(2,1)} %collective-permute-done.18.refs_2_), channel_id=1, source_target_pairs={{2,0},{3,1},{4,6},{5,7},{10,8},{11,9},{12,14},{13,15},{18,16},{19,... | collective-permute-start | bytes 1179656 | tf_op jit(solution)/shard_map/ppermute | solution.py:634
  126.2 14.5 %collective-permute-start.15 = (bf16[256,768]{1,0:T(8,128)(2,1)}, bf16[256,768]{1,0:T(8,128)(2,1)S(1)}, u32[]{:S(2)}, u32[]{:S(2)}) collective-permute-start(bf16[256,768]{1,0:T(8,128)(2,1)} %get-tuple-element.72), channel_id=1, source_target_pairs={{0,16},{8,24},{16,0},{24,8},{1,17},{9,25},{17,1},{25,9},{2,18},{10... | collective-permute-start | bytes 1179656 | tf_op jit(solution)/shard_map/ppermute | solution.py:582
  127.4 13.2 %collective-permute-start.16 = (bf16[256,768]{1,0:T(8,128)(2,1)}, bf16[256,768]{1,0:T(8,128)(2,1)}, u32[]{:S(2)}, u32[]{:S(2)}) collective-permute-start(bf16[256,768]{1,0:T(8,128)(2,1)} %get-tuple-element.73), channel_id=1, source_target_pairs={{0,8},{8,0},{16,24},{24,16},{1,9},{9,1},{17,25},{25,17},{2,10},{10... | collective-permute-start | bytes 1179656 | tf_op jit(solution)/shard_map/ppermute | solution.py:582
  140.6 5.9 %collective-permute-start.26 = (bf16[1,512,384]{2,1,0:T(8,128)(2,1)S(1)}, bf16[1,512,384]{2,1,0:T(8,128)(2,1)S(1)}, u32[]{:S(2)}, u32[]{:S(2)}) collective-permute-start(bf16[1,512,384]{2,1,0:T(8,128)(2,1)S(1)} %get-tuple-element.82.own), channel_id=1, source_target_pairs={{0,1},{1,0},{2,3},{3,2},{4,5},{5,4},{6,7},{7,6},{8,9},{9,8},{10,11... | collective-permute-start | bytes 1179656 | tf_op jit(solution)/shard_map/ppermute | solution.py:588
  142.1 21.4 %collective-permute-start.23 = (bf16[512,384]{1,0:T(8,128)(2,1)S(1)}, bf16[512,384]{1,0:T(8,128)(2,1)S(1)}, u32[]{:S(2)}, u32[]{:S(2)}) collective-permute-start(bf16[512,384]{1,0:T(8,128)(2,1)S(1)} %get-tuple-element.81.refs_0_), channel_id=1, source_target_pairs={{0,4},{1,5},{2,6},{3,7},{4,0},{5,1},{6,2},{7,3},{8,12},{9,13},{10,... | collective-permute-start | bytes 1179656 | tf_op jit(solution)/shard_map/ppermute | solution.py:585
  146.4 17.8 %collective-permute-start.25 = (bf16[512,384]{1,0:T(8,128)(2,1)S(1)}, bf16[512,384]{1,0:T(8,128)(2,1)S(1)}, u32[]{:S(2)}, u32[]{:S(2)}) collective-permute-start(bf16[512,384]{1,0:T(8,128)(2,1)S(1)} %get-tuple-element.81.refs_0_), channel_id=1, source_target_pairs={{0,2},{1,3},{2,0},{3,1},{4,6},{5,7},{6,4},{7,5},{8,10},{9,11},{10,... | collective-permute-start | bytes 1179656 | tf_op jit(solution)/shard_map/ppermute | solution.py:585
  164.4 2.9 %collective-permute-start.27 = (bf16[3,512,384]{2,1,0:T(8,128)(2,1)S(1)}, bf16[3,512,384]{2,1,0:T(8,128)(2,1)S(1)}, u32[]{:S(2)}, u32[]{:S(2)}) collective-permute-start(bf16[3,512,384]{2,1,0:T(8,128)(2,1)S(1)} %get-tuple-element.86.own), channel_id=1, source_target_pairs={{0,1},{1,0},{2,3},{3,2},{4,5},{5,4},{6,7},{7,6},{8,9},{9,8},{10,11... | collective-permute-start | bytes 3538952 | tf_op jit(solution)/shard_map/ppermute | solution.py:588
  164.5 8.9 %collective-permute-start.22 = (bf16[512,384]{1,0:T(8,128)(2,1)S(1)}, bf16[512,384]{1,0:T(8,128)(2,1)S(1)}, u32[]{:S(2)}, u32[]{:S(2)}) collective-permute-start(bf16[512,384]{1,0:T(8,128)(2,1)S(1)} %get-tuple-element.81.refs_0_), channel_id=1, source_target_pairs={{2,4},{3,5},{4,2},{5,3},{10,12},{11,13},{12,10},{13,11},{18,20},{1... | collective-permute-start | bytes 1179656 | tf_op jit(solution)/shard_map/ppermute | solution.py:633
  165.2 13.4 %collective-permute-start.24 = (bf16[512,384]{1,0:T(8,128)(2,1)S(1)}, bf16[512,384]{1,0:T(8,128)(2,1)S(1)}, u32[]{:S(2)}, u32[]{:S(2)}) collective-permute-start(bf16[512,384]{1,0:T(8,128)(2,1)S(1)} %collective-permute-done.23.refs_2_), channel_id=1, source_target_pairs={{2,0},{3,1},{4,6},{5,7},{10,8},{11,9},{12,14},{13,15},{18,16},{19,... | collective-permute-start | bytes 1179656 | tf_op jit(solution)/shard_map/ppermute | solution.py:634
  178.6 1.8 collective-permute-start.28
  184.2 10.1 %collective-permute-start.31 = (bf16[128,1024]{1,0:T(8,128)(2,1)S(1)}, bf16[128,1024]{1,0:T(8,128)(2,1)S(1)}, u32[]{:S(2)}, u32[]{:S(2)}) collective-permute-start(bf16[128,1024]{1,0:T(8,128)(2,1)S(1)} %get-tuple-element.96), channel_id=1, source_target_pairs={{0,24},{8,16},{16,8},{24,0},{1,25},{9,17},{17,9},{25,1},{2,26},{10... | collective-permute-start | bytes 786440 | tf_op jit(solution)/shard_map/ppermute | solution.py:582
  186.0 13.1 %collective-permute-start.30 = (bf16[128,1024]{1,0:T(8,128)(2,1)S(1)}, bf16[128,1024]{1,0:T(8,128)(2,1)S(1)}, u32[]{:S(2)}, u32[]{:S(2)}) collective-permute-start(bf16[128,1024]{1,0:T(8,128)(2,1)S(1)} %get-tuple-element.95), channel_id=1, source_target_pairs={{0,16},{8,24},{16,0},{24,8},{1,17},{9,25},{17,1},{25,9},{2,18},{10... | collective-permute-start | bytes 786440 | tf_op jit(solution)/shard_map/ppermute | solution.py:582
  187.2 11.9 %collective-permute-start.29 = (bf16[128,1024]{1,0:T(8,128)(2,1)S(1)}, bf16[128,1024]{1,0:T(8,128)(2,1)S(1)}, u32[]{:S(2)}, u32[]{:S(2)}) collective-permute-start(bf16[128,1024]{1,0:T(8,128)(2,1)S(1)} %get-tuple-element.94), channel_id=1, source_target_pairs={{0,8},{8,0},{16,24},{24,16},{1,9},{9,1},{17,25},{25,17},{2,10},{10... | collective-permute-start | bytes 786440 | tf_op jit(solution)/shard_map/ppermute | solution.py:582
  (14 other events, 81.1 us)

commit v11 on v10

--- a/solution.py
+++ b/solution.py
@@ -644,17 +644,14 @@
         last_a, last_b = swap_tok(last_a, 2), swap_tok(last_b, 1)
         if chunk:
             held, mark = stack(early, (0, 1, 2), mark)
-            mixed, mark = down_steps(
-                place, held, swap_core(held), (0, 1, 2), down_dense, None, 0, False, mark
-            )
-            held, mark = stack(late, (3,), mark)
         else:
             *sums, mark = panel_product(own, other, dense, [mark], 1)
         hidden, mark = combine(kept_a, came_a, last_a, kept_b, came_b, last_b, [mark], chunk)
         if chunk:
             mixed, mark = down_steps(
-                place, held, swap_core(held), (3,), down_dense, mixed, 0, False, mark
+                place, held, swap_core(held), (0, 1, 2), down_dense, None, 0, False, mark
             )
+            waiting = late
         else:
             kept_a, sent_a, kept_b, sent_b = sums
             sent_a, sent_b = hold([sent_a, sent_b], [mark])
@@ -666,6 +663,10 @@
     held, mark = stack(early, (0, 1, 2), mark)
     mixed, mark = down_steps(
         place, held, swap_core(held), (0, 1, 2), down_dense, mixed, 1, False, mark
+    )
+    before, mark = stack(waiting, (3,), mark)
+    mixed, mark = down_steps(
+        place, before, swap_core(before), (3,), down_dense, mixed, 0, False, mark
     )
     held, mark = stack(late, (3,), mark)
     *mixed, _ = down_steps(place, held, swap_core(held), (3,), down_dense, mixed, 1, True, mark)

time: 201 us -> 208 us (1.035)
  waiting for transfers between devices: 48.3 us -> 59 us
  Pallas kernels: 92.3 us -> 87.7 us
    ppermute x11, waiting for transfers between devices: 17.2 us -> 26.9 us  [swap_tok(): return lax.ppermute(array, 'tok', [(i, i ^ step) for i in parts])]
    ppermute x2, waiting for transfers between devices: 8.41 us -> 15 us  [send(): ends = lax.ppermute(far, 'col', [(i, i ^ 2) for i in range(2, 6)])]
    ppermute x7, waiting for transfers between devices: 17.7 us -> 11.8 us  [swap_chip(): lax.ppermute(array, 'col', [(i, i ^ 2 * step) for i in range(col_size)])]
    pallas_call x4, Pallas kernels: 3.56 us -> 1.31 us  [stack(): pl.pallas_call(functools.partial(stack_kernel, steps=steps), out_shape=[j...]
    unnamed x28 -> x32, local copies, waits for them, and re-layouts: 5.83 us -> 7.57 us
  transfers between devices with their start and end apart: 32 -> 32, of which waited for: 13 -> 15; matrix products, arithmetic and copies ran while one was open for 2% -> 2% of each run, Pallas kernels for 36% -> 34%
where the time goes in v11:
time: 208 us; the launch traced here: 207 us
  Pallas kernels  87.7 us (42%)
  waiting for transfers between devices  59 us (28%)
  starting transfers between devices  47 us (23%)
  local copies, waits for them, and re-layouts  10.1 us (5%)
  other arithmetic  3.21 us (2%)
    ppermute x11, waiting for transfers between devices, swap_tok(): return lax.ppermute(array, 'tok', [(i, i ^ step) for i in parts])  26.9 us
    pallas_call x2, Pallas kernels, spread_shares(): pl.pallas_call(functools.partial(spread_shares_kernel, rows=rows // steps...  24.3 us
    ppermute x11, starting transfers between devices, swap_tok(): return lax.ppermute(array, 'tok', [(i, i ^ step) for i in parts])  23.3 us
    pallas_call x2, Pallas kernels, panel_product(): pl.pallas_call(panel_product_kernel, out_shape=[out] * 4 + [MARK], grid=(...  23.2 us
    pallas_call x4, Pallas kernels, down_steps(): pl.pallas_call(functools.partial(down_steps_kernel, added=len(added), out...  19.8 us
    pallas_call x1, Pallas kernels, spread_panels(): pl.pallas_call(functools.partial(spread_panels_kernel, chunks=chunks, row...  16.3 us
    ppermute x2, waiting for transfers between devices, send(): ends = lax.ppermute(far, 'col', [(i, i ^ 2) for i in range(2, 6)])  15 us
    ppermute x7, waiting for transfers between devices, swap_chip(): lax.ppermute(array, 'col', [(i, i ^ 2 * step) for i in range(col_size)])  11.8 us
  transfers between devices with their start and end apart: 32, of which 15 were waited for; matrix products, arithmetic and copies ran while one was open for 2% of the time, Pallas kernels for 34%

profile of v11, /device:TPU:0, one launch (start us, length us, event | category | flops | bytes accessed | tf_op | source)
XLA Modules:
  0.0 207.4 jit_solution(6194397994313131557)
XLA Ops:
  2.8 4.7 %collective-permute-start.3 = (f32[1,128]{1,0:T(1,128)S(1)}, f32[1,128]{1,0:T(1,128)S(1)}, u32[]{:S(2)}, u32[]{:S(2)}) collective-permute-start(f32[1,128]{1,0:T(1,128)S(1)} %add.90), channel_id=1, source_target_pairs={{0,6},{1,7},{2,4},{3,5},{4,2},{5,3},{6,0},{7,1},{8,14},{9,15},{10,... | collective-permute-start | bytes 1544 | tf_op jit(solution)/shard_map/ppermute | solution.py:585
  9.0 2.0 collective-permute-done.1
  13.7 4.2 %collective-permute-start.5 = (bf16[128,1024]{1,0:T(8,128)(2,1)S(1)}, bf16[128,1024]{1,0:T(8,128)(2,1)S(1)}, u32[]{:S(2)}, u32[]{:S(2)}) collective-permute-start(bf16[128,1024]{1,0:T(8,128)(2,1)S(1)} %multiply_convert_fusion), channel_id=1, source_target_pairs={{0,2},{1,3},{2,10},{3,11},{4,18},{5,19},{6,26},{7,27},{8,0},{9,1},... | collective-permute-start | bytes 786440 | tf_op jit(solution)/shard_map/ppermute | solution.py:596
  18.0 1.7 collective-permute-start.6
  19.6 1.6 collective-permute-start.7
  22.8 12.1 %spread_gate_up_0.1 = (bf16[1,2048,3072]{2,1,0:T(8,128)(2,1)}, f32[8,128]{1,0:T(8,128)}) custom-call(s32[192]{0:T(256)} %get-tuple-element.103.gate_at, s32[192]{0:T(256)} %get-tuple-element.100.up_at, bf16[1,216,128,128]{3,2,1,0:T(8,128)(2,1)} %refs_0_.3, bf16[1,216,128,128]{3,2,1,0:T(8,128)(2,1)} %refs_1_.3), custom_call_target="tpu_custom_call" | custom-call | flops 1 | bytes 1 | tf_op jit(solution)/shard_map/spread_gate_up_0/pallas_call | solution.py:275
  35.8 2.6 %collective-permute-done.8.other = bf16[512,1024]{1,0:T(8,128)(2,1)S(1)} collective-permute-done((bf16[512,1024]{1,0:T(8,128)(2,1)S(1)}, bf16[512,1024]{1,0:T(8,128)(2,1)S(1)}, u32[]{:S(2)}, u32[]{:S(2)}) %collective-permute-start.8) | collective-permute-done | bytes 1048608 | tf_op jit(solution)/shard_map/ppermute | solution.py:588
  39.4 11.6 %gate_up_0.1 = (bf16[2,256,768]{2,1,0:T(8,128)(2,1)}, bf16[2,256,768]{2,1,0:T(8,128)(2,1)}, bf16[2,256,768]{2,1,0:T(8,128)(2,1)}, bf16[2,256,768]{2,1,0:T(8,128)(2,1)}, f32[8,128]{1,0:T(8,128)}) custom-call(bf16[512,1024]{1,0:T(8,128)(2,1)} %copy-done, bf16[512,1024]{1,0:T(8,128)(2,1)} %copy-done.14, bf16[1,2048,3072]{2,1,0:T(8,128)(2,1)} %get-tuple-element.52.weight), custom_call_target="tpu_custom_call" | custom-call | flops 1 | bytes 1 | tf_op jit(solution)/shard_map/gate_up_0/pallas_call | solution.py:482
  51.0 1.5 collective-permute-start.9
  52.5 11.4 %collective-permute-start.10 = (bf16[2,256,768]{2,1,0:T(8,128)(2,1)}, bf16[2,256,768]{2,1,0:T(8,128)(2,1)S(1)}, u32[]{:S(2)}, u32[]{:S(2)}) collective-permute-start(bf16[2,256,768]{2,1,0:T(8,128)(2,1)} %get-tuple-element.58), channel_id=1, source_target_pairs={{0,16},{8,24},{16,0},{24,8},{1,17},{9,25},{17,1},{25,9},{2,18},{10... | collective-permute-start | bytes 2359304 | tf_op jit(solution)/shard_map/ppermute | solution.py:582
  63.8 12.2 %spread_gate_up_1.1 = (bf16[1,2048,3072]{2,1,0:T(8,128)(2,1)}, f32[8,128]{1,0:T(8,128)}) custom-call(s32[192]{0:T(256)} %get-tuple-element.104.gate_at, s32[192]{0:T(256)} %get-tuple-element.99.up_at, bf16[1,216,128,128]{3,2,1,0:T(8,128)(2,1)} %refs_0_.3, bf16[1,216,128,128]{3,2,1,0:T(8,128)(2,1)} %refs_1_.3, f32[8,128]{1,0:T(8,128)} %get-tuple-element.53.refs_2_), custom_call_target="tpu_custom_call" | custom-call | flops 1 | bytes 1 | tf_op jit(solution)/shard_map/spread_gate_up_1/pallas_call | solution.py:275
  76.0 5.8 %collective-permute-done.10.came_b.refs_4_ = bf16[2,256,768]{2,1,0:T(8,128)(2,1)S(1)} collective-permute-done((bf16[2,256,768]{2,1,0:T(8,128)(2,1)}, bf16[2,256,768]{2,1,0:T(8,128)(2,1)S(1)}, u32[]{:S(2)}, u32[]{:S(2)}) %collective-permute-start.10) | collective-permute-done | bytes 786464 | tf_op jit(solution)/shard_map/ppermute | solution.py:582
  83.3 1.7 collective-permute-start.11
  85.1 1.7 collective-permute-start.12
  86.8 11.6 %gate_up_1.1 = (bf16[2,256,768]{2,1,0:T(8,128)(2,1)}, bf16[2,256,768]{2,1,0:T(8,128)(2,1)}, bf16[2,256,768]{2,1,0:T(8,128)(2,1)}, bf16[2,256,768]{2,1,0:T(8,128)(2,1)}, f32[8,128]{1,0:T(8,128)}) custom-call(bf16[512,1024]{1,0:T(8,128)(2,1)} %copy-done, bf16[512,1024]{1,0:T(8,128)(2,1)} %copy-done.14, bf16[1,2048,3072]{2,1,0:T(8,128)(2,1)} %get-tuple-element.54.weight, ...), custom_call_target="tpu_custom_call" | custom-call | flops 1 | bytes 1 | tf_op jit(solution)/shard_map/gate_up_1/pallas_call | solution.py:482
  103.0 16.3 %spread_down.1 = (bf16[2,3072,1024]{2,1,0:T(8,128)(2,1)}, f32[8,128]{1,0:T(8,128)S(1)}) custom-call(s32[384]{0:T(512)S(1)} %reshape.90.at_ref, bf16[8,108,128,128]{3,2,1,0:T(8,128)(2,1)} %values_ref.1, f32[8,128]{1,0:T(8,128)S(1)} %copy-done.9), custom_call_target="tpu_custom_call" | custom-call | flops 1 | bytes 1 | tf_op jit(solution)/shard_map/spread_down/pallas_call | solution.py:304
  121.5 1.4 collective-permute-start.15
  122.9 1.5 collective-permute-start.16
  124.4 8.6 %collective-permute-done.15.refs_2_ = bf16[256,768]{1,0:T(8,128)(2,1)S(1)} collective-permute-done((bf16[256,768]{1,0:T(8,128)(2,1)S(1)}, bf16[256,768]{1,0:T(8,128)(2,1)S(1)}, u32[]{:S(2)}, u32[]{:S(2)}) %collective-permute-start.15) | collective-permute-done | bytes 393248 | tf_op jit(solution)/shard_map/ppermute | solution.py:582
  135.3 2.7 %collective-permute-start.20 = (bf16[512,384]{1,0:T(8,128)(2,1)}, bf16[512,384]{1,0:T(8,128)(2,1)S(1)}, u32[]{:S(2)}, u32[]{:S(2)}) collective-permute-start(bf16[512,384]{1,0:T(8,128)(2,1)} %get-tuple-element.77.refs_0_), channel_id=1, source_target_pairs={{0,4},{1,5},{2,6},{3,7},{4,0},{5,1},{6,2},{7,3},{8,12},{9,13},{10,... | collective-permute-start | bytes 1179656 | tf_op jit(solution)/shard_map/ppermute | solution.py:585
  138.0 2.0 collective-permute-start.24
  140.1 6.7 %down_0_0.1 = (f32[512,1024]{1,0:T(8,128)S(1)}, f32[8,128]{1,0:T(8,128)S(1)}) custom-call(s32[3]{0:T(128)S(1)} %pad_add_fusion.place, bf16[3,512,384]{2,1,0:T(8,128)(2,1)S(1)} %get-tuple-element.78.own, bf16[3,512,384]{2,1,0:T(8,128)(2,1)} %collective-permute-done.25.other, bf16[2,8,384,1024]{3,2,1,0:T(8,128)(2,1)} %bitcast.8, ...), custom_call_target="tpu_custom_call" | custom-call | flops 1 | bytes 1 | tf_op jit(solution)/shard_map/down_0_0/pallas_call | solution.py:542
  146.8 8.6 %collective-permute-done.20.refs_2_ = bf16[512,384]{1,0:T(8,128)(2,1)S(1)} collective-permute-done((bf16[512,384]{1,0:T(8,128)(2,1)}, bf16[512,384]{1,0:T(8,128)(2,1)S(1)}, u32[]{:S(2)}, u32[]{:S(2)}) %collective-permute-start.20) | collective-permute-done | bytes 393248 | tf_op jit(solution)/shard_map/ppermute | solution.py:585
  159.5 6.0 %down_1_0.1 = (f32[512,1024]{1,0:T(8,128)S(1)}, f32[8,128]{1,0:T(8,128)S(1)}) custom-call(s32[3]{0:T(128)S(1)} %pad_add_fusion.place, bf16[3,512,384]{2,1,0:T(8,128)(2,1)S(1)} %get-tuple-element.82.own, bf16[3,512,384]{2,1,0:T(8,128)(2,1)S(1)} %collective-permute-done.26.other, bf16[2,8,384,1024]{3,2,1,0:T(8,128)(2,1)} %bitcast.14, ...), custom_call_target="tpu_custom_call" | custom-call | flops 1 | bytes 1 | tf_op jit(solution)/shard_map/down_1_0/pallas_call | solution.py:542
  165.5 6.2 %collective-permute-done.23.refs_1_ = bf16[512,384]{1,0:T(8,128)(2,1)S(1)} collective-permute-done((bf16[512,384]{1,0:T(8,128)(2,1)S(1)}, bf16[512,384]{1,0:T(8,128)(2,1)S(1)}, u32[]{:S(2)}, u32[]{:S(2)}) %collective-permute-start.23) | collective-permute-done | bytes 393248 | tf_op jit(solution)/shard_map/ppermute | solution.py:634
  173.9 3.3 %down_0_3.1 = (f32[512,1024]{1,0:T(8,128)S(1)}, f32[8,128]{1,0:T(8,128)S(1)}) custom-call(s32[3]{0:T(128)S(1)} %pad_add_fusion.place, bf16[1,512,384]{2,1,0:T(8,128)(2,1)S(1)} %get-tuple-element.86.own, bf16[1,512,384]{2,1,0:T(8,128)(2,1)S(1)} %collective-permute-done.27.other, bf16[2,8,384,1024]{3,2,1,0:T(8,128)(2,1)} %bitcast.20, ...), custom_call_target="tpu_custom_call" | custom-call | flops 1 | bytes 1 | tf_op jit(solution)/shard_map/down_0_3/pallas_call | solution.py:542
  177.2 8.8 %collective-permute-done.21.refs_1_ = bf16[512,384]{1,0:T(8,128)(2,1)S(1)} collective-permute-done((bf16[512,384]{1,0:T(8,128)(2,1)S(1)}, bf16[512,384]{1,0:T(8,128)(2,1)S(1)}, u32[]{:S(2)}, u32[]{:S(2)}) %collective-permute-start.21) | collective-permute-done | bytes 393248 | tf_op jit(solution)/shard_map/ppermute | solution.py:634
  186.2 1.7 collective-permute-done.28.other
  187.9 3.8 %down_1_3.1 = (bf16[128,1024]{1,0:T(8,128)(2,1)S(1)}, bf16[128,1024]{1,0:T(8,128)(2,1)S(1)}, bf16[128,1024]{1,0:T(8,128)(2,1)S(1)}, bf16[128,1024]{1,0:T(8,128)(2,1)S(1)}, f32[8,128]{1,0:T(8,128)}) custom-call(s32[3]{0:T(128)S(1)} %pad_add_fusion.place, bf16[1,512,384]{2,1,0:T(8,128)(2,1)S(1)} %get-tuple-element.90.own, ...), custom_call_target="tpu_custom_call" | custom-call | flops 1 | bytes 1 | tf_op jit(solution)/shard_map/down_1_3/pallas_call | solution.py:542
  191.7 1.7 collective-permute-start.31
  195.2 6.6 %collective-permute-done.31 = bf16[128,1024]{1,0:T(8,128)(2,1)S(1)} collective-permute-done((bf16[128,1024]{1,0:T(8,128)(2,1)S(1)}, bf16[128,1024]{1,0:T(8,128)(2,1)S(1)}, u32[]{:S(2)}, u32[]{:S(2)}) %collective-permute-start.31) | collective-permute-done | bytes 262176 | tf_op jit(solution)/shard_map/ppermute | solution.py:582
  201.8 4.8 %collective-permute-done.30 = bf16[128,1024]{1,0:T(8,128)(2,1)S(1)} collective-permute-done((bf16[128,1024]{1,0:T(8,128)(2,1)S(1)}, bf16[128,1024]{1,0:T(8,128)(2,1)S(1)}, u32[]{:S(2)}, u32[]{:S(2)}) %collective-permute-start.30) | collective-permute-done | bytes 262176 | tf_op jit(solution)/shard_map/ppermute | solution.py:582
  (107 shorter events, 29.8 us)
Async XLA Ops:
  1.1 1.7 collective-permute-start
  2.8 6.2 %collective-permute-start.3 = (f32[1,128]{1,0:T(1,128)S(1)}, f32[1,128]{1,0:T(1,128)S(1)}, u32[]{:S(2)}, u32[]{:S(2)}) collective-permute-start(f32[1,128]{1,0:T(1,128)S(1)} %add.90), channel_id=1, source_target_pairs={{0,6},{1,7},{2,4},{3,5},{4,2},{5,3},{6,0},{7,1},{8,14},{9,15},{10,... | collective-permute-start | bytes 1544 | tf_op jit(solution)/shard_map/ppermute | solution.py:585
  7.5 3.5 %collective-permute-start.1 = (f32[1,128]{1,0:T(1,128)S(1)}, f32[1,128]{1,0:T(1,128)S(1)}, u32[]{:S(2)}, u32[]{:S(2)}) collective-permute-start(f32[1,128]{1,0:T(1,128)S(1)} %add.90), channel_id=1, source_target_pairs={{0,2},{1,3},{2,0},{3,1},{4,6},{5,7},{6,4},{7,5},{8,10},{9,11},{10,... | collective-permute-start | bytes 1544 | tf_op jit(solution)/shard_map/ppermute | solution.py:585
  7.5 4.4 %collective-permute-start.2 = (f32[1,128]{1,0:T(1,128)S(1)}, f32[1,128]{1,0:T(1,128)S(1)}, u32[]{:S(2)}, u32[]{:S(2)}) collective-permute-start(f32[1,128]{1,0:T(1,128)S(1)} %add.90), channel_id=1, source_target_pairs={{0,4},{1,5},{2,6},{3,7},{4,0},{5,1},{6,2},{7,3},{8,12},{9,13},{10,... | collective-permute-start | bytes 1544 | tf_op jit(solution)/shard_map/ppermute | solution.py:585
  13.0 21.9 %collective-permute-start.4 = (bf16[128,1024]{1,0:T(8,128)(2,1)S(1)}, bf16[128,1024]{1,0:T(8,128)(2,1)S(1)}, u32[]{:S(2)}, u32[]{:S(2)}) collective-permute-start(bf16[128,1024]{1,0:T(8,128)(2,1)S(1)} %multiply_convert_fusion), channel_id=1, source_target_pairs={{0,0},{1,1},{2,8},{3,9},{4,16},{5,17},{6,24},{7,25},{8,2},{9,3},{1... | collective-permute-start | bytes 786440 | tf_op jit(solution)/shard_map/ppermute | solution.py:596
  13.7 21.2 %collective-permute-start.5 = (bf16[128,1024]{1,0:T(8,128)(2,1)S(1)}, bf16[128,1024]{1,0:T(8,128)(2,1)S(1)}, u32[]{:S(2)}, u32[]{:S(2)}) collective-permute-start(bf16[128,1024]{1,0:T(8,128)(2,1)S(1)} %multiply_convert_fusion), channel_id=1, source_target_pairs={{0,2},{1,3},{2,10},{3,11},{4,18},{5,19},{6,26},{7,27},{8,0},{9,1},... | collective-permute-start | bytes 786440 | tf_op jit(solution)/shard_map/ppermute | solution.py:596
  18.0 17.0 %collective-permute-start.6 = (bf16[128,1024]{1,0:T(8,128)(2,1)S(1)}, bf16[128,1024]{1,0:T(8,128)(2,1)S(1)}, u32[]{:S(2)}, u32[]{:S(2)}) collective-permute-start(bf16[128,1024]{1,0:T(8,128)(2,1)S(1)} %multiply_convert_fusion), channel_id=1, source_target_pairs={{0,4},{1,5},{2,12},{3,13},{4,20},{5,21},{6,28},{7,29},{8,6},{9,7},... | collective-permute-start | bytes 786440 | tf_op jit(solution)/shard_map/ppermute | solution.py:596
  19.6 15.3 %collective-permute-start.7 = (bf16[128,1024]{1,0:T(8,128)(2,1)S(1)}, bf16[128,1024]{1,0:T(8,128)(2,1)S(1)}, u32[]{:S(2)}, u32[]{:S(2)}) collective-permute-start(bf16[128,1024]{1,0:T(8,128)(2,1)S(1)} %multiply_convert_fusion), channel_id=1, source_target_pairs={{0,6},{1,7},{2,14},{3,15},{4,22},{5,23},{6,30},{7,31},{8,4},{9,5},... | collective-permute-start | bytes 786440 | tf_op jit(solution)/shard_map/ppermute | solution.py:596
  35.7 2.7 %collective-permute-start.8 = (bf16[512,1024]{1,0:T(8,128)(2,1)S(1)}, bf16[512,1024]{1,0:T(8,128)(2,1)S(1)}, u32[]{:S(2)}, u32[]{:S(2)}) collective-permute-start(bf16[512,1024]{1,0:T(8,128)(2,1)S(1)} %pack.1.own), channel_id=1, source_target_pairs={{0,1},{1,0},{2,3},{3,2},{4,5},{5,4},{6,7},{7,6},{8,9},{9,8},{10,11... | collective-permute-start | bytes 3145736 | tf_op jit(solution)/shard_map/ppermute | solution.py:588
  51.0 25.1 %collective-permute-start.9 = (bf16[2,256,768]{2,1,0:T(8,128)(2,1)}, bf16[2,256,768]{2,1,0:T(8,128)(2,1)S(1)}, u32[]{:S(2)}, u32[]{:S(2)}) collective-permute-start(bf16[2,256,768]{2,1,0:T(8,128)(2,1)} %get-tuple-element.56), channel_id=1, source_target_pairs={{0,8},{8,0},{16,24},{24,16},{1,9},{9,1},{17,25},{25,17},{2,10},{10... | collective-permute-start | bytes 2359304 | tf_op jit(solution)/shard_map/ppermute | solution.py:582
  52.5 29.4 %collective-permute-start.10 = (bf16[2,256,768]{2,1,0:T(8,128)(2,1)}, bf16[2,256,768]{2,1,0:T(8,128)(2,1)S(1)}, u32[]{:S(2)}, u32[]{:S(2)}) collective-permute-start(bf16[2,256,768]{2,1,0:T(8,128)(2,1)} %get-tuple-element.58), channel_id=1, source_target_pairs={{0,16},{8,24},{16,0},{24,8},{1,17},{9,25},{17,1},{25,9},{2,18},{10... | collective-permute-start | bytes 2359304 | tf_op jit(solution)/shard_map/ppermute | solution.py:582
  83.3 15.0 %collective-permute-start.11 = (bf16[256,768]{1,0:T(8,128)(2,1)S(1)}, bf16[256,768]{1,0:T(8,128)(2,1)S(1)}, u32[]{:S(2)}, u32[]{:S(2)}) collective-permute-start(bf16[256,768]{1,0:T(8,128)(2,1)S(1)} %get-tuple-element.64), channel_id=1, source_target_pairs={{0,16},{8,24},{16,0},{24,8},{1,17},{9,25},{17,1},{25,9},{2,18},{10... | collective-permute-start | bytes 1179656 | tf_op jit(solution)/shard_map/ppermute | solution.py:582
  85.1 13.3 %collective-permute-start.12 = (bf16[256,768]{1,0:T(8,128)(2,1)S(1)}, bf16[256,768]{1,0:T(8,128)(2,1)S(1)}, u32[]{:S(2)}, u32[]{:S(2)}) collective-permute-start(bf16[256,768]{1,0:T(8,128)(2,1)S(1)} %get-tuple-element.65), channel_id=1, source_target_pairs={{0,8},{8,0},{16,24},{24,16},{1,9},{9,1},{17,25},{25,17},{2,10},{10... | collective-permute-start | bytes 1179656 | tf_op jit(solution)/shard_map/ppermute | solution.py:582
  100.7 18.6 %collective-permute-start.13 = (bf16[2,256,768]{2,1,0:T(8,128)(2,1)}, bf16[2,256,768]{2,1,0:T(8,128)(2,1)S(1)}, u32[]{:S(2)}, u32[]{:S(2)}) collective-permute-start(bf16[2,256,768]{2,1,0:T(8,128)(2,1)} %get-tuple-element.68), channel_id=1, source_target_pairs={{0,8},{8,0},{16,24},{24,16},{1,9},{9,1},{17,25},{25,17},{2,10},{10... | collective-permute-start | bytes 2359304 | tf_op jit(solution)/shard_map/ppermute | solution.py:582
  101.1 18.3 %collective-permute-start.14 = (bf16[2,256,768]{2,1,0:T(8,128)(2,1)}, bf16[2,256,768]{2,1,0:T(8,128)(2,1)S(1)}, u32[]{:S(2)}, u32[]{:S(2)}) collective-permute-start(bf16[2,256,768]{2,1,0:T(8,128)(2,1)} %get-tuple-element.70), channel_id=1, source_target_pairs={{0,16},{8,24},{16,0},{24,8},{1,17},{9,25},{17,1},{25,9},{2,18},{10... | collective-permute-start | bytes 2359304 | tf_op jit(solution)/shard_map/ppermute | solution.py:582
  101.3 18.2 %collective-permute-start.17 = (bf16[512,384]{1,0:T(8,128)(2,1)S(1)}, bf16[512,384]{1,0:T(8,128)(2,1)S(1)}, u32[]{:S(2)}, u32[]{:S(2)}) collective-permute-start(bf16[512,384]{1,0:T(8,128)(2,1)S(1)} %get-tuple-element.74.refs_0_), channel_id=1, source_target_pairs={{0,2},{1,3},{2,0},{3,1},{4,6},{5,7},{6,4},{7,5},{8,10},{9,11},{10,... | collective-permute-start | bytes 1179656 | tf_op jit(solution)/shard_map/ppermute | solution.py:585
  101.3 18.9 %collective-permute-start.18 = (bf16[512,384]{1,0:T(8,128)(2,1)S(1)}, bf16[512,384]{1,0:T(8,128)(2,1)S(1)}, u32[]{:S(2)}, u32[]{:S(2)}) collective-permute-start(bf16[512,384]{1,0:T(8,128)(2,1)S(1)} %get-tuple-element.74.refs_0_), channel_id=1, source_target_pairs={{0,4},{1,5},{2,6},{3,7},{4,0},{5,1},{6,2},{7,3},{8,12},{9,13},{10,... | collective-permute-start | bytes 1179656 | tf_op jit(solution)/shard_map/ppermute | solution.py:585
  121.4 18.8 %collective-permute-start.25 = (bf16[3,512,384]{2,1,0:T(8,128)(2,1)S(1)}, bf16[3,512,384]{2,1,0:T(8,128)(2,1)}, u32[]{:S(2)}, u32[]{:S(2)}) collective-permute-start(bf16[3,512,384]{2,1,0:T(8,128)(2,1)S(1)} %get-tuple-element.78.own), channel_id=1, source_target_pairs={{0,1},{1,0},{2,3},{3,2},{4,5},{5,4},{6,7},{7,6},{8,9},{9,8},{10,11... | collective-permute-start | bytes 3538952 | tf_op jit(solution)/shard_map/ppermute | solution.py:588
  121.5 11.5 %collective-permute-start.15 = (bf16[256,768]{1,0:T(8,128)(2,1)S(1)}, bf16[256,768]{1,0:T(8,128)(2,1)S(1)}, u32[]{:S(2)}, u32[]{:S(2)}) collective-permute-start(bf16[256,768]{1,0:T(8,128)(2,1)S(1)} %get-tuple-element.72), channel_id=1, source_target_pairs={{0,16},{8,24},{16,0},{24,8},{1,17},{9,25},{17,1},{25,9},{2,18},{10... | collective-permute-start | bytes 1179656 | tf_op jit(solution)/shard_map/ppermute | solution.py:582
  122.9 11.2 %collective-permute-start.16 = (bf16[256,768]{1,0:T(8,128)(2,1)S(1)}, bf16[256,768]{1,0:T(8,128)(2,1)S(1)}, u32[]{:S(2)}, u32[]{:S(2)}) collective-permute-start(bf16[256,768]{1,0:T(8,128)(2,1)S(1)} %get-tuple-element.73), channel_id=1, source_target_pairs={{0,8},{8,0},{16,24},{24,16},{1,9},{9,1},{17,25},{25,17},{2,10},{10... | collective-permute-start | bytes 1179656 | tf_op jit(solution)/shard_map/ppermute | solution.py:582
  135.3 20.1 %collective-permute-start.20 = (bf16[512,384]{1,0:T(8,128)(2,1)}, bf16[512,384]{1,0:T(8,128)(2,1)S(1)}, u32[]{:S(2)}, u32[]{:S(2)}) collective-permute-start(bf16[512,384]{1,0:T(8,128)(2,1)} %get-tuple-element.77.refs_0_), channel_id=1, source_target_pairs={{0,4},{1,5},{2,6},{3,7},{4,0},{5,1},{6,2},{7,3},{8,12},{9,13},{10,... | collective-permute-start | bytes 1179656 | tf_op jit(solution)/shard_map/ppermute | solution.py:585
  138.0 17.5 %collective-permute-start.24 = (bf16[512,384]{1,0:T(8,128)(2,1)}, bf16[512,384]{1,0:T(8,128)(2,1)S(1)}, u32[]{:S(2)}, u32[]{:S(2)}) collective-permute-start(bf16[512,384]{1,0:T(8,128)(2,1)} %get-tuple-element.77.refs_0_), channel_id=1, source_target_pairs={{0,2},{1,3},{2,0},{3,1},{4,6},{5,7},{6,4},{7,5},{8,10},{9,11},{10,... | collective-permute-start | bytes 1179656 | tf_op jit(solution)/shard_map/ppermute | solution.py:585
  156.6 2.9 %collective-permute-start.26 = (bf16[3,512,384]{2,1,0:T(8,128)(2,1)S(1)}, bf16[3,512,384]{2,1,0:T(8,128)(2,1)S(1)}, u32[]{:S(2)}, u32[]{:S(2)}) collective-permute-start(bf16[3,512,384]{2,1,0:T(8,128)(2,1)S(1)} %get-tuple-element.82.own), channel_id=1, source_target_pairs={{0,1},{1,0},{2,3},{3,2},{4,5},{5,4},{6,7},{7,6},{8,9},{9,8},{10,11... | collective-permute-start | bytes 3538952 | tf_op jit(solution)/shard_map/ppermute | solution.py:588
  156.7 8.9 %collective-permute-start.22 = (bf16[512,384]{1,0:T(8,128)(2,1)S(1)}, bf16[512,384]{1,0:T(8,128)(2,1)S(1)}, u32[]{:S(2)}, u32[]{:S(2)}) collective-permute-start(bf16[512,384]{1,0:T(8,128)(2,1)S(1)} %get-tuple-element.74.refs_0_), channel_id=1, source_target_pairs={{2,4},{3,5},{4,2},{5,3},{10,12},{11,13},{12,10},{13,11},{18,20},{1... | collective-permute-start | bytes 1179656 | tf_op jit(solution)/shard_map/ppermute | solution.py:633
  157.4 14.4 %collective-permute-start.23 = (bf16[512,384]{1,0:T(8,128)(2,1)S(1)}, bf16[512,384]{1,0:T(8,128)(2,1)S(1)}, u32[]{:S(2)}, u32[]{:S(2)}) collective-permute-start(bf16[512,384]{1,0:T(8,128)(2,1)S(1)} %collective-permute-done.18.refs_2_), channel_id=1, source_target_pairs={{2,0},{3,1},{4,6},{5,7},{10,8},{11,9},{12,14},{13,15},{18,16},{19,... | collective-permute-start | bytes 1179656 | tf_op jit(solution)/shard_map/ppermute | solution.py:634
  171.8 2.1 %collective-permute-start.27 = (bf16[1,512,384]{2,1,0:T(8,128)(2,1)S(1)}, bf16[1,512,384]{2,1,0:T(8,128)(2,1)S(1)}, u32[]{:S(2)}, u32[]{:S(2)}) collective-permute-start(bf16[1,512,384]{2,1,0:T(8,128)(2,1)S(1)} %get-tuple-element.86.own), channel_id=1, source_target_pairs={{0,1},{1,0},{2,3},{3,2},{4,5},{5,4},{6,7},{7,6},{8,9},{9,8},{10,11... | collective-permute-start | bytes 1179656 | tf_op jit(solution)/shard_map/ppermute | solution.py:588
  171.9 5.3 %collective-permute-start.19 = (bf16[512,384]{1,0:T(8,128)(2,1)}, bf16[512,384]{1,0:T(8,128)(2,1)S(1)}, u32[]{:S(2)}, u32[]{:S(2)}) collective-permute-start(bf16[512,384]{1,0:T(8,128)(2,1)} %get-tuple-element.77.refs_0_), channel_id=1, source_target_pairs={{2,4},{3,5},{4,2},{5,3},{10,12},{11,13},{12,10},{13,11},{18,20},{1... | collective-permute-start | bytes 1179656 | tf_op jit(solution)/shard_map/ppermute | solution.py:633
  172.6 13.4 %collective-permute-start.21 = (bf16[512,384]{1,0:T(8,128)(2,1)S(1)}, bf16[512,384]{1,0:T(8,128)(2,1)S(1)}, u32[]{:S(2)}, u32[]{:S(2)}) collective-permute-start(bf16[512,384]{1,0:T(8,128)(2,1)S(1)} %collective-permute-done.20.refs_2_), channel_id=1, source_target_pairs={{2,0},{3,1},{4,6},{5,7},{10,8},{11,9},{12,14},{13,15},{18,16},{19,... | collective-permute-start | bytes 1179656 | tf_op jit(solution)/shard_map/ppermute | solution.py:634
  186.1 1.8 collective-permute-start.28
  191.7 10.1 %collective-permute-start.31 = (bf16[128,1024]{1,0:T(8,128)(2,1)S(1)}, bf16[128,1024]{1,0:T(8,128)(2,1)S(1)}, u32[]{:S(2)}, u32[]{:S(2)}) collective-permute-start(bf16[128,1024]{1,0:T(8,128)(2,1)S(1)} %get-tuple-element.96), channel_id=1, source_target_pairs={{0,24},{8,16},{16,8},{24,0},{1,25},{9,17},{17,9},{25,1},{2,26},{10... | collective-permute-start | bytes 786440 | tf_op jit(solution)/shard_map/ppermute | solution.py:582
  193.4 13.1 %collective-permute-start.30 = (bf16[128,1024]{1,0:T(8,128)(2,1)S(1)}, bf16[128,1024]{1,0:T(8,128)(2,1)S(1)}, u32[]{:S(2)}, u32[]{:S(2)}) collective-permute-start(bf16[128,1024]{1,0:T(8,128)(2,1)S(1)} %get-tuple-element.95), channel_id=1, source_target_pairs={{0,16},{8,24},{16,0},{24,8},{1,17},{9,25},{17,1},{25,9},{2,18},{10... | collective-permute-start | bytes 786440 | tf_op jit(solution)/shard_map/ppermute | solution.py:582
  194.8 11.7 %collective-permute-start.29 = (bf16[128,1024]{1,0:T(8,128)(2,1)S(1)}, bf16[128,1024]{1,0:T(8,128)(2,1)S(1)}, u32[]{:S(2)}, u32[]{:S(2)}) collective-permute-start(bf16[128,1024]{1,0:T(8,128)(2,1)S(1)} %get-tuple-element.94), channel_id=1, source_target_pairs={{0,8},{8,0},{16,24},{24,16},{1,9},{9,1},{17,25},{25,17},{2,10},{10... | collective-permute-start | bytes 786440 | tf_op jit(solution)/shard_map/ppermute | solution.py:582
  (16 other events, 82.0 us)

commit v12 on v10

--- a/solution.py
+++ b/solution.py
@@ -281,7 +281,7 @@
             in_specs=[whole, whole] + [ANY_SPEC] * len(after),
             out_specs=[pl.BlockSpec(block, lambda k, *_: (0, k, 0)), MARK_SPEC],
         ),
-        compiler_params=pltpu.CompilerParams(vmem_limit_bytes=54 * MIB),
+        compiler_params=pltpu.CompilerParams(vmem_limit_bytes=53 * MIB),
         cost_estimate=LITTLE,
         name=f"spread_gate_up_{chunk}",
     )(gate_at, up_at, gate, up, *after)
@@ -493,7 +493,7 @@
             pl.BlockSpec((1,) + out.shape[1:], lambda n: (jnp.maximum(n - 2, 0), 0, 0)),
             MARK_SPEC,
         ],
-        compiler_params=pltpu.CompilerParams(vmem_limit_bytes=54 * MIB),
+        compiler_params=pltpu.CompilerParams(vmem_limit_bytes=53 * MIB),
         cost_estimate=LITTLE,
         name=f"gate_up_{chunk}",
     )(own, other, dense, *after)
@@ -644,14 +644,14 @@
         last_a, last_b = swap_tok(last_a, 2), swap_tok(last_b, 1)
         if chunk:
             held, mark = stack(early, (0, 1, 2), mark)
+        else:
+            *sums, mark = panel_product(own, other, dense, [mark], 1)
+        hidden, mark = combine(kept_a, came_a, last_a, kept_b, came_b, last_b, [mark], chunk)
+        if chunk:
             mixed, mark = down_steps(
                 place, held, swap_core(held), (0, 1, 2), down_dense, None, 0, False, mark
             )
             held, mark = stack(late, (3,), mark)
-        else:
-            *sums, mark = panel_product(own, other, dense, [mark], 1)
-        hidden, mark = combine(kept_a, came_a, last_a, kept_b, came_b, last_b, [mark], chunk)
-        if chunk:
             mixed, mark = down_steps(
                 place, held, swap_core(held), (3,), down_dense, mixed, 0, False, mark
             )

time: 201 us -> 201 us (level)
  waiting for transfers between devices: 48.3 us -> 52.2 us
  local copies, waits for them, and re-layouts: 8.38 us -> 5.17 us
    ppermute x11, waiting for transfers between devices: 17.2 us -> 24.8 us  [swap_tok(): return lax.ppermute(array, 'tok', [(i, i ^ step) for i in parts])]
    unnamed x28 -> x18, local copies, waits for them, and re-layouts: 5.83 us -> 3.22 us
    ppermute x2, waiting for transfers between devices: 8.41 us -> 6.25 us  [send(): ends = lax.ppermute(far, 'col', [(i, i ^ 2) for i in range(2, 6)])]
  transfers between devices with their start and end apart: 32 -> 32, of which waited for: 13 -> 14; matrix products, arithmetic and copies ran while one was open for 2% -> 2% of each run, Pallas kernels for 36% -> 35%
where the time goes in v12:
time: 201 us; the launch traced here: 200 us
  Pallas kernels  90.6 us (45%)
  waiting for transfers between devices  52.2 us (26%)
  starting transfers between devices  48.6 us (24%)
  local copies, waits for them, and re-layouts  5.17 us (3%)
  other arithmetic  3.21 us (2%)
    ppermute x11, waiting for transfers between devices, swap_tok(): return lax.ppermute(array, 'tok', [(i, i ^ step) for i in parts])  24.8 us
    ppermute x11, starting transfers between devices, swap_tok(): return lax.ppermute(array, 'tok', [(i, i ^ step) for i in parts])  24 us
    pallas_call x2, Pallas kernels, spread_shares(): pl.pallas_call(functools.partial(spread_shares_kernel, rows=rows // steps...  23.9 us
    pallas_call x2, Pallas kernels, panel_product(): pl.pallas_call(panel_product_kernel, out_shape=[out] * 4 + [MARK], grid=(...  22.7 us
    pallas_call x4, Pallas kernels, down_steps(): pl.pallas_call(functools.partial(down_steps_kernel, added=len(added), out...  20.1 us
    pallas_call x1, Pallas kernels, spread_panels(): pl.pallas_call(functools.partial(spread_panels_kernel, chunks=chunks, row...  16.3 us
    ppermute x7, waiting for transfers between devices, swap_chip(): lax.ppermute(array, 'col', [(i, i ^ 2 * step) for i in range(col_size)])  16.1 us
    ppermute x7, starting transfers between devices, swap_chip(): lax.ppermute(array, 'col', [(i, i ^ 2 * step) for i in range(col_size)])  10.7 us
  transfers between devices with their start and end apart: 32, of which 14 were waited for; matrix products, arithmetic and copies ran while one was open for 2% of the time, Pallas kernels for 35%

profile of v12, /device:TPU:0, one launch (start us, length us, event | category | flops | bytes accessed | tf_op | source)
XLA Modules:
  0.0 200.1 jit_solution(4909828496841896718)
XLA Ops:
  2.8 4.7 %collective-permute-start.3 = (f32[1,128]{1,0:T(1,128)S(1)}, f32[1,128]{1,0:T(1,128)S(1)}, u32[]{:S(2)}, u32[]{:S(2)}) collective-permute-start(f32[1,128]{1,0:T(1,128)S(1)} %add.90), channel_id=1, source_target_pairs={{0,6},{1,7},{2,4},{3,5},{4,2},{5,3},{6,0},{7,1},{8,14},{9,15},{10,... | collective-permute-start | bytes 1544 | tf_op jit(solution)/shard_map/ppermute | solution.py:585
  9.0 2.0 %collective-permute-done.1 = f32[1,128]{1,0:T(1,128)S(1)} collective-permute-done((f32[1,128]{1,0:T(1,128)S(1)}, f32[1,128]{1,0:T(1,128)S(1)}, u32[]{:S(2)}, u32[]{:S(2)}) %collective-permute-start.1) | collective-permute-done | bytes 544 | tf_op jit(solution)/shard_map/ppermute | solution.py:585
  13.7 4.2 %collective-permute-start.5 = (bf16[128,1024]{1,0:T(8,128)(2,1)S(1)}, bf16[128,1024]{1,0:T(8,128)(2,1)S(1)}, u32[]{:S(2)}, u32[]{:S(2)}) collective-permute-start(bf16[128,1024]{1,0:T(8,128)(2,1)S(1)} %multiply_convert_fusion), channel_id=1, source_target_pairs={{0,2},{1,3},{2,10},{3,11},{4,18},{5,19},{6,26},{7,27},{8,0},{9,1},... | collective-permute-start | bytes 786440 | tf_op jit(solution)/shard_map/ppermute | solution.py:596
  18.0 1.7 collective-permute-start.6
  19.6 1.6 collective-permute-start.7
  22.2 11.9 %spread_gate_up_0.1 = (bf16[1,2048,3072]{2,1,0:T(8,128)(2,1)}, f32[8,128]{1,0:T(8,128)S(1)}) custom-call(s32[192]{0:T(256)S(1)} %get-tuple-element.103.gate_at, s32[192]{0:T(256)S(1)} %get-tuple-element.100.up_at, bf16[1,216,128,128]{3,2,1,0:T(8,128)(2,1)} %refs_0_.3, bf16[1,216,128,128]{3,2,1,0:T(8,128)(2,1)} %refs_1_.3), custom_call_target="tpu_custom_call" | custom-call | flops 1 | bytes 1 | tf_op jit(solution)/shard_map/spread_gate_up_0/pallas_call | solution.py:275
  34.3 2.6 %collective-permute-done.8.other = bf16[512,1024]{1,0:T(8,128)(2,1)S(1)} collective-permute-done((bf16[512,1024]{1,0:T(8,128)(2,1)S(1)}, bf16[512,1024]{1,0:T(8,128)(2,1)S(1)}, u32[]{:S(2)}, u32[]{:S(2)}) %collective-permute-start.8) | collective-permute-done | bytes 1048608 | tf_op jit(solution)/shard_map/ppermute | solution.py:588
  38.0 11.4 %gate_up_0.1 = (bf16[2,256,768]{2,1,0:T(8,128)(2,1)S(1)}, bf16[2,256,768]{2,1,0:T(8,128)(2,1)}, bf16[2,256,768]{2,1,0:T(8,128)(2,1)}, bf16[2,256,768]{2,1,0:T(8,128)(2,1)}, f32[8,128]{1,0:T(8,128)S(1)}) custom-call(bf16[512,1024]{1,0:T(8,128)(2,1)} %copy-done, bf16[512,1024]{1,0:T(8,128)(2,1)} %copy-done.7, bf16[1,2048,3072]{2,1,0:T(8,128)(2,1)} %get-tuple-element.52.weight), custom_call_target="tpu_custom_call" | custom-call | flops 1 | bytes 1 | tf_op jit(solution)/shard_map/gate_up_0/pallas_call | solution.py:482
  49.3 1.5 collective-permute-start.9
  50.8 12.0 %collective-permute-start.10 = (bf16[2,256,768]{2,1,0:T(8,128)(2,1)}, bf16[2,256,768]{2,1,0:T(8,128)(2,1)S(1)}, u32[]{:S(2)}, u32[]{:S(2)}) collective-permute-start(bf16[2,256,768]{2,1,0:T(8,128)(2,1)} %get-tuple-element.58), channel_id=1, source_target_pairs={{0,16},{8,24},{16,0},{24,8},{1,17},{9,25},{17,1},{25,9},{2,18},{10... | collective-permute-start | bytes 2359304 | tf_op jit(solution)/shard_map/ppermute | solution.py:582
  62.8 11.9 %spread_gate_up_1.1 = (bf16[1,2048,3072]{2,1,0:T(8,128)(2,1)}, f32[8,128]{1,0:T(8,128)S(1)}) custom-call(s32[192]{0:T(256)S(1)} %get-tuple-element.104.gate_at, s32[192]{0:T(256)S(1)} %get-tuple-element.99.up_at, bf16[1,216,128,128]{3,2,1,0:T(8,128)(2,1)} %refs_0_.3, bf16[1,216,128,128]{3,2,1,0:T(8,128)(2,1)} %refs_1_.3, f32[8,128]{1,0:T(8,128)S(1)} %get-tuple-element.53.refs_2_), custom_call_target="tpu_custom_call" | custom-call | flops 1 | bytes 1 | tf_op jit(solution)/shard_map/spread_gate_up_1/pallas_call | solution.py:275
  74.8 6.1 %collective-permute-done.10.came_b.refs_4_ = bf16[2,256,768]{2,1,0:T(8,128)(2,1)S(1)} collective-permute-done((bf16[2,256,768]{2,1,0:T(8,128)(2,1)}, bf16[2,256,768]{2,1,0:T(8,128)(2,1)S(1)}, u32[]{:S(2)}, u32[]{:S(2)}) %collective-permute-start.10) | collective-permute-done | bytes 786464 | tf_op jit(solution)/shard_map/ppermute | solution.py:582
  81.1 1.8 collective-permute-start.11
  82.9 1.7 collective-permute-start.12
  84.6 11.4 %gate_up_1.1 = (bf16[2,256,768]{2,1,0:T(8,128)(2,1)S(1)}, bf16[2,256,768]{2,1,0:T(8,128)(2,1)}, bf16[2,256,768]{2,1,0:T(8,128)(2,1)}, bf16[2,256,768]{2,1,0:T(8,128)(2,1)}, f32[8,128]{1,0:T(8,128)S(1)}) custom-call(bf16[512,1024]{1,0:T(8,128)(2,1)} %copy-done, bf16[512,1024]{1,0:T(8,128)(2,1)} %copy-done.7, bf16[1,2048,3072]{2,1,0:T(8,128)(2,1)} %get-tuple-element.54.weight, ...), custom_call_target="tpu_custom_call" | custom-call | flops 1 | bytes 1 | tf_op jit(solution)/shard_map/gate_up_1/pallas_call | solution.py:482
  100.0 16.3 %spread_down.1 = (bf16[2,3072,1024]{2,1,0:T(8,128)(2,1)}, f32[8,128]{1,0:T(8,128)S(1)}) custom-call(s32[384]{0:T(512)S(1)} %reshape.90.at_ref, bf16[8,108,128,128]{3,2,1,0:T(8,128)(2,1)} %values_ref.1, f32[8,128]{1,0:T(8,128)S(1)} %copy-done.6), custom_call_target="tpu_custom_call" | custom-call | flops 1 | bytes 1 | tf_op jit(solution)/shard_map/spread_down/pallas_call | solution.py:304
  117.4 2.2 %stack.20 = (bf16[3,512,384]{2,1,0:T(8,128)(2,1)}, f32[8,128]{1,0:T(8,128)S(1)}) custom-call(bf16[512,384]{1,0:T(8,128)(2,1)S(1)} %get-tuple-element.74.refs_0_, bf16[512,384]{1,0:T(8,128)(2,1)} %collective-permute-done.17.refs_1_, bf16[512,384]{1,0:T(8,128)(2,1)} %collective-permute-done.18.refs_2_, f32[8,128]{1,0:T(8,128)S(1)} %get-tuple-element.75.refs_3_), custom_call_target="tpu_custom_call" | custom-call | flops 1 | bytes 1 | tf_op jit(solution)/shard_map/stack/pallas_call | solution.py:392
  120.9 1.5 collective-permute-start.16
  125.2 6.1 %collective-permute-done.15.refs_2_ = bf16[256,768]{1,0:T(8,128)(2,1)S(1)} collective-permute-done((bf16[256,768]{1,0:T(8,128)(2,1)}, bf16[256,768]{1,0:T(8,128)(2,1)S(1)}, u32[]{:S(2)}, u32[]{:S(2)}) %collective-permute-start.15) | collective-permute-done | bytes 393248 | tf_op jit(solution)/shard_map/ppermute | solution.py:582
  134.0 7.0 %down_0_0.1 = (f32[512,1024]{1,0:T(8,128)S(1)}, f32[8,128]{1,0:T(8,128)S(1)}) custom-call(s32[3]{0:T(128)S(1)} %pad_add_fusion.place, bf16[3,512,384]{2,1,0:T(8,128)(2,1)} %get-tuple-element.78.own, bf16[3,512,384]{2,1,0:T(8,128)(2,1)} %collective-permute-done.25.other, bf16[2,8,384,1024]{3,2,1,0:T(8,128)(2,1)} %bitcast.8, ...), custom_call_target="tpu_custom_call" | custom-call | flops 1 | bytes 1 | tf_op jit(solution)/shard_map/down_0_0/pallas_call | solution.py:542
  142.3 2.7 %collective-permute-start.20 = (bf16[512,384]{1,0:T(8,128)(2,1)S(1)}, bf16[512,384]{1,0:T(8,128)(2,1)S(1)}, u32[]{:S(2)}, u32[]{:S(2)}) collective-permute-start(bf16[512,384]{1,0:T(8,128)(2,1)S(1)} %get-tuple-element.77.refs_0_), channel_id=1, source_target_pairs={{0,4},{1,5},{2,6},{3,7},{4,0},{5,1},{6,2},{7,3},{8,12},{9,13},{10,... | collective-permute-start | bytes 1179656 | tf_op jit(solution)/shard_map/ppermute | solution.py:585
  145.0 2.0 %collective-permute-start.22 = (bf16[512,384]{1,0:T(8,128)(2,1)S(1)}, bf16[512,384]{1,0:T(8,128)(2,1)S(1)}, u32[]{:S(2)}, u32[]{:S(2)}) collective-permute-start(bf16[512,384]{1,0:T(8,128)(2,1)S(1)} %get-tuple-element.77.refs_0_), channel_id=1, source_target_pairs={{0,2},{1,3},{2,0},{3,1},{4,6},{5,7},{6,4},{7,5},{8,10},{9,11},{10,... | collective-permute-start | bytes 1179656 | tf_op jit(solution)/shard_map/ppermute | solution.py:585
  147.1 3.3 %down_0_3.1 = (f32[512,1024]{1,0:T(8,128)S(1)}, f32[8,128]{1,0:T(8,128)S(1)}) custom-call(s32[3]{0:T(128)S(1)} %pad_add_fusion.place, bf16[1,512,384]{2,1,0:T(8,128)(2,1)S(1)} %get-tuple-element.82.own, bf16[1,512,384]{2,1,0:T(8,128)(2,1)S(1)} %collective-permute-done.26.other, bf16[2,8,384,1024]{3,2,1,0:T(8,128)(2,1)} %bitcast.14, ...), custom_call_target="tpu_custom_call" | custom-call | flops 1 | bytes 1 | tf_op jit(solution)/shard_map/down_0_3/pallas_call | solution.py:542
  150.3 12.9 %collective-permute-done.20.refs_2_ = bf16[512,384]{1,0:T(8,128)(2,1)S(1)} collective-permute-done((bf16[512,384]{1,0:T(8,128)(2,1)S(1)}, bf16[512,384]{1,0:T(8,128)(2,1)S(1)}, u32[]{:S(2)}, u32[]{:S(2)}) %collective-permute-start.20) | collective-permute-done | bytes 393248 | tf_op jit(solution)/shard_map/ppermute | solution.py:585
  164.2 1.5 collective-permute-start.21
  166.4 6.0 %down_1_0.1 = (f32[512,1024]{1,0:T(8,128)S(1)}, f32[8,128]{1,0:T(8,128)S(1)}) custom-call(s32[3]{0:T(128)S(1)} %pad_add_fusion.place, bf16[3,512,384]{2,1,0:T(8,128)(2,1)S(1)} %get-tuple-element.86.own, bf16[3,512,384]{2,1,0:T(8,128)(2,1)S(1)} %collective-permute-done.27.other, bf16[2,8,384,1024]{3,2,1,0:T(8,128)(2,1)} %bitcast.16, ...), custom_call_target="tpu_custom_call" | custom-call | flops 1 | bytes 1 | tf_op jit(solution)/shard_map/down_1_0/pallas_call | solution.py:542
  172.4 6.2 %collective-permute-done.21.refs_1_ = bf16[512,384]{1,0:T(8,128)(2,1)S(1)} collective-permute-done((bf16[512,384]{1,0:T(8,128)(2,1)S(1)}, bf16[512,384]{1,0:T(8,128)(2,1)S(1)}, u32[]{:S(2)}, u32[]{:S(2)}) %collective-permute-start.21) | collective-permute-done | bytes 393248 | tf_op jit(solution)/shard_map/ppermute | solution.py:634
  178.8 1.7 collective-permute-done.28.other
  180.5 3.8 %down_1_3.1 = (bf16[128,1024]{1,0:T(8,128)(2,1)S(1)}, bf16[128,1024]{1,0:T(8,128)(2,1)S(1)}, bf16[128,1024]{1,0:T(8,128)(2,1)S(1)}, bf16[128,1024]{1,0:T(8,128)(2,1)S(1)}, f32[8,128]{1,0:T(8,128)}) custom-call(s32[3]{0:T(128)S(1)} %pad_add_fusion.place, bf16[1,512,384]{2,1,0:T(8,128)(2,1)S(1)} %get-tuple-element.90.own, ...), custom_call_target="tpu_custom_call" | custom-call | flops 1 | bytes 1 | tf_op jit(solution)/shard_map/down_1_3/pallas_call | solution.py:542
  185.8 1.7 collective-permute-start.30
  187.8 6.6 %collective-permute-done.31 = bf16[128,1024]{1,0:T(8,128)(2,1)S(1)} collective-permute-done((bf16[128,1024]{1,0:T(8,128)(2,1)S(1)}, bf16[128,1024]{1,0:T(8,128)(2,1)S(1)}, u32[]{:S(2)}, u32[]{:S(2)}) %collective-permute-start.31) | collective-permute-done | bytes 262176 | tf_op jit(solution)/shard_map/ppermute | solution.py:582
  194.4 4.8 %collective-permute-done.30 = bf16[128,1024]{1,0:T(8,128)(2,1)S(1)} collective-permute-done((bf16[128,1024]{1,0:T(8,128)(2,1)S(1)}, bf16[128,1024]{1,0:T(8,128)(2,1)S(1)}, u32[]{:S(2)}, u32[]{:S(2)}) %collective-permute-start.30) | collective-permute-done | bytes 262176 | tf_op jit(solution)/shard_map/ppermute | solution.py:582
  (93 shorter events, 26.5 us)
Async XLA Ops:
  1.1 1.7 collective-permute-start
  2.8 6.2 %collective-permute-start.3 = (f32[1,128]{1,0:T(1,128)S(1)}, f32[1,128]{1,0:T(1,128)S(1)}, u32[]{:S(2)}, u32[]{:S(2)}) collective-permute-start(f32[1,128]{1,0:T(1,128)S(1)} %add.90), channel_id=1, source_target_pairs={{0,6},{1,7},{2,4},{3,5},{4,2},{5,3},{6,0},{7,1},{8,14},{9,15},{10,... | collective-permute-start | bytes 1544 | tf_op jit(solution)/shard_map/ppermute | solution.py:585
  7.5 3.5 %collective-permute-start.1 = (f32[1,128]{1,0:T(1,128)S(1)}, f32[1,128]{1,0:T(1,128)S(1)}, u32[]{:S(2)}, u32[]{:S(2)}) collective-permute-start(f32[1,128]{1,0:T(1,128)S(1)} %add.90), channel_id=1, source_target_pairs={{0,2},{1,3},{2,0},{3,1},{4,6},{5,7},{6,4},{7,5},{8,10},{9,11},{10,... | collective-permute-start | bytes 1544 | tf_op jit(solution)/shard_map/ppermute | solution.py:585
  7.5 4.4 %collective-permute-start.2 = (f32[1,128]{1,0:T(1,128)S(1)}, f32[1,128]{1,0:T(1,128)S(1)}, u32[]{:S(2)}, u32[]{:S(2)}) collective-permute-start(f32[1,128]{1,0:T(1,128)S(1)} %add.90), channel_id=1, source_target_pairs={{0,4},{1,5},{2,6},{3,7},{4,0},{5,1},{6,2},{7,3},{8,12},{9,13},{10,... | collective-permute-start | bytes 1544 | tf_op jit(solution)/shard_map/ppermute | solution.py:585
  13.0 21.1 %collective-permute-start.4 = (bf16[128,1024]{1,0:T(8,128)(2,1)S(1)}, bf16[128,1024]{1,0:T(8,128)(2,1)S(1)}, u32[]{:S(2)}, u32[]{:S(2)}) collective-permute-start(bf16[128,1024]{1,0:T(8,128)(2,1)S(1)} %multiply_convert_fusion), channel_id=1, source_target_pairs={{0,0},{1,1},{2,8},{3,9},{4,16},{5,17},{6,24},{7,25},{8,2},{9,3},{1... | collective-permute-start | bytes 786440 | tf_op jit(solution)/shard_map/ppermute | solution.py:596
  13.7 20.4 %collective-permute-start.5 = (bf16[128,1024]{1,0:T(8,128)(2,1)S(1)}, bf16[128,1024]{1,0:T(8,128)(2,1)S(1)}, u32[]{:S(2)}, u32[]{:S(2)}) collective-permute-start(bf16[128,1024]{1,0:T(8,128)(2,1)S(1)} %multiply_convert_fusion), channel_id=1, source_target_pairs={{0,2},{1,3},{2,10},{3,11},{4,18},{5,19},{6,26},{7,27},{8,0},{9,1},... | collective-permute-start | bytes 786440 | tf_op jit(solution)/shard_map/ppermute | solution.py:596
  18.0 16.2 %collective-permute-start.6 = (bf16[128,1024]{1,0:T(8,128)(2,1)S(1)}, bf16[128,1024]{1,0:T(8,128)(2,1)S(1)}, u32[]{:S(2)}, u32[]{:S(2)}) collective-permute-start(bf16[128,1024]{1,0:T(8,128)(2,1)S(1)} %multiply_convert_fusion), channel_id=1, source_target_pairs={{0,4},{1,5},{2,12},{3,13},{4,20},{5,21},{6,28},{7,29},{8,6},{9,7},... | collective-permute-start | bytes 786440 | tf_op jit(solution)/shard_map/ppermute | solution.py:596
  19.6 14.5 %collective-permute-start.7 = (bf16[128,1024]{1,0:T(8,128)(2,1)S(1)}, bf16[128,1024]{1,0:T(8,128)(2,1)S(1)}, u32[]{:S(2)}, u32[]{:S(2)}) collective-permute-start(bf16[128,1024]{1,0:T(8,128)(2,1)S(1)} %multiply_convert_fusion), channel_id=1, source_target_pairs={{0,6},{1,7},{2,14},{3,15},{4,22},{5,23},{6,30},{7,31},{8,4},{9,5},... | collective-permute-start | bytes 786440 | tf_op jit(solution)/shard_map/ppermute | solution.py:596
  34.3 2.7 %collective-permute-start.8 = (bf16[512,1024]{1,0:T(8,128)(2,1)S(1)}, bf16[512,1024]{1,0:T(8,128)(2,1)S(1)}, u32[]{:S(2)}, u32[]{:S(2)}) collective-permute-start(bf16[512,1024]{1,0:T(8,128)(2,1)S(1)} %pack.1.own), channel_id=1, source_target_pairs={{0,1},{1,0},{2,3},{3,2},{4,5},{5,4},{6,7},{7,6},{8,9},{9,8},{10,11... | collective-permute-start | bytes 3145736 | tf_op jit(solution)/shard_map/ppermute | solution.py:588
  49.3 25.4 %collective-permute-start.9 = (bf16[2,256,768]{2,1,0:T(8,128)(2,1)}, bf16[2,256,768]{2,1,0:T(8,128)(2,1)S(1)}, u32[]{:S(2)}, u32[]{:S(2)}) collective-permute-start(bf16[2,256,768]{2,1,0:T(8,128)(2,1)} %get-tuple-element.56), channel_id=1, source_target_pairs={{0,8},{8,0},{16,24},{24,16},{1,9},{9,1},{17,25},{25,17},{2,10},{10... | collective-permute-start | bytes 2359304 | tf_op jit(solution)/shard_map/ppermute | solution.py:582
  50.8 30.1 %collective-permute-start.10 = (bf16[2,256,768]{2,1,0:T(8,128)(2,1)}, bf16[2,256,768]{2,1,0:T(8,128)(2,1)S(1)}, u32[]{:S(2)}, u32[]{:S(2)}) collective-permute-start(bf16[2,256,768]{2,1,0:T(8,128)(2,1)} %get-tuple-element.58), channel_id=1, source_target_pairs={{0,16},{8,24},{16,0},{24,8},{1,17},{9,25},{17,1},{25,9},{2,18},{10... | collective-permute-start | bytes 2359304 | tf_op jit(solution)/shard_map/ppermute | solution.py:582
  81.1 14.9 %collective-permute-start.11 = (bf16[256,768]{1,0:T(8,128)(2,1)S(1)}, bf16[256,768]{1,0:T(8,128)(2,1)S(1)}, u32[]{:S(2)}, u32[]{:S(2)}) collective-permute-start(bf16[256,768]{1,0:T(8,128)(2,1)S(1)} %get-tuple-element.64), channel_id=1, source_target_pairs={{0,16},{8,24},{16,0},{24,8},{1,17},{9,25},{17,1},{25,9},{2,18},{10... | collective-permute-start | bytes 1179656 | tf_op jit(solution)/shard_map/ppermute | solution.py:582
  82.9 13.1 %collective-permute-start.12 = (bf16[256,768]{1,0:T(8,128)(2,1)S(1)}, bf16[256,768]{1,0:T(8,128)(2,1)S(1)}, u32[]{:S(2)}, u32[]{:S(2)}) collective-permute-start(bf16[256,768]{1,0:T(8,128)(2,1)S(1)} %get-tuple-element.65), channel_id=1, source_target_pairs={{0,8},{8,0},{16,24},{24,16},{1,9},{9,1},{17,25},{25,17},{2,10},{10... | collective-permute-start | bytes 1179656 | tf_op jit(solution)/shard_map/ppermute | solution.py:582
  97.7 18.6 %collective-permute-start.13 = (bf16[2,256,768]{2,1,0:T(8,128)(2,1)}, bf16[2,256,768]{2,1,0:T(8,128)(2,1)S(1)}, u32[]{:S(2)}, u32[]{:S(2)}) collective-permute-start(bf16[2,256,768]{2,1,0:T(8,128)(2,1)} %get-tuple-element.68), channel_id=1, source_target_pairs={{0,8},{8,0},{16,24},{24,16},{1,9},{9,1},{17,25},{25,17},{2,10},{10... | collective-permute-start | bytes 2359304 | tf_op jit(solution)/shard_map/ppermute | solution.py:582
  98.0 18.3 %collective-permute-start.14 = (bf16[2,256,768]{2,1,0:T(8,128)(2,1)}, bf16[2,256,768]{2,1,0:T(8,128)(2,1)S(1)}, u32[]{:S(2)}, u32[]{:S(2)}) collective-permute-start(bf16[2,256,768]{2,1,0:T(8,128)(2,1)} %get-tuple-element.70), channel_id=1, source_target_pairs={{0,16},{8,24},{16,0},{24,8},{1,17},{9,25},{17,1},{25,9},{2,18},{10... | collective-permute-start | bytes 2359304 | tf_op jit(solution)/shard_map/ppermute | solution.py:582
  98.3 19.1 %collective-permute-start.17 = (bf16[512,384]{1,0:T(8,128)(2,1)S(1)}, bf16[512,384]{1,0:T(8,128)(2,1)}, u32[]{:S(2)}, u32[]{:S(2)}) collective-permute-start(bf16[512,384]{1,0:T(8,128)(2,1)S(1)} %get-tuple-element.74.refs_0_), channel_id=1, source_target_pairs={{0,2},{1,3},{2,0},{3,1},{4,6},{5,7},{6,4},{7,5},{8,10},{9,11},{10,... | collective-permute-start | bytes 1179656 | tf_op jit(solution)/shard_map/ppermute | solution.py:585
  98.3 19.1 %collective-permute-start.18 = (bf16[512,384]{1,0:T(8,128)(2,1)S(1)}, bf16[512,384]{1,0:T(8,128)(2,1)}, u32[]{:S(2)}, u32[]{:S(2)}) collective-permute-start(bf16[512,384]{1,0:T(8,128)(2,1)S(1)} %get-tuple-element.74.refs_0_), channel_id=1, source_target_pairs={{0,4},{1,5},{2,6},{3,7},{4,0},{5,1},{6,2},{7,3},{8,12},{9,13},{10,... | collective-permute-start | bytes 1179656 | tf_op jit(solution)/shard_map/ppermute | solution.py:585
  119.6 14.4 %collective-permute-start.25 = (bf16[3,512,384]{2,1,0:T(8,128)(2,1)}, bf16[3,512,384]{2,1,0:T(8,128)(2,1)}, u32[]{:S(2)}, u32[]{:S(2)}) collective-permute-start(bf16[3,512,384]{2,1,0:T(8,128)(2,1)} %get-tuple-element.78.own), channel_id=1, source_target_pairs={{0,1},{1,0},{2,3},{3,2},{4,5},{5,4},{6,7},{7,6},{8,9},{9,8},{10,11... | collective-permute-start | bytes 3538952 | tf_op jit(solution)/shard_map/ppermute | solution.py:588
  119.6 11.7 %collective-permute-start.15 = (bf16[256,768]{1,0:T(8,128)(2,1)}, bf16[256,768]{1,0:T(8,128)(2,1)S(1)}, u32[]{:S(2)}, u32[]{:S(2)}) collective-permute-start(bf16[256,768]{1,0:T(8,128)(2,1)} %get-tuple-element.72), channel_id=1, source_target_pairs={{0,16},{8,24},{16,0},{24,8},{1,17},{9,25},{17,1},{25,9},{2,18},{10... | collective-permute-start | bytes 1179656 | tf_op jit(solution)/shard_map/ppermute | solution.py:582
  120.9 11.6 %collective-permute-start.16 = (bf16[256,768]{1,0:T(8,128)(2,1)}, bf16[256,768]{1,0:T(8,128)(2,1)}, u32[]{:S(2)}, u32[]{:S(2)}) collective-permute-start(bf16[256,768]{1,0:T(8,128)(2,1)} %get-tuple-element.73), channel_id=1, source_target_pairs={{0,8},{8,0},{16,24},{24,16},{1,9},{9,1},{17,25},{25,17},{2,10},{10... | collective-permute-start | bytes 1179656 | tf_op jit(solution)/shard_map/ppermute | solution.py:582
  122.4 18.6 %collective-permute-start.23 = (bf16[512,384]{1,0:T(8,128)(2,1)}, bf16[512,384]{1,0:T(8,128)(2,1)}, u32[]{:S(2)}, u32[]{:S(2)}) collective-permute-start(bf16[512,384]{1,0:T(8,128)(2,1)} %copy-done.4), channel_id=1, source_target_pairs={{2,4},{3,5},{4,2},{5,3},{10,12},{11,13},{12,10},{13,11},{18,20},{1... | collective-permute-start | bytes 1179656 | tf_op jit(solution)/shard_map/ppermute | solution.py:633
  123.9 17.2 %collective-permute-start.24 = (bf16[512,384]{1,0:T(8,128)(2,1)}, bf16[512,384]{1,0:T(8,128)(2,1)}, u32[]{:S(2)}, u32[]{:S(2)}) collective-permute-start(bf16[512,384]{1,0:T(8,128)(2,1)} %collective-permute-done.18.refs_2_), channel_id=1, source_target_pairs={{2,0},{3,1},{4,6},{5,7},{10,8},{11,9},{12,14},{13,15},{18,16},{19,... | collective-permute-start | bytes 1179656 | tf_op jit(solution)/shard_map/ppermute | solution.py:634
  142.2 4.8 %collective-permute-start.26 = (bf16[1,512,384]{2,1,0:T(8,128)(2,1)S(1)}, bf16[1,512,384]{2,1,0:T(8,128)(2,1)S(1)}, u32[]{:S(2)}, u32[]{:S(2)}) collective-permute-start(bf16[1,512,384]{2,1,0:T(8,128)(2,1)S(1)} %get-tuple-element.82.own), channel_id=1, source_target_pairs={{0,1},{1,0},{2,3},{3,2},{4,5},{5,4},{6,7},{7,6},{8,9},{9,8},{10,11... | collective-permute-start | bytes 1179656 | tf_op jit(solution)/shard_map/ppermute | solution.py:588
  142.3 21.0 %collective-permute-start.20 = (bf16[512,384]{1,0:T(8,128)(2,1)S(1)}, bf16[512,384]{1,0:T(8,128)(2,1)S(1)}, u32[]{:S(2)}, u32[]{:S(2)}) collective-permute-start(bf16[512,384]{1,0:T(8,128)(2,1)S(1)} %get-tuple-element.77.refs_0_), channel_id=1, source_target_pairs={{0,4},{1,5},{2,6},{3,7},{4,0},{5,1},{6,2},{7,3},{8,12},{9,13},{10,... | collective-permute-start | bytes 1179656 | tf_op jit(solution)/shard_map/ppermute | solution.py:585
  145.0 18.3 %collective-permute-start.22 = (bf16[512,384]{1,0:T(8,128)(2,1)S(1)}, bf16[512,384]{1,0:T(8,128)(2,1)S(1)}, u32[]{:S(2)}, u32[]{:S(2)}) collective-permute-start(bf16[512,384]{1,0:T(8,128)(2,1)S(1)} %get-tuple-element.77.refs_0_), channel_id=1, source_target_pairs={{0,2},{1,3},{2,0},{3,1},{4,6},{5,7},{6,4},{7,5},{8,10},{9,11},{10,... | collective-permute-start | bytes 1179656 | tf_op jit(solution)/shard_map/ppermute | solution.py:585
  163.5 2.9 %collective-permute-start.27 = (bf16[3,512,384]{2,1,0:T(8,128)(2,1)S(1)}, bf16[3,512,384]{2,1,0:T(8,128)(2,1)S(1)}, u32[]{:S(2)}, u32[]{:S(2)}) collective-permute-start(bf16[3,512,384]{2,1,0:T(8,128)(2,1)S(1)} %get-tuple-element.86.own), channel_id=1, source_target_pairs={{0,1},{1,0},{2,3},{3,2},{4,5},{5,4},{6,7},{7,6},{8,9},{9,8},{10,11... | collective-permute-start | bytes 3538952 | tf_op jit(solution)/shard_map/ppermute | solution.py:588
  163.5 8.9 %collective-permute-start.19 = (bf16[512,384]{1,0:T(8,128)(2,1)S(1)}, bf16[512,384]{1,0:T(8,128)(2,1)S(1)}, u32[]{:S(2)}, u32[]{:S(2)}) collective-permute-start(bf16[512,384]{1,0:T(8,128)(2,1)S(1)} %get-tuple-element.77.refs_0_), channel_id=1, source_target_pairs={{2,4},{3,5},{4,2},{5,3},{10,12},{11,13},{12,10},{13,11},{18,20},{1... | collective-permute-start | bytes 1179656 | tf_op jit(solution)/shard_map/ppermute | solution.py:633
  164.2 14.4 %collective-permute-start.21 = (bf16[512,384]{1,0:T(8,128)(2,1)S(1)}, bf16[512,384]{1,0:T(8,128)(2,1)S(1)}, u32[]{:S(2)}, u32[]{:S(2)}) collective-permute-start(bf16[512,384]{1,0:T(8,128)(2,1)S(1)} %collective-permute-done.20.refs_2_), channel_id=1, source_target_pairs={{2,0},{3,1},{4,6},{5,7},{10,8},{11,9},{12,14},{13,15},{18,16},{19,... | collective-permute-start | bytes 1179656 | tf_op jit(solution)/shard_map/ppermute | solution.py:634
  178.7 1.8 collective-permute-start.28
  184.3 10.1 %collective-permute-start.31 = (bf16[128,1024]{1,0:T(8,128)(2,1)S(1)}, bf16[128,1024]{1,0:T(8,128)(2,1)S(1)}, u32[]{:S(2)}, u32[]{:S(2)}) collective-permute-start(bf16[128,1024]{1,0:T(8,128)(2,1)S(1)} %get-tuple-element.96), channel_id=1, source_target_pairs={{0,24},{8,16},{16,8},{24,0},{1,25},{9,17},{17,9},{25,1},{2,26},{10... | collective-permute-start | bytes 786440 | tf_op jit(solution)/shard_map/ppermute | solution.py:582
  185.8 13.4 %collective-permute-start.30 = (bf16[128,1024]{1,0:T(8,128)(2,1)S(1)}, bf16[128,1024]{1,0:T(8,128)(2,1)S(1)}, u32[]{:S(2)}, u32[]{:S(2)}) collective-permute-start(bf16[128,1024]{1,0:T(8,128)(2,1)S(1)} %get-tuple-element.95), channel_id=1, source_target_pairs={{0,16},{8,24},{16,0},{24,8},{1,17},{9,25},{17,1},{25,9},{2,18},{10... | collective-permute-start | bytes 786440 | tf_op jit(solution)/shard_map/ppermute | solution.py:582
  187.5 11.7 %collective-permute-start.29 = (bf16[128,1024]{1,0:T(8,128)(2,1)S(1)}, bf16[128,1024]{1,0:T(8,128)(2,1)S(1)}, u32[]{:S(2)}, u32[]{:S(2)}) collective-permute-start(bf16[128,1024]{1,0:T(8,128)(2,1)S(1)} %get-tuple-element.94), channel_id=1, source_target_pairs={{0,8},{8,0},{16,24},{24,16},{1,9},{9,1},{17,25},{25,17},{2,10},{10... | collective-permute-start | bytes 786440 | tf_op jit(solution)/shard_map/ppermute | solution.py:582
  (9 other events, 63.6 us)
